TPU v7x, 128 devices: a whole 4x4x4 slice. The times are simulated.
128 devices in a mesh: dp: 16 (over x, z), mp: 8 (over y, core).
Axes of the slice: x: 4, y: 4, z: 4, core: 2. Of those that a mesh axis runs over, the one named last changes fastest.
Arguments:
- tokens: bfloat16 [16, 512, 1536], P('dp'), may hold values from -6 to 6
- lengths: int32 [16], P('dp'), may hold values from 1 to 512, as said below
- cotangent: bfloat16 [16, 512, 1536], P('dp'), may hold values from -6 to 6
- joint_weight: float32 [1536, 2048], P('dp', 'mp'), may hold values from -0.15625 to 0.15625
- joint_moment: float32 [1536, 2048], P('dp', 'mp')
- joint_square: float32 [1536, 2048], P('dp', 'mp')
- mixer_weight: float32 [1536, 1536], P('dp', 'mp'), may hold values from -0.875 to 0.875
- mixer_moment: float32 [1536, 1536], P('dp', 'mp')
- mixer_square: float32 [1536, 1536], P('dp', 'mp')
- expand_weight: float32 [2, 1536, 8960], P(None, 'dp', 'mp')
- expand_moment: float32 [2, 1536, 8960], P(None, 'dp', 'mp')
- expand_square: float32 [2, 1536, 8960], P(None, 'dp', 'mp')
- shrink_weight: float32 [8960, 1536], P('mp', 'dp')
- shrink_moment: float32 [8960, 1536], P('mp', 'dp')
- shrink_square: float32 [8960, 1536], P('mp', 'dp')
- vector_params: float32 [5120], P(('dp', 'mp'))
- vector_moment: float32 [5120], P(('dp', 'mp'))
- vector_square: float32 [5120], P(('dp', 'mp'))
Outputs:
- output: float32 [16, 512, 1536], P('dp')
- input_grad: float32 [16, 512, 1536], P('dp')
- grad_norm: float32 [], replicated
- joint_next: float32 [1536, 2048], P('dp', 'mp')
- joint_moment_next: float32 [1536, 2048], P('dp', 'mp')
- joint_square_next: float32 [1536, 2048], P('dp', 'mp')
- mixer_next: float32 [1536, 1536], P('dp', 'mp')
- mixer_moment_next: float32 [1536, 1536], P('dp', 'mp')
- mixer_square_next: float32 [1536, 1536], P('dp', 'mp')
- expand_next: float32 [2, 1536, 8960], P(None, 'dp', 'mp')
- expand_moment_next: float32 [2, 1536, 8960], P(None, 'dp', 'mp')
- expand_square_next: float32 [2, 1536, 8960], P(None, 'dp', 'mp')
- shrink_next: float32 [8960, 1536], P('mp', 'dp')
- shrink_moment_next: float32 [8960, 1536], P('mp', 'dp')
- shrink_square_next: float32 [8960, 1536], P('mp', 'dp')
- vector_next: float32 [5120], P(('dp', 'mp'))
- vector_moment_next: float32 [5120], P(('dp', 'mp'))
- vector_square_next: float32 [5120], P(('dp', 'mp'))
Inputs may be any that keep to these rules, and one draw needn't show every extreme that they name: `lengths`: valid positions of each row, counted from its start; some row is full.
All inputs are finite; a program needn't handle non-finite values.
Results may differ from a plain program's by a relative error of at most 0.02.
Values may be sent and summed in bfloat16 or wider, within the bound.
No kernel may reach another device: no remote copies, remote signals or barrier semaphores. Data moves between devices by JAX's collectives and lax.ppermute only.
A program may use at most 192 MiB of HBM per device.

v0:
```python
import jax
import jax.numpy as jnp
from jax import lax
from jax.sharding import PartitionSpec as P

QUERY_HEADS = 12
KEY_VALUE_HEADS = 2
HEAD_SIZE = 128
STEP = 5


EPS_NORM = 1e-06
ROPE_BASE = 1000000.0
MAX_NORM = 1.0
BETA_ONE = 0.9
BETA_TWO = 0.95
ADAM_EPS = 1e-08
DECAY = 0.1
RATE_MATRIX = 0.06
RATE_VECTOR = 0.8
MASKED = -1e30


def tables(length_all, head):
    places = jnp.arange(length_all, dtype=jnp.float32)
    freq = ROPE_BASE ** (-jnp.arange(0, head, 2, dtype=jnp.float32) / head)
    angle = places[:, None] * freq[None, :]
    cosine_table = jnp.concatenate([jnp.cos(angle), jnp.cos(angle)], -1)
    sine_table = jnp.concatenate([jnp.sin(angle), jnp.sin(angle)], -1)
    return (cosine_table, sine_table)


def apply_rotary(value_rows, cosine_table, sine_table):
    half = value_rows.shape[-1] // 2
    turned = jnp.concatenate([-value_rows[..., half:], value_rows[..., :half]], -1)
    return value_rows * cosine_table[:, None, :] + turned * sine_table[:, None, :]


def unrotate(grads, cosine_table, sine_table):
    half = grads.shape[-1] // 2
    scaled = grads * sine_table[:, None, :]
    turned = jnp.concatenate([scaled[..., half:], -scaled[..., :half]], -1)
    return grads * cosine_table[:, None, :] + turned


def inner_rows(left, right):
    return lax.dot_general(
        left, right, (((0,), (0,)), ((), ())), preferred_element_type=jnp.float32
    )


def outer_columns(left, right):
    return lax.dot_general(
        left, right, (((1,), (1,)), ((), ())), preferred_element_type=jnp.float32
    )


def unstack(block, outer, inner):
    rows_each = block.shape[0] // (outer * inner)
    cols_each = block.shape[1]
    return (
        block.reshape(outer, inner, rows_each, cols_each)
        .transpose(0, 2, 1, 3)
        .reshape(outer * rows_each, inner * cols_each)
    )


def restack(full, outer, inner):
    rows_each = full.shape[0] // outer
    cols_each = full.shape[1] // inner
    return (
        full.reshape(outer, rows_each, inner, cols_each)
        .transpose(0, 2, 1, 3)
        .reshape(outer * inner * rows_each, cols_each)
    )


def norm_back(value_rows, scale, gain, grad):
    scaled = gain * grad
    return scale * scaled - value_rows * scale * scale * scale * jnp.mean(
        scaled * value_rows, -1, keepdims=True
    )


def adam_step(weight, grad, moment, square, rate, decay):
    moment_next = BETA_ONE * moment + (1.0 - BETA_ONE) * grad
    square_next = BETA_TWO * square + (1.0 - BETA_TWO) * grad * grad
    first_hat = moment_next / (1.0 - BETA_ONE**STEP)
    second_hat = square_next / (1.0 - BETA_TWO**STEP)
    weight_next = weight - rate * (first_hat / (jnp.sqrt(second_hat) + ADAM_EPS) + decay * weight)
    return (weight_next, moment_next, square_next)


def masked_scores(query_rows, key_rows, allowed, scale):
    raw = (
        jnp.einsum("qhgd,khd->hgqk", query_rows, key_rows, preferred_element_type=jnp.float32)
        * scale
    )
    return jnp.where(allowed, raw, MASKED)


def attend_forward(query_rows, key_rows, value_rows, allowed, scale, width_out):
    scores = masked_scores(query_rows, key_rows, allowed, scale)
    top = jnp.max(scores, -1, keepdims=True)
    expo = jnp.exp(scores - top)
    total = jnp.sum(expo, -1, keepdims=True)
    probs_low = (expo / total).astype(jnp.bfloat16)
    log_total = top + jnp.log(total)
    attended = jnp.einsum(
        "hgqk,khd->qhgd", probs_low, value_rows, preferred_element_type=jnp.float32
    )
    return (attended.reshape(query_rows.shape[0], width_out).astype(jnp.bfloat16), log_total)


def attend_backward(query_rows, key_rows, value_rows, allowed, scale, log_total, attended_grad):
    scores = masked_scores(query_rows, key_rows, allowed, scale)
    probs = jnp.exp(scores - log_total)
    probs_low = probs.astype(jnp.bfloat16)
    value_grad = jnp.einsum(
        "hgqk,qhgd->khd", probs_low, attended_grad, preferred_element_type=jnp.float32
    )
    prob_grad = jnp.einsum(
        "qhgd,khd->hgqk", attended_grad, value_rows, preferred_element_type=jnp.float32
    )
    score_grad = (probs * (prob_grad - jnp.sum(probs * prob_grad, -1, keepdims=True))).astype(
        jnp.bfloat16
    )
    query_grad = (
        jnp.einsum("hgqk,khd->qhgd", score_grad, key_rows, preferred_element_type=jnp.float32)
        * scale
    )
    key_grad = (
        jnp.einsum("hgqk,qhgd->khd", score_grad, query_rows, preferred_element_type=jnp.float32)
        * scale
    )
    return (query_grad, key_grad, value_grad)


def body(
    tokens,
    lengths,
    cotangent,
    joint_weight,
    joint_moment,
    joint_square,
    mixer_weight,
    mixer_moment,
    mixer_square,
    expand_weight,
    expand_moment,
    expand_square,
    shrink_weight,
    shrink_moment,
    shrink_square,
    vector_params,
    vector_moment,
    vector_square,
):
    lanes_dp = lax.axis_size("dp")
    lanes_mp = lax.axis_size("mp")
    sequence_length = tokens.shape[1]
    width = tokens.shape[2]
    query_group = QUERY_HEADS // KEY_VALUE_HEADS
    attention_width = QUERY_HEADS * HEAD_SIZE
    key_value_width = KEY_VALUE_HEADS * HEAD_SIZE
    scale = HEAD_SIZE ** (-0.5)
    inputs = tokens[0].astype(jnp.float32)
    length = lengths[0]
    joint_stack, mixer_stack = (
        lax.all_gather(joint_weight.astype(jnp.bfloat16), ("dp", "mp"), axis=0, tiled=True),
        lax.all_gather(mixer_weight.astype(jnp.bfloat16), ("dp", "mp"), axis=0, tiled=True),
    )
    joint_full = unstack(joint_stack, lanes_dp, lanes_mp)
    mixer_gathered = unstack(mixer_stack, lanes_dp, lanes_mp)
    vector_full = lax.all_gather(vector_params, ("dp", "mp"), axis=0, tiled=True)
    gain_first = vector_full[:width]
    gain_second = vector_full[width : 2 * width]
    bias = vector_full[2 * width :]
    expand_full, shrink_full = (
        lax.all_gather(expand_weight.astype(jnp.bfloat16), "dp", axis=1, tiled=True),
        lax.all_gather(shrink_weight.astype(jnp.bfloat16), "dp", axis=1, tiled=True),
    )
    cosine_table, sine_table = tables(sequence_length, HEAD_SIZE)
    places = jnp.arange(sequence_length)
    valid = (places < length)[:, None]
    piece = sequence_length // lanes_mp
    start = lax.axis_index("mp") * piece

    def own_rows(array):
        return lax.dynamic_slice_in_dim(array, start, piece, 0)

    scale_first = lax.rsqrt(jnp.mean(inputs * inputs, -1, keepdims=True) + EPS_NORM)
    normed = (inputs * scale_first * gain_first).astype(jnp.bfloat16)
    back = jnp.where(valid, cotangent[0].astype(jnp.float32), 0.0)
    allowed = (places[:, None] >= places[None, :]) & (places[None, :] < length)
    joint_input = jnp.dot(normed, joint_full, preferred_element_type=jnp.float32) + bias
    query_rows = (
        apply_rotary(
            joint_input[:, :attention_width].reshape(sequence_length, QUERY_HEADS, HEAD_SIZE),
            cosine_table,
            sine_table,
        )
        .astype(jnp.bfloat16)
        .reshape(sequence_length, KEY_VALUE_HEADS, query_group, HEAD_SIZE)
    )
    key_rows = apply_rotary(
        joint_input[:, attention_width : attention_width + key_value_width].reshape(
            sequence_length, KEY_VALUE_HEADS, HEAD_SIZE
        ),
        cosine_table,
        sine_table,
    ).astype(jnp.bfloat16)
    value_rows = (
        joint_input[:, attention_width + key_value_width :]
        .reshape(sequence_length, KEY_VALUE_HEADS, HEAD_SIZE)
        .astype(jnp.bfloat16)
    )
    attended, log_total = attend_forward(
        query_rows, key_rows, value_rows, allowed, scale, attention_width
    )
    hidden = inputs + jnp.dot(attended, mixer_gathered, preferred_element_type=jnp.float32)
    scale_second = lax.rsqrt(jnp.mean(hidden * hidden, -1, keepdims=True) + EPS_NORM)
    normed_second = (hidden * scale_second * gain_second).astype(jnp.bfloat16)
    gate = jnp.dot(normed_second, expand_full[0], preferred_element_type=jnp.float32)
    lifted = jnp.dot(normed_second, expand_full[1], preferred_element_type=jnp.float32)
    sigma = jax.nn.sigmoid(gate)
    swished = gate * sigma
    active = (swished * lifted).astype(jnp.bfloat16)
    partial_out = jnp.dot(active, shrink_full, preferred_element_type=jnp.float32)
    feed = lax.psum(partial_out.astype(jnp.bfloat16), "mp").astype(jnp.float32)
    output = jnp.where(valid, hidden + feed, 0.0)
    back_low = back.astype(jnp.bfloat16)
    expand_back, shrink_back = (expand_full, shrink_full)
    shrink_grad = inner_rows(active, back_low)
    active_grad = outer_columns(back_low, shrink_back)
    gate_grad = (active_grad * lifted * sigma * (1.0 + gate * (1.0 - sigma))).astype(jnp.bfloat16)
    lifted_grad = (active_grad * swished).astype(jnp.bfloat16)
    expand_grad = jnp.stack(
        [inner_rows(normed_second, gate_grad), inner_rows(normed_second, lifted_grad)]
    )
    normed_second_part = outer_columns(gate_grad, expand_back[0]) + outer_columns(
        lifted_grad, expand_back[1]
    )
    gain_second_part = jnp.sum(normed_second_part * hidden * scale_second, 0)
    normed_second_grad = lax.psum(normed_second_part, "mp")
    hidden_grad = back + norm_back(hidden, scale_second, gain_second, normed_second_grad)
    hidden_reduced = hidden_grad.astype(jnp.bfloat16)
    attended_grad = (
        outer_columns(hidden_reduced, mixer_gathered)
        .astype(jnp.bfloat16)
        .reshape(sequence_length, KEY_VALUE_HEADS, query_group, HEAD_SIZE)
    )
    query_grad, key_grad, value_grad = attend_backward(
        query_rows, key_rows, value_rows, allowed, scale, log_total, attended_grad
    )
    joint_grad = jnp.concatenate(
        [
            unrotate(
                query_grad.reshape(sequence_length, QUERY_HEADS, HEAD_SIZE),
                cosine_table,
                sine_table,
            ).reshape(sequence_length, attention_width),
            unrotate(key_grad, cosine_table, sine_table).reshape(sequence_length, key_value_width),
            value_grad.reshape(sequence_length, key_value_width),
        ],
        1,
    ).astype(jnp.bfloat16)
    normed_grad = outer_columns(joint_grad, joint_full)
    input_grad = hidden_grad + norm_back(inputs, scale_first, gain_first, normed_grad)
    normed_own = own_rows(normed)
    joint_grad_own = own_rows(joint_grad)
    attended_own = own_rows(attended)
    hidden_low_own = own_rows(hidden_reduced)
    gain_first_part = jnp.sum(own_rows(normed_grad * inputs * scale_first), 0)
    bias_part = jnp.sum(joint_grad_own.astype(jnp.float32), 0)
    vector_part = jnp.concatenate([gain_first_part, gain_second_part, bias_part])
    expand_shard, shrink_shard = (
        lax.psum_scatter(
            expand_grad.astype(jnp.bfloat16), "dp", scatter_dimension=1, tiled=True
        ).astype(jnp.float32),
        lax.psum_scatter(
            shrink_grad.astype(jnp.bfloat16), "dp", scatter_dimension=1, tiled=True
        ).astype(jnp.float32),
    )
    joint_part = inner_rows(normed_own, joint_grad_own)
    mixer_part = inner_rows(attended_own, hidden_low_own)
    joint_shard, mixer_shard, vector_shard = (
        lax.psum_scatter(
            restack(joint_part, lanes_dp, lanes_mp), ("dp", "mp"), scatter_dimension=0, tiled=True
        ),
        lax.psum_scatter(
            restack(mixer_part, lanes_dp, lanes_mp), ("dp", "mp"), scatter_dimension=0, tiled=True
        ),
        lax.psum_scatter(vector_part, ("dp", "mp"), scatter_dimension=0, tiled=True),
    )
    squares = (
        jnp.sum(joint_shard * joint_shard)
        + jnp.sum(mixer_shard * mixer_shard)
        + jnp.sum(expand_shard * expand_shard)
        + jnp.sum(shrink_shard * shrink_shard)
        + jnp.sum(vector_shard * vector_shard)
    )
    grad_norm = jnp.sqrt(lax.psum(squares, ("dp", "mp")))
    clip = jnp.minimum(1.0, MAX_NORM / (grad_norm + 1e-06))
    joint_next, joint_moment_next, joint_square_next = adam_step(
        joint_weight, clip * joint_shard, joint_moment, joint_square, RATE_MATRIX, DECAY
    )
    mixer_next, mixer_moment_next, mixer_square_next = adam_step(
        mixer_weight, clip * mixer_shard, mixer_moment, mixer_square, RATE_MATRIX, DECAY
    )
    expand_next, expand_moment_next, expand_square_next = adam_step(
        expand_weight, clip * expand_shard, expand_moment, expand_square, RATE_MATRIX, DECAY
    )
    shrink_next, shrink_moment_next, shrink_square_next = adam_step(
        shrink_weight, clip * shrink_shard, shrink_moment, shrink_square, RATE_MATRIX, DECAY
    )
    vector_next, vector_moment_next, vector_square_next = adam_step(
        vector_params, clip * vector_shard, vector_moment, vector_square, RATE_VECTOR, 0.0
    )
    return (
        output[None],
        input_grad[None],
        grad_norm,
        joint_next,
        joint_moment_next,
        joint_square_next,
        mixer_next,
        mixer_moment_next,
        mixer_square_next,
        expand_next,
        expand_moment_next,
        expand_square_next,
        shrink_next,
        shrink_moment_next,
        shrink_square_next,
        vector_next,
        vector_moment_next,
        vector_square_next,
    )


def solution(mesh):
    placed = (
        P("dp", None, None),
        P("dp"),
        P("dp", None, None),
        P("dp", "mp"),
        P("dp", "mp"),
        P("dp", "mp"),
        P("dp", "mp"),
        P("dp", "mp"),
        P("dp", "mp"),
        P(None, "dp", "mp"),
        P(None, "dp", "mp"),
        P(None, "dp", "mp"),
        P("mp", "dp"),
        P("mp", "dp"),
        P("mp", "dp"),
        P(("dp", "mp")),
        P(("dp", "mp")),
        P(("dp", "mp")),
    )
    return jax.shard_map(
        body,
        mesh=mesh,
        in_specs=placed,
        out_specs=(
            P("dp", None, None),
            P("dp", None, None),
            P(),
            P("dp", "mp"),
            P("dp", "mp"),
            P("dp", "mp"),
            P("dp", "mp"),
            P("dp", "mp"),
            P("dp", "mp"),
            P(None, "dp", "mp"),
            P(None, "dp", "mp"),
            P(None, "dp", "mp"),
            P("mp", "dp"),
            P("mp", "dp"),
            P("mp", "dp"),
            P(("dp", "mp")),
            P(("dp", "mp")),
            P(("dp", "mp")),
        ),
        check_vma=False,
    )
```

profile of v0, /device:TPU:1, one launch (start us, length us, event | category | flops | bytes accessed | tf_op | source)
XLA Modules:
  0.0 1171.3 jit_solution(1799002827221928887)
XLA Ops:
  15.3 69.9 %all-reduce = f32[5120]{0:T(1024)S(1)} all-reduce(f32[5120]{0:T(1024)S(1)} %dynamic-update-slice), channel_id=1, replica_groups=mesh['dp'=16,'mp'=8] {'dp','mp'}, use_global_device_ids=true, to_apply=%add | all-reduce | flops 5120 | bytes 40960
  88.0 9.8 copy.168
  97.8 10.8 reshape.177
  108.5 44.7 %all-gather.5.cloned.1.call-done = bf16[12288,256]{1,0:T(8,128)(2,1)} async-done(((bf16[96,256]{1,0:T(8,128)(2,1)}), bf16[12288,256]{1,0:T(8,128)(2,1)}) %all-gather.5.cloned.1.call-update) | async-done | bytes 6291472 | tf_op jit(solution)/shard_map/all_gather | solution.py:170
  153.3 7.1 copy.114
  198.4 19.9 %all-gather.9.cloned.1.call-done = bf16[2,1536,1120]{2,1,0:T(8,128)(2,1)} async-done(((bf16[2,96,1120]{2,1,0:T(8,128)(2,1)}), bf16[2,1536,1120]{2,1,0:T(8,128)(2,1)}) %all-gather.9.cloned.1.call-update) | async-done | bytes 6881296 | tf_op jit(solution)/shard_map/all_gather | solution.py:180
  218.3 6.0 fusion.26
  227.7 41.3 %all-gather.11.cloned.1.call-done = bf16[1120,1536]{0,1:T(8,128)(2,1)} async-done(((bf16[1120,96]{0,1:T(8,128)(2,1)}), bf16[1120,1536]{0,1:T(8,128)(2,1)}) %all-gather.11.cloned.1.call-update) | async-done | bytes 3440656 | tf_op jit(solution)/shard_map/all_gather | solution.py:181
  268.9 7.8 multiply_convert_fusion.1
  309.2 18.2 %copy.133 = bf16[2,1536,1120]{2,0,1:T(2,128)(2,1)} copy(bf16[2,1536,1120]{1,2,0:T(8,128)(2,1)} %pad_maximum_fusion) | data formatting | bytes 13762560 | tf_op jit(solution)/shard_map/stack | solution.py:238
  327.9 26.7 %all-reduce.9.cloned.1.call-done = f32[512,1536]{1,0:T(8,128)} async-done(((f32[512,1536]{1,0:T(8,128)}), f32[512,1536]{1,0:T(8,128)}) %all-reduce.9.cloned.1.call-update) | async-done | bytes 3145744 | tf_op jit(solution)/shard_map/psum | solution.py:245
  358.2 62.9 %all-reduce.7.cloned.1.call-done = bf16[512,1536]{1,0:T(8,128)(2,1)} async-done(((bf16[512,1536]{1,0:T(8,128)(2,1)}), bf16[512,1536]{1,0:T(8,128)(2,1)}) %all-reduce.7.cloned.1.call-update) | async-done | bytes 1572880 | tf_op jit(solution)/shard_map/psum | solution.py:230
  433.7 12.6 %reshape.185 = f32[16,96,8,192]{3,2,1,0:T(8,128)} reshape(f32[1536,1536]{1,0:T(8,128)} %fusion.60) | data formatting | bytes 18874368 | tf_op jit(solution)/shard_map/reshape | solution.py:72
  446.3 13.2 %copy.132 = f32[16,8,96,192]{3,2,1,0:T(8,128)} copy(f32[16,8,96,192]{3,1,2,0:T(8,128)} %bitcast.178) | data formatting | bytes 18874368 | tf_op jit(solution)/shard_map/transpose | solution.py:73
  466.7 11.6 fusion
  480.0 7.2 fusion.2
  508.9 7.6 fusion.52
  516.5 15.5 %copy.155 = f32[192,8,8,256]{3,2,1,0:T(8,128)} copy(f32[192,8,8,256]{3,1,2,0:T(8,128)} %bitcast.174) | data formatting | bytes 25165824
  532.0 10.5 bitcast_bitcast_fusion
  542.5 13.6 %copy.131 = f32[16,8,96,256]{3,2,1,0:T(8,128)} copy(f32[16,8,96,256]{3,1,2,0:T(8,128)} %bitcast_bitcast_fusion) | data formatting | bytes 25165824 | tf_op jit(solution)/shard_map/transpose | solution.py:73
  561.1 68.6 %all-reduce.2 = f32[5120]{0:T(1024)S(1)} all-reduce(f32[5120]{0:T(1024)S(1)} %pad_maximum_fusion.5), channel_id=6, replica_groups=mesh['dp'=16,'mp'=8] {'dp','mp'}, use_global_device_ids=true, to_apply=%region_20.21.clone | all-reduce | flops 5120 | bytes 40960
  637.7 222.8 %reduce-scatter.6.cloned.1.call-done = f32[96,192]{1,0:T(8,128)} async-done(((f32[12288,192]{1,0:T(8,128)}), f32[96,192]{1,0:T(8,128)}) %reduce-scatter.6.cloned.1.call-update) | async-done | bytes 73744 | tf_op jit(solution)/shard_map/reduce_scatter | solution.py:291
  862.0 223.3 %reduce-scatter.4.cloned.1.call-done = f32[96,256]{1,0:T(8,128)} async-done(((f32[12288,256]{1,0:T(8,128)}), f32[96,256]{1,0:T(8,128)}) %reduce-scatter.4.cloned.1.call-update) | async-done | bytes 98320 | tf_op jit(solution)/shard_map/reduce_scatter | solution.py:288
  1090.1 64.3 %psum.23 = f32[]{:T(128)} all-reduce(f32[]{:T(128)S(6)} %add.200), channel_id=1, replica_groups=mesh['dp'=16,'mp'=8] {'dp','mp'}, use_global_device_ids=true, to_apply=%region_22.23 | all-reduce | flops 1 | bytes 8 | tf_op jit(solution)/shard_map/psum | solution.py:303
  (218 shorter events, 153.8 us)
Async XLA Ops:
  7.2 78.8 %copy-start.3 = (bf16[1,512,1536]{2,1,0:T(8,128)(2,1)S(1)}, bf16[1,512,1536]{2,1,0:T(8,128)(2,1)}, u32[]{:S(2)}) copy-start(bf16[1,512,1536]{2,1,0:T(8,128)(2,1)} %param.18) | copy-start | bytes 4718596
  7.2 80.8 %all-gather.7.cloned.1.call-start = ((), (), s32[]{:S(2)}) async-start(), calls=%async_computation.4 | async-start | bytes 6340608 | tf_op jit(solution)/shard_map/all_gather | solution.py:171
  8.9 144.4 %all-gather.5.cloned.1.call-start = ((), (), s32[]{:S(2)}) async-start(), calls=%async_computation.3 | async-start | bytes 6340608 | tf_op jit(solution)/shard_map/all_gather | solution.py:170
  10.5 207.8 %all-gather.9.cloned.1.call-start = ((), (), s32[]{:S(2)}) async-start(), calls=%async_computation.5 | async-start | bytes 7520256 | tf_op jit(solution)/shard_map/all_gather | solution.py:180
  12.6 256.4 %all-gather.11.cloned.1.call-start = ((), (), s32[]{:S(2)}) async-start(), calls=%async_computation.6 | async-start | bytes 3760128 | tf_op jit(solution)/shard_map/all_gather | solution.py:181
  14.4 340.2 %all-reduce.9.cloned.1.call-start = ((), (), s32[]{:S(2)}) async-start(), calls=%async_computation.8 | async-start | bytes 6291456 | tf_op jit(solution)/shard_map/psum | solution.py:245
  85.2 12.6 %copy-start.38 = (f32[5120]{0:T(1024)}, f32[5120]{0:T(1024)S(1)}, u32[]{:S(2)}) copy-start(f32[5120]{0:T(1024)S(1)} %all-reduce) | copy-start | bytes 61444
  85.2 77.9 %copy-start.36 = (f32[1536]{0:T(1024)}, f32[1536]{0:T(1024)S(1)}, u32[]{:S(2)}) copy-start(f32[1536]{0:T(1024)S(1)} %get-tuple-element.110) | copy-start | bytes 18436
  86.4 76.7 %copy-start.42 = (f32[512]{0:T(512)}, f32[512]{0:T(512)S(1)}, u32[]{:S(2)}) copy-start(f32[512]{0:T(512)S(1)} %add_rsqrt_fusion.1) | copy-start | bytes 6148
  287.9 133.2 %all-reduce.7.cloned.1.call-start = ((), (), s32[]{:S(2)}) async-start(), calls=%async_computation.7 | async-start | bytes 3145728 | tf_op jit(solution)/shard_map/psum | solution.py:230
  294.0 336.4 %reduce-scatter.8.cloned.1.call-start = ((), (), s32[]{:S(2)}) async-start(), calls=%async_computation.11 | async-start | bytes 3760128 | tf_op jit(solution)/shard_map/reduce_scatter | solution.py:281
  299.9 335.6 %all-reduce.11.cloned.1.call-start = ((), (), s32[]{:S(2)}) async-start(), calls=%async_computation.12 | async-start | bytes 14155776
  327.4 533.0 %reduce-scatter.6.cloned.1.call-start = ((), (), s32[]{:S(2)}) async-start(), calls=%async_computation.10 | async-start | bytes 12681216 | tf_op jit(solution)/shard_map/reduce_scatter | solution.py:291
  459.5 625.8 %reduce-scatter.4.cloned.1.call-start = ((), (), s32[]{:S(2)}) async-start(), calls=%async_computation.9 | async-start | bytes 12681216 | tf_op jit(solution)/shard_map/reduce_scatter | solution.py:288
  466.6 11.6 copy-start.8
  466.7 11.6 slice-start
  466.7 13.4 %slice-start.2 = ((s8[12582912]{0:T(1024)(128)(4,1)}), s8[4194304]{0:T(1024)(128)(4,1)S(1)}, s32[]{:S(2)}) async-start(s8[12582912]{0:T(1024)(128)(4,1)} %bitcast.172), calls=%async_computation.15 | async-start | bytes 8388608
  558.0 597.2 %copy-start.17 = (f32[2,96,1120]{2,1,0:T(8,128)S(1)}, f32[2,96,1120]{2,1,0:T(8,128)}, u32[]{:S(2)}) copy-start(f32[2,96,1120]{2,1,0:T(8,128)} %param.27) | copy-start | bytes 2580484
  558.0 597.2 %copy-start.29 = (f32[2,96,1120]{2,1,0:T(8,128)S(1)}, f32[2,96,1120]{2,1,0:T(8,128)}, u32[]{:S(2)}) copy-start(f32[2,96,1120]{2,1,0:T(8,128)} %param.28) | copy-start | bytes 2580484
  636.8 521.7 %copy-start.44 = (f32[40]{0:T(128)S(1)}, f32[40]{0:T(128)}, u32[]{:S(2)}) copy-start(f32[40]{0:T(128)} %param.33) | copy-start | bytes 484
  636.8 521.7 %copy-start.45 = (f32[40]{0:T(128)S(1)}, f32[40]{0:T(128)}, u32[]{:S(2)}) copy-start(f32[40]{0:T(128)} %param.34) | copy-start | bytes 484
  636.8 521.7 %copy-start.46 = (f32[40]{0:T(128)S(1)}, f32[40]{0:T(128)}, u32[]{:S(2)}) copy-start(f32[40]{0:T(128)} %param.35) | copy-start | bytes 484
  636.9 522.3 %copy-start.32 = (f32[96,256]{1,0:T(8,128)S(1)}, f32[96,256]{1,0:T(8,128)}, u32[]{:S(2)}) copy-start(f32[96,256]{1,0:T(8,128)} %param.21) | copy-start | bytes 294916
  1085.3 73.9 %copy-start.35 = (f32[96,256]{1,0:T(8,128)S(1)}, f32[96,256]{1,0:T(8,128)}, u32[]{:S(2)}) copy-start(f32[96,256]{1,0:T(8,128)} %reduce-scatter.4.cloned.1.call-done) | copy-start | bytes 294916
  (44 other events, 187.8 us)
Sparse Core Ops, SparseCore 0:
  11.7 72.3 all-gather.6
  87.8 65.4 all-gather.4
  156.0 62.2 all-gather.8
  220.3 48.5 all-gather.10
  288.0 66.5 all-reduce.8
  357.4 63.6 all-reduce.6
  424.5 76.1 reduce-scatter.7
  504.2 131.2 all-reduce.10
  641.3 219.1 reduce-scatter.5
  866.1 219.1 reduce-scatter.3
where the time goes:
time: 1180 us; the launch traced here: 1170 us
  waiting for transfers between devices  645 us (55%)
  blocking collectives  203 us (17%)
  local copies, waits for them, and re-layouts  139 us (12%)
  matrix products  103 us (9%)
  other arithmetic  58.8 us (5%)
  between operations  21.9 us (2%)
    reduce_scatter x1, waiting for transfers between devices, body(): lax.psum_scatter(restack(joint_part, lanes_dp, lanes_mp), ('dp', 'mp'), s...  223 us
    reduce_scatter x1, waiting for transfers between devices, body(): lax.psum_scatter(restack(mixer_part, lanes_dp, lanes_mp), ('dp', 'mp'), s...  223 us
    unnamed x2, blocking collectives  139 us
    psum x1, blocking collectives, body(): grad_norm = jnp.sqrt(lax.psum(squares, ('dp', 'mp')))  64.3 us
    psum x1, waiting for transfers between devices, body(): feed = lax.psum(partial_out.astype(jnp.bfloat16), 'mp').astype(jnp.float32)  62.9 us
    all_gather x1, waiting for transfers between devices, body(): lax.all_gather(joint_weight.astype(jnp.bfloat16), ('dp', 'mp'), axis=0, t...  44.7 us
    all_gather x1, waiting for transfers between devices, body(): lax.all_gather(shrink_weight.astype(jnp.bfloat16), 'dp', axis=1, tiled=True)  41.3 us
    transpose x3, local copies, waits for them, and re-layouts, restack(): return full.reshape(outer, rows_each, inner, cols_each).transpose(0, 2, 1...  37.3 us
  transfers between devices with their start and end apart: 10, of which 8 were waited for; matrix products, arithmetic and copies ran while one was open for 22% of the time, Pallas kernels for 0%

commit v1 on v0

v1 whole, which is shorter than its diff:
```python
import jax
import jax.numpy as jnp
import numpy as np
from jax import lax
from jax.experimental import pallas as pl
from jax.experimental.pallas import tpu as pltpu
from jax.sharding import PartitionSpec as P

QUERY_HEADS = 12
KEY_VALUE_HEADS = 2
HEAD = 128
STEP = 5
EPS_NORM = 1e-06
ROPE_BASE = 1000000.0
MAX_NORM = 1.0
BETA_ONE = 0.9
BETA_TWO = 0.95
ADAM_EPS = 1e-08
DECAY = 0.1
RATE_MATRIX = 0.06
RATE_VECTOR = 0.8
MASKED = -1e30

T = 512
HALF = 256
PART = 64
D = 1536
FF = 1120
FP = 1152
DP = 16
MP = 8
ROWS = D // DP
JC = 256
MC = 192
KEY_AT = 6
SCALE = HEAD ** (-0.5)

f32 = jnp.float32
bf16 = jnp.bfloat16
VM = pl.BlockSpec(memory_space=pltpu.VMEM)
SM = pl.BlockSpec(memory_space=pltpu.SMEM)
MiB = 1 << 20
SMALL = pl.CostEstimate(flops=1, bytes_accessed=1, transcendentals=0)


def shift_y(v, k):
    return lax.ppermute(v, "mp", [(i, (i + 2 * k) % MP) for i in range(MP)])


def from_last_chip(v, k):
    return lax.ppermute(v, "mp", [(i, (i + 2 * k) % MP) for i in (MP - 2, MP - 1)])


def swap_core(v):
    return lax.ppermute(v, "mp", [(i, i ^ 1) for i in range(MP)])


def exchange(v, axis):
    return lax.all_to_all(v, axis, split_axis=0, concat_axis=0, tiled=True)


RELATIVE = (0, -1, 1, 2)


def gather(shift, v):
    return [v, shift(v, 1), shift(v, -1), shift(v, 2)]


def nn(a, b):
    return lax.dot_general(a, b, (((1,), (0,)), ((), ())), preferred_element_type=f32)


def nt(a, b):
    return lax.dot_general(a, b, (((1,), (1,)), ((), ())), preferred_element_type=f32)


def tn(a, b):
    return lax.dot_general(a, b, (((0,), (0,)), ((), ())), preferred_element_type=f32)


def whole(body, outs, args, scratch=(), limit=60, after=()):
    n = len(args)

    def bare(*refs):
        body(*refs[:n], *refs[n + len(after) :])

    return pl.pallas_call(
        bare,
        out_shape=[jax.ShapeDtypeStruct(s, d) for s, d in outs],
        in_specs=[SM] + [VM] * (n - 1) + [pl.BlockSpec(memory_space=pl.ANY)] * len(after),
        out_specs=[VM] * len(outs),
        scratch_shapes=list(scratch),
        compiler_params=pltpu.CompilerParams(vmem_limit_bytes=limit * MiB),
        cost_estimate=SMALL,
    )(*args, *after)


def at(start, size, step):
    return pl.ds(pl.multiple_of(start, step), size)


def prepare(ids, cotangent, tok, back, back_t, back_part, tok_part):
    length, y, c = ids[0], ids[3], ids[4]
    for h in range(2):
        start = HALF * ((c + h) % 2)
        t = lax.broadcasted_iota(jnp.int32, (HALF, 1), 0) + start
        v = cotangent[at(start, HALF, HALF), :]
        v = jnp.where(t < length, v, jnp.zeros_like(v))
        back[HALF * h : HALF * (h + 1), :] = v
        back_t[:, HALF * h : HALF * (h + 1)] = v.T
    back_part[...] = back[at(PART * y, PART, PART), :]
    tok_part[...] = tok[at(HALF * c + PART * y, PART, PART), :]


def kept(i, n, length):
    t = lax.broadcasted_iota(jnp.int32, (128, n), 0) + 128 * i
    s = lax.broadcasted_iota(jnp.int32, (128, n), 1)
    return (s <= t) & (s < length)


def attend(
    ids, tok, gain, bias, cosine, sine, query_w, pair_w,
    normed, heads, out, lse, w,
):
    w[:, :JC] = query_w[:, :ROWS, :].reshape(D, JC)
    w[:, JC:] = pair_w[:, :ROWS, :].reshape(D, JC)

    @pl.loop(0, T // 128)
    def _(i):
        rows = at(i * 128, 128, 128)
        x = tok[rows, :].astype(f32)
        s = lax.rsqrt(jnp.mean(x * x, -1, keepdims=True) + EPS_NORM)
        n = (x * s * gain[...]).astype(bf16)
        normed[rows, :] = n
        j = nn(n, w[...]) + bias[...]
        for h in range(4):
            cols = slice(HEAD * h, HEAD * (h + 1))
            u = j[:, cols]
            if h < 3:
                u = u * cosine[rows, :] + pltpu.roll(u, HEAD // 2, 1) * sine[rows, :]
            heads[rows, cols] = u.astype(bf16)

    for h in range(2):
        for i in range(4):
            n = 128 * (i + 1)
            q = heads[128 * i : n, HEAD * h : HEAD * (h + 1)]
            k, v = heads[:n, 2 * HEAD : 3 * HEAD], heads[:n, 3 * HEAD :]
            s = jnp.where(kept(i, n, ids[0]), nt(q, k) * SCALE, MASKED)
            m = jnp.max(s, -1, keepdims=True)
            e = jnp.exp(s - m)
            total = jnp.sum(e, -1, keepdims=True)
            o = nn((e / total).astype(bf16), v).astype(bf16)
            lse[128 * i : n, HEAD * h : HEAD * (h + 1)] = jnp.broadcast_to(
                m + jnp.log(total), (128, HEAD)
            )
            at_row = 128 * (i % 2)
            for y in range(4):
                out[2 * y + i // 2, at_row : at_row + 128, HEAD * h : HEAD * (h + 1)] = o


def mix(
    ids, att, a0, a1, a2, a3, b0, b1, b2, b3, tok, gain,
    hidden_part, normed, rows_w, hidden, side, mixer,
):
    y, c = ids[3], ids[4]
    for j in range(KEY_AT):
        side[:, JC * j : JC * (j + 1)] = att[j]
    mine = at(HALF * c, HALF, HALF)
    for e, a, b in zip(RELATIVE, (a0, a1, a2, a3), (b0, b1, b2, b3)):
        cols = at(384 * lax.rem(y + e + 4, 4), 384, 384)
        first = 384 * lax.rem(y + e + 4, 4)
        left, right = at(first, JC, 128), at(first + JC, HEAD, 128)
        for d in range(DP):
            for half, v in ((c, a), (1 - c, b)):
                row = ROWS * d + 48 * half
                mixer[at(row, 48, 16), left] = v[d, :48, :]
                mixer[at(row, 32, 16), right] = v[d, 48:80, :HEAD]
                mixer[at(row + 32, 16, 16), right] = v[d, 48:64, HEAD:]
        hidden[:, cols] = nn(side[...], mixer[:, cols]) + tok[mine, cols].astype(f32)
    hidden_part[...] = hidden[at(PART * y, PART, PART), :]
    rows_w[...] = mixer[at(JC * jnp.minimum(ids[2], KEY_AT - 1), JC, JC), :]
    for r in range(0, HALF, 64):
        v = hidden[r : r + 64, :]
        s = lax.rsqrt(jnp.mean(v * v, -1, keepdims=True) + EPS_NORM)
        normed[r : r + 64, :] = (v * s * gain[...]).astype(bf16)


def gated(near, far, back, back_t, w, act, gate_grad, up_grad, grads, near_t):
    @pl.when(pl.program_id(0) == 0)
    def _():
        near_t[:, :HALF] = near[...].T
        near_t[:, HALF:] = far[...].T

    gate_w, up_w, down_w = [w[:, m].reshape(D, 256) for m in range(3)]
    for r, normed in ((0, near), (HALF, far)):
        rows = slice(r, r + HALF)
        g = nn(normed[...], gate_w)
        u = nn(normed[...], up_w)
        a = nn(back[rows, :], down_w)
        sigma = 1.0 / (1.0 + jnp.exp(-g))
        swished = g * sigma
        act[rows, :] = (swished * u).astype(bf16)
        gate_grad[rows, :] = (a * u * sigma * (1.0 + g * (1.0 - sigma))).astype(bf16)
        up_grad[rows, :] = (a * swished).astype(bf16)
    for m, (left, right) in enumerate(((near_t, gate_grad), (near_t, up_grad), (back_t, act))):
        for r in range(4):
            part = nn(left[384 * r : 384 * (r + 1), :], right[...]).astype(bf16)
            grads[4 * r : 4 * (r + 1), m] = part.reshape(4, ROWS, 256)


def spread(gate_grad, up_grad, w, near, far):
    gate_w, up_w = [w[:, m].reshape(768, FP) for m in range(2)]
    for b in range(3):
        cols = slice(256 * b, 256 * (b + 1))
        part = nt(gate_grad[...], gate_w[cols]) + nt(up_grad[...], up_w[cols])
        near[:, cols] = part[:HALF].astype(bf16)
        far[:, cols] = part[HALF:].astype(bf16)


def spread_out(act, w, near, far):
    down_w = w[:, 0].reshape(768, FP)
    for b in range(3):
        cols = slice(256 * b, 256 * (b + 1))
        part = nt(act[...], down_w[cols])
        near[:, cols] = part[:HALF].astype(bf16)
        far[:, cols] = part[HALF:].astype(bf16)


def halve(ids, near, other, own, p1, p2, p3):
    y = ids[3]
    for k, out in ((0, own), (1, p1), (3, p2), (2, p3)):
        rows = at(PART * lax.rem(y + k, 4), PART, PART)
        out[...] = (near[rows, :].astype(f32) + other[rows, :].astype(f32)).astype(out.dtype)


def summed(own, parts):
    total = own[...]
    for part in parts:
        total += part[...].astype(f32)
    return total


def hidden_back(ids, own, a1, a2, a3, hidden, back, gain, grad, low, gain_part):
    h = hidden[...]
    g = summed(own, (a1, a2, a3))
    scale = lax.rsqrt(jnp.mean(h * h, -1, keepdims=True) + EPS_NORM)
    gain_part[...] = jnp.sum(g * h * scale, 0, keepdims=True)
    v = back[...].astype(f32) + norm_back(h, scale, gain[...], g)
    grad[...] = v
    low[...] = v.astype(bf16)


def add_parts(ids, own, a1, a2, a3, total):
    total[...] = summed(own, (a1, a2, a3))


def finish(ids, out_sum, own_b, b1, b2, b3, hidden, tok, grad, gain, done):
    length, y, c = ids[0], ids[3], ids[4]
    o, g = out_sum[...], summed(own_b, (b1, b2, b3))
    t = lax.broadcasted_iota(jnp.int32, (PART, 1), 0) + HALF * c + PART * y
    done[0] = jnp.where(t < length, o + hidden[...], 0.0).astype(bf16)
    x = tok[...].astype(f32)
    scale = lax.rsqrt(jnp.mean(x * x, -1, keepdims=True) + EPS_NORM)
    done[1] = (grad[...] + norm_back(x, scale, gain[...], g)).astype(bf16)


def attend_back(
    ids, near, far, rows_w, heads, lse, cosine, sine,
    grads, low, att_grad, key_grad, value_grad,
):
    length, y, c = ids[0], ids[3], ids[4]
    for k, e in enumerate(RELATIVE):
        place = PART * lax.rem(y + e + 4, 4)
        low[at(HALF * c + place, PART, PART), :] = near[k]
        low[at(HALF * (1 - c) + place, PART, PART), :] = far[k]
    has_heads = (ids[2] < KEY_AT).astype(f32)
    att_grad[...] = (nt(low[...], rows_w[...]) * has_heads).astype(bf16)
    key_grad[...] = jnp.zeros_like(key_grad)
    value_grad[...] = jnp.zeros_like(value_grad)
    for h in range(2):
        cols = slice(HEAD * h, HEAD * (h + 1))
        for i in range(4):
            n = 128 * (i + 1)
            rows = slice(128 * i, n)
            q = heads[rows, cols]
            k, v = heads[:n, 2 * HEAD : 3 * HEAD], heads[:n, 3 * HEAD :]
            o = att_grad[rows, cols]
            s = nt(q, k) * SCALE
            p = jnp.where(kept(i, n, length), jnp.exp(s - lse[rows, HEAD * h : HEAD * h + 1]), 0.0)
            d = nt(o, v)
            g = (p * (d - jnp.sum(p * d, -1, keepdims=True))).astype(bf16)
            value_grad[:n, :] += tn(p.astype(bf16), o)
            key_grad[:n, :] += tn(g, q)
            dq = nn(g, k) * SCALE
            dq = dq * cosine[rows, :] - pltpu.roll(dq, HEAD // 2, 1) * sine[rows, :]
            grads[rows, cols] = dq.astype(bf16)
    dk = key_grad[...] * SCALE
    dk = dk * cosine[...] - pltpu.roll(dk, HEAD // 2, 1) * sine[...]
    grads[:, 2 * HEAD : 3 * HEAD] = dk.astype(bf16)
    grads[:, 3 * HEAD :] = value_grad[...].astype(bf16)


def joint_back(
    ids, grads, w, tok, second_part,
    near, far, chunks, gain_part, vec, blocks,
):
    g = grads[...]
    gain_part[...] = jnp.zeros_like(gain_part)
    for r in range(0, T, 128):
        rows = slice(r, r + 128)
        back = nt(g[rows], w[...])
        half, place = r // HALF, slice(r % HALF, r % HALF + 128)
        moves = back.astype(bf16)

        @pl.when(ids[4] == half)
        def _():
            near[place, :] = moves

        @pl.when(ids[4] != half)
        def _():
            far[place, :] = moves

        x = tok[rows, :].astype(f32)
        s = lax.rsqrt(jnp.mean(x * x, -1, keepdims=True) + EPS_NORM)
        gain_part[...] += jnp.sum(back * x * s, 0, keepdims=True)
    vec[...] = jnp.zeros_like(vec)
    vec[:, :D] = gain_part[...]
    vec[:, D : 2 * D] = second_part[...]
    bias = jnp.sum(g.astype(f32), 0, keepdims=True)
    head_at = jnp.minimum(ids[2], KEY_AT - 1)
    key_start = 2 * D + JC * KEY_AT + HEAD * lax.div(head_at, 3)
    vec[:, at(2 * D + JC * head_at, JC, JC)] = bias[:, :JC]
    vec[:, at(key_start, HEAD, HEAD)] = bias[:, JC : JC + HEAD]
    vec[:, at(key_start + JC, HEAD, HEAD)] = bias[:, JC + HEAD :]
    for d in range(DP):
        blocks[d : d + 1, :] = vec[:, 320 * d : 320 * (d + 1)]
    for m in range(MP):
        chunks[m, :T, :] = g[:, 2 * HEAD : 3 * HEAD] if m < MP - 1 else g[:, 3 * HEAD :]
        piece = blocks[:, 40 * m : 40 * (m + 1)]
        piece = jnp.concatenate([piece, jnp.zeros((DP, HEAD - 40), f32)], 1)
        high = piece.astype(bf16)
        chunks[m, T : T + DP, :] = high
        chunks[m, T + DP :, :] = (piece - high.astype(f32)).astype(bf16)


def weigh_joint(ids, normed, grads, moved, mixer_parts, parts):
    keys = [moved[j, :T, :].astype(f32) for j in range(KEY_AT)]
    pair = jnp.concatenate([keys[0] + keys[1] + keys[2], keys[3] + keys[4] + keys[5]], 1)
    own = grads[:, :JC].astype(f32)
    g = jnp.where(ids[2] < KEY_AT, own, pair).astype(bf16)
    for r in range(4):
        cols = slice(384 * r, 384 * (r + 1))
        part = tn(normed[:, cols], g).astype(bf16)
        parts[4 * r : 4 * (r + 1), :ROWS, :JC] = part.reshape(4, ROWS, JC)
    parts[:, :ROWS, JC:] = mixer_parts[...]
    vec = moved[0, T:, :].astype(f32)
    for j in range(1, MP):
        vec += moved[j, T:, :].astype(f32)
    vec = vec[:DP] + vec[DP:]
    high = vec.astype(bf16).astype(f32)
    rest = jnp.zeros((8, MC), bf16)
    for d in range(DP):
        parts[d, ROWS:, :HEAD] = jnp.broadcast_to(high[d : d + 1], (8, HEAD)).astype(bf16)
        low = (vec - high)[d : d + 1]
        parts[d, ROWS:, HEAD:JC] = jnp.broadcast_to(low, (8, HEAD)).astype(bf16)
        parts[d, ROWS:, JC:] = rest


def weigh_mixer(ids, near, far, low, parts):
    y, c = ids[3], ids[4]

    def own_columns(half):
        v = low[at(HALF * half, HALF, HALF), at(384 * y, 384, 384)].astype(f32)
        return jnp.where(c == 0, v[:, :MC], v[:, MC:]).astype(bf16)

    mine, other = own_columns(c), own_columns(1 - c)
    for j in range(KEY_AT):
        part = (tn(near[j], mine) + tn(far[j], other)).astype(bf16)
        start = JC * j
        while start < JC * (j + 1):
            stop = min((start // ROWS + 1) * ROWS, JC * (j + 1))
            first = start % ROWS
            parts[start // ROWS, first : first + stop - start, :] = part[
                start - JC * j : stop - JC * j
            ]
            start = stop


def settle_grads(ids, moved, ff, joint, mixer, vector, squares):
    total = moved[0].astype(f32)
    for d in range(1, DP):
        total += moved[d].astype(f32)
    joint[...] = total[:ROWS, :JC]
    mixer[...] = total[:ROWS, JC:]
    vec = total[ROWS : ROWS + 1, :HEAD] + total[ROWS : ROWS + 1, HEAD:JC]
    vector[...] = vec
    total = total[:ROWS]
    total = jnp.sum(total * total) + jnp.sum(vec * vec)
    for m in range(3):
        v = ff[m].astype(f32)
        total += jnp.sum(v * v)
    squares[...] = jnp.full(squares.shape, total, f32)


def update(
    squares, joint_grad, mixer_grad, ff_grad, vector_grad,
    joint_w, joint_m, joint_v, mixer_w, mixer_m, mixer_v, expand_w, expand_m, expand_v,
    shrink_w, shrink_m, shrink_v, vector_w, vector_m, vector_v,
    norm_out, joint_wn, joint_mn, joint_vn, mixer_wn, mixer_mn, mixer_vn,
    expand_wn, expand_mn, expand_vn, shrink_wn, shrink_mn, shrink_vn,
    vector_wn, vector_mn, vector_vn,
):
    norm = jnp.sqrt(jnp.sum(squares[:, 0, :], 0, keepdims=True))
    norm_out[...] = norm
    clip = jnp.minimum(1.0, MAX_NORM / (norm[:, :1] + 1e-06))

    def step(grad, before, after, rate, decay, part=Ellipsis):
        w, m, v = [ref[part] for ref in before]
        results = adam_step(w, clip * grad, m, v, rate, decay)
        for ref, new in zip(after, results):
            ref[part] = new

    step(
        joint_grad[...], (joint_w, joint_m, joint_v), (joint_wn, joint_mn, joint_vn),
        RATE_MATRIX, DECAY,
    )
    step(
        mixer_grad[...], (mixer_w, mixer_m, mixer_v), (mixer_wn, mixer_mn, mixer_vn),
        RATE_MATRIX, DECAY,
    )
    for m in range(2):
        step(
            ff_grad[m, :, :FF].astype(f32),
            (expand_w, expand_m, expand_v), (expand_wn, expand_mn, expand_vn),
            RATE_MATRIX, DECAY, m,
        )
    step(
        ff_grad[2, :, :FF].astype(f32),
        (shrink_w, shrink_m, shrink_v), (shrink_wn, shrink_mn, shrink_vn),
        RATE_MATRIX, DECAY,
    )
    step(
        vector_grad[:, :40], (vector_w, vector_m, vector_v), (vector_wn, vector_mn, vector_vn),
        RATE_VECTOR, 0.0,
    )


def settle(ids, near, far, output, input_grad):
    y, c = ids[3], ids[4]
    for n, out in enumerate((output, input_grad)):
        for k, e in enumerate(RELATIVE):
            place = PART * lax.rem(y + e + 4, 4)
            out[0, at(HALF * c + place, PART, PART), :] = near[k, n].astype(f32)
            out[0, at(HALF * (1 - c) + place, PART, PART), :] = far[k, n].astype(f32)


def pile(ids, p0, p1, p2, p3, out):
    for k, p in enumerate((p0, p1, p2, p3)):
        out[k] = p[...]


def norm_back(v, scale, gain, grad):
    scaled = gain * grad
    return scale * scaled - v * scale * scale * scale * jnp.mean(scaled * v, -1, keepdims=True)


def adam_step(weight, grad, moment, square, rate, decay):
    moment_next = BETA_ONE * moment + (1.0 - BETA_ONE) * grad
    square_next = BETA_TWO * square + (1.0 - BETA_TWO) * grad * grad
    first_hat = moment_next / (1.0 - BETA_ONE**STEP)
    second_hat = square_next / (1.0 - BETA_TWO**STEP)
    weight_next = weight - rate * (first_hat / (jnp.sqrt(second_hat) + ADAM_EPS) + decay * weight)
    return (weight_next, moment_next, square_next)


def tables():
    freq = np.float32(ROPE_BASE) ** (-np.arange(0, HEAD, 2, dtype=np.float32) / np.float32(HEAD))
    angle = np.arange(T, dtype=np.float32)[:, None] * freq.astype(np.float32)[None, :]
    cosine, sine = np.cos(angle), np.sin(angle)
    return (
        np.concatenate([cosine, cosine], -1).astype(np.float32),
        np.concatenate([-sine, sine], -1).astype(np.float32),
    )


def split_low(v):
    high = lax.reduce_precision(v, 8, 7)
    middle = lax.reduce_precision(v - high, 8, 7)
    return [part.astype(bf16) for part in (high, middle, v - high - middle)]


def body(
    tokens, lengths, cotangent,
    joint_weight, joint_moment, joint_square,
    mixer_weight, mixer_moment, mixer_square,
    expand_weight, expand_moment, expand_square,
    shrink_weight, shrink_moment, shrink_square,
    vector_params, vector_moment, vector_square,
):
    dp, mp = lax.axis_index("dp"), lax.axis_index("mp")
    y, c = mp // 2, mp % 2
    tok, length = tokens[0], lengths[0]
    ids = jnp.stack([length, dp, mp, y, c]).astype(jnp.int32)

    stack = jnp.concatenate(
        [expand_weight.astype(bf16), shrink_weight.T.astype(bf16)[None]], 0
    )
    stack = jnp.pad(stack, ((0, 0), (0, 0), (0, FP - FF)))
    ff = lax.all_gather(stack, "dp", axis=0, tiled=False)

    low = jnp.concatenate([joint_weight.astype(bf16), mixer_weight.astype(bf16)], 1)
    vec = jnp.pad(jnp.stack(split_low(vector_params)), ((0, 13), (0, JC + MC - 40)))
    low = jnp.concatenate([low, vec], 0)
    other = swap_core(low)
    first, second = jnp.where(c == 0, low, other), jnp.where(c == 0, other, low)
    pairs = [
        jnp.concatenate([first[:ROWS, cols], second[:ROWS, cols]], 1)
        for cols in (slice(0, HEAD), slice(HEAD, JC))
    ]
    chip = jnp.concatenate([first[:ROWS, JC:], second[:ROWS, JC:]], 1)
    chip = lax.dynamic_slice_in_dim(chip, 48 * c, 48, 0)
    rest = jnp.concatenate([chip[:32, JC:], jnp.pad(chip[32:, JC:], ((0, 16), (0, 0)))], 1)
    sent = jnp.concatenate([low[:ROWS, :JC], chip[:, :JC], rest], 0)
    query_w = exchange(jnp.broadcast_to(sent, (DP,) + sent.shape), "dp")
    vec = jnp.concatenate([first[ROWS:, :HEAD], second[ROWS:, :HEAD]], 1)
    sends = [pairs[0], pairs[1], jnp.where(c == 0, pairs[0], pairs[1])]
    sends = [jnp.concatenate([v, vec], 0) for v in sends]
    a1, a2, a3 = [shift_y(v, k) for v, k in zip(sends, (1, -1, 2))]
    pair = jnp.where(y == 0, a1[:ROWS], jnp.where(y == 2, a2[:ROWS], a3[:ROWS]))
    vec = jnp.stack([vec, a2[ROWS:], a3[ROWS:], a1[ROWS:]])[:, :3]
    vec = lax.dynamic_slice_in_dim(jnp.concatenate([vec, vec]), (4 - y) % 4, 4, 0)
    sent = jnp.concatenate([pair, vec.reshape(12, JC), query_w[0, :4]], 0)
    pair_w = exchange(jnp.broadcast_to(sent, (DP,) + sent.shape), "dp")
    vec = pair_w[:, ROWS : ROWS + 12].astype(f32).reshape(DP, 4, 3, 2, HEAD)[..., :40]
    vec = vec[:, :, 0] + vec[:, :, 1] + vec[:, :, 2]
    vec = vec.reshape(-1)

    gain_first, gain_second = vec[None, :D], vec[None, D : 2 * D]
    key_start = JC * KEY_AT + HEAD * (jnp.minimum(mp, KEY_AT - 1) // 3)
    starts = ((JC * mp, JC), (key_start, HEAD), (key_start + JC, HEAD))
    bias = jnp.concatenate(
        [lax.dynamic_slice_in_dim(vec, 2 * D + start, size, 0) for start, size in starts]
    )[None]

    cosine, sine = tables()
    back, back_t, back_part, tok_part = whole(
        prepare,
        [((T, D), bf16), ((D, T), bf16), ((PART, D), bf16), ((PART, D), bf16)],
        [ids, cotangent[0], tok],
    )
    normed, heads, att_sent, lse, joint_w = whole(
        attend,
        [
            ((T, D), bf16), ((T, 2 * JC), bf16), ((MP, HALF, JC), bf16),
            ((T, JC), f32), ((D, 2 * JC), bf16),
        ],
        [ids, tok, gain_first, bias, cosine, sine, query_w, pair_w],
        after=[back],
    )
    att_near = exchange(att_sent, "mp")
    att_far = swap_core(att_near)
    mixer_near = gather(shift_y, query_w[:, ROWS:])
    mixer_far = [swap_core(v) for v in mixer_near]
    hidden_part, normed_near, rows_w = whole(
        mix,
        [((PART, D), f32), ((HALF, D), bf16), ((JC, D), bf16)],
        [ids, att_near] + mixer_near + mixer_far + [tok, gain_second],
        scratch=[
            pltpu.VMEM((HALF, D), f32), pltpu.VMEM((HALF, D), bf16), pltpu.VMEM((D, D), bf16),
        ],
    )
    normed_far = swap_core(normed_near)

    def columns(n):
        return pl.BlockSpec((n, 256), lambda i: (0, i))

    def fixed(shape):
        return pl.BlockSpec(shape, lambda i: (0,) * len(shape))

    block = pl.BlockSpec((DP, 3, ROWS, 256), lambda i: (0, 0, 0, i))
    act, gate_grad, up_grad, ff_grads = pl.pallas_call(
        gated,
        grid=(pl.cdiv(FP, 256),),
        out_shape=[jax.ShapeDtypeStruct((T, FP), bf16)] * 3
        + [jax.ShapeDtypeStruct((DP, 3, ROWS, FP), bf16)],
        in_specs=[fixed((HALF, D)), fixed((HALF, D)), fixed((T, D)), fixed((D, T)), block],
        out_specs=[columns(T)] * 3 + [block],
        scratch_shapes=[pltpu.VMEM((D, T), bf16)],
        compiler_params=pltpu.CompilerParams(vmem_limit_bytes=60 * MiB),
        cost_estimate=SMALL,
    )(normed_near, normed_far, back, back_t, ff)
    ff_shard = lax.psum_scatter(ff_grads, "dp", scatter_dimension=0, tiled=False)

    near, far = pl.pallas_call(
        spread,
        grid=(2,),
        out_shape=[jax.ShapeDtypeStruct((HALF, D), bf16)] * 2,
        in_specs=[fixed((T, FP))] * 2
        + [pl.BlockSpec((DP // 2, 2, ROWS, FP), lambda i: (i, 0, 0, 0))],
        out_specs=[pl.BlockSpec((HALF, 768), lambda i: (0, i))] * 2,
        compiler_params=pltpu.CompilerParams(vmem_limit_bytes=60 * MiB),
        cost_estimate=SMALL,
    )(gate_grad, up_grad, ff)

    def half_sum(near, far, after=()):
        own, *parts = whole(
            halve,
            [((PART, D), f32)] + [((PART, D), bf16)] * 3,
            [ids, near, swap_core(far)],
            after=after,
            limit=8,
        )
        return [own] + [shift_y(v, k) for v, k in zip(parts, (1, -1, 2))]

    normed_second_parts = half_sum(near, far)
    out_near, out_far = pl.pallas_call(
        spread_out,
        grid=(2,),
        out_shape=[jax.ShapeDtypeStruct((HALF, D), bf16)] * 2,
        in_specs=[
            fixed((T, FP)),
            pl.BlockSpec((DP // 2, 1, ROWS, FP), lambda i: (i, 2, 0, 0)),
        ],
        out_specs=[pl.BlockSpec((HALF, 768), lambda i: (0, i))] * 2,
        compiler_params=pltpu.CompilerParams(vmem_limit_bytes=60 * MiB),
        cost_estimate=SMALL,
    )(act, ff)
    hidden_grad, low, gain_second_part = whole(
        hidden_back,
        [((PART, D), f32), ((PART, D), bf16), ((1, D), f32)],
        [ids] + normed_second_parts + [hidden_part, back_part, gain_second],
        after=[out_far],
        limit=8,
    )
    low_near = jnp.stack(gather(shift_y, low))
    low_far = swap_core(low_near)
    out_parts = half_sum(out_near, out_far)
    heads_grad, hidden_low = whole(
        attend_back,
        [((T, 2 * JC), bf16), ((T, D), bf16)],
        [ids, low_near, low_far, rows_w, heads, lse, cosine, sine],
        scratch=[
            pltpu.VMEM((T, JC), bf16),
            pltpu.VMEM((T, HEAD), f32),
            pltpu.VMEM((T, HEAD), f32),
        ],
        after=[out_parts[0]],
    )
    (out_sum,) = whole(add_parts, [((PART, D), f32)], [ids] + out_parts, limit=8, after=[heads_grad])
    input_near, input_far, chunks = whole(
        joint_back,
        [((HALF, D), bf16), ((HALF, D), bf16), ((MP, T + 2 * DP, HEAD), bf16)],
        [ids, heads_grad, joint_w, tok, gain_second_part],
        scratch=[
            pltpu.VMEM((1, D), f32),
            pltpu.VMEM((1, DP * MP * 40), f32),
            pltpu.VMEM((DP, MP * 40), f32),
        ],
        after=[out_sum],
    )
    moved = exchange(chunks, "mp")
    (mixer_parts,) = whole(
        weigh_mixer,
        [((DP, ROWS, MC), bf16)],
        [ids, att_near, att_far, hidden_low],
    )
    (joint_parts,) = whole(
        weigh_joint,
        [((DP, ROWS + 8, JC + MC), bf16)],
        [ids, normed, heads_grad, moved, mixer_parts],
    )
    joint_shard, mixer_shard, vector_shard, squares = whole(
        settle_grads,
        [((ROWS, JC), f32), ((ROWS, MC), f32), ((1, HEAD), f32), ((DP * MP, 1, HEAD), f32)],
        [ids, exchange(joint_parts, "dp"), ff_shard],
    )

    squares = exchange(squares, ("dp", "mp"))

    input_parts = half_sum(input_near, input_far, after=[joint_parts])
    (done,) = whole(
        finish,
        [((2, PART, D), bf16)],
        [ids, out_sum] + input_parts + [hidden_part, tok_part, hidden_grad, gain_first],
        limit=8,
    )
    (done_near,) = whole(
        pile, [((4, 2, PART, D), bf16)], [ids] + gather(shift_y, done), after=[squares], limit=8
    )
    done_far = swap_core(done_near)
    output, input_grad = whole(settle, [((1, T, D), f32)] * 2, [ids, done_near, done_far])

    matrices = [joint_weight, joint_moment, joint_square]
    matrices += [mixer_weight, mixer_moment, mixer_square]
    matrices += [expand_weight, expand_moment, expand_square]
    matrices += [v.T for v in (shrink_weight, shrink_moment, shrink_square)]
    matrices += [v[None] for v in (vector_params, vector_moment, vector_square)]
    def sixth(shape):
        n = len(shape)
        if shape[-2] != ROWS:
            return pl.BlockSpec(shape, lambda i: (0,) * n)
        return pl.BlockSpec(
            shape[:-2] + (ROWS // 6, shape[-1]), lambda i: (0,) * (n - 2) + (i, 0)
        )

    given = [squares, joint_shard, mixer_shard, ff_shard, vector_shard] + matrices
    made = [(1, HEAD)] + [v.shape for v in matrices]
    norm, *new = pl.pallas_call(
        update,
        grid=(6,),
        out_shape=[jax.ShapeDtypeStruct(shape, f32) for shape in made],
        in_specs=[sixth(v.shape) for v in given],
        out_specs=[sixth(shape) for shape in made],
        compiler_params=pltpu.CompilerParams(vmem_limit_bytes=60 * MiB),
        cost_estimate=SMALL,
    )(*given)
    new[9:12] = [v.T for v in new[9:12]]
    new[12:] = [v[0] for v in new[12:]]
    return (output, input_grad, norm[0, 0], *new)


def solution(mesh):
    row = P("dp", None, None)
    matrix = [P("dp", "mp")] * 6 + [P(None, "dp", "mp")] * 3 + [P("mp", "dp")] * 3
    vector = [P(("dp", "mp"))] * 3
    return jax.shard_map(
        body,
        mesh=mesh,
        in_specs=tuple([row, P("dp"), row] + matrix + vector),
        out_specs=tuple([row, row, P()] + matrix + vector),
        check_vma=False,
    )
```

time: 1180 us -> 299 us (0.25)
  waiting for transfers between devices: 645 us -> 82.7 us
  blocking collectives: 203 us -> 0 us
  local copies, waits for them, and re-layouts: 139 us -> 13.3 us
  matrix products: 103 us -> 0 us
  Pallas kernels: 0 us -> 94.3 us
  starting transfers between devices: 1.03 us -> 89.2 us
  other arithmetic: 58.8 us -> 3.25 us
    reduce_scatter x3 -> x0, waiting for transfers between devices: 446 us -> none  [the longest x1 223 us: body(): lax.psum_scatter(restack(joint_part, lanes_dp, lanes_mp), ('dp', 'mp'), s...]
    unnamed x2 -> x0, blocking collectives: 139 us -> none
    all_gather x4 -> x1, waiting for transfers between devices: 106 us -> 0.01 us  [body(): ff = lax.all_gather(stack, 'dp', axis=0, tiled=False)]
    dot_general x21 -> x0, matrix products: 103 us -> none  [the longest x5 27.5 us: outer_columns(): lax.dot_general(left, right, (((1,), (1,)), ((), ())), preferred_element_...]
    pallas_call x0 -> x20, Pallas kernels: none -> 94.3 us  [the longest x16 55.3 us: whole(): pl.pallas_call(bare, out_shape=[jax.ShapeDtypeStruct(s, d) for s, d in ou...]
    psum x2 -> x0, waiting for transfers between devices: 89.6 us -> none  [the longest x1 62.9 us: body(): feed = lax.psum(partial_out.astype(jnp.bfloat16), 'mp').astype(jnp.float32)]
    psum x1 -> x0, blocking collectives: 64.3 us -> none  [body(): grad_norm = jnp.sqrt(lax.psum(squares, ('dp', 'mp')))]
    all_to_all x0 -> x6, waiting for transfers between devices: none -> 52.2 us  [exchange(): return lax.all_to_all(v, axis, split_axis=0, concat_axis=0, tiled=True)]
  transfers between devices with their start and end apart: 10 -> 41, of which waited for: 8 -> 21; matrix products, arithmetic and copies ran while one was open for 22% -> 2% of each run, Pallas kernels for 0% -> 24%
where the time goes in v1:
time: 299 us; the launch traced here: 298 us
  Pallas kernels  94.3 us (32%)
  starting transfers between devices  89.2 us (30%)
  waiting for transfers between devices  82.7 us (28%)
  between operations  15.3 us (5%)
  local copies, waits for them, and re-layouts  13.3 us (4%)
  other arithmetic  3.25 us (1%)
    pallas_call x16, Pallas kernels, whole(): pl.pallas_call(bare, out_shape=[jax.ShapeDtypeStruct(s, d) for s, d in ou...  55.3 us
    all_to_all x6, waiting for transfers between devices, exchange(): return lax.all_to_all(v, axis, split_axis=0, concat_axis=0, tiled=True)  52.2 us
    all_to_all x6, starting transfers between devices, exchange(): return lax.all_to_all(v, axis, split_axis=0, concat_axis=0, tiled=True)  50.9 us
    ppermute x21, starting transfers between devices, shift_y(): return lax.ppermute(v, 'mp', [(i, (i + 2 * k) % MP) for i in range(MP)])  25.3 us
    ppermute x21, waiting for transfers between devices, shift_y(): return lax.ppermute(v, 'mp', [(i, (i + 2 * k) % MP) for i in range(MP)])  19.7 us
    pallas_call x1, Pallas kernels, body(): pl.pallas_call(gated, grid=(pl.cdiv(FP, 256),), out_shape=[jax.ShapeDtype...  18.3 us
    ppermute x12, starting transfers between devices, swap_core(): return lax.ppermute(v, 'mp', [(i, i ^ 1) for i in range(MP)])  13 us
    ppermute x12, waiting for transfers between devices, swap_core(): return lax.ppermute(v, 'mp', [(i, i ^ 1) for i in range(MP)])  10.8 us
  transfers between devices with their start and end apart: 41, of which 21 were waited for; matrix products, arithmetic and copies ran while one was open for 2% of the time, Pallas kernels for 24%

profile of v1, /device:TPU:1, one launch (start us, length us, event | category | flops | bytes accessed | tf_op | source)
XLA Modules:
  0.0 298.1 jit_solution(6261031710189235937)
XLA Ops:
  13.5 7.7 %all-to-all-start = ((bf16[16,176,256]{2,1,0:T(8,128)(2,1)}), bf16[16,176,256]{2,1,0:T(8,128)(2,1)S(1)}, u32[]{:S(2)}, u32[]{:S(2)}) async-start(bf16[16,176,256]{2,1,0:T(8,128)(2,1)} %broadcast_in_dim.27), calls=%async_computation | async-start | bytes 2883584 | tf_op jit(solution)/shard_map/all_to_all | solution.py:59
  28.8 19.3 %all-to-all-done.refs_6_ = bf16[16,176,256]{2,1,0:T(8,128)(2,1)S(1)} async-done(((bf16[16,176,256]{2,1,0:T(8,128)(2,1)}), bf16[16,176,256]{2,1,0:T(8,128)(2,1)S(1)}, u32[]{:S(2)}, u32[]{:S(2)}) %all-to-all-start) | async-done | bytes 1441824 | tf_op jit(solution)/shard_map/all_to_all | solution.py:59
  49.2 6.6 %all-to-all-start.1 = ((bf16[16,112,256]{2,1,0:T(8,128)(2,1)}), bf16[16,112,256]{2,1,0:T(8,128)(2,1)S(1)}, u32[]{:S(2)}, u32[]{:S(2)}) async-start(bf16[16,112,256]{2,1,0:T(8,128)(2,1)} %broadcast_in_dim.28), calls=%async_computation.1 | async-start | bytes 1835008 | tf_op jit(solution)/shard_map/all_to_all | solution.py:59
  57.1 4.3 %shard_map.331 = (bf16[512,1536]{1,0:T(8,128)(2,1)}, bf16[1536,512]{1,0:T(8,128)(2,1)}, bf16[64,1536]{1,0:T(8,128)(2,1)}, bf16[64,1536]{1,0:T(8,128)(2,1)}) custom-call(s32[5]{0:T(128)} %stack.61.refs_0_, bf16[512,1536]{1,0:T(8,128)(2,1)} %bitcast.60, bf16[512,1536]{1,0:T(8,128)(2,1)} %bitcast.53), custom_call_target="tpu_custom_call" | custom-call | flops 1 | bytes 1 | tf_op jit(solution)/shard_map/pallas_call | solution.py:87
  69.4 8.8 %shard_map.332 = (bf16[512,1536]{1,0:T(8,128)(2,1)}, bf16[512,512]{1,0:T(8,128)(2,1)}, bf16[8,256,256]{2,1,0:T(8,128)(2,1)}, f32[512,256]{1,0:T(8,128)}, bf16[1536,512]{1,0:T(8,128)(2,1)}) custom-call(s32[5]{0:T(128)} %stack.61.refs_0_, bf16[512,1536]{1,0:T(8,128)(2,1)} %bitcast.54, f32[1,1536]{1,0:T(1,128)} %broadcast_in_dim.29.refs_2_.refs_9_, ...), custom_call_target="tpu_custom_call" | custom-call | flops 1 | bytes 1 | tf_op jit(solution)/shard_map/pallas_call | solution.py:87
  78.2 16.2 %all-to-all-start.2 = ((bf16[8,256,256]{2,1,0:T(8,128)(2,1)}), bf16[8,256,256]{2,1,0:T(8,128)(2,1)S(1)}, u32[]{:S(2)}, u32[]{:S(2)}) async-start(bf16[8,256,256]{2,1,0:T(8,128)(2,1)} %get-tuple-element.81), calls=%async_computation.2 | async-start | bytes 2097152 | tf_op jit(solution)/shard_map/all_to_all | solution.py:59
  100.5 9.0 %all-to-all-done.2.refs_1_ = bf16[8,256,256]{2,1,0:T(8,128)(2,1)S(1)} async-done(((bf16[8,256,256]{2,1,0:T(8,128)(2,1)}), bf16[8,256,256]{2,1,0:T(8,128)(2,1)S(1)}, u32[]{:S(2)}, u32[]{:S(2)}) %all-to-all-start.2) | async-done | bytes 1048608 | tf_op jit(solution)/shard_map/all_to_all | solution.py:59
  110.6 7.2 %shard_map.333 = (f32[64,1536]{1,0:T(8,128)}, bf16[256,1536]{1,0:T(8,128)(2,1)}, bf16[256,1536]{1,0:T(8,128)(2,1)}) custom-call(s32[5]{0:T(128)} %stack.61.refs_0_, bf16[8,256,256]{2,1,0:T(8,128)(2,1)} %copy-done.21, bf16[16,80,256]{2,1,0:T(8,128)(2,1)} %copy-done.26, bf16[16,80,256]{2,1,0:T(8,128)(2,1)} %collective-permute-done.4.refs_3_, ...), custom_call_target="tpu_custom_call" | custom-call | flops 1 | bytes 1 | tf_op jit(solution)/shard_map/pallas_call | solution.py:87
  121.7 18.3 %shard_map.334 = (bf16[512,1152]{1,0:T(8,128)(2,1)}, bf16[512,1152]{1,0:T(8,128)(2,1)}, bf16[512,1152]{1,0:T(8,128)(2,1)}, bf16[16,3,96,1152]{3,2,1,0:T(8,128)(2,1)}) custom-call(bf16[256,1536]{1,0:T(8,128)(2,1)} %get-tuple-element.82.near, bf16[256,1536]{1,0:T(8,128)(2,1)} %copy-done.30, bf16[512,1536]{1,0:T(8,128)(2,1)} %get-tuple-element.80.refs_8_.back, ...), custom_call_target="tpu_custom_call" | custom-call | flops 1 | bytes 1 | tf_op jit(solution)/shard_map/pallas_call | solution.py:581
  140.0 8.0 %shard_map.337 = (bf16[256,1536]{1,0:T(8,128)(2,1)}, bf16[256,1536]{1,0:T(8,128)(2,1)}) custom-call(bf16[512,1152]{1,0:T(8,128)(2,1)} %get-tuple-element.91.gate_grad, bf16[512,1152]{1,0:T(8,128)(2,1)} %get-tuple-element.92.up_grad, bf16[16,3,96,1152]{3,2,1,0:T(8,128)(2,1)} %bitcast.51), custom_call_target="tpu_custom_call" | custom-call | flops 1 | bytes 1 | tf_op jit(solution)/shard_map/pallas_call | solution.py:594
  155.2 5.2 %shard_map.335 = (bf16[256,1536]{1,0:T(8,128)(2,1)}, bf16[256,1536]{1,0:T(8,128)(2,1)}) custom-call(bf16[512,1152]{1,0:T(8,128)(2,1)} %get-tuple-element.84.act, bf16[16,3,96,1152]{3,2,1,0:T(8,128)(2,1)} %bitcast.52), custom_call_target="tpu_custom_call" | custom-call | flops 1 | bytes 1 | tf_op jit(solution)/shard_map/pallas_call | solution.py:616
  170.9 4.1 %collective-permute-done.22 = bf16[64,1536]{1,0:T(8,128)(2,1)S(1)} collective-permute-done((bf16[64,1536]{1,0:T(8,128)(2,1)S(1)}, bf16[64,1536]{1,0:T(8,128)(2,1)S(1)}, u32[]{:S(2)}, u32[]{:S(2)}) %collective-permute-start.22) | collective-permute-done | bytes 196640 | tf_op jit(solution)/shard_map/ppermute | solution.py:47
  184.5 7.3 %shard_map.340 = (bf16[512,512]{1,0:T(8,128)(2,1)}, bf16[512,1536]{1,0:T(8,128)(2,1)}) custom-call(s32[5]{0:T(128)} %stack.61.refs_0_, bf16[4,64,1536]{2,1,0:T(8,128)(2,1)} %copy-done.25, bf16[4,64,1536]{2,1,0:T(8,128)(2,1)} %copy-done.29, bf16[256,1536]{1,0:T(8,128)(2,1)} %get-tuple-element.102.refs_3_, bf16[512,512]{1,0:T(8,128)(2,1)} %get-tuple-element.103.refs_4_, ...), custom_call_target="tpu_custom_call" | custom-call | flops 1 | bytes 1 | tf_op jit(solution)/shard_map/pallas_call | solution.py:87
  194.7 6.7 %shard_map.342 = (bf16[256,1536]{1,0:T(8,128)(2,1)}, bf16[256,1536]{1,0:T(8,128)(2,1)}, bf16[8,544,128]{2,1,0:T(8,128)(2,1)}) custom-call(s32[5]{0:T(128)} %stack.61.refs_0_, bf16[512,512]{1,0:T(8,128)(2,1)} %get-tuple-element.105.refs_5_.refs_1_.refs_2_, bf16[1536,512]{1,0:T(8,128)(2,1)} %get-tuple-element.106.refs_2_, bf16[512,1536]{1,0:T(8,128)(2,1)} %bitcast.56, ...), custom_call_target="tpu_custom_call" | custom-call | flops 1 | bytes 1 | tf_op jit(solution)/shard_map/pallas_call | solution.py:87
  201.4 5.0 %all-to-all-start.3 = ((bf16[8,544,128]{2,1,0:T(8,128)(2,1)}), bf16[8,544,128]{2,1,0:T(8,128)(2,1)}, u32[]{:S(2)}, u32[]{:S(2)}) async-start(bf16[8,544,128]{2,1,0:T(8,128)(2,1)} %get-tuple-element.111), calls=%async_computation.3 | async-start | bytes 2228224 | tf_op jit(solution)/shard_map/all_to_all | solution.py:59
  206.4 3.7 %shard_map.343.refs_4_ = bf16[16,96,192]{2,1,0:T(8,128)(2,1)} custom-call(s32[5]{0:T(128)} %stack.61.refs_0_, bf16[8,256,256]{2,1,0:T(8,128)(2,1)} %copy-done.21, bf16[8,256,256]{2,1,0:T(8,128)(2,1)} %collective-permute-done.25.refs_2_, bf16[512,1536]{1,0:T(8,128)(2,1)} %get-tuple-element.112.refs_3_), custom_call_target="tpu_custom_call" | custom-call | flops 1 | bytes 1 | tf_op jit(solution)/shard_map/pallas_call | solution.py:87
  210.0 12.3 %all-to-all-done.3.refs_3_ = bf16[8,544,128]{2,1,0:T(8,128)(2,1)} async-done(((bf16[8,544,128]{2,1,0:T(8,128)(2,1)}), bf16[8,544,128]{2,1,0:T(8,128)(2,1)}, u32[]{:S(2)}, u32[]{:S(2)}) %all-to-all-start.3) | async-done | bytes 1114144 | tf_op jit(solution)/shard_map/all_to_all | solution.py:59
  222.3 4.0 %shard_map.344.refs_3_ = bf16[16,104,448]{2,1,0:T(8,128)(2,1)} custom-call(s32[5]{0:T(128)} %stack.61.refs_0_, bf16[512,1536]{1,0:T(8,128)(2,1)} %get-tuple-element.110.refs_1_, bf16[512,512]{1,0:T(8,128)(2,1)} %get-tuple-element.105.refs_5_.refs_1_.refs_2_, bf16[8,544,128]{2,1,0:T(8,128)(2,1)} %all-to-all-done.3.refs_3_, ...), custom_call_target="tpu_custom_call" | custom-call | flops 1 | bytes 1 | tf_op jit(solution)/shard_map/pallas_call | solution.py:87
  226.3 6.3 %all-to-all-start.4 = ((bf16[16,104,448]{2,1,0:T(8,128)(2,1)}), bf16[16,104,448]{2,1,0:T(8,128)(2,1)}, u32[]{:S(2)}, u32[]{:S(2)}) async-start(bf16[16,104,448]{2,1,0:T(8,128)(2,1)} %shard_map.344.refs_3_), calls=%async_computation.4 | async-start | bytes 3407872 | tf_op jit(solution)/shard_map/all_to_all | solution.py:59
  239.7 5.1 %collective-permute-done.26.refs_3_ = bf16[64,1536]{1,0:T(8,128)(2,1)S(1)} collective-permute-done((bf16[64,1536]{1,0:T(8,128)(2,1)S(1)}, bf16[64,1536]{1,0:T(8,128)(2,1)S(1)}, u32[]{:S(2)}, u32[]{:S(2)}) %collective-permute-start.26) | collective-permute-done | bytes 196640 | tf_op jit(solution)/shard_map/ppermute | solution.py:47
  257.4 9.0 %all-to-all-start.5 = ((f32[128,1,128]{2,1,0:T(1,128)}), f32[128,1,128]{2,1,0:T(1,128)S(1)}, u32[]{:S(2)}, u32[]{:S(2)}) async-start(f32[128,1,128]{2,1,0:T(1,128)} %get-tuple-element.120), calls=%async_computation.5 | async-start | bytes 131072 | tf_op jit(solution)/shard_map/all_to_all | solution.py:59
  267.1 8.8 %all-to-all-done.5.refs_5_.squares = f32[128,1,128]{2,1,0:T(1,128)S(1)} async-done(((f32[128,1,128]{2,1,0:T(1,128)}), f32[128,1,128]{2,1,0:T(1,128)S(1)}, u32[]{:S(2)}, u32[]{:S(2)}) %all-to-all-start.5) | async-done | bytes 65568 | tf_op jit(solution)/shard_map/all_to_all | solution.py:59
  277.5 7.5 %shard_map.350 = (f32[1,128]{1,0:T(1,128)}, f32[96,256]{1,0:T(8,128)}, f32[96,256]{1,0:T(8,128)}, f32[96,256]{1,0:T(8,128)}, f32[96,192]{1,0:T(8,128)}, /*index=...) custom-call(f32[128,1,128]{2,1,0:T(1,128)} %copy-done.11, ...), custom_call_target="tpu_custom_call" | custom-call | flops 1 | bytes 1 | tf_op jit(solution)/shard_map/pallas_call | solution.py:708
  286.2 5.0 %shard_map.349 = (f32[1,512,1536]{2,1,0:T(8,128)}, f32[1,512,1536]{2,1,0:T(8,128)}) custom-call(s32[5]{0:T(128)} %stack.61.refs_0_, bf16[4,2,64,1536]{3,2,1,0:T(8,128)(2,1)} %copy-done.1, bf16[4,2,64,1536]{3,2,1,0:T(8,128)(2,1)} %copy-done.28), custom_call_target="tpu_custom_call" | custom-call | flops 1 | bytes 1 | tf_op jit(solution)/shard_map/pallas_call | solution.py:87
  (202 shorter events, 87.3 us)
Async XLA Ops:
  7.2 113.6 %all-gather.3.cloned.1.call-start = ((), (), s32[]{:S(2)}) async-start(), calls=%async_computation.7 | async-start | bytes 11280384 | tf_op jit(solution)/shard_map/all_gather | solution.py:509
  13.5 34.6 %all-to-all-start = ((bf16[16,176,256]{2,1,0:T(8,128)(2,1)}), bf16[16,176,256]{2,1,0:T(8,128)(2,1)S(1)}, u32[]{:S(2)}, u32[]{:S(2)}) async-start(bf16[16,176,256]{2,1,0:T(8,128)(2,1)} %broadcast_in_dim.27), calls=%async_computation | async-start | bytes 2883584 | tf_op jit(solution)/shard_map/all_to_all | solution.py:59
  49.2 18.4 %all-to-all-start.1 = ((bf16[16,112,256]{2,1,0:T(8,128)(2,1)}), bf16[16,112,256]{2,1,0:T(8,128)(2,1)S(1)}, u32[]{:S(2)}, u32[]{:S(2)}) async-start(bf16[16,112,256]{2,1,0:T(8,128)(2,1)} %broadcast_in_dim.28), calls=%async_computation.1 | async-start | bytes 1835008 | tf_op jit(solution)/shard_map/all_to_all | solution.py:59
  61.5 33.1 %collective-permute-start.6 = (bf16[16,80,256]{2,1,0:T(8,128)(2,1)S(1)}, bf16[16,80,256]{2,1,0:T(8,128)(2,1)}, u32[]{:S(2)}, u32[]{:S(2)}) collective-permute-start(bf16[16,80,256]{2,1,0:T(8,128)(2,1)S(1)} %slice.135.refs_2_), channel_id=1, source_target_pairs={{0,4},{1,5},{2,6},{3,7},{4,0},{5,1},{6,2},{7,3},{8,12},{9,13},{10,... | collective-permute-start | bytes 1966088 | tf_op jit(solution)/shard_map/ppermute | solution.py:47
  64.6 30.5 %collective-permute-start.4 = (bf16[16,80,256]{2,1,0:T(8,128)(2,1)S(1)}, bf16[16,80,256]{2,1,0:T(8,128)(2,1)}, u32[]{:S(2)}, u32[]{:S(2)}) collective-permute-start(bf16[16,80,256]{2,1,0:T(8,128)(2,1)S(1)} %slice.135.refs_2_), channel_id=1, source_target_pairs={{0,2},{1,3},{2,4},{3,5},{4,6},{5,7},{6,0},{7,1},{8,10},{9,11},{10,... | collective-permute-start | bytes 1966088 | tf_op jit(solution)/shard_map/ppermute | solution.py:47
  64.9 30.2 %collective-permute-start.5 = (bf16[16,80,256]{2,1,0:T(8,128)(2,1)S(1)}, bf16[16,80,256]{2,1,0:T(8,128)(2,1)}, u32[]{:S(2)}, u32[]{:S(2)}) collective-permute-start(bf16[16,80,256]{2,1,0:T(8,128)(2,1)S(1)} %slice.135.refs_2_), channel_id=1, source_target_pairs={{0,6},{1,7},{2,0},{3,1},{4,2},{5,3},{6,4},{7,5},{8,14},{9,15},{10,... | collective-permute-start | bytes 1966088 | tf_op jit(solution)/shard_map/ppermute | solution.py:47
  78.2 31.3 %all-to-all-start.2 = ((bf16[8,256,256]{2,1,0:T(8,128)(2,1)}), bf16[8,256,256]{2,1,0:T(8,128)(2,1)S(1)}, u32[]{:S(2)}, u32[]{:S(2)}) async-start(bf16[8,256,256]{2,1,0:T(8,128)(2,1)} %get-tuple-element.81), calls=%async_computation.2 | async-start | bytes 2097152 | tf_op jit(solution)/shard_map/all_to_all | solution.py:59
  94.5 160.1 %reduce-scatter.4.cloned.1.call-start = ((), (), s32[]{:S(2)}) async-start(), calls=%async_computation.8 | async-start | bytes 11280384
  152.4 8.0 %collective-permute-start.17 = (bf16[64,1536]{1,0:T(8,128)(2,1)S(1)}, bf16[64,1536]{1,0:T(8,128)(2,1)S(1)}, u32[]{:S(2)}, u32[]{:S(2)}) collective-permute-start(bf16[64,1536]{1,0:T(8,128)(2,1)S(1)} %get-tuple-element.96), channel_id=1, source_target_pairs={{0,2},{1,3},{2,4},{3,5},{4,6},{5,7},{6,0},{7,1},{8,10},{9,11},{10,... | collective-permute-start | bytes 589832 | tf_op jit(solution)/shard_map/ppermute | solution.py:47
  155.2 8.3 %collective-permute-start.19 = (bf16[64,1536]{1,0:T(8,128)(2,1)S(1)}, bf16[64,1536]{1,0:T(8,128)(2,1)S(1)}, u32[]{:S(2)}, u32[]{:S(2)}) collective-permute-start(bf16[64,1536]{1,0:T(8,128)(2,1)S(1)} %get-tuple-element.98), channel_id=1, source_target_pairs={{0,4},{1,5},{2,6},{3,7},{4,0},{5,1},{6,2},{7,3},{8,12},{9,13},{10,... | collective-permute-start | bytes 589832 | tf_op jit(solution)/shard_map/ppermute | solution.py:47
  167.7 10.7 %collective-permute-start.12 = (bf16[256,1536]{1,0:T(8,128)(2,1)}, bf16[256,1536]{1,0:T(8,128)(2,1)S(1)}, u32[]{:S(2)}, u32[]{:S(2)}) collective-permute-start(bf16[256,1536]{1,0:T(8,128)(2,1)} %get-tuple-element.86.refs_8_), channel_id=1, source_target_pairs={{0,1},{1,0},{2,3},{3,2},{4,5},{5,4},{6,7},{7,6},{8,9},{9,8},{10,11... | collective-permute-start | bytes 2359304 | tf_op jit(solution)/shard_map/ppermute | solution.py:55
  175.1 8.5 %collective-permute-start.23 = (bf16[4,64,1536]{2,1,0:T(8,128)(2,1)S(1)}, bf16[4,64,1536]{2,1,0:T(8,128)(2,1)S(1)}, u32[]{:S(2)}, u32[]{:S(2)}) collective-permute-start(bf16[4,64,1536]{2,1,0:T(8,128)(2,1)S(1)} %pad_maximum_fusion.refs_1_), channel_id=1, source_target_pairs={{0,1},{1,0},{2,3},{3,2},{4,5},{5,4},{6,7},{7,6},{8,9},{9,8},{10,11... | collective-permute-start | bytes 2359304 | tf_op jit(solution)/shard_map/ppermute | solution.py:55
  179.9 12.0 %collective-permute-start.13 = (bf16[64,1536]{1,0:T(8,128)(2,1)S(1)}, bf16[64,1536]{1,0:T(8,128)(2,1)S(1)}, u32[]{:S(2)}, u32[]{:S(2)}) collective-permute-start(bf16[64,1536]{1,0:T(8,128)(2,1)S(1)} %get-tuple-element.88), channel_id=1, source_target_pairs={{0,2},{1,3},{2,4},{3,5},{4,6},{5,7},{6,0},{7,1},{8,10},{9,11},{10,... | collective-permute-start | bytes 589832 | tf_op jit(solution)/shard_map/ppermute | solution.py:47
  180.1 11.7 %collective-permute-start.14 = (bf16[64,1536]{1,0:T(8,128)(2,1)S(1)}, bf16[64,1536]{1,0:T(8,128)(2,1)S(1)}, u32[]{:S(2)}, u32[]{:S(2)}) collective-permute-start(bf16[64,1536]{1,0:T(8,128)(2,1)S(1)} %get-tuple-element.89), channel_id=1, source_target_pairs={{0,6},{1,7},{2,0},{3,1},{4,2},{5,3},{6,4},{7,5},{8,14},{9,15},{10,... | collective-permute-start | bytes 589832 | tf_op jit(solution)/shard_map/ppermute | solution.py:47
  182.5 9.7 %collective-permute-start.15 = (bf16[64,1536]{1,0:T(8,128)(2,1)S(1)}, bf16[64,1536]{1,0:T(8,128)(2,1)S(1)}, u32[]{:S(2)}, u32[]{:S(2)}) collective-permute-start(bf16[64,1536]{1,0:T(8,128)(2,1)S(1)} %get-tuple-element.90), channel_id=1, source_target_pairs={{0,4},{1,5},{2,6},{3,7},{4,0},{5,1},{6,2},{7,3},{8,12},{9,13},{10,... | collective-permute-start | bytes 589832 | tf_op jit(solution)/shard_map/ppermute | solution.py:47
  183.0 23.3 %collective-permute-start.25 = (bf16[8,256,256]{2,1,0:T(8,128)(2,1)S(1)}, bf16[8,256,256]{2,1,0:T(8,128)(2,1)}, u32[]{:S(2)}, u32[]{:S(2)}) collective-permute-start(bf16[8,256,256]{2,1,0:T(8,128)(2,1)S(1)} %copy-done.22), channel_id=1, source_target_pairs={{0,1},{1,0},{2,3},{3,2},{4,5},{5,4},{6,7},{7,6},{8,9},{9,8},{10,11... | collective-permute-start | bytes 3145736 | tf_op jit(solution)/shard_map/ppermute | solution.py:55
  201.4 20.9 %all-to-all-start.3 = ((bf16[8,544,128]{2,1,0:T(8,128)(2,1)}), bf16[8,544,128]{2,1,0:T(8,128)(2,1)}, u32[]{:S(2)}, u32[]{:S(2)}) async-start(bf16[8,544,128]{2,1,0:T(8,128)(2,1)} %get-tuple-element.111), calls=%async_computation.3 | async-start | bytes 2228224 | tf_op jit(solution)/shard_map/all_to_all | solution.py:59
  226.3 28.2 %all-to-all-start.4 = ((bf16[16,104,448]{2,1,0:T(8,128)(2,1)}), bf16[16,104,448]{2,1,0:T(8,128)(2,1)}, u32[]{:S(2)}, u32[]{:S(2)}) async-start(bf16[16,104,448]{2,1,0:T(8,128)(2,1)} %shard_map.344.refs_3_), calls=%async_computation.4 | async-start | bytes 3407872 | tf_op jit(solution)/shard_map/all_to_all | solution.py:59
  239.7 8.2 %collective-permute-start.28 = (bf16[64,1536]{1,0:T(8,128)(2,1)S(1)}, bf16[64,1536]{1,0:T(8,128)(2,1)S(1)}, u32[]{:S(2)}, u32[]{:S(2)}) collective-permute-start(bf16[64,1536]{1,0:T(8,128)(2,1)S(1)} %get-tuple-element.116), channel_id=1, source_target_pairs={{0,4},{1,5},{2,6},{3,7},{4,0},{5,1},{6,2},{7,3},{8,12},{9,13},{10,... | collective-permute-start | bytes 589832 | tf_op jit(solution)/shard_map/ppermute | solution.py:47
  248.9 17.6 %collective-permute-start.29 = (bf16[2,64,1536]{2,1,0:T(8,128)(2,1)S(1)}, bf16[2,64,1536]{2,1,0:T(8,128)(2,1)S(1)}, u32[]{:S(2)}, u32[]{:S(2)}) collective-permute-start(bf16[2,64,1536]{2,1,0:T(8,128)(2,1)S(1)} %shard_map.346.refs_1_), channel_id=1, source_target_pairs={{0,2},{1,3},{2,4},{3,5},{4,6},{5,7},{6,0},{7,1},{8,10},{9,11},{10,... | collective-permute-start | bytes 1179656 | tf_op jit(solution)/shard_map/ppermute | solution.py:47
  250.2 16.2 %collective-permute-start.30 = (bf16[2,64,1536]{2,1,0:T(8,128)(2,1)S(1)}, bf16[2,64,1536]{2,1,0:T(8,128)(2,1)S(1)}, u32[]{:S(2)}, u32[]{:S(2)}) collective-permute-start(bf16[2,64,1536]{2,1,0:T(8,128)(2,1)S(1)} %shard_map.346.refs_1_), channel_id=1, source_target_pairs={{0,6},{1,7},{2,0},{3,1},{4,2},{5,3},{6,4},{7,5},{8,14},{9,15},{10,... | collective-permute-start | bytes 1179656 | tf_op jit(solution)/shard_map/ppermute | solution.py:47
  251.6 15.5 %collective-permute-start.31 = (bf16[2,64,1536]{2,1,0:T(8,128)(2,1)S(1)}, bf16[2,64,1536]{2,1,0:T(8,128)(2,1)S(1)}, u32[]{:S(2)}, u32[]{:S(2)}) collective-permute-start(bf16[2,64,1536]{2,1,0:T(8,128)(2,1)S(1)} %shard_map.346.refs_1_), channel_id=1, source_target_pairs={{0,4},{1,5},{2,6},{3,7},{4,0},{5,1},{6,2},{7,3},{8,12},{9,13},{10,... | collective-permute-start | bytes 1179656 | tf_op jit(solution)/shard_map/ppermute | solution.py:47
  257.4 18.5 %all-to-all-start.5 = ((f32[128,1,128]{2,1,0:T(1,128)}), f32[128,1,128]{2,1,0:T(1,128)S(1)}, u32[]{:S(2)}, u32[]{:S(2)}) async-start(f32[128,1,128]{2,1,0:T(1,128)} %get-tuple-element.120), calls=%async_computation.5 | async-start | bytes 131072 | tf_op jit(solution)/shard_map/all_to_all | solution.py:59
  276.6 8.5 %collective-permute-start.32 = (bf16[4,2,64,1536]{3,2,1,0:T(8,128)(2,1)S(1)}, bf16[4,2,64,1536]{3,2,1,0:T(8,128)(2,1)S(1)}, u32[]{:S(2)}, u32[]{:S(2)}) collective-permute-start(bf16[4,2,64,1536]{3,2,1,0:T(8,128)(2,1)S(1)} %shard_map.348.refs_1_), channel_id=1, source_target_pairs={{0,1},{1,0},{2,3},{3,2},{4,5},{5,4},{6,7},{7,6},{8,9},{9,8},{10,11... | collective-permute-start | bytes 4718600 | tf_op jit(solution)/shard_map/ppermute | solution.py:55
  (54 other events, 367.3 us)
Sparse Core Ops, SparseCore 0:
  10.2 103.7 all-gather.2
  140.2 88.5 reduce-scatter.3

commit v2 on v1

--- a/solution.py
+++ b/solution.py
@@ -233,6 +233,11 @@
         out[...] = (near[rows, :].astype(f32) + other[rows, :].astype(f32)).astype(out.dtype)
 
 
+def halve_two(ids, near_a, other_a, near_b, other_b, own, p1, p2, p3):
+    for n, (near, other) in enumerate(((near_a, other_a), (near_b, other_b))):
+        halve(ids, near, other, own.at[n], p1.at[n], p2.at[n], p3.at[n])
+
+
 def summed(own, parts):
     total = own[...]
     for part in parts:
@@ -250,13 +255,9 @@
     low[...] = v.astype(bf16)
 
 
-def add_parts(ids, own, a1, a2, a3, total):
-    total[...] = summed(own, (a1, a2, a3))
-
-
-def finish(ids, out_sum, own_b, b1, b2, b3, hidden, tok, grad, gain, done):
+def finish(ids, own, a1, a2, a3, hidden, tok, grad, gain, done):
     length, y, c = ids[0], ids[3], ids[4]
-    o, g = out_sum[...], summed(own_b, (b1, b2, b3))
+    o, g = [summed(own.at[n], [a.at[n] for a in (a1, a2, a3)]) for n in range(2)]
     t = lax.broadcasted_iota(jnp.int32, (PART, 1), 0) + HALF * c + PART * y
     done[0] = jnp.where(t < length, o + hidden[...], 0.0).astype(bf16)
     x = tok[...].astype(f32)
@@ -266,13 +267,14 @@
 
 def attend_back(
     ids, near, far, rows_w, heads, lse, cosine, sine,
-    grads, low, att_grad, key_grad, value_grad,
+    grads, window, low, att_grad, key_grad, value_grad,
 ):
     length, y, c = ids[0], ids[3], ids[4]
     for k, e in enumerate(RELATIVE):
         place = PART * lax.rem(y + e + 4, 4)
         low[at(HALF * c + place, PART, PART), :] = near[k]
         low[at(HALF * (1 - c) + place, PART, PART), :] = far[k]
+    window[...] = low[:, at(384 * y, 384, 384)]
     has_heads = (ids[2] < KEY_AT).astype(f32)
     att_grad[...] = (nt(low[...], rows_w[...]) * has_heads).astype(bf16)
     key_grad[...] = jnp.zeros_like(key_grad)
@@ -343,6 +345,18 @@
         chunks[m, T + DP :, :] = (piece - high.astype(f32)).astype(bf16)
 
 
+def back_to_input(
+    ids, near_low, far_low, rows_w, heads, lse, cosine, sine, w, tok, second_part,
+    grads, window, near, far, chunks,
+    low, att_grad, key_grad, value_grad, gain_part, vec, blocks,
+):
+    attend_back(
+        ids, near_low, far_low, rows_w, heads, lse, cosine, sine,
+        grads, window, low, att_grad, key_grad, value_grad,
+    )
+    joint_back(ids, grads, w, tok, second_part, near, far, chunks, gain_part, vec, blocks)
+
+
 def weigh_joint(ids, normed, grads, moved, mixer_parts, parts):
     keys = [moved[j, :T, :].astype(f32) for j in range(KEY_AT)]
     pair = jnp.concatenate([keys[0] + keys[1] + keys[2], keys[3] + keys[4] + keys[5]], 1)
@@ -367,10 +381,10 @@
 
 
 def weigh_mixer(ids, near, far, low, parts):
-    y, c = ids[3], ids[4]
+    c = ids[4]
 
     def own_columns(half):
-        v = low[at(HALF * half, HALF, HALF), at(384 * y, 384, 384)].astype(f32)
+        v = low[at(HALF * half, HALF, HALF), :].astype(f32)
         return jnp.where(c == 0, v[:, :MC], v[:, MC:]).astype(bf16)
 
     mine, other = own_columns(c), own_columns(1 - c)
@@ -602,17 +616,15 @@
         cost_estimate=SMALL,
     )(gate_grad, up_grad, ff)
 
-    def half_sum(near, far, after=()):
+    def half_sum(body, pairs, after=()):
+        shape = (PART, D) if len(pairs) == 1 else (len(pairs), PART, D)
+        given = [v for near, far in pairs for v in (near, swap_core(far))]
         own, *parts = whole(
-            halve,
-            [((PART, D), f32)] + [((PART, D), bf16)] * 3,
-            [ids, near, swap_core(far)],
-            after=after,
-            limit=8,
+            body, [(shape, f32)] + [(shape, bf16)] * 3, [ids] + given, after=after, limit=16
         )
         return [own] + [shift_y(v, k) for v, k in zip(parts, (1, -1, 2))]
 
-    normed_second_parts = half_sum(near, far)
+    normed_second_parts = half_sum(halve, [(near, far)])
     out_near, out_far = pl.pallas_call(
         spread_out,
         grid=(2,),
@@ -634,29 +646,22 @@
     )
     low_near = jnp.stack(gather(shift_y, low))
     low_far = swap_core(low_near)
-    out_parts = half_sum(out_near, out_far)
-    heads_grad, hidden_low = whole(
-        attend_back,
-        [((T, 2 * JC), bf16), ((T, D), bf16)],
-        [ids, low_near, low_far, rows_w, heads, lse, cosine, sine],
+    heads_grad, hidden_low, input_near, input_far, chunks = whole(
+        back_to_input,
+        [
+            ((T, 2 * JC), bf16), ((T, 2 * MC), bf16), ((HALF, D), bf16), ((HALF, D), bf16),
+            ((MP, T + 2 * DP, HEAD), bf16),
+        ],
+        [ids, low_near, low_far, rows_w, heads, lse, cosine, sine, joint_w, tok, gain_second_part],
         scratch=[
+            pltpu.VMEM((T, D), bf16),
             pltpu.VMEM((T, JC), bf16),
             pltpu.VMEM((T, HEAD), f32),
             pltpu.VMEM((T, HEAD), f32),
-        ],
-        after=[out_parts[0]],
-    )
-    (out_sum,) = whole(add_parts, [((PART, D), f32)], [ids] + out_parts, limit=8, after=[heads_grad])
-    input_near, input_far, chunks = whole(
-        joint_back,
-        [((HALF, D), bf16), ((HALF, D), bf16), ((MP, T + 2 * DP, HEAD), bf16)],
-        [ids, heads_grad, joint_w, tok, gain_second_part],
-        scratch=[
             pltpu.VMEM((1, D), f32),
             pltpu.VMEM((1, DP * MP * 40), f32),
             pltpu.VMEM((DP, MP * 40), f32),
         ],
-        after=[out_sum],
     )
     moved = exchange(chunks, "mp")
     (mixer_parts,) = whole(
@@ -677,11 +682,13 @@
 
     squares = exchange(squares, ("dp", "mp"))
 
-    input_parts = half_sum(input_near, input_far, after=[joint_parts])
+    parts = half_sum(
+        halve_two, [(out_near, out_far), (input_near, input_far)], after=[joint_parts]
+    )
     (done,) = whole(
         finish,
         [((2, PART, D), bf16)],
-        [ids, out_sum] + input_parts + [hidden_part, tok_part, hidden_grad, gain_first],
+        [ids] + parts + [hidden_part, tok_part, hidden_grad, gain_first],
         limit=8,
     )
     (done_near,) = whole(
@@ -695,22 +702,22 @@
     matrices += [expand_weight, expand_moment, expand_square]
     matrices += [v.T for v in (shrink_weight, shrink_moment, shrink_square)]
     matrices += [v[None] for v in (vector_params, vector_moment, vector_square)]
-    def sixth(shape):
+    def third(shape):
         n = len(shape)
         if shape[-2] != ROWS:
             return pl.BlockSpec(shape, lambda i: (0,) * n)
         return pl.BlockSpec(
-            shape[:-2] + (ROWS // 6, shape[-1]), lambda i: (0,) * (n - 2) + (i, 0)
+            shape[:-2] + (ROWS // 3, shape[-1]), lambda i: (0,) * (n - 2) + (i, 0)
         )
 
     given = [squares, joint_shard, mixer_shard, ff_shard, vector_shard] + matrices
     made = [(1, HEAD)] + [v.shape for v in matrices]
     norm, *new = pl.pallas_call(
         update,
-        grid=(6,),
+        grid=(3,),
         out_shape=[jax.ShapeDtypeStruct(shape, f32) for shape in made],
-        in_specs=[sixth(v.shape) for v in given],
-        out_specs=[sixth(shape) for shape in made],
+        in_specs=[third(v.shape) for v in given],
+        out_specs=[third(shape) for shape in made],
         compiler_params=pltpu.CompilerParams(vmem_limit_bytes=60 * MiB),
         cost_estimate=SMALL,
     )(*given)

time: 299 us -> 297 us (level)
  waiting for transfers between devices: 82.7 us -> 91 us
  starting transfers between devices: 89.2 us -> 83.7 us
  Pallas kernels: 94.3 us -> 91 us
    ppermute x21 -> x18, waiting for transfers between devices: 19.7 us -> 30 us  [shift_y(): return lax.ppermute(v, 'mp', [(i, (i + 2 * k) % MP) for i in range(MP)])]
    ppermute x12, starting transfers between devices: 13 us -> 8.64 us  [swap_core(): return lax.ppermute(v, 'mp', [(i, i ^ 1) for i in range(MP)])]
    ppermute x21 -> x18, starting transfers between devices: 25.3 us -> 21.6 us  [shift_y(): return lax.ppermute(v, 'mp', [(i, (i + 2 * k) % MP) for i in range(MP)])]
    pallas_call x16 -> x13, Pallas kernels: 55.3 us -> 52.7 us  [whole(): pl.pallas_call(bare, out_shape=[jax.ShapeDtypeStruct(s, d) for s, d in ou...]
    unnamed x74 -> x62, local copies, waits for them, and re-layouts: 8.59 us -> 7.15 us
  transfers between devices with their start and end apart: 41 -> 38, of which waited for: 21 -> 19; matrix products, arithmetic and copies ran while one was open for 2% -> 2% of each run, Pallas kernels for 24% -> 23%
where the time goes in v2:
time: 297 us; the launch traced here: 296 us
  waiting for transfers between devices  91 us (31%)
  Pallas kernels  91 us (31%)
  starting transfers between devices  83.7 us (28%)
  between operations  15.3 us (5%)
  local copies, waits for them, and re-layouts  11.9 us (4%)
  other arithmetic  3.29 us (1%)
    all_to_all x6, starting transfers between devices, exchange(): return lax.all_to_all(v, axis, split_axis=0, concat_axis=0, tiled=True)  53.4 us
    pallas_call x13, Pallas kernels, whole(): pl.pallas_call(bare, out_shape=[jax.ShapeDtypeStruct(s, d) for s, d in ou...  52.7 us
    all_to_all x6, waiting for transfers between devices, exchange(): return lax.all_to_all(v, axis, split_axis=0, concat_axis=0, tiled=True)  50.4 us
    ppermute x18, waiting for transfers between devices, shift_y(): return lax.ppermute(v, 'mp', [(i, (i + 2 * k) % MP) for i in range(MP)])  30 us
    ppermute x18, starting transfers between devices, shift_y(): return lax.ppermute(v, 'mp', [(i, (i + 2 * k) % MP) for i in range(MP)])  21.6 us
    pallas_call x1, Pallas kernels, body(): pl.pallas_call(gated, grid=(pl.cdiv(FP, 256),), out_shape=[jax.ShapeDtype...  18.4 us
    ppermute x12, waiting for transfers between devices, swap_core(): return lax.ppermute(v, 'mp', [(i, i ^ 1) for i in range(MP)])  10.6 us
    ppermute x12, starting transfers between devices, swap_core(): return lax.ppermute(v, 'mp', [(i, i ^ 1) for i in range(MP)])  8.64 us
  transfers between devices with their start and end apart: 38, of which 19 were waited for; matrix products, arithmetic and copies ran while one was open for 2% of the time, Pallas kernels for 23%

profile of v2, /device:TPU:1, one launch (start us, length us, event | category | flops | bytes accessed | tf_op | source)
XLA Modules:
  0.0 296.1 jit_solution(588850246801622295)
XLA Ops:
  13.6 7.7 %all-to-all-start = ((bf16[16,176,256]{2,1,0:T(8,128)(2,1)}), bf16[16,176,256]{2,1,0:T(8,128)(2,1)S(1)}, u32[]{:S(2)}, u32[]{:S(2)}) async-start(bf16[16,176,256]{2,1,0:T(8,128)(2,1)} %broadcast_in_dim.27), calls=%async_computation | async-start | bytes 2883584 | tf_op jit(solution)/shard_map/all_to_all | solution.py:59
  28.9 19.3 %all-to-all-done.refs_6_ = bf16[16,176,256]{2,1,0:T(8,128)(2,1)S(1)} async-done(((bf16[16,176,256]{2,1,0:T(8,128)(2,1)}), bf16[16,176,256]{2,1,0:T(8,128)(2,1)S(1)}, u32[]{:S(2)}, u32[]{:S(2)}) %all-to-all-start) | async-done | bytes 1441824 | tf_op jit(solution)/shard_map/all_to_all | solution.py:59
  49.2 6.6 %all-to-all-start.1 = ((bf16[16,112,256]{2,1,0:T(8,128)(2,1)}), bf16[16,112,256]{2,1,0:T(8,128)(2,1)S(1)}, u32[]{:S(2)}, u32[]{:S(2)}) async-start(bf16[16,112,256]{2,1,0:T(8,128)(2,1)} %broadcast_in_dim.28), calls=%async_computation.1 | async-start | bytes 1835008 | tf_op jit(solution)/shard_map/all_to_all | solution.py:59
  57.2 4.3 %shard_map.331 = (bf16[512,1536]{1,0:T(8,128)(2,1)}, bf16[1536,512]{1,0:T(8,128)(2,1)}, bf16[64,1536]{1,0:T(8,128)(2,1)}, bf16[64,1536]{1,0:T(8,128)(2,1)}) custom-call(s32[5]{0:T(128)} %stack.61.refs_0_, bf16[512,1536]{1,0:T(8,128)(2,1)} %bitcast.60, bf16[512,1536]{1,0:T(8,128)(2,1)} %bitcast.53), custom_call_target="tpu_custom_call" | custom-call | flops 1 | bytes 1 | tf_op jit(solution)/shard_map/pallas_call | solution.py:87
  69.6 8.8 %shard_map.332 = (bf16[512,1536]{1,0:T(8,128)(2,1)}, bf16[512,512]{1,0:T(8,128)(2,1)}, bf16[8,256,256]{2,1,0:T(8,128)(2,1)}, f32[512,256]{1,0:T(8,128)}, bf16[1536,512]{1,0:T(8,128)(2,1)}) custom-call(s32[5]{0:T(128)} %stack.61.refs_0_, bf16[512,1536]{1,0:T(8,128)(2,1)} %bitcast.54, f32[1,1536]{1,0:T(1,128)} %broadcast_in_dim.29.refs_2_.refs_8_, ...), custom_call_target="tpu_custom_call" | custom-call | flops 1 | bytes 1 | tf_op jit(solution)/shard_map/pallas_call | solution.py:87
  78.4 16.1 %all-to-all-start.2 = ((bf16[8,256,256]{2,1,0:T(8,128)(2,1)}), bf16[8,256,256]{2,1,0:T(8,128)(2,1)S(1)}, u32[]{:S(2)}, u32[]{:S(2)}) async-start(bf16[8,256,256]{2,1,0:T(8,128)(2,1)} %get-tuple-element.77), calls=%async_computation.2 | async-start | bytes 2097152 | tf_op jit(solution)/shard_map/all_to_all | solution.py:59
  100.6 9.0 %all-to-all-done.2.refs_1_ = bf16[8,256,256]{2,1,0:T(8,128)(2,1)S(1)} async-done(((bf16[8,256,256]{2,1,0:T(8,128)(2,1)}), bf16[8,256,256]{2,1,0:T(8,128)(2,1)S(1)}, u32[]{:S(2)}, u32[]{:S(2)}) %all-to-all-start.2) | async-done | bytes 1048608 | tf_op jit(solution)/shard_map/all_to_all | solution.py:59
  110.6 7.2 %shard_map.333 = (f32[64,1536]{1,0:T(8,128)}, bf16[256,1536]{1,0:T(8,128)(2,1)}, bf16[256,1536]{1,0:T(8,128)(2,1)}) custom-call(s32[5]{0:T(128)} %stack.61.refs_0_, bf16[8,256,256]{2,1,0:T(8,128)(2,1)} %copy-done.15, bf16[16,80,256]{2,1,0:T(8,128)(2,1)} %copy-done.20, bf16[16,80,256]{2,1,0:T(8,128)(2,1)} %collective-permute-done.4.refs_3_, ...), custom_call_target="tpu_custom_call" | custom-call | flops 1 | bytes 1 | tf_op jit(solution)/shard_map/pallas_call | solution.py:87
  121.7 18.4 %shard_map.334 = (bf16[512,1152]{1,0:T(8,128)(2,1)}, bf16[512,1152]{1,0:T(8,128)(2,1)}, bf16[512,1152]{1,0:T(8,128)(2,1)}, bf16[16,3,96,1152]{3,2,1,0:T(8,128)(2,1)}) custom-call(bf16[256,1536]{1,0:T(8,128)(2,1)} %get-tuple-element.78.near, bf16[256,1536]{1,0:T(8,128)(2,1)} %copy-done.24, bf16[512,1536]{1,0:T(8,128)(2,1)} %get-tuple-element.76.refs_8_.back, ...), custom_call_target="tpu_custom_call" | custom-call | flops 1 | bytes 1 | tf_op jit(solution)/shard_map/pallas_call | solution.py:595
  140.1 8.0 %shard_map.336 = (bf16[256,1536]{1,0:T(8,128)(2,1)}, bf16[256,1536]{1,0:T(8,128)(2,1)}) custom-call(bf16[512,1152]{1,0:T(8,128)(2,1)} %get-tuple-element.83.gate_grad, bf16[512,1152]{1,0:T(8,128)(2,1)} %get-tuple-element.84.up_grad, bf16[16,3,96,1152]{3,2,1,0:T(8,128)(2,1)} %bitcast.51), custom_call_target="tpu_custom_call" | custom-call | flops 1 | bytes 1 | tf_op jit(solution)/shard_map/pallas_call | solution.py:608
  155.3 5.2 %shard_map.335 = (bf16[256,1536]{1,0:T(8,128)(2,1)}, bf16[256,1536]{1,0:T(8,128)(2,1)}) custom-call(bf16[512,1152]{1,0:T(8,128)(2,1)} %get-tuple-element.80.act, bf16[16,3,96,1152]{3,2,1,0:T(8,128)(2,1)} %bitcast.52), custom_call_target="tpu_custom_call" | custom-call | flops 1 | bytes 1 | tf_op jit(solution)/shard_map/pallas_call | solution.py:628
  171.0 4.1 %collective-permute-done.19 = bf16[64,1536]{1,0:T(8,128)(2,1)S(1)} collective-permute-done((bf16[64,1536]{1,0:T(8,128)(2,1)S(1)}, bf16[64,1536]{1,0:T(8,128)(2,1)S(1)}, u32[]{:S(2)}, u32[]{:S(2)}) %collective-permute-start.19) | collective-permute-done | bytes 196640 | tf_op jit(solution)/shard_map/ppermute | solution.py:47
  181.4 12.0 %shard_map.339 = (bf16[512,512]{1,0:T(8,128)(2,1)}, bf16[512,384]{1,0:T(8,128)(2,1)}, bf16[256,1536]{1,0:T(8,128)(2,1)}, bf16[256,1536]{1,0:T(8,128)(2,1)}, bf16[8,544,128]{2,1,0:T(8,128)(2,1)}) custom-call(s32[5]{0:T(128)} %stack.61.refs_0_, bf16[4,64,1536]{2,1,0:T(8,128)(2,1)} %copy-done.19, bf16[4,64,1536]{2,1,0:T(8,128)(2,1)} %copy-done.23, ...), custom_call_target="tpu_custom_call" | custom-call | flops 1 | bytes 1 | tf_op jit(solution)/shard_map/pallas_call | solution.py:87
  193.4 4.5 %all-to-all-start.3 = ((bf16[8,544,128]{2,1,0:T(8,128)(2,1)}), bf16[8,544,128]{2,1,0:T(8,128)(2,1)}, u32[]{:S(2)}, u32[]{:S(2)}) async-start(bf16[8,544,128]{2,1,0:T(8,128)(2,1)} %get-tuple-element.103), calls=%async_computation.3 | async-start | bytes 2228224 | tf_op jit(solution)/shard_map/all_to_all | solution.py:59
  198.4 3.3 %shard_map.340.refs_4_ = bf16[16,96,192]{2,1,0:T(8,128)(2,1)} custom-call(s32[5]{0:T(128)} %stack.61.refs_0_, bf16[8,256,256]{2,1,0:T(8,128)(2,1)} %copy-done.15, bf16[8,256,256]{2,1,0:T(8,128)(2,1)} %collective-permute-done.22.refs_2_, bf16[512,384]{1,0:T(8,128)(2,1)} %get-tuple-element.104.refs_3_), custom_call_target="tpu_custom_call" | custom-call | flops 1 | bytes 1 | tf_op jit(solution)/shard_map/pallas_call | solution.py:87
  201.7 12.2 %all-to-all-done.3.refs_3_ = bf16[8,544,128]{2,1,0:T(8,128)(2,1)} async-done(((bf16[8,544,128]{2,1,0:T(8,128)(2,1)}), bf16[8,544,128]{2,1,0:T(8,128)(2,1)}, u32[]{:S(2)}, u32[]{:S(2)}) %all-to-all-start.3) | async-done | bytes 1114144 | tf_op jit(solution)/shard_map/all_to_all | solution.py:59
  213.8 4.0 %shard_map.341.refs_5_ = bf16[16,104,448]{2,1,0:T(8,128)(2,1)} custom-call(s32[5]{0:T(128)} %stack.61.refs_0_, bf16[512,1536]{1,0:T(8,128)(2,1)} %get-tuple-element.101.refs_1_, bf16[512,512]{1,0:T(8,128)(2,1)} %get-tuple-element.102.refs_2_, bf16[8,544,128]{2,1,0:T(8,128)(2,1)} %all-to-all-done.3.refs_3_, bf16[16,96,192]{2,1,0:T(8,128)(2,1)} %shard_map.340.refs_4_), custom_call_target="tpu_custom_call" | custom-call | flops 1 | bytes 1 | tf_op jit(solution)/shard_map/pallas_call | solution.py:87
  217.8 6.7 %all-to-all-start.4 = ((bf16[16,104,448]{2,1,0:T(8,128)(2,1)}), bf16[16,104,448]{2,1,0:T(8,128)(2,1)}, u32[]{:S(2)}, u32[]{:S(2)}) async-start(bf16[16,104,448]{2,1,0:T(8,128)(2,1)} %shard_map.341.refs_5_), calls=%async_computation.4 | async-start | bytes 3407872 | tf_op jit(solution)/shard_map/all_to_all | solution.py:59
  230.3 8.1 %collective-permute-done.23.refs_2_ = bf16[2,64,1536]{2,1,0:T(8,128)(2,1)S(1)} collective-permute-done((bf16[2,64,1536]{2,1,0:T(8,128)(2,1)S(1)}, bf16[2,64,1536]{2,1,0:T(8,128)(2,1)S(1)}, u32[]{:S(2)}, u32[]{:S(2)}) %collective-permute-start.23) | collective-permute-done | bytes 393248 | tf_op jit(solution)/shard_map/ppermute | solution.py:47
  238.3 8.5 %collective-permute-done.25.refs_4_ = bf16[2,64,1536]{2,1,0:T(8,128)(2,1)S(1)} collective-permute-done((bf16[2,64,1536]{2,1,0:T(8,128)(2,1)S(1)}, bf16[2,64,1536]{2,1,0:T(8,128)(2,1)S(1)}, u32[]{:S(2)}, u32[]{:S(2)}) %collective-permute-start.25) | collective-permute-done | bytes 393248 | tf_op jit(solution)/shard_map/ppermute | solution.py:47
  253.5 11.8 %all-to-all-start.5 = ((f32[128,1,128]{2,1,0:T(1,128)}), f32[128,1,128]{2,1,0:T(1,128)S(1)}, u32[]{:S(2)}, u32[]{:S(2)}) async-start(f32[128,1,128]{2,1,0:T(1,128)} %get-tuple-element.112), calls=%async_computation.5 | async-start | bytes 131072 | tf_op jit(solution)/shard_map/all_to_all | solution.py:59
  265.4 9.4 %all-to-all-done.5.refs_5_.squares = f32[128,1,128]{2,1,0:T(1,128)S(1)} async-done(((f32[128,1,128]{2,1,0:T(1,128)}), f32[128,1,128]{2,1,0:T(1,128)S(1)}, u32[]{:S(2)}, u32[]{:S(2)}) %all-to-all-start.5) | async-done | bytes 65568 | tf_op jit(solution)/shard_map/all_to_all | solution.py:59
  276.4 6.7 %shard_map.347 = (f32[1,128]{1,0:T(1,128)}, f32[96,256]{1,0:T(8,128)}, f32[96,256]{1,0:T(8,128)}, f32[96,256]{1,0:T(8,128)}, f32[96,192]{1,0:T(8,128)}, /*index=...) custom-call(f32[128,1,128]{2,1,0:T(1,128)} %copy-done.6, ...), custom_call_target="tpu_custom_call" | custom-call | flops 1 | bytes 1 | tf_op jit(solution)/shard_map/pallas_call | solution.py:715
  284.3 5.0 %shard_map.346 = (f32[1,512,1536]{2,1,0:T(8,128)}, f32[1,512,1536]{2,1,0:T(8,128)}) custom-call(s32[5]{0:T(128)} %stack.61.refs_0_, bf16[4,2,64,1536]{3,2,1,0:T(8,128)(2,1)} %copy-done.1, bf16[4,2,64,1536]{3,2,1,0:T(8,128)(2,1)} %copy-done.22), custom_call_target="tpu_custom_call" | custom-call | flops 1 | bytes 1 | tf_op jit(solution)/shard_map/pallas_call | solution.py:87
  (181 shorter events, 74.0 us)
Async XLA Ops:
  7.2 113.7 %all-gather.3.cloned.1.call-start = ((), (), s32[]{:S(2)}) async-start(), calls=%async_computation.7 | async-start | bytes 11280384 | tf_op jit(solution)/shard_map/all_gather | solution.py:523
  13.6 34.6 %all-to-all-start = ((bf16[16,176,256]{2,1,0:T(8,128)(2,1)}), bf16[16,176,256]{2,1,0:T(8,128)(2,1)S(1)}, u32[]{:S(2)}, u32[]{:S(2)}) async-start(bf16[16,176,256]{2,1,0:T(8,128)(2,1)} %broadcast_in_dim.27), calls=%async_computation | async-start | bytes 2883584 | tf_op jit(solution)/shard_map/all_to_all | solution.py:59
  49.2 18.5 %all-to-all-start.1 = ((bf16[16,112,256]{2,1,0:T(8,128)(2,1)}), bf16[16,112,256]{2,1,0:T(8,128)(2,1)S(1)}, u32[]{:S(2)}, u32[]{:S(2)}) async-start(bf16[16,112,256]{2,1,0:T(8,128)(2,1)} %broadcast_in_dim.28), calls=%async_computation.1 | async-start | bytes 1835008 | tf_op jit(solution)/shard_map/all_to_all | solution.py:59
  61.5 33.1 %collective-permute-start.6 = (bf16[16,80,256]{2,1,0:T(8,128)(2,1)S(1)}, bf16[16,80,256]{2,1,0:T(8,128)(2,1)}, u32[]{:S(2)}, u32[]{:S(2)}) collective-permute-start(bf16[16,80,256]{2,1,0:T(8,128)(2,1)S(1)} %slice.135.refs_2_), channel_id=1, source_target_pairs={{0,4},{1,5},{2,6},{3,7},{4,0},{5,1},{6,2},{7,3},{8,12},{9,13},{10,... | collective-permute-start | bytes 1966088 | tf_op jit(solution)/shard_map/ppermute | solution.py:47
  64.6 30.5 %collective-permute-start.4 = (bf16[16,80,256]{2,1,0:T(8,128)(2,1)S(1)}, bf16[16,80,256]{2,1,0:T(8,128)(2,1)}, u32[]{:S(2)}, u32[]{:S(2)}) collective-permute-start(bf16[16,80,256]{2,1,0:T(8,128)(2,1)S(1)} %slice.135.refs_2_), channel_id=1, source_target_pairs={{0,2},{1,3},{2,4},{3,5},{4,6},{5,7},{6,0},{7,1},{8,10},{9,11},{10,... | collective-permute-start | bytes 1966088 | tf_op jit(solution)/shard_map/ppermute | solution.py:47
  65.0 30.2 %collective-permute-start.5 = (bf16[16,80,256]{2,1,0:T(8,128)(2,1)S(1)}, bf16[16,80,256]{2,1,0:T(8,128)(2,1)}, u32[]{:S(2)}, u32[]{:S(2)}) collective-permute-start(bf16[16,80,256]{2,1,0:T(8,128)(2,1)S(1)} %slice.135.refs_2_), channel_id=1, source_target_pairs={{0,6},{1,7},{2,0},{3,1},{4,2},{5,3},{6,4},{7,5},{8,14},{9,15},{10,... | collective-permute-start | bytes 1966088 | tf_op jit(solution)/shard_map/ppermute | solution.py:47
  78.4 31.2 %all-to-all-start.2 = ((bf16[8,256,256]{2,1,0:T(8,128)(2,1)}), bf16[8,256,256]{2,1,0:T(8,128)(2,1)S(1)}, u32[]{:S(2)}, u32[]{:S(2)}) async-start(bf16[8,256,256]{2,1,0:T(8,128)(2,1)} %get-tuple-element.77), calls=%async_computation.2 | async-start | bytes 2097152 | tf_op jit(solution)/shard_map/all_to_all | solution.py:59
  94.5 156.2 %reduce-scatter.4.cloned.1.call-start = ((), (), s32[]{:S(2)}) async-start(), calls=%async_computation.8 | async-start | bytes 11280384
  152.5 8.0 %collective-permute-start.14 = (bf16[64,1536]{1,0:T(8,128)(2,1)S(1)}, bf16[64,1536]{1,0:T(8,128)(2,1)S(1)}, u32[]{:S(2)}, u32[]{:S(2)}) collective-permute-start(bf16[64,1536]{1,0:T(8,128)(2,1)S(1)} %get-tuple-element.88), channel_id=1, source_target_pairs={{0,2},{1,3},{2,4},{3,5},{4,6},{5,7},{6,0},{7,1},{8,10},{9,11},{10,... | collective-permute-start | bytes 589832 | tf_op jit(solution)/shard_map/ppermute | solution.py:47
  155.3 8.3 %collective-permute-start.16 = (bf16[64,1536]{1,0:T(8,128)(2,1)S(1)}, bf16[64,1536]{1,0:T(8,128)(2,1)S(1)}, u32[]{:S(2)}, u32[]{:S(2)}) collective-permute-start(bf16[64,1536]{1,0:T(8,128)(2,1)S(1)} %get-tuple-element.90), channel_id=1, source_target_pairs={{0,4},{1,5},{2,6},{3,7},{4,0},{5,1},{6,2},{7,3},{8,12},{9,13},{10,... | collective-permute-start | bytes 589832 | tf_op jit(solution)/shard_map/ppermute | solution.py:47
  167.3 7.8 %collective-permute-start.19 = (bf16[64,1536]{1,0:T(8,128)(2,1)S(1)}, bf16[64,1536]{1,0:T(8,128)(2,1)S(1)}, u32[]{:S(2)}, u32[]{:S(2)}) collective-permute-start(bf16[64,1536]{1,0:T(8,128)(2,1)S(1)} %get-tuple-element.93), channel_id=1, source_target_pairs={{0,4},{1,5},{2,6},{3,7},{4,0},{5,1},{6,2},{7,3},{8,12},{9,13},{10,... | collective-permute-start | bytes 589832 | tf_op jit(solution)/shard_map/ppermute | solution.py:47
  178.5 19.9 %collective-permute-start.22 = (bf16[8,256,256]{2,1,0:T(8,128)(2,1)S(1)}, bf16[8,256,256]{2,1,0:T(8,128)(2,1)}, u32[]{:S(2)}, u32[]{:S(2)}) collective-permute-start(bf16[8,256,256]{2,1,0:T(8,128)(2,1)S(1)} %copy-done.16), channel_id=1, source_target_pairs={{0,1},{1,0},{2,3},{3,2},{4,5},{5,4},{6,7},{7,6},{8,9},{9,8},{10,11... | collective-permute-start | bytes 3145736 | tf_op jit(solution)/shard_map/ppermute | solution.py:55
  193.4 20.4 %all-to-all-start.3 = ((bf16[8,544,128]{2,1,0:T(8,128)(2,1)}), bf16[8,544,128]{2,1,0:T(8,128)(2,1)}, u32[]{:S(2)}, u32[]{:S(2)}) async-start(bf16[8,544,128]{2,1,0:T(8,128)(2,1)} %get-tuple-element.103), calls=%async_computation.3 | async-start | bytes 2228224 | tf_op jit(solution)/shard_map/all_to_all | solution.py:59
  197.9 26.6 %collective-permute-start.12 = (bf16[256,1536]{1,0:T(8,128)(2,1)}, bf16[256,1536]{1,0:T(8,128)(2,1)}, u32[]{:S(2)}, u32[]{:S(2)}) collective-permute-start(bf16[256,1536]{1,0:T(8,128)(2,1)} %get-tuple-element.82.refs_8_), channel_id=1, source_target_pairs={{0,1},{1,0},{2,3},{3,2},{4,5},{5,4},{6,7},{7,6},{8,9},{9,8},{10,11... | collective-permute-start | bytes 2359304 | tf_op jit(solution)/shard_map/ppermute | solution.py:55
  198.1 26.4 %collective-permute-start.21 = (bf16[256,1536]{1,0:T(8,128)(2,1)}, bf16[256,1536]{1,0:T(8,128)(2,1)}, u32[]{:S(2)}, u32[]{:S(2)}) collective-permute-start(bf16[256,1536]{1,0:T(8,128)(2,1)} %get-tuple-element.100), channel_id=1, source_target_pairs={{0,1},{1,0},{2,3},{3,2},{4,5},{5,4},{6,7},{7,6},{8,9},{9,8},{10,11... | collective-permute-start | bytes 2359304 | tf_op jit(solution)/shard_map/ppermute | solution.py:55
  217.8 32.8 %all-to-all-start.4 = ((bf16[16,104,448]{2,1,0:T(8,128)(2,1)}), bf16[16,104,448]{2,1,0:T(8,128)(2,1)}, u32[]{:S(2)}, u32[]{:S(2)}) async-start(bf16[16,104,448]{2,1,0:T(8,128)(2,1)} %shard_map.341.refs_5_), calls=%async_computation.4 | async-start | bytes 3407872 | tf_op jit(solution)/shard_map/all_to_all | solution.py:59
  227.5 10.8 %collective-permute-start.23 = (bf16[2,64,1536]{2,1,0:T(8,128)(2,1)S(1)}, bf16[2,64,1536]{2,1,0:T(8,128)(2,1)S(1)}, u32[]{:S(2)}, u32[]{:S(2)}) collective-permute-start(bf16[2,64,1536]{2,1,0:T(8,128)(2,1)S(1)} %get-tuple-element.106), channel_id=1, source_target_pairs={{0,2},{1,3},{2,4},{3,5},{4,6},{5,7},{6,0},{7,1},{8,10},{9,11},{10,... | collective-permute-start | bytes 1179656 | tf_op jit(solution)/shard_map/ppermute | solution.py:47
  227.9 10.4 %collective-permute-start.24 = (bf16[2,64,1536]{2,1,0:T(8,128)(2,1)S(1)}, bf16[2,64,1536]{2,1,0:T(8,128)(2,1)S(1)}, u32[]{:S(2)}, u32[]{:S(2)}) collective-permute-start(bf16[2,64,1536]{2,1,0:T(8,128)(2,1)S(1)} %get-tuple-element.107), channel_id=1, source_target_pairs={{0,6},{1,7},{2,0},{3,1},{4,2},{5,3},{6,4},{7,5},{8,14},{9,15},{10,... | collective-permute-start | bytes 1179656 | tf_op jit(solution)/shard_map/ppermute | solution.py:47
  230.3 16.6 %collective-permute-start.25 = (bf16[2,64,1536]{2,1,0:T(8,128)(2,1)S(1)}, bf16[2,64,1536]{2,1,0:T(8,128)(2,1)S(1)}, u32[]{:S(2)}, u32[]{:S(2)}) collective-permute-start(bf16[2,64,1536]{2,1,0:T(8,128)(2,1)S(1)} %get-tuple-element.108), channel_id=1, source_target_pairs={{0,4},{1,5},{2,6},{3,7},{4,0},{5,1},{6,2},{7,3},{8,12},{9,13},{10,... | collective-permute-start | bytes 1179656 | tf_op jit(solution)/shard_map/ppermute | solution.py:47
  247.9 17.4 %collective-permute-start.26 = (bf16[2,64,1536]{2,1,0:T(8,128)(2,1)S(1)}, bf16[2,64,1536]{2,1,0:T(8,128)(2,1)S(1)}, u32[]{:S(2)}, u32[]{:S(2)}) collective-permute-start(bf16[2,64,1536]{2,1,0:T(8,128)(2,1)S(1)} %shard_map.343.refs_1_), channel_id=1, source_target_pairs={{0,2},{1,3},{2,4},{3,5},{4,6},{5,7},{6,0},{7,1},{8,10},{9,11},{10,... | collective-permute-start | bytes 1179656 | tf_op jit(solution)/shard_map/ppermute | solution.py:47
  248.5 16.9 %collective-permute-start.27 = (bf16[2,64,1536]{2,1,0:T(8,128)(2,1)S(1)}, bf16[2,64,1536]{2,1,0:T(8,128)(2,1)S(1)}, u32[]{:S(2)}, u32[]{:S(2)}) collective-permute-start(bf16[2,64,1536]{2,1,0:T(8,128)(2,1)S(1)} %shard_map.343.refs_1_), channel_id=1, source_target_pairs={{0,6},{1,7},{2,0},{3,1},{4,2},{5,3},{6,4},{7,5},{8,14},{9,15},{10,... | collective-permute-start | bytes 1179656 | tf_op jit(solution)/shard_map/ppermute | solution.py:47
  250.7 14.7 %collective-permute-start.28 = (bf16[2,64,1536]{2,1,0:T(8,128)(2,1)S(1)}, bf16[2,64,1536]{2,1,0:T(8,128)(2,1)S(1)}, u32[]{:S(2)}, u32[]{:S(2)}) collective-permute-start(bf16[2,64,1536]{2,1,0:T(8,128)(2,1)S(1)} %shard_map.343.refs_1_), channel_id=1, source_target_pairs={{0,4},{1,5},{2,6},{3,7},{4,0},{5,1},{6,2},{7,3},{8,12},{9,13},{10,... | collective-permute-start | bytes 1179656 | tf_op jit(solution)/shard_map/ppermute | solution.py:47
  253.5 21.2 %all-to-all-start.5 = ((f32[128,1,128]{2,1,0:T(1,128)}), f32[128,1,128]{2,1,0:T(1,128)S(1)}, u32[]{:S(2)}, u32[]{:S(2)}) async-start(f32[128,1,128]{2,1,0:T(1,128)} %get-tuple-element.112), calls=%async_computation.5 | async-start | bytes 131072 | tf_op jit(solution)/shard_map/all_to_all | solution.py:59
  275.4 7.7 %collective-permute-start.29 = (bf16[4,2,64,1536]{3,2,1,0:T(8,128)(2,1)S(1)}, bf16[4,2,64,1536]{3,2,1,0:T(8,128)(2,1)S(1)}, u32[]{:S(2)}, u32[]{:S(2)}) collective-permute-start(bf16[4,2,64,1536]{3,2,1,0:T(8,128)(2,1)S(1)} %shard_map.345.refs_1_), channel_id=1, source_target_pairs={{0,1},{1,0},{2,3},{3,2},{4,5},{5,4},{6,7},{7,6},{8,9},{9,8},{10,11... | collective-permute-start | bytes 4718600 | tf_op jit(solution)/shard_map/ppermute | solution.py:55
  (45 other events, 316.0 us)
Sparse Core Ops, SparseCore 0:
  10.2 103.7 all-gather.2
  140.3 88.2 reduce-scatter.3

commit v3 on v2

--- a/solution.py
+++ b/solution.py
@@ -49,6 +49,10 @@
 
 def from_last_chip(v, k):
     return lax.ppermute(v, "mp", [(i, (i + 2 * k) % MP) for i in (MP - 2, MP - 1)])
+
+
+def to_last_chip(v, y):
+    return lax.ppermute(v, "mp", [(2 * y + c, MP - 2 + c) for c in range(2)])
 
 
 def swap_core(v):
@@ -267,7 +271,7 @@
 
 def attend_back(
     ids, near, far, rows_w, heads, lse, cosine, sine,
-    grads, window, low, att_grad, key_grad, value_grad,
+    grads, window, own_kind, other_kind, low, att_grad, key_grad, value_grad,
 ):
     length, y, c = ids[0], ids[3], ids[4]
     for k, e in enumerate(RELATIVE):
@@ -300,6 +304,17 @@
     dk = dk * cosine[...] - pltpu.roll(dk, HEAD // 2, 1) * sine[...]
     grads[:, 2 * HEAD : 3 * HEAD] = dk.astype(bf16)
     grads[:, 3 * HEAD :] = value_grad[...].astype(bf16)
+    k, v = grads[:, 2 * HEAD : 3 * HEAD], grads[:, 3 * HEAD :]
+
+    @pl.when(c == 0)
+    def _():
+        own_kind[...] = k
+        other_kind[...] = v
+
+    @pl.when(c != 0)
+    def _():
+        own_kind[...] = v
+        other_kind[...] = k
 
 
 def joint_back(
@@ -337,29 +352,39 @@
     for d in range(DP):
         blocks[d : d + 1, :] = vec[:, 320 * d : 320 * (d + 1)]
     for m in range(MP):
-        chunks[m, :T, :] = g[:, 2 * HEAD : 3 * HEAD] if m < MP - 1 else g[:, 3 * HEAD :]
         piece = blocks[:, 40 * m : 40 * (m + 1)]
         piece = jnp.concatenate([piece, jnp.zeros((DP, HEAD - 40), f32)], 1)
         high = piece.astype(bf16)
-        chunks[m, T : T + DP, :] = high
-        chunks[m, T + DP :, :] = (piece - high.astype(f32)).astype(bf16)
+        chunks[m, :DP, :] = high
+        chunks[m, DP:, :] = (piece - high.astype(f32)).astype(bf16)
 
 
 def back_to_input(
     ids, near_low, far_low, rows_w, heads, lse, cosine, sine, w, tok, second_part,
-    grads, window, near, far, chunks,
+    grads, window, own_kind, other_kind, near, far, chunks,
     low, att_grad, key_grad, value_grad, gain_part, vec, blocks,
 ):
     attend_back(
         ids, near_low, far_low, rows_w, heads, lse, cosine, sine,
-        grads, window, low, att_grad, key_grad, value_grad,
+        grads, window, own_kind, other_kind, low, att_grad, key_grad, value_grad,
     )
     joint_back(ids, grads, w, tok, second_part, near, far, chunks, gain_part, vec, blocks)
 
 
-def weigh_joint(ids, normed, grads, moved, mixer_parts, parts):
-    keys = [moved[j, :T, :].astype(f32) for j in range(KEY_AT)]
-    pair = jnp.concatenate([keys[0] + keys[1] + keys[2], keys[3] + keys[4] + keys[5]], 1)
+def group_parts(ids, own, other, both, left, right):
+    own_group = lax.div(jnp.minimum(ids[2], KEY_AT - 1), 3)
+    partner = ids[2] + 1 - 2 * ids[4]
+    other_group = lax.div(jnp.minimum(partner, KEY_AT - 1), 3)
+    a, b = own[...].astype(f32), other[...].astype(f32)
+    for g, out in ((0, left), (1, right)):
+        part = a * (own_group == g).astype(f32) + b * (other_group == g).astype(f32)
+        out[...] = part.astype(bf16)
+        both[:, HEAD * g : HEAD * (g + 1)] = part.astype(bf16)
+
+
+def weigh_joint(ids, normed, grads, left, right, both, moved, mixer_parts, parts):
+    pair = jnp.concatenate([left[...].astype(f32), right[...].astype(f32)], 1)
+    pair = pair + both[...].astype(f32)
     own = grads[:, :JC].astype(f32)
     g = jnp.where(ids[2] < KEY_AT, own, pair).astype(bf16)
     for r in range(4):
@@ -367,9 +392,9 @@
         part = tn(normed[:, cols], g).astype(bf16)
         parts[4 * r : 4 * (r + 1), :ROWS, :JC] = part.reshape(4, ROWS, JC)
     parts[:, :ROWS, JC:] = mixer_parts[...]
-    vec = moved[0, T:, :].astype(f32)
+    vec = moved[0].astype(f32)
     for j in range(1, MP):
-        vec += moved[j, T:, :].astype(f32)
+        vec += moved[j].astype(f32)
     vec = vec[:DP] + vec[DP:]
     high = vec.astype(bf16).astype(f32)
     rest = jnp.zeros((8, MC), bf16)
@@ -459,13 +484,29 @@
     )
 
 
-def settle(ids, near, far, output, input_grad):
-    y, c = ids[3], ids[4]
-    for n, out in enumerate((output, input_grad)):
-        for k, e in enumerate(RELATIVE):
-            place = PART * lax.rem(y + e + 4, 4)
-            out[0, at(HALF * c + place, PART, PART), :] = near[k, n].astype(f32)
-            out[0, at(HALF * (1 - c) + place, PART, PART), :] = far[k, n].astype(f32)
+def write_half(ids, half, pieces, outs, rows, sems):
+    for k, e in enumerate(RELATIVE):
+        place = at(PART * lax.rem(ids[3] + e + 4, 4), PART, PART)
+        for n in range(2):
+            rows[n, place, :] = pieces[k][n].astype(f32)
+    copies = [
+        pltpu.make_async_copy(rows.at[n], out.at[0, at(HALF * half, HALF, HALF)], sems.at[n])
+        for n, out in enumerate(outs)
+    ]
+    for copy in copies:
+        copy.start()
+    for copy in copies:
+        copy.wait()
+
+
+def settle_near(ids, p0, p1, p2, p3, output, input_grad, token, rows, sems):
+    token[...] = jnp.zeros_like(token)
+    write_half(ids, ids[4], (p0, p1, p2, p3), (output, input_grad), rows, sems)
+
+
+def settle_far(ids, far, _a, _b, output, input_grad, rows, sems):
+    pieces = [far.at[k] for k in range(4)]
+    write_half(ids, 1 - ids[4], pieces, (output, input_grad), rows, sems)
 
 
 def pile(ids, p0, p1, p2, p3, out):
@@ -481,8 +522,8 @@
 def adam_step(weight, grad, moment, square, rate, decay):
     moment_next = BETA_ONE * moment + (1.0 - BETA_ONE) * grad
     square_next = BETA_TWO * square + (1.0 - BETA_TWO) * grad * grad
-    first_hat = moment_next / (1.0 - BETA_ONE**STEP)
-    second_hat = square_next / (1.0 - BETA_TWO**STEP)
+    first_hat = moment_next * (1.0 / (1.0 - BETA_ONE**STEP))
+    second_hat = square_next * (1.0 / (1.0 - BETA_TWO**STEP))
     weight_next = weight - rate * (first_hat / (jnp.sqrt(second_hat) + ADAM_EPS) + decay * weight)
     return (weight_next, moment_next, square_next)
 
@@ -646,11 +687,11 @@
     )
     low_near = jnp.stack(gather(shift_y, low))
     low_far = swap_core(low_near)
-    heads_grad, hidden_low, input_near, input_far, chunks = whole(
+    heads_grad, hidden_low, own_kind, other_kind, input_near, input_far, chunks = whole(
         back_to_input,
         [
-            ((T, 2 * JC), bf16), ((T, 2 * MC), bf16), ((HALF, D), bf16), ((HALF, D), bf16),
-            ((MP, T + 2 * DP, HEAD), bf16),
+            ((T, 2 * JC), bf16), ((T, 2 * MC), bf16), ((T, HEAD), bf16), ((T, HEAD), bf16),
+            ((HALF, D), bf16), ((HALF, D), bf16), ((MP, 2 * DP, HEAD), bf16),
         ],
         [ids, low_near, low_far, rows_w, heads, lse, cosine, sine, joint_w, tok, gain_second_part],
         scratch=[
@@ -663,6 +704,13 @@
             pltpu.VMEM((DP, MP * 40), f32),
         ],
     )
+    both, left, right = whole(
+        group_parts,
+        [((T, JC), bf16), ((T, HEAD), bf16), ((T, HEAD), bf16)],
+        [ids, own_kind, swap_core(other_kind)],
+        limit=8,
+    )
+    left, right, both = to_last_chip(left, 0), to_last_chip(right, 2), to_last_chip(both, 1)
     moved = exchange(chunks, "mp")
     (mixer_parts,) = whole(
         weigh_mixer,
@@ -672,7 +720,7 @@
     (joint_parts,) = whole(
         weigh_joint,
         [((DP, ROWS + 8, JC + MC), bf16)],
-        [ids, normed, heads_grad, moved, mixer_parts],
+        [ids, normed, heads_grad, left, right, both, moved, mixer_parts],
     )
     joint_shard, mixer_shard, vector_shard, squares = whole(
         settle_grads,
@@ -691,11 +739,32 @@
         [ids] + parts + [hidden_part, tok_part, hidden_grad, gain_first],
         limit=8,
     )
+    done_parts = gather(shift_y, done)
+    anywhere = pl.BlockSpec(memory_space=pl.ANY)
+    results = [jax.ShapeDtypeStruct((1, T, D), f32)] * 2
+    held = [pltpu.VMEM((2, HALF, D), f32), pltpu.SemaphoreType.DMA((2,))]
+    *halves, token = pl.pallas_call(
+        settle_near,
+        out_shape=results + [jax.ShapeDtypeStruct((8, HEAD), f32)],
+        in_specs=[SM] + [VM] * 4,
+        out_specs=[anywhere] * 2 + [VM],
+        scratch_shapes=held,
+        compiler_params=pltpu.CompilerParams(vmem_limit_bytes=16 * MiB),
+        cost_estimate=SMALL,
+    )(ids, *done_parts)
     (done_near,) = whole(
-        pile, [((4, 2, PART, D), bf16)], [ids] + gather(shift_y, done), after=[squares], limit=8
-    )
-    done_far = swap_core(done_near)
-    output, input_grad = whole(settle, [((1, T, D), f32)] * 2, [ids, done_near, done_far])
+        pile, [((4, 2, PART, D), bf16)], [ids] + done_parts, after=[squares, token], limit=8
+    )
+    output, input_grad = pl.pallas_call(
+        settle_far,
+        out_shape=results,
+        in_specs=[SM, VM] + [anywhere] * 2,
+        out_specs=[anywhere] * 2,
+        input_output_aliases={2: 0, 3: 1},
+        scratch_shapes=held,
+        compiler_params=pltpu.CompilerParams(vmem_limit_bytes=16 * MiB),
+        cost_estimate=SMALL,
+    )(ids, swap_core(done_near), *halves)
 
     matrices = [joint_weight, joint_moment, joint_square]
     matrices += [mixer_weight, mixer_moment, mixer_square]

time: 297 us -> 294 us (0.990)
  waiting for transfers between devices: 91 us -> 79.5 us
  starting transfers between devices: 83.7 us -> 90.1 us
    all_to_all x6, waiting for transfers between devices: 50.4 us -> 37.3 us  [exchange(): return lax.all_to_all(v, axis, split_axis=0, concat_axis=0, tiled=True)]
    ppermute x0 -> x3, starting transfers between devices: none -> 5.85 us  [to_last_chip(): return lax.ppermute(v, 'mp', [(2 * y + c, MP - 2 + c) for c in range(2)])]
    pallas_call x0 -> x2, Pallas kernels: none -> 4.86 us  [the longest x1 2.43 us: body(): pl.pallas_call(settle_far, out_shape=results, in_specs=[SM, VM] + [anywhe...]
    pallas_call x13, Pallas kernels: 52.7 us -> 48.2 us  [whole(): pl.pallas_call(bare, out_shape=[jax.ShapeDtypeStruct(s, d) for s, d in ou...]
    ppermute x12 -> x13, waiting for transfers between devices: 10.6 us -> 11.8 us  [swap_core(): return lax.ppermute(v, 'mp', [(i, i ^ 1) for i in range(MP)])]
    unnamed x62 -> x70, local copies, waits for them, and re-layouts: 7.15 us -> 8.31 us
    ppermute x12 -> x13, starting transfers between devices: 8.64 us -> 9.27 us  [swap_core(): return lax.ppermute(v, 'mp', [(i, i ^ 1) for i in range(MP)])]
  transfers between devices with their start and end apart: 38 -> 42, of which waited for: 19 -> 20; matrix products, arithmetic and copies ran while one was open for 2% -> 2% of each run, Pallas kernels for 23% -> 24%
where the time goes in v3:
time: 294 us; the launch traced here: 293 us
  Pallas kernels  91.4 us (31%)
  starting transfers between devices  90.1 us (31%)
  waiting for transfers between devices  79.5 us (27%)
  between operations  15.3 us (5%)
  local copies, waits for them, and re-layouts  13 us (4%)
  other arithmetic  3.25 us (1%)
    all_to_all x6, starting transfers between devices, exchange(): return lax.all_to_all(v, axis, split_axis=0, concat_axis=0, tiled=True)  52.6 us
    pallas_call x13, Pallas kernels, whole(): pl.pallas_call(bare, out_shape=[jax.ShapeDtypeStruct(s, d) for s, d in ou...  48.2 us
    all_to_all x6, waiting for transfers between devices, exchange(): return lax.all_to_all(v, axis, split_axis=0, concat_axis=0, tiled=True)  37.3 us
    ppermute x18, waiting for transfers between devices, shift_y(): return lax.ppermute(v, 'mp', [(i, (i + 2 * k) % MP) for i in range(MP)])  30.3 us
    ppermute x18, starting transfers between devices, shift_y(): return lax.ppermute(v, 'mp', [(i, (i + 2 * k) % MP) for i in range(MP)])  22.4 us
    pallas_call x1, Pallas kernels, body(): pl.pallas_call(gated, grid=(pl.cdiv(FP, 256),), out_shape=[jax.ShapeDtype...  18.4 us
    ppermute x13, waiting for transfers between devices, swap_core(): return lax.ppermute(v, 'mp', [(i, i ^ 1) for i in range(MP)])  11.8 us
    ppermute x13, starting transfers between devices, swap_core(): return lax.ppermute(v, 'mp', [(i, i ^ 1) for i in range(MP)])  9.27 us
  transfers between devices with their start and end apart: 42, of which 20 were waited for; matrix products, arithmetic and copies ran while one was open for 2% of the time, Pallas kernels for 24%

profile of v3, /device:TPU:1, one launch (start us, length us, event | category | flops | bytes accessed | tf_op | source)
XLA Modules:
  0.0 292.6 jit_solution(8756599483577501303)
XLA Ops:
  13.5 7.7 %all-to-all-start = ((bf16[16,176,256]{2,1,0:T(8,128)(2,1)}), bf16[16,176,256]{2,1,0:T(8,128)(2,1)S(1)}, u32[]{:S(2)}, u32[]{:S(2)}) async-start(bf16[16,176,256]{2,1,0:T(8,128)(2,1)} %broadcast_in_dim.27), calls=%async_computation | async-start | bytes 2883584 | tf_op jit(solution)/shard_map/all_to_all | solution.py:63
  28.8 19.3 %all-to-all-done.refs_6_ = bf16[16,176,256]{2,1,0:T(8,128)(2,1)S(1)} async-done(((bf16[16,176,256]{2,1,0:T(8,128)(2,1)}), bf16[16,176,256]{2,1,0:T(8,128)(2,1)S(1)}, u32[]{:S(2)}, u32[]{:S(2)}) %all-to-all-start) | async-done | bytes 1441824 | tf_op jit(solution)/shard_map/all_to_all | solution.py:63
  49.2 6.6 %all-to-all-start.1 = ((bf16[16,112,256]{2,1,0:T(8,128)(2,1)}), bf16[16,112,256]{2,1,0:T(8,128)(2,1)S(1)}, u32[]{:S(2)}, u32[]{:S(2)}) async-start(bf16[16,112,256]{2,1,0:T(8,128)(2,1)} %broadcast_in_dim.28), calls=%async_computation.1 | async-start | bytes 1835008 | tf_op jit(solution)/shard_map/all_to_all | solution.py:63
  57.1 4.3 %shard_map.331 = (bf16[512,1536]{1,0:T(8,128)(2,1)}, bf16[1536,512]{1,0:T(8,128)(2,1)}, bf16[64,1536]{1,0:T(8,128)(2,1)}, bf16[64,1536]{1,0:T(8,128)(2,1)}) custom-call(s32[5]{0:T(128)} %stack.61.refs_0_.ids, bf16[512,1536]{1,0:T(8,128)(2,1)} %bitcast.60, bf16[512,1536]{1,0:T(8,128)(2,1)} %bitcast.53), custom_call_target="tpu_custom_call" | custom-call | flops 1 | bytes 1 | tf_op jit(solution)/shard_map/pallas_call | solution.py:91
  69.4 8.8 %shard_map.332 = (bf16[512,1536]{1,0:T(8,128)(2,1)}, bf16[512,512]{1,0:T(8,128)(2,1)}, bf16[8,256,256]{2,1,0:T(8,128)(2,1)}, f32[512,256]{1,0:T(8,128)}, bf16[1536,512]{1,0:T(8,128)(2,1)}) custom-call(s32[5]{0:T(128)} %stack.61.refs_0_.ids, bf16[512,1536]{1,0:T(8,128)(2,1)} %bitcast.54, f32[1,1536]{1,0:T(1,128)} %broadcast_in_dim.29.refs_2_.refs_8_, ...), custom_call_target="tpu_custom_call" | custom-call | flops 1 | bytes 1 | tf_op jit(solution)/shard_map/pallas_call | solution.py:91
  78.2 16.2 %all-to-all-start.2 = ((bf16[8,256,256]{2,1,0:T(8,128)(2,1)}), bf16[8,256,256]{2,1,0:T(8,128)(2,1)S(1)}, u32[]{:S(2)}, u32[]{:S(2)}) async-start(bf16[8,256,256]{2,1,0:T(8,128)(2,1)} %get-tuple-element.85), calls=%async_computation.2 | async-start | bytes 2097152 | tf_op jit(solution)/shard_map/all_to_all | solution.py:63
  100.5 9.0 %all-to-all-done.2.refs_1_ = bf16[8,256,256]{2,1,0:T(8,128)(2,1)S(1)} async-done(((bf16[8,256,256]{2,1,0:T(8,128)(2,1)}), bf16[8,256,256]{2,1,0:T(8,128)(2,1)S(1)}, u32[]{:S(2)}, u32[]{:S(2)}) %all-to-all-start.2) | async-done | bytes 1048608 | tf_op jit(solution)/shard_map/all_to_all | solution.py:63
  110.6 7.2 %shard_map.333 = (f32[64,1536]{1,0:T(8,128)}, bf16[256,1536]{1,0:T(8,128)(2,1)}, bf16[256,1536]{1,0:T(8,128)(2,1)}) custom-call(s32[5]{0:T(128)} %stack.61.refs_0_.ids, bf16[8,256,256]{2,1,0:T(8,128)(2,1)} %copy-done.16, bf16[16,80,256]{2,1,0:T(8,128)(2,1)} %copy-done.21, bf16[16,80,256]{2,1,0:T(8,128)(2,1)} %collective-permute-done.4.refs_3_, ...), custom_call_target="tpu_custom_call" | custom-call | flops 1 | bytes 1 | tf_op jit(solution)/shard_map/pallas_call | solution.py:91
  121.7 18.4 %shard_map.334 = (bf16[512,1152]{1,0:T(8,128)(2,1)}, bf16[512,1152]{1,0:T(8,128)(2,1)}, bf16[512,1152]{1,0:T(8,128)(2,1)}, bf16[16,3,96,1152]{3,2,1,0:T(8,128)(2,1)}) custom-call(bf16[256,1536]{1,0:T(8,128)(2,1)} %get-tuple-element.86.near, bf16[256,1536]{1,0:T(8,128)(2,1)} %copy-done.24, bf16[512,1536]{1,0:T(8,128)(2,1)} %get-tuple-element.84.refs_8_.back, ...), custom_call_target="tpu_custom_call" | custom-call | flops 1 | bytes 1 | tf_op jit(solution)/shard_map/pallas_call | solution.py:636
  140.1 8.0 %shard_map.336 = (bf16[256,1536]{1,0:T(8,128)(2,1)}, bf16[256,1536]{1,0:T(8,128)(2,1)}) custom-call(bf16[512,1152]{1,0:T(8,128)(2,1)} %get-tuple-element.91.gate_grad, bf16[512,1152]{1,0:T(8,128)(2,1)} %get-tuple-element.92.up_grad, bf16[16,3,96,1152]{3,2,1,0:T(8,128)(2,1)} %bitcast.51), custom_call_target="tpu_custom_call" | custom-call | flops 1 | bytes 1 | tf_op jit(solution)/shard_map/pallas_call | solution.py:649
  155.2 5.2 %shard_map.335 = (bf16[256,1536]{1,0:T(8,128)(2,1)}, bf16[256,1536]{1,0:T(8,128)(2,1)}) custom-call(bf16[512,1152]{1,0:T(8,128)(2,1)} %get-tuple-element.88.act, bf16[16,3,96,1152]{3,2,1,0:T(8,128)(2,1)} %bitcast.52), custom_call_target="tpu_custom_call" | custom-call | flops 1 | bytes 1 | tf_op jit(solution)/shard_map/pallas_call | solution.py:669
  170.9 4.1 %collective-permute-done.19 = bf16[64,1536]{1,0:T(8,128)(2,1)S(1)} collective-permute-done((bf16[64,1536]{1,0:T(8,128)(2,1)S(1)}, bf16[64,1536]{1,0:T(8,128)(2,1)S(1)}, u32[]{:S(2)}, u32[]{:S(2)}) %collective-permute-start.19) | collective-permute-done | bytes 196640 | tf_op jit(solution)/shard_map/ppermute | solution.py:47
  175.2 3.2 %collective-permute-start.20 = (bf16[4,64,1536]{2,1,0:T(8,128)(2,1)S(1)}, bf16[4,64,1536]{2,1,0:T(8,128)(2,1)S(1)}, u32[]{:S(2)}, u32[]{:S(2)}) collective-permute-start(bf16[4,64,1536]{2,1,0:T(8,128)(2,1)S(1)} %pad_maximum_fusion.refs_1_), channel_id=1, source_target_pairs={{0,1},{1,0},{2,3},{3,2},{4,5},{5,4},{6,7},{7,6},{8,9},{9,8},{10,11... | collective-permute-start | bytes 2359304 | tf_op jit(solution)/shard_map/ppermute | solution.py:59
  181.3 12.1 %shard_map.339 = (bf16[512,512]{1,0:T(8,128)(2,1)}, bf16[512,384]{1,0:T(8,128)(2,1)}, bf16[512,128]{1,0:T(8,128)(2,1)}, bf16[512,128]{1,0:T(8,128)(2,1)}, bf16[2...) custom-call(s32[5]{0:T(128)} %stack.61.refs_0_.ids, bf16[4,64,1536]{2,1,0:T(8,128)(2,1)} %copy-done.20, ...), custom_call_target="tpu_custom_call" | custom-call | flops 1 | bytes 1 | tf_op jit(solution)/shard_map/pallas_call | solution.py:91
  197.3 4.5 %collective-permute-start.23 = (bf16[512,128]{1,0:T(8,128)(2,1)S(1)}, bf16[512,128]{1,0:T(8,128)(2,1)S(1)}, u32[]{:S(2)}, u32[]{:S(2)}) collective-permute-start(bf16[512,128]{1,0:T(8,128)(2,1)S(1)} %get-tuple-element.113), channel_id=1, source_target_pairs={{0,6},{1,7},{8,14},{9,15},{16,22},{17,23},{24,30},{25,31},{32,38},... | collective-permute-start | bytes 393224 | tf_op jit(solution)/shard_map/ppermute | solution.py:55
  203.3 3.8 %all-to-all-start.3 = ((bf16[8,32,128]{2,1,0:T(8,128)(2,1)}), bf16[8,32,128]{2,1,0:T(8,128)(2,1)S(1)}, u32[]{:S(2)}, u32[]{:S(2)}) async-start(bf16[8,32,128]{2,1,0:T(8,128)(2,1)} %get-tuple-element.116), calls=%async_computation.3 | async-start | bytes 131072 | tf_op jit(solution)/shard_map/all_to_all | solution.py:63
  207.1 3.2 %shard_map.341.refs_7_ = bf16[16,96,192]{2,1,0:T(8,128)(2,1)} custom-call(s32[5]{0:T(128)} %stack.61.refs_0_.ids, bf16[8,256,256]{2,1,0:T(8,128)(2,1)} %copy-done.16, bf16[8,256,256]{2,1,0:T(8,128)(2,1)} %collective-permute-done.26.refs_2_, bf16[512,384]{1,0:T(8,128)(2,1)} %get-tuple-element.117.refs_3_), custom_call_target="tpu_custom_call" | custom-call | flops 1 | bytes 1 | tf_op jit(solution)/shard_map/pallas_call | solution.py:91
  212.7 3.9 %shard_map.342.refs_5_ = bf16[16,104,448]{2,1,0:T(8,128)(2,1)} custom-call(s32[5]{0:T(128)} %stack.61.refs_0_.ids, bf16[512,1536]{1,0:T(8,128)(2,1)} %get-tuple-element.109.refs_1_, bf16[512,512]{1,0:T(8,128)(2,1)} %get-tuple-element.110.refs_2_, bf16[512,128]{1,0:T(8,128)(2,1)} %copy-done.32, bf16[512,128]{1,0:T(8,128)(2,1)} %copy-done.33, ...), custom_call_target="tpu_custom_call" | custom-call | flops 1 | bytes 1 | tf_op jit(solution)/shard_map/pallas_call | solution.py:91
  216.6 6.8 %all-to-all-start.4 = ((bf16[16,104,448]{2,1,0:T(8,128)(2,1)}), bf16[16,104,448]{2,1,0:T(8,128)(2,1)}, u32[]{:S(2)}, u32[]{:S(2)}) async-start(bf16[16,104,448]{2,1,0:T(8,128)(2,1)} %shard_map.342.refs_5_), calls=%async_computation.4 | async-start | bytes 3407872 | tf_op jit(solution)/shard_map/all_to_all | solution.py:63
  229.9 7.5 %collective-permute-done.27.refs_2_ = bf16[2,64,1536]{2,1,0:T(8,128)(2,1)S(1)} collective-permute-done((bf16[2,64,1536]{2,1,0:T(8,128)(2,1)S(1)}, bf16[2,64,1536]{2,1,0:T(8,128)(2,1)S(1)}, u32[]{:S(2)}, u32[]{:S(2)}) %collective-permute-start.27) | collective-permute-done | bytes 393248 | tf_op jit(solution)/shard_map/ppermute | solution.py:47
  237.4 9.4 %collective-permute-done.29.refs_4_ = bf16[2,64,1536]{2,1,0:T(8,128)(2,1)S(1)} collective-permute-done((bf16[2,64,1536]{2,1,0:T(8,128)(2,1)S(1)}, bf16[2,64,1536]{2,1,0:T(8,128)(2,1)S(1)}, u32[]{:S(2)}, u32[]{:S(2)}) %collective-permute-start.29) | collective-permute-done | bytes 393248 | tf_op jit(solution)/shard_map/ppermute | solution.py:47
  253.5 11.5 %all-to-all-start.5 = ((f32[128,1,128]{2,1,0:T(1,128)}), f32[128,1,128]{2,1,0:T(1,128)S(1)}, u32[]{:S(2)}, u32[]{:S(2)}) async-start(f32[128,1,128]{2,1,0:T(1,128)} %get-tuple-element.125), calls=%async_computation.5 | async-start | bytes 131072 | tf_op jit(solution)/shard_map/all_to_all | solution.py:63
  267.5 6.9 %all-to-all-done.5.refs_5_.squares = f32[128,1,128]{2,1,0:T(1,128)S(1)} async-done(((f32[128,1,128]{2,1,0:T(1,128)}), f32[128,1,128]{2,1,0:T(1,128)S(1)}, u32[]{:S(2)}, u32[]{:S(2)}) %all-to-all-start.5) | async-done | bytes 65568 | tf_op jit(solution)/shard_map/all_to_all | solution.py:63
  276.6 6.7 %shard_map.349 = (f32[1,128]{1,0:T(1,128)}, f32[96,256]{1,0:T(8,128)}, f32[96,256]{1,0:T(8,128)}, f32[96,256]{1,0:T(8,128)}, f32[96,192]{1,0:T(8,128)}, /*index=...) custom-call(f32[128,1,128]{2,1,0:T(1,128)} %copy-done.5, ...), custom_call_target="tpu_custom_call" | custom-call | flops 1 | bytes 1 | tf_op jit(solution)/shard_map/pallas_call | solution.py:784
  (199 shorter events, 82.9 us)
Async XLA Ops:
  7.2 113.6 %all-gather.3.cloned.1.call-start = ((), (), s32[]{:S(2)}) async-start(), calls=%async_computation.7 | async-start | bytes 11280384 | tf_op jit(solution)/shard_map/all_gather | solution.py:564
  13.5 34.6 %all-to-all-start = ((bf16[16,176,256]{2,1,0:T(8,128)(2,1)}), bf16[16,176,256]{2,1,0:T(8,128)(2,1)S(1)}, u32[]{:S(2)}, u32[]{:S(2)}) async-start(bf16[16,176,256]{2,1,0:T(8,128)(2,1)} %broadcast_in_dim.27), calls=%async_computation | async-start | bytes 2883584 | tf_op jit(solution)/shard_map/all_to_all | solution.py:63
  49.2 18.4 %all-to-all-start.1 = ((bf16[16,112,256]{2,1,0:T(8,128)(2,1)}), bf16[16,112,256]{2,1,0:T(8,128)(2,1)S(1)}, u32[]{:S(2)}, u32[]{:S(2)}) async-start(bf16[16,112,256]{2,1,0:T(8,128)(2,1)} %broadcast_in_dim.28), calls=%async_computation.1 | async-start | bytes 1835008 | tf_op jit(solution)/shard_map/all_to_all | solution.py:63
  61.5 33.1 %collective-permute-start.6 = (bf16[16,80,256]{2,1,0:T(8,128)(2,1)S(1)}, bf16[16,80,256]{2,1,0:T(8,128)(2,1)}, u32[]{:S(2)}, u32[]{:S(2)}) collective-permute-start(bf16[16,80,256]{2,1,0:T(8,128)(2,1)S(1)} %slice.135.refs_2_), channel_id=1, source_target_pairs={{0,4},{1,5},{2,6},{3,7},{4,0},{5,1},{6,2},{7,3},{8,12},{9,13},{10,... | collective-permute-start | bytes 1966088 | tf_op jit(solution)/shard_map/ppermute | solution.py:47
  64.6 30.5 %collective-permute-start.4 = (bf16[16,80,256]{2,1,0:T(8,128)(2,1)S(1)}, bf16[16,80,256]{2,1,0:T(8,128)(2,1)}, u32[]{:S(2)}, u32[]{:S(2)}) collective-permute-start(bf16[16,80,256]{2,1,0:T(8,128)(2,1)S(1)} %slice.135.refs_2_), channel_id=1, source_target_pairs={{0,2},{1,3},{2,4},{3,5},{4,6},{5,7},{6,0},{7,1},{8,10},{9,11},{10,... | collective-permute-start | bytes 1966088 | tf_op jit(solution)/shard_map/ppermute | solution.py:47
  64.9 30.2 %collective-permute-start.5 = (bf16[16,80,256]{2,1,0:T(8,128)(2,1)S(1)}, bf16[16,80,256]{2,1,0:T(8,128)(2,1)}, u32[]{:S(2)}, u32[]{:S(2)}) collective-permute-start(bf16[16,80,256]{2,1,0:T(8,128)(2,1)S(1)} %slice.135.refs_2_), channel_id=1, source_target_pairs={{0,6},{1,7},{2,0},{3,1},{4,2},{5,3},{6,4},{7,5},{8,14},{9,15},{10,... | collective-permute-start | bytes 1966088 | tf_op jit(solution)/shard_map/ppermute | solution.py:47
  78.2 31.3 %all-to-all-start.2 = ((bf16[8,256,256]{2,1,0:T(8,128)(2,1)}), bf16[8,256,256]{2,1,0:T(8,128)(2,1)S(1)}, u32[]{:S(2)}, u32[]{:S(2)}) async-start(bf16[8,256,256]{2,1,0:T(8,128)(2,1)} %get-tuple-element.85), calls=%async_computation.2 | async-start | bytes 2097152 | tf_op jit(solution)/shard_map/all_to_all | solution.py:63
  94.5 156.1 %reduce-scatter.4.cloned.1.call-start = ((), (), s32[]{:S(2)}) async-start(), calls=%async_computation.8 | async-start | bytes 11280384
  155.2 8.3 %collective-permute-start.16 = (bf16[64,1536]{1,0:T(8,128)(2,1)S(1)}, bf16[64,1536]{1,0:T(8,128)(2,1)S(1)}, u32[]{:S(2)}, u32[]{:S(2)}) collective-permute-start(bf16[64,1536]{1,0:T(8,128)(2,1)S(1)} %get-tuple-element.98), channel_id=1, source_target_pairs={{0,4},{1,5},{2,6},{3,7},{4,0},{5,1},{6,2},{7,3},{8,12},{9,13},{10,... | collective-permute-start | bytes 589832 | tf_op jit(solution)/shard_map/ppermute | solution.py:47
  178.4 24.8 %collective-permute-start.26 = (bf16[8,256,256]{2,1,0:T(8,128)(2,1)S(1)}, bf16[8,256,256]{2,1,0:T(8,128)(2,1)}, u32[]{:S(2)}, u32[]{:S(2)}) collective-permute-start(bf16[8,256,256]{2,1,0:T(8,128)(2,1)S(1)} %copy-done.17), channel_id=1, source_target_pairs={{0,1},{1,0},{2,3},{3,2},{4,5},{5,4},{6,7},{7,6},{8,9},{9,8},{10,11... | collective-permute-start | bytes 3145736 | tf_op jit(solution)/shard_map/ppermute | solution.py:59
  196.6 15.3 %collective-permute-start.25 = (bf16[512,256]{1,0:T(8,128)(2,1)S(1)}, bf16[512,256]{1,0:T(8,128)(2,1)S(1)}, u32[]{:S(2)}, u32[]{:S(2)}) collective-permute-start(bf16[512,256]{1,0:T(8,128)(2,1)S(1)} %get-tuple-element.115), channel_id=1, source_target_pairs={{2,6},{3,7},{10,14},{11,15},{18,22},{19,23},{26,30},{27,31},{34,38... | collective-permute-start | bytes 786440 | tf_op jit(solution)/shard_map/ppermute | solution.py:55
  197.3 14.6 %collective-permute-start.23 = (bf16[512,128]{1,0:T(8,128)(2,1)S(1)}, bf16[512,128]{1,0:T(8,128)(2,1)S(1)}, u32[]{:S(2)}, u32[]{:S(2)}) collective-permute-start(bf16[512,128]{1,0:T(8,128)(2,1)S(1)} %get-tuple-element.113), channel_id=1, source_target_pairs={{0,6},{1,7},{8,14},{9,15},{16,22},{17,23},{24,30},{25,31},{32,38},... | collective-permute-start | bytes 393224 | tf_op jit(solution)/shard_map/ppermute | solution.py:55
  201.8 10.1 %collective-permute-start.24 = (bf16[512,128]{1,0:T(8,128)(2,1)S(1)}, bf16[512,128]{1,0:T(8,128)(2,1)S(1)}, u32[]{:S(2)}, u32[]{:S(2)}) collective-permute-start(bf16[512,128]{1,0:T(8,128)(2,1)S(1)} %get-tuple-element.114), channel_id=1, source_target_pairs={{4,6},{5,7},{12,14},{13,15},{20,22},{21,23},{28,30},{29,31},{36,38... | collective-permute-start | bytes 393224 | tf_op jit(solution)/shard_map/ppermute | solution.py:55
  202.5 20.9 %collective-permute-start.12 = (bf16[256,1536]{1,0:T(8,128)(2,1)}, bf16[256,1536]{1,0:T(8,128)(2,1)}, u32[]{:S(2)}, u32[]{:S(2)}) collective-permute-start(bf16[256,1536]{1,0:T(8,128)(2,1)} %get-tuple-element.90.refs_8_), channel_id=1, source_target_pairs={{0,1},{1,0},{2,3},{3,2},{4,5},{5,4},{6,7},{7,6},{8,9},{9,8},{10,11... | collective-permute-start | bytes 2359304 | tf_op jit(solution)/shard_map/ppermute | solution.py:59
  203.2 20.2 %collective-permute-start.21 = (bf16[256,1536]{1,0:T(8,128)(2,1)}, bf16[256,1536]{1,0:T(8,128)(2,1)}, u32[]{:S(2)}, u32[]{:S(2)}) collective-permute-start(bf16[256,1536]{1,0:T(8,128)(2,1)} %get-tuple-element.108), channel_id=1, source_target_pairs={{0,1},{1,0},{2,3},{3,2},{4,5},{5,4},{6,7},{7,6},{8,9},{9,8},{10,11... | collective-permute-start | bytes 2359304 | tf_op jit(solution)/shard_map/ppermute | solution.py:59
  203.3 8.6 %all-to-all-start.3 = ((bf16[8,32,128]{2,1,0:T(8,128)(2,1)}), bf16[8,32,128]{2,1,0:T(8,128)(2,1)S(1)}, u32[]{:S(2)}, u32[]{:S(2)}) async-start(bf16[8,32,128]{2,1,0:T(8,128)(2,1)} %get-tuple-element.116), calls=%async_computation.3 | async-start | bytes 131072 | tf_op jit(solution)/shard_map/all_to_all | solution.py:63
  216.6 34.0 %all-to-all-start.4 = ((bf16[16,104,448]{2,1,0:T(8,128)(2,1)}), bf16[16,104,448]{2,1,0:T(8,128)(2,1)}, u32[]{:S(2)}, u32[]{:S(2)}) async-start(bf16[16,104,448]{2,1,0:T(8,128)(2,1)} %shard_map.342.refs_5_), calls=%async_computation.4 | async-start | bytes 3407872 | tf_op jit(solution)/shard_map/all_to_all | solution.py:63
  226.4 11.0 %collective-permute-start.27 = (bf16[2,64,1536]{2,1,0:T(8,128)(2,1)S(1)}, bf16[2,64,1536]{2,1,0:T(8,128)(2,1)S(1)}, u32[]{:S(2)}, u32[]{:S(2)}) collective-permute-start(bf16[2,64,1536]{2,1,0:T(8,128)(2,1)S(1)} %get-tuple-element.119), channel_id=1, source_target_pairs={{0,2},{1,3},{2,4},{3,5},{4,6},{5,7},{6,0},{7,1},{8,10},{9,11},{10,... | collective-permute-start | bytes 1179656 | tf_op jit(solution)/shard_map/ppermute | solution.py:47
  227.0 10.4 %collective-permute-start.28 = (bf16[2,64,1536]{2,1,0:T(8,128)(2,1)S(1)}, bf16[2,64,1536]{2,1,0:T(8,128)(2,1)S(1)}, u32[]{:S(2)}, u32[]{:S(2)}) collective-permute-start(bf16[2,64,1536]{2,1,0:T(8,128)(2,1)S(1)} %get-tuple-element.120), channel_id=1, source_target_pairs={{0,6},{1,7},{2,0},{3,1},{4,2},{5,3},{6,4},{7,5},{8,14},{9,15},{10,... | collective-permute-start | bytes 1179656 | tf_op jit(solution)/shard_map/ppermute | solution.py:47
  229.1 17.7 %collective-permute-start.29 = (bf16[2,64,1536]{2,1,0:T(8,128)(2,1)S(1)}, bf16[2,64,1536]{2,1,0:T(8,128)(2,1)S(1)}, u32[]{:S(2)}, u32[]{:S(2)}) collective-permute-start(bf16[2,64,1536]{2,1,0:T(8,128)(2,1)S(1)} %get-tuple-element.121), channel_id=1, source_target_pairs={{0,4},{1,5},{2,6},{3,7},{4,0},{5,1},{6,2},{7,3},{8,12},{9,13},{10,... | collective-permute-start | bytes 1179656 | tf_op jit(solution)/shard_map/ppermute | solution.py:47
  247.8 17.2 %collective-permute-start.30 = (bf16[2,64,1536]{2,1,0:T(8,128)(2,1)S(1)}, bf16[2,64,1536]{2,1,0:T(8,128)(2,1)S(1)}, u32[]{:S(2)}, u32[]{:S(2)}) collective-permute-start(bf16[2,64,1536]{2,1,0:T(8,128)(2,1)S(1)} %shard_map.344.p0.refs_1_), channel_id=1, source_target_pairs={{0,2},{1,3},{2,4},{3,5},{4,6},{5,7},{6,0},{7,1},{8,10},{9,11},{10,... | collective-permute-start | bytes 1179656 | tf_op jit(solution)/shard_map/ppermute | solution.py:47
  248.5 16.6 %collective-permute-start.31 = (bf16[2,64,1536]{2,1,0:T(8,128)(2,1)S(1)}, bf16[2,64,1536]{2,1,0:T(8,128)(2,1)S(1)}, u32[]{:S(2)}, u32[]{:S(2)}) collective-permute-start(bf16[2,64,1536]{2,1,0:T(8,128)(2,1)S(1)} %shard_map.344.p0.refs_1_), channel_id=1, source_target_pairs={{0,6},{1,7},{2,0},{3,1},{4,2},{5,3},{6,4},{7,5},{8,14},{9,15},{10,... | collective-permute-start | bytes 1179656 | tf_op jit(solution)/shard_map/ppermute | solution.py:47
  250.6 14.4 %collective-permute-start.32 = (bf16[2,64,1536]{2,1,0:T(8,128)(2,1)S(1)}, bf16[2,64,1536]{2,1,0:T(8,128)(2,1)S(1)}, u32[]{:S(2)}, u32[]{:S(2)}) collective-permute-start(bf16[2,64,1536]{2,1,0:T(8,128)(2,1)S(1)} %shard_map.344.p0.refs_1_), channel_id=1, source_target_pairs={{0,4},{1,5},{2,6},{3,7},{4,0},{5,1},{6,2},{7,3},{8,12},{9,13},{10,... | collective-permute-start | bytes 1179656 | tf_op jit(solution)/shard_map/ppermute | solution.py:47
  253.5 21.0 %all-to-all-start.5 = ((f32[128,1,128]{2,1,0:T(1,128)}), f32[128,1,128]{2,1,0:T(1,128)S(1)}, u32[]{:S(2)}, u32[]{:S(2)}) async-start(f32[128,1,128]{2,1,0:T(1,128)} %get-tuple-element.125), calls=%async_computation.5 | async-start | bytes 131072 | tf_op jit(solution)/shard_map/all_to_all | solution.py:63
  (53 other events, 342.1 us)
Sparse Core Ops, SparseCore 0:
  10.2 103.7 all-gather.2
  140.2 91.7 reduce-scatter.3

commit v4 on v3

--- a/solution.py
+++ b/solution.py
@@ -103,7 +103,7 @@
     return pl.ds(pl.multiple_of(start, step), size)
 
 
-def prepare(ids, cotangent, tok, back, back_t, back_part, tok_part):
+def prepare(ids, cotangent, tok, back, back_t, back_part, tok_part, tok_half):
     length, y, c = ids[0], ids[3], ids[4]
     for h in range(2):
         start = HALF * ((c + h) % 2)
@@ -114,6 +114,7 @@
         back_t[:, HALF * h : HALF * (h + 1)] = v.T
     back_part[...] = back[at(PART * y, PART, PART), :]
     tok_part[...] = tok[at(HALF * c + PART * y, PART, PART), :]
+    tok_half[...] = tok[at(HALF * c, HALF, HALF), :]
 
 
 def kept(i, n, length):
@@ -124,54 +125,51 @@
 
 def attend(
     ids, tok, gain, bias, cosine, sine, query_w, pair_w,
-    normed, heads, out, lse, w,
+    normed, heads_out, out, lse, w, heads,
 ):
-    w[:, :JC] = query_w[:, :ROWS, :].reshape(D, JC)
-    w[:, JC:] = pair_w[:, :ROWS, :].reshape(D, JC)
-
-    @pl.loop(0, T // 128)
-    def _(i):
-        rows = at(i * 128, 128, 128)
-        x = tok[rows, :].astype(f32)
-        s = lax.rsqrt(jnp.mean(x * x, -1, keepdims=True) + EPS_NORM)
-        n = (x * s * gain[...]).astype(bf16)
-        normed[rows, :] = n
-        j = nn(n, w[...]) + bias[...]
-        for h in range(4):
-            cols = slice(HEAD * h, HEAD * (h + 1))
-            u = j[:, cols]
-            if h < 3:
-                u = u * cosine[rows, :] + pltpu.roll(u, HEAD // 2, 1) * sine[rows, :]
-            heads[rows, cols] = u.astype(bf16)
-
-    for h in range(2):
-        for i in range(4):
+    step = pl.program_id(0)
+
+    @pl.when(step == 0)
+    def _():
+        w[:, :JC] = query_w[:, :ROWS, :].reshape(D, JC)
+        w[:, JC:] = pair_w[:, :ROWS, :].reshape(D, JC)
+
+    x = tok[...].astype(f32)
+    s = lax.rsqrt(jnp.mean(x * x, -1, keepdims=True) + EPS_NORM)
+    n = (x * s * gain[...]).astype(bf16)
+    normed[...] = n
+    j = nn(n, w[...]) + bias[...]
+    rows = at(128 * step, 128, 128)
+    for h in range(4):
+        cols = slice(HEAD * h, HEAD * (h + 1))
+        u = j[:, cols]
+        if h < 3:
+            u = u * cosine[...] + pltpu.roll(u, HEAD // 2, 1) * sine[...]
+        heads[rows, cols] = u.astype(bf16)
+        heads_out[:, cols] = u.astype(bf16)
+
+    for i in range(4):
+
+        @pl.when(step == i)
+        def _():
             n = 128 * (i + 1)
-            q = heads[128 * i : n, HEAD * h : HEAD * (h + 1)]
             k, v = heads[:n, 2 * HEAD : 3 * HEAD], heads[:n, 3 * HEAD :]
-            s = jnp.where(kept(i, n, ids[0]), nt(q, k) * SCALE, MASKED)
-            m = jnp.max(s, -1, keepdims=True)
-            e = jnp.exp(s - m)
-            total = jnp.sum(e, -1, keepdims=True)
-            o = nn((e / total).astype(bf16), v).astype(bf16)
-            lse[128 * i : n, HEAD * h : HEAD * (h + 1)] = jnp.broadcast_to(
-                m + jnp.log(total), (128, HEAD)
-            )
-            at_row = 128 * (i % 2)
-            for y in range(4):
-                out[2 * y + i // 2, at_row : at_row + 128, HEAD * h : HEAD * (h + 1)] = o
-
-
-def mix(
-    ids, att, a0, a1, a2, a3, b0, b1, b2, b3, tok, gain,
-    hidden_part, normed, rows_w, hidden, side, mixer,
-):
+            for h in range(2):
+                cols = slice(HEAD * h, HEAD * (h + 1))
+                s = nt(heads[128 * i : n, cols], k) * SCALE
+                s = jnp.where(kept(i, n, ids[0]), s, MASKED)
+                m = jnp.max(s, -1, keepdims=True)
+                e = jnp.exp(s - m)
+                total = jnp.sum(e, -1, keepdims=True)
+                o = nn((e / total).astype(bf16), v).astype(bf16)
+                lse[:, cols] = jnp.broadcast_to(m + jnp.log(total), (128, HEAD))
+                for y in range(4):
+                    out[y, 0, 0, :, cols] = o
+
+
+def assemble(ids, a0, a1, a2, a3, b0, b1, b2, b3, mixer, rows_w):
     y, c = ids[3], ids[4]
-    for j in range(KEY_AT):
-        side[:, JC * j : JC * (j + 1)] = att[j]
-    mine = at(HALF * c, HALF, HALF)
     for e, a, b in zip(RELATIVE, (a0, a1, a2, a3), (b0, b1, b2, b3)):
-        cols = at(384 * lax.rem(y + e + 4, 4), 384, 384)
         first = 384 * lax.rem(y + e + 4, 4)
         left, right = at(first, JC, 128), at(first + JC, HEAD, 128)
         for d in range(DP):
@@ -180,13 +178,27 @@
                 mixer[at(row, 48, 16), left] = v[d, :48, :]
                 mixer[at(row, 32, 16), right] = v[d, 48:80, :HEAD]
                 mixer[at(row + 32, 16, 16), right] = v[d, 48:64, HEAD:]
-        hidden[:, cols] = nn(side[...], mixer[:, cols]) + tok[mine, cols].astype(f32)
-    hidden_part[...] = hidden[at(PART * y, PART, PART), :]
     rows_w[...] = mixer[at(JC * jnp.minimum(ids[2], KEY_AT - 1), JC, JC), :]
-    for r in range(0, HALF, 64):
-        v = hidden[r : r + 64, :]
-        s = lax.rsqrt(jnp.mean(v * v, -1, keepdims=True) + EPS_NORM)
-        normed[r : r + 64, :] = (v * s * gain[...]).astype(bf16)
+
+
+def mix(ids, att, mixer, tok, gain, hidden_part, normed, hidden, side):
+    i = pl.program_id(0)
+
+    @pl.when(i == 0)
+    def _():
+        for j in range(KEY_AT):
+            side[:, JC * j : JC * (j + 1)] = att[j]
+
+    cols = at(384 * i, 384, 384)
+    hidden[:, cols] = nn(side[...], mixer[...]) + tok[...].astype(f32)
+
+    @pl.when(i == 3)
+    def _():
+        hidden_part[...] = hidden[at(PART * ids[3], PART, PART), :]
+        for r in range(0, HALF, 64):
+            v = hidden[r : r + 64, :]
+            s = lax.rsqrt(jnp.mean(v * v, -1, keepdims=True) + EPS_NORM)
+            normed[r : r + 64, :] = (v * s * gain[...]).astype(bf16)
 
 
 def gated(near, far, back, back_t, w, act, gate_grad, up_grad, grads, near_t):
@@ -598,39 +610,72 @@
     )[None]
 
     cosine, sine = tables()
-    back, back_t, back_part, tok_part = whole(
+    back, back_t, back_part, tok_part, tok_half = whole(
         prepare,
-        [((T, D), bf16), ((D, T), bf16), ((PART, D), bf16), ((PART, D), bf16)],
+        [
+            ((T, D), bf16), ((D, T), bf16),
+            ((PART, D), bf16), ((PART, D), bf16), ((HALF, D), bf16),
+        ],
         [ids, cotangent[0], tok],
     )
-    normed, heads, att_sent, lse, joint_w = whole(
-        attend,
-        [
-            ((T, D), bf16), ((T, 2 * JC), bf16), ((MP, HALF, JC), bf16),
-            ((T, JC), f32), ((D, 2 * JC), bf16),
+    def fixed(shape):
+        return pl.BlockSpec(shape, lambda i: (0,) * len(shape))
+
+    def rows(columns):
+        return pl.BlockSpec((128, columns), lambda i: (i, 0))
+
+    normed, heads, att_sent, lse, joint_w = pl.pallas_call(
+        lambda *refs: attend(*refs[:8], *refs[9:]),
+        grid=(4,),
+        out_shape=[
+            jax.ShapeDtypeStruct((T, D), bf16),
+            jax.ShapeDtypeStruct((T, 2 * JC), bf16),
+            jax.ShapeDtypeStruct((4, 2, 2, 128, JC), bf16),
+            jax.ShapeDtypeStruct((T, JC), f32),
+            jax.ShapeDtypeStruct((D, 2 * JC), bf16),
         ],
-        [ids, tok, gain_first, bias, cosine, sine, query_w, pair_w],
-        after=[back],
-    )
+        in_specs=[
+            SM, rows(D), fixed((1, D)), fixed((1, 2 * JC)), rows(HEAD), rows(HEAD),
+            fixed(query_w.shape), fixed(pair_w.shape), pl.BlockSpec(memory_space=pl.ANY),
+        ],
+        out_specs=[
+            rows(D), rows(2 * JC),
+            pl.BlockSpec((4, 1, 1, 128, JC), lambda i: (0, i // 2, i % 2, 0, 0)),
+            rows(JC), fixed((D, 2 * JC)),
+        ],
+        scratch_shapes=[pltpu.VMEM((T, 2 * JC), bf16)],
+        compiler_params=pltpu.CompilerParams(vmem_limit_bytes=60 * MiB),
+        cost_estimate=SMALL,
+    )(ids, tok, gain_first, bias, cosine, sine, query_w, pair_w, back)
+    att_sent = att_sent.reshape(MP, HALF, JC)
     att_near = exchange(att_sent, "mp")
     att_far = swap_core(att_near)
     mixer_near = gather(shift_y, query_w[:, ROWS:])
     mixer_far = [swap_core(v) for v in mixer_near]
-    hidden_part, normed_near, rows_w = whole(
+    mixer, rows_w = whole(
+        assemble, [((D, D), bf16), ((JC, D), bf16)], [ids] + mixer_near + mixer_far
+    )
+
+    hidden_part, normed_near = pl.pallas_call(
         mix,
-        [((PART, D), f32), ((HALF, D), bf16), ((JC, D), bf16)],
-        [ids, att_near] + mixer_near + mixer_far + [tok, gain_second],
-        scratch=[
-            pltpu.VMEM((HALF, D), f32), pltpu.VMEM((HALF, D), bf16), pltpu.VMEM((D, D), bf16),
+        grid=(4,),
+        out_shape=[jax.ShapeDtypeStruct((PART, D), f32), jax.ShapeDtypeStruct((HALF, D), bf16)],
+        in_specs=[
+            SM,
+            fixed((MP, HALF, JC)),
+            pl.BlockSpec((D, 384), lambda i: (0, i)),
+            pl.BlockSpec((HALF, 384), lambda i: (0, i)),
+            fixed((1, D)),
         ],
-    )
+        out_specs=[fixed((PART, D)), fixed((HALF, D))],
+        scratch_shapes=[pltpu.VMEM((HALF, D), f32), pltpu.VMEM((HALF, D), bf16)],
+        compiler_params=pltpu.CompilerParams(vmem_limit_bytes=60 * MiB),
+        cost_estimate=SMALL,
+    )(ids, att_near, mixer, tok_half, gain_second)
     normed_far = swap_core(normed_near)
 
     def columns(n):
         return pl.BlockSpec((n, 256), lambda i: (0, i))
-
-    def fixed(shape):
-        return pl.BlockSpec(shape, lambda i: (0,) * len(shape))
 
     block = pl.BlockSpec((DP, 3, ROWS, 256), lambda i: (0, 0, 0, i))
     act, gate_grad, up_grad, ff_grads = pl.pallas_call(

time: 294 us -> 293 us (level)
  Pallas kernels: 91.4 us -> 96.8 us
  waiting for transfers between devices: 79.5 us -> 74.5 us
    pallas_call x0 -> x2, Pallas kernels: none -> 15.6 us  [the longest x1 9.41 us: body(): pl.pallas_call(lambda *refs: attend(*refs[:8], *refs[9:]), grid=(4,), out...]
    pallas_call x13 -> x12, Pallas kernels: 48.2 us -> 38 us  [whole(): pl.pallas_call(bare, out_shape=[jax.ShapeDtypeStruct(s, d) for s, d in ou...]
    all_to_all x6, waiting for transfers between devices: 37.3 us -> 32.2 us  [exchange(): return lax.all_to_all(v, axis, split_axis=0, concat_axis=0, tiled=True)]
    unnamed x70 -> x68, local copies, waits for them, and re-layouts: 8.31 us -> 7.47 us
  transfers between devices with their start and end apart: 42 -> 42, of which waited for: 20 -> 21; matrix products, arithmetic and copies ran while one was open for 2% -> 2% of each run, Pallas kernels for 24% -> 26%
where the time goes in v4:
time: 293 us; the launch traced here: 292 us
  Pallas kernels  96.8 us (33%)
  starting transfers between devices  90 us (31%)
  waiting for transfers between devices  74.5 us (25%)
  between operations  15.4 us (5%)
  local copies, waits for them, and re-layouts  12.2 us (4%)
  other arithmetic  3.25 us (1%)
    all_to_all x6, starting transfers between devices, exchange(): return lax.all_to_all(v, axis, split_axis=0, concat_axis=0, tiled=True)  52.4 us
    pallas_call x12, Pallas kernels, whole(): pl.pallas_call(bare, out_shape=[jax.ShapeDtypeStruct(s, d) for s, d in ou...  38 us
    all_to_all x6, waiting for transfers between devices, exchange(): return lax.all_to_all(v, axis, split_axis=0, concat_axis=0, tiled=True)  32.2 us
    ppermute x18, waiting for transfers between devices, shift_y(): return lax.ppermute(v, 'mp', [(i, (i + 2 * k) % MP) for i in range(MP)])  30.3 us
    ppermute x18, starting transfers between devices, shift_y(): return lax.ppermute(v, 'mp', [(i, (i + 2 * k) % MP) for i in range(MP)])  22.4 us
    pallas_call x1, Pallas kernels, body(): pl.pallas_call(gated, grid=(pl.cdiv(FP, 256),), out_shape=[jax.ShapeDtype...  18.4 us
    ppermute x13, waiting for transfers between devices, swap_core(): return lax.ppermute(v, 'mp', [(i, i ^ 1) for i in range(MP)])  11.9 us
    pallas_call x1, Pallas kernels, body(): pl.pallas_call(lambda *refs: attend(*refs[:8], *refs[9:]), grid=(4,), out...  9.41 us
  transfers between devices with their start and end apart: 42, of which 21 were waited for; matrix products, arithmetic and copies ran while one was open for 2% of the time, Pallas kernels for 26%

profile of v4, /device:TPU:1, one launch (start us, length us, event | category | flops | bytes accessed | tf_op | source)
XLA Modules:
  0.0 292.1 jit_solution(11905029860033908360)
XLA Ops:
  13.5 7.7 %all-to-all-start = ((bf16[16,176,256]{2,1,0:T(8,128)(2,1)}), bf16[16,176,256]{2,1,0:T(8,128)(2,1)S(1)}, u32[]{:S(2)}, u32[]{:S(2)}) async-start(bf16[16,176,256]{2,1,0:T(8,128)(2,1)} %broadcast_in_dim.27), calls=%async_computation | async-start | bytes 2883584 | tf_op jit(solution)/shard_map/all_to_all | solution.py:63
  28.8 19.3 %all-to-all-done.refs_6_ = bf16[16,176,256]{2,1,0:T(8,128)(2,1)S(1)} async-done(((bf16[16,176,256]{2,1,0:T(8,128)(2,1)}), bf16[16,176,256]{2,1,0:T(8,128)(2,1)S(1)}, u32[]{:S(2)}, u32[]{:S(2)}) %all-to-all-start) | async-done | bytes 1441824 | tf_op jit(solution)/shard_map/all_to_all | solution.py:63
  49.2 6.6 %all-to-all-start.1 = ((bf16[16,112,256]{2,1,0:T(8,128)(2,1)}), bf16[16,112,256]{2,1,0:T(8,128)(2,1)S(1)}, u32[]{:S(2)}, u32[]{:S(2)}) async-start(bf16[16,112,256]{2,1,0:T(8,128)(2,1)} %broadcast_in_dim.28), calls=%async_computation.1 | async-start | bytes 1835008 | tf_op jit(solution)/shard_map/all_to_all | solution.py:63
  57.1 4.6 %shard_map.331 = (bf16[512,1536]{1,0:T(8,128)(2,1)}, bf16[1536,512]{1,0:T(8,128)(2,1)}, bf16[64,1536]{1,0:T(8,128)(2,1)}, bf16[64,1536]{1,0:T(8,128)(2,1)}, bf16[256,1536]{1,0:T(8,128)(2,1)}) custom-call(s32[5]{0:T(128)} %stack.61.refs_0_.ids, bf16[512,1536]{1,0:T(8,128)(2,1)} %bitcast.60, bf16[512,1536]{1,0:T(8,128)(2,1)} %bitcast.54), custom_call_target="tpu_custom_call" | custom-call | flops 1 | bytes 1 | tf_op jit(solution)/shard_map/pallas_call | solution.py:91
  69.4 9.4 %shard_map.332 = (bf16[512,1536]{1,0:T(8,128)(2,1)}, bf16[512,512]{1,0:T(8,128)(2,1)}, bf16[4,2,2,128,256]{4,3,2,1,0:T(8,128)(2,1)}, f32[512,256]{1,0:T(8,128)}, bf16[1536,512]{1,0:T(8,128)(2,1)}) custom-call(s32[5]{0:T(128)} %stack.61.refs_0_.ids, bf16[512,1536]{1,0:T(8,128)(2,1)} %bitcast.55, f32[1,1536]{1,0:T(1,128)} %broadcast_in_dim.29.refs_2_.refs_8_, ...), custom_call_target="tpu_custom_call" | custom-call | flops 1 | bytes 1 | tf_op jit(solution)/shard_map/pallas_call | solution.py:627
  78.9 16.2 %all-to-all-start.2 = ((bf16[8,256,256]{2,1,0:T(8,128)(2,1)}), bf16[8,256,256]{2,1,0:T(8,128)(2,1)S(1)}, u32[]{:S(2)}, u32[]{:S(2)}) async-start(bf16[8,256,256]{2,1,0:T(8,128)(2,1)} %bitcast.61), calls=%async_computation.2 | async-start | bytes 2097152 | tf_op jit(solution)/shard_map/all_to_all | solution.py:63
  100.4 5.5 %shard_map.333 = (bf16[1536,1536]{1,0:T(8,128)(2,1)}, bf16[256,1536]{1,0:T(8,128)(2,1)}) custom-call(s32[5]{0:T(128)} %stack.61.refs_0_.ids, bf16[16,80,256]{2,1,0:T(8,128)(2,1)} %copy-done.21, bf16[16,80,256]{2,1,0:T(8,128)(2,1)} %collective-permute-done.4.refs_2_, bf16[16,80,256]{2,1,0:T(8,128)(2,1)} %collective-permute-done.5.refs_3_, ...), custom_call_target="tpu_custom_call" | custom-call | flops 1 | bytes 1 | tf_op jit(solution)/shard_map/pallas_call | solution.py:91
  106.0 4.2 %all-to-all-done.2.att.refs_1_ = bf16[8,256,256]{2,1,0:T(8,128)(2,1)S(1)} async-done(((bf16[8,256,256]{2,1,0:T(8,128)(2,1)}), bf16[8,256,256]{2,1,0:T(8,128)(2,1)S(1)}, u32[]{:S(2)}, u32[]{:S(2)}) %all-to-all-start.2) | async-done | bytes 1048608 | tf_op jit(solution)/shard_map/all_to_all | solution.py:63
  111.2 6.2 %shard_map.334 = (f32[64,1536]{1,0:T(8,128)}, bf16[256,1536]{1,0:T(8,128)(2,1)}) custom-call(s32[5]{0:T(128)} %stack.61.refs_0_.ids, bf16[8,256,256]{2,1,0:T(8,128)(2,1)} %copy-done.16, bf16[1536,1536]{1,0:T(8,128)(2,1)} %get-tuple-element.88.mixer, bf16[256,1536]{1,0:T(8,128)(2,1)} %get-tuple-element.89.tok, f32[1,1536]{1,0:T(1,128)} %broadcast_in_dim.31.gain.refs_7_), custom_call_target="tpu_custom_call" | custom-call | flops 1 | bytes 1 | tf_op jit(solution)/shard_map/pallas_call | solution.py:659
  121.3 18.4 %shard_map.335 = (bf16[512,1152]{1,0:T(8,128)(2,1)}, bf16[512,1152]{1,0:T(8,128)(2,1)}, bf16[512,1152]{1,0:T(8,128)(2,1)}, bf16[16,3,96,1152]{3,2,1,0:T(8,128)(2,1)}) custom-call(bf16[256,1536]{1,0:T(8,128)(2,1)} %get-tuple-element.90.near, bf16[256,1536]{1,0:T(8,128)(2,1)} %copy-done.24, bf16[512,1536]{1,0:T(8,128)(2,1)} %get-tuple-element.86.refs_8_.back, ...), custom_call_target="tpu_custom_call" | custom-call | flops 1 | bytes 1 | tf_op jit(solution)/shard_map/pallas_call | solution.py:681
  139.7 8.0 %shard_map.337 = (bf16[256,1536]{1,0:T(8,128)(2,1)}, bf16[256,1536]{1,0:T(8,128)(2,1)}) custom-call(bf16[512,1152]{1,0:T(8,128)(2,1)} %get-tuple-element.95.gate_grad, bf16[512,1152]{1,0:T(8,128)(2,1)} %get-tuple-element.96.up_grad, bf16[16,3,96,1152]{3,2,1,0:T(8,128)(2,1)} %bitcast.52), custom_call_target="tpu_custom_call" | custom-call | flops 1 | bytes 1 | tf_op jit(solution)/shard_map/pallas_call | solution.py:694
  154.9 5.2 %shard_map.336 = (bf16[256,1536]{1,0:T(8,128)(2,1)}, bf16[256,1536]{1,0:T(8,128)(2,1)}) custom-call(bf16[512,1152]{1,0:T(8,128)(2,1)} %get-tuple-element.92.act, bf16[16,3,96,1152]{3,2,1,0:T(8,128)(2,1)} %bitcast.53), custom_call_target="tpu_custom_call" | custom-call | flops 1 | bytes 1 | tf_op jit(solution)/shard_map/pallas_call | solution.py:714
  170.6 4.1 %collective-permute-done.19 = bf16[64,1536]{1,0:T(8,128)(2,1)S(1)} collective-permute-done((bf16[64,1536]{1,0:T(8,128)(2,1)S(1)}, bf16[64,1536]{1,0:T(8,128)(2,1)S(1)}, u32[]{:S(2)}, u32[]{:S(2)}) %collective-permute-start.19) | collective-permute-done | bytes 196640 | tf_op jit(solution)/shard_map/ppermute | solution.py:47
  180.9 12.1 %shard_map.340 = (bf16[512,512]{1,0:T(8,128)(2,1)}, bf16[512,384]{1,0:T(8,128)(2,1)}, bf16[512,128]{1,0:T(8,128)(2,1)}, bf16[512,128]{1,0:T(8,128)(2,1)}, bf16[2...) custom-call(s32[5]{0:T(128)} %stack.61.refs_0_.ids, bf16[4,64,1536]{2,1,0:T(8,128)(2,1)} %copy-done.20, ...), custom_call_target="tpu_custom_call" | custom-call | flops 1 | bytes 1 | tf_op jit(solution)/shard_map/pallas_call | solution.py:91
  196.9 4.5 %collective-permute-start.23 = (bf16[512,128]{1,0:T(8,128)(2,1)S(1)}, bf16[512,128]{1,0:T(8,128)(2,1)S(1)}, u32[]{:S(2)}, u32[]{:S(2)}) collective-permute-start(bf16[512,128]{1,0:T(8,128)(2,1)S(1)} %get-tuple-element.117), channel_id=1, source_target_pairs={{0,6},{1,7},{8,14},{9,15},{16,22},{17,23},{24,30},{25,31},{32,38},... | collective-permute-start | bytes 393224 | tf_op jit(solution)/shard_map/ppermute | solution.py:55
  202.9 3.8 %all-to-all-start.3 = ((bf16[8,32,128]{2,1,0:T(8,128)(2,1)}), bf16[8,32,128]{2,1,0:T(8,128)(2,1)S(1)}, u32[]{:S(2)}, u32[]{:S(2)}) async-start(bf16[8,32,128]{2,1,0:T(8,128)(2,1)} %get-tuple-element.120), calls=%async_computation.3 | async-start | bytes 131072 | tf_op jit(solution)/shard_map/all_to_all | solution.py:63
  206.7 3.2 %shard_map.342.refs_7_ = bf16[16,96,192]{2,1,0:T(8,128)(2,1)} custom-call(s32[5]{0:T(128)} %stack.61.refs_0_.ids, bf16[8,256,256]{2,1,0:T(8,128)(2,1)} %copy-done.16, bf16[8,256,256]{2,1,0:T(8,128)(2,1)} %collective-permute-done.26.refs_2_, bf16[512,384]{1,0:T(8,128)(2,1)} %get-tuple-element.121.refs_3_), custom_call_target="tpu_custom_call" | custom-call | flops 1 | bytes 1 | tf_op jit(solution)/shard_map/pallas_call | solution.py:91
  212.4 3.8 %shard_map.343.refs_5_ = bf16[16,104,448]{2,1,0:T(8,128)(2,1)} custom-call(s32[5]{0:T(128)} %stack.61.refs_0_.ids, bf16[512,1536]{1,0:T(8,128)(2,1)} %get-tuple-element.113.refs_1_, bf16[512,512]{1,0:T(8,128)(2,1)} %get-tuple-element.114.refs_2_, bf16[512,128]{1,0:T(8,128)(2,1)} %copy-done.31, bf16[512,128]{1,0:T(8,128)(2,1)} %copy-done.32, ...), custom_call_target="tpu_custom_call" | custom-call | flops 1 | bytes 1 | tf_op jit(solution)/shard_map/pallas_call | solution.py:91
  216.2 6.6 %all-to-all-start.4 = ((bf16[16,104,448]{2,1,0:T(8,128)(2,1)}), bf16[16,104,448]{2,1,0:T(8,128)(2,1)}, u32[]{:S(2)}, u32[]{:S(2)}) async-start(bf16[16,104,448]{2,1,0:T(8,128)(2,1)} %shard_map.343.refs_5_), calls=%async_computation.4 | async-start | bytes 3407872 | tf_op jit(solution)/shard_map/all_to_all | solution.py:63
  229.4 7.5 %collective-permute-done.27.refs_2_ = bf16[2,64,1536]{2,1,0:T(8,128)(2,1)S(1)} collective-permute-done((bf16[2,64,1536]{2,1,0:T(8,128)(2,1)S(1)}, bf16[2,64,1536]{2,1,0:T(8,128)(2,1)S(1)}, u32[]{:S(2)}, u32[]{:S(2)}) %collective-permute-start.27) | collective-permute-done | bytes 393248 | tf_op jit(solution)/shard_map/ppermute | solution.py:47
  236.9 9.4 %collective-permute-done.29.refs_4_ = bf16[2,64,1536]{2,1,0:T(8,128)(2,1)S(1)} collective-permute-done((bf16[2,64,1536]{2,1,0:T(8,128)(2,1)S(1)}, bf16[2,64,1536]{2,1,0:T(8,128)(2,1)S(1)}, u32[]{:S(2)}, u32[]{:S(2)}) %collective-permute-start.29) | collective-permute-done | bytes 393248 | tf_op jit(solution)/shard_map/ppermute | solution.py:47
  253.0 11.5 %all-to-all-start.5 = ((f32[128,1,128]{2,1,0:T(1,128)}), f32[128,1,128]{2,1,0:T(1,128)S(1)}, u32[]{:S(2)}, u32[]{:S(2)}) async-start(f32[128,1,128]{2,1,0:T(1,128)} %get-tuple-element.129), calls=%async_computation.5 | async-start | bytes 131072 | tf_op jit(solution)/shard_map/all_to_all | solution.py:63
  267.0 6.9 %all-to-all-done.5.refs_5_.squares = f32[128,1,128]{2,1,0:T(1,128)S(1)} async-done(((f32[128,1,128]{2,1,0:T(1,128)}), f32[128,1,128]{2,1,0:T(1,128)S(1)}, u32[]{:S(2)}, u32[]{:S(2)}) %all-to-all-start.5) | async-done | bytes 65568 | tf_op jit(solution)/shard_map/all_to_all | solution.py:63
  276.1 6.7 %shard_map.350 = (f32[1,128]{1,0:T(1,128)}, f32[96,256]{1,0:T(8,128)}, f32[96,256]{1,0:T(8,128)}, f32[96,256]{1,0:T(8,128)}, f32[96,192]{1,0:T(8,128)}, /*index=...) custom-call(f32[128,1,128]{2,1,0:T(1,128)} %copy-done.5, ...), custom_call_target="tpu_custom_call" | custom-call | flops 1 | bytes 1 | tf_op jit(solution)/shard_map/pallas_call | solution.py:829
  (198 shorter events, 85.2 us)
Async XLA Ops:
  7.2 113.2 %all-gather.3.cloned.1.call-start = ((), (), s32[]{:S(2)}) async-start(), calls=%async_computation.7 | async-start | bytes 11280384 | tf_op jit(solution)/shard_map/all_gather | solution.py:576
  13.5 34.6 %all-to-all-start = ((bf16[16,176,256]{2,1,0:T(8,128)(2,1)}), bf16[16,176,256]{2,1,0:T(8,128)(2,1)S(1)}, u32[]{:S(2)}, u32[]{:S(2)}) async-start(bf16[16,176,256]{2,1,0:T(8,128)(2,1)} %broadcast_in_dim.27), calls=%async_computation | async-start | bytes 2883584 | tf_op jit(solution)/shard_map/all_to_all | solution.py:63
  49.2 18.4 %all-to-all-start.1 = ((bf16[16,112,256]{2,1,0:T(8,128)(2,1)}), bf16[16,112,256]{2,1,0:T(8,128)(2,1)S(1)}, u32[]{:S(2)}, u32[]{:S(2)}) async-start(bf16[16,112,256]{2,1,0:T(8,128)(2,1)} %broadcast_in_dim.28), calls=%async_computation.1 | async-start | bytes 1835008 | tf_op jit(solution)/shard_map/all_to_all | solution.py:63
  61.7 33.5 %collective-permute-start.6 = (bf16[16,80,256]{2,1,0:T(8,128)(2,1)S(1)}, bf16[16,80,256]{2,1,0:T(8,128)(2,1)}, u32[]{:S(2)}, u32[]{:S(2)}) collective-permute-start(bf16[16,80,256]{2,1,0:T(8,128)(2,1)S(1)} %slice.135.refs_1_), channel_id=1, source_target_pairs={{0,4},{1,5},{2,6},{3,7},{4,0},{5,1},{6,2},{7,3},{8,12},{9,13},{10,... | collective-permute-start | bytes 1966088 | tf_op jit(solution)/shard_map/ppermute | solution.py:47
  64.8 30.9 %collective-permute-start.4 = (bf16[16,80,256]{2,1,0:T(8,128)(2,1)S(1)}, bf16[16,80,256]{2,1,0:T(8,128)(2,1)}, u32[]{:S(2)}, u32[]{:S(2)}) collective-permute-start(bf16[16,80,256]{2,1,0:T(8,128)(2,1)S(1)} %slice.135.refs_1_), channel_id=1, source_target_pairs={{0,2},{1,3},{2,4},{3,5},{4,6},{5,7},{6,0},{7,1},{8,10},{9,11},{10,... | collective-permute-start | bytes 1966088 | tf_op jit(solution)/shard_map/ppermute | solution.py:47
  65.2 30.6 %collective-permute-start.5 = (bf16[16,80,256]{2,1,0:T(8,128)(2,1)S(1)}, bf16[16,80,256]{2,1,0:T(8,128)(2,1)}, u32[]{:S(2)}, u32[]{:S(2)}) collective-permute-start(bf16[16,80,256]{2,1,0:T(8,128)(2,1)S(1)} %slice.135.refs_1_), channel_id=1, source_target_pairs={{0,6},{1,7},{2,0},{3,1},{4,2},{5,3},{6,4},{7,5},{8,14},{9,15},{10,... | collective-permute-start | bytes 1966088 | tf_op jit(solution)/shard_map/ppermute | solution.py:47
  78.9 31.3 %all-to-all-start.2 = ((bf16[8,256,256]{2,1,0:T(8,128)(2,1)}), bf16[8,256,256]{2,1,0:T(8,128)(2,1)S(1)}, u32[]{:S(2)}, u32[]{:S(2)}) async-start(bf16[8,256,256]{2,1,0:T(8,128)(2,1)} %bitcast.61), calls=%async_computation.2 | async-start | bytes 2097152 | tf_op jit(solution)/shard_map/all_to_all | solution.py:63
  95.1 155.0 %reduce-scatter.4.cloned.1.call-start = ((), (), s32[]{:S(2)}) async-start(), calls=%async_computation.8 | async-start | bytes 11280384
  154.8 8.3 %collective-permute-start.16 = (bf16[64,1536]{1,0:T(8,128)(2,1)S(1)}, bf16[64,1536]{1,0:T(8,128)(2,1)S(1)}, u32[]{:S(2)}, u32[]{:S(2)}) collective-permute-start(bf16[64,1536]{1,0:T(8,128)(2,1)S(1)} %get-tuple-element.102), channel_id=1, source_target_pairs={{0,4},{1,5},{2,6},{3,7},{4,0},{5,1},{6,2},{7,3},{8,12},{9,13},{10,... | collective-permute-start | bytes 589832 | tf_op jit(solution)/shard_map/ppermute | solution.py:47
  178.0 24.8 %collective-permute-start.26 = (bf16[8,256,256]{2,1,0:T(8,128)(2,1)S(1)}, bf16[8,256,256]{2,1,0:T(8,128)(2,1)}, u32[]{:S(2)}, u32[]{:S(2)}) collective-permute-start(bf16[8,256,256]{2,1,0:T(8,128)(2,1)S(1)} %copy-done.17), channel_id=1, source_target_pairs={{0,1},{1,0},{2,3},{3,2},{4,5},{5,4},{6,7},{7,6},{8,9},{9,8},{10,11... | collective-permute-start | bytes 3145736 | tf_op jit(solution)/shard_map/ppermute | solution.py:59
  196.3 15.3 %collective-permute-start.25 = (bf16[512,256]{1,0:T(8,128)(2,1)S(1)}, bf16[512,256]{1,0:T(8,128)(2,1)S(1)}, u32[]{:S(2)}, u32[]{:S(2)}) collective-permute-start(bf16[512,256]{1,0:T(8,128)(2,1)S(1)} %get-tuple-element.119), channel_id=1, source_target_pairs={{2,6},{3,7},{10,14},{11,15},{18,22},{19,23},{26,30},{27,31},{34,38... | collective-permute-start | bytes 786440 | tf_op jit(solution)/shard_map/ppermute | solution.py:55
  196.9 14.6 %collective-permute-start.23 = (bf16[512,128]{1,0:T(8,128)(2,1)S(1)}, bf16[512,128]{1,0:T(8,128)(2,1)S(1)}, u32[]{:S(2)}, u32[]{:S(2)}) collective-permute-start(bf16[512,128]{1,0:T(8,128)(2,1)S(1)} %get-tuple-element.117), channel_id=1, source_target_pairs={{0,6},{1,7},{8,14},{9,15},{16,22},{17,23},{24,30},{25,31},{32,38},... | collective-permute-start | bytes 393224 | tf_op jit(solution)/shard_map/ppermute | solution.py:55
  201.4 10.1 %collective-permute-start.24 = (bf16[512,128]{1,0:T(8,128)(2,1)S(1)}, bf16[512,128]{1,0:T(8,128)(2,1)S(1)}, u32[]{:S(2)}, u32[]{:S(2)}) collective-permute-start(bf16[512,128]{1,0:T(8,128)(2,1)S(1)} %get-tuple-element.118), channel_id=1, source_target_pairs={{4,6},{5,7},{12,14},{13,15},{20,22},{21,23},{28,30},{29,31},{36,38... | collective-permute-start | bytes 393224 | tf_op jit(solution)/shard_map/ppermute | solution.py:55
  202.1 20.7 %collective-permute-start.12 = (bf16[256,1536]{1,0:T(8,128)(2,1)}, bf16[256,1536]{1,0:T(8,128)(2,1)}, u32[]{:S(2)}, u32[]{:S(2)}) collective-permute-start(bf16[256,1536]{1,0:T(8,128)(2,1)} %get-tuple-element.94.refs_8_), channel_id=1, source_target_pairs={{0,1},{1,0},{2,3},{3,2},{4,5},{5,4},{6,7},{7,6},{8,9},{9,8},{10,11... | collective-permute-start | bytes 2359304 | tf_op jit(solution)/shard_map/ppermute | solution.py:59
  202.8 20.0 %collective-permute-start.21 = (bf16[256,1536]{1,0:T(8,128)(2,1)}, bf16[256,1536]{1,0:T(8,128)(2,1)}, u32[]{:S(2)}, u32[]{:S(2)}) collective-permute-start(bf16[256,1536]{1,0:T(8,128)(2,1)} %get-tuple-element.112), channel_id=1, source_target_pairs={{0,1},{1,0},{2,3},{3,2},{4,5},{5,4},{6,7},{7,6},{8,9},{9,8},{10,11... | collective-permute-start | bytes 2359304 | tf_op jit(solution)/shard_map/ppermute | solution.py:59
  202.9 8.6 %all-to-all-start.3 = ((bf16[8,32,128]{2,1,0:T(8,128)(2,1)}), bf16[8,32,128]{2,1,0:T(8,128)(2,1)S(1)}, u32[]{:S(2)}, u32[]{:S(2)}) async-start(bf16[8,32,128]{2,1,0:T(8,128)(2,1)} %get-tuple-element.120), calls=%async_computation.3 | async-start | bytes 131072 | tf_op jit(solution)/shard_map/all_to_all | solution.py:63
  216.2 33.9 %all-to-all-start.4 = ((bf16[16,104,448]{2,1,0:T(8,128)(2,1)}), bf16[16,104,448]{2,1,0:T(8,128)(2,1)}, u32[]{:S(2)}, u32[]{:S(2)}) async-start(bf16[16,104,448]{2,1,0:T(8,128)(2,1)} %shard_map.343.refs_5_), calls=%async_computation.4 | async-start | bytes 3407872 | tf_op jit(solution)/shard_map/all_to_all | solution.py:63
  225.8 11.0 %collective-permute-start.27 = (bf16[2,64,1536]{2,1,0:T(8,128)(2,1)S(1)}, bf16[2,64,1536]{2,1,0:T(8,128)(2,1)S(1)}, u32[]{:S(2)}, u32[]{:S(2)}) collective-permute-start(bf16[2,64,1536]{2,1,0:T(8,128)(2,1)S(1)} %get-tuple-element.123), channel_id=1, source_target_pairs={{0,2},{1,3},{2,4},{3,5},{4,6},{5,7},{6,0},{7,1},{8,10},{9,11},{10,... | collective-permute-start | bytes 1179656 | tf_op jit(solution)/shard_map/ppermute | solution.py:47
  226.6 10.3 %collective-permute-start.28 = (bf16[2,64,1536]{2,1,0:T(8,128)(2,1)S(1)}, bf16[2,64,1536]{2,1,0:T(8,128)(2,1)S(1)}, u32[]{:S(2)}, u32[]{:S(2)}) collective-permute-start(bf16[2,64,1536]{2,1,0:T(8,128)(2,1)S(1)} %get-tuple-element.124), channel_id=1, source_target_pairs={{0,6},{1,7},{2,0},{3,1},{4,2},{5,3},{6,4},{7,5},{8,14},{9,15},{10,... | collective-permute-start | bytes 1179656 | tf_op jit(solution)/shard_map/ppermute | solution.py:47
  228.6 17.7 %collective-permute-start.29 = (bf16[2,64,1536]{2,1,0:T(8,128)(2,1)S(1)}, bf16[2,64,1536]{2,1,0:T(8,128)(2,1)S(1)}, u32[]{:S(2)}, u32[]{:S(2)}) collective-permute-start(bf16[2,64,1536]{2,1,0:T(8,128)(2,1)S(1)} %get-tuple-element.125), channel_id=1, source_target_pairs={{0,4},{1,5},{2,6},{3,7},{4,0},{5,1},{6,2},{7,3},{8,12},{9,13},{10,... | collective-permute-start | bytes 1179656 | tf_op jit(solution)/shard_map/ppermute | solution.py:47
  247.4 17.2 %collective-permute-start.30 = (bf16[2,64,1536]{2,1,0:T(8,128)(2,1)S(1)}, bf16[2,64,1536]{2,1,0:T(8,128)(2,1)S(1)}, u32[]{:S(2)}, u32[]{:S(2)}) collective-permute-start(bf16[2,64,1536]{2,1,0:T(8,128)(2,1)S(1)} %shard_map.345.p0.refs_1_), channel_id=1, source_target_pairs={{0,2},{1,3},{2,4},{3,5},{4,6},{5,7},{6,0},{7,1},{8,10},{9,11},{10,... | collective-permute-start | bytes 1179656 | tf_op jit(solution)/shard_map/ppermute | solution.py:47
  248.0 16.6 %collective-permute-start.31 = (bf16[2,64,1536]{2,1,0:T(8,128)(2,1)S(1)}, bf16[2,64,1536]{2,1,0:T(8,128)(2,1)S(1)}, u32[]{:S(2)}, u32[]{:S(2)}) collective-permute-start(bf16[2,64,1536]{2,1,0:T(8,128)(2,1)S(1)} %shard_map.345.p0.refs_1_), channel_id=1, source_target_pairs={{0,6},{1,7},{2,0},{3,1},{4,2},{5,3},{6,4},{7,5},{8,14},{9,15},{10,... | collective-permute-start | bytes 1179656 | tf_op jit(solution)/shard_map/ppermute | solution.py:47
  250.1 14.4 %collective-permute-start.32 = (bf16[2,64,1536]{2,1,0:T(8,128)(2,1)S(1)}, bf16[2,64,1536]{2,1,0:T(8,128)(2,1)S(1)}, u32[]{:S(2)}, u32[]{:S(2)}) collective-permute-start(bf16[2,64,1536]{2,1,0:T(8,128)(2,1)S(1)} %shard_map.345.p0.refs_1_), channel_id=1, source_target_pairs={{0,4},{1,5},{2,6},{3,7},{4,0},{5,1},{6,2},{7,3},{8,12},{9,13},{10,... | collective-permute-start | bytes 1179656 | tf_op jit(solution)/shard_map/ppermute | solution.py:47
  253.0 20.9 %all-to-all-start.5 = ((f32[128,1,128]{2,1,0:T(1,128)}), f32[128,1,128]{2,1,0:T(1,128)S(1)}, u32[]{:S(2)}, u32[]{:S(2)}) async-start(f32[128,1,128]{2,1,0:T(1,128)} %get-tuple-element.129), calls=%async_computation.5 | async-start | bytes 131072 | tf_op jit(solution)/shard_map/all_to_all | solution.py:63
  (52 other events, 320.6 us)
Sparse Core Ops, SparseCore 0:
  10.2 103.7 all-gather.2
  139.8 91.3 reduce-scatter.3

commit v5 on v3

--- a/solution.py
+++ b/solution.py
@@ -103,7 +103,7 @@
     return pl.ds(pl.multiple_of(start, step), size)
 
 
-def prepare(ids, cotangent, tok, back, back_t, back_part, tok_part):
+def prepare(ids, cotangent, tok, back, back_t, back_part, tok_part, tok_half):
     length, y, c = ids[0], ids[3], ids[4]
     for h in range(2):
         start = HALF * ((c + h) % 2)
@@ -114,6 +114,7 @@
         back_t[:, HALF * h : HALF * (h + 1)] = v.T
     back_part[...] = back[at(PART * y, PART, PART), :]
     tok_part[...] = tok[at(HALF * c + PART * y, PART, PART), :]
+    tok_half[...] = tok[at(HALF * c, HALF, HALF), :]
 
 
 def kept(i, n, length):
@@ -162,16 +163,9 @@
                 out[2 * y + i // 2, at_row : at_row + 128, HEAD * h : HEAD * (h + 1)] = o
 
 
-def mix(
-    ids, att, a0, a1, a2, a3, b0, b1, b2, b3, tok, gain,
-    hidden_part, normed, rows_w, hidden, side, mixer,
-):
+def assemble(ids, a0, a1, a2, a3, b0, b1, b2, b3, mixer, rows_w):
     y, c = ids[3], ids[4]
-    for j in range(KEY_AT):
-        side[:, JC * j : JC * (j + 1)] = att[j]
-    mine = at(HALF * c, HALF, HALF)
     for e, a, b in zip(RELATIVE, (a0, a1, a2, a3), (b0, b1, b2, b3)):
-        cols = at(384 * lax.rem(y + e + 4, 4), 384, 384)
         first = 384 * lax.rem(y + e + 4, 4)
         left, right = at(first, JC, 128), at(first + JC, HEAD, 128)
         for d in range(DP):
@@ -180,13 +174,27 @@
                 mixer[at(row, 48, 16), left] = v[d, :48, :]
                 mixer[at(row, 32, 16), right] = v[d, 48:80, :HEAD]
                 mixer[at(row + 32, 16, 16), right] = v[d, 48:64, HEAD:]
-        hidden[:, cols] = nn(side[...], mixer[:, cols]) + tok[mine, cols].astype(f32)
-    hidden_part[...] = hidden[at(PART * y, PART, PART), :]
     rows_w[...] = mixer[at(JC * jnp.minimum(ids[2], KEY_AT - 1), JC, JC), :]
-    for r in range(0, HALF, 64):
-        v = hidden[r : r + 64, :]
-        s = lax.rsqrt(jnp.mean(v * v, -1, keepdims=True) + EPS_NORM)
-        normed[r : r + 64, :] = (v * s * gain[...]).astype(bf16)
+
+
+def mix(ids, att, mixer, tok, gain, hidden_part, normed, hidden, side):
+    i = pl.program_id(0)
+
+    @pl.when(i == 0)
+    def _():
+        for j in range(KEY_AT):
+            side[:, JC * j : JC * (j + 1)] = att[j]
+
+    cols = at(384 * i, 384, 384)
+    hidden[:, cols] = nn(side[...], mixer[...]) + tok[...].astype(f32)
+
+    @pl.when(i == 3)
+    def _():
+        hidden_part[...] = hidden[at(PART * ids[3], PART, PART), :]
+        for r in range(0, HALF, 64):
+            v = hidden[r : r + 64, :]
+            s = lax.rsqrt(jnp.mean(v * v, -1, keepdims=True) + EPS_NORM)
+            normed[r : r + 64, :] = (v * s * gain[...]).astype(bf16)
 
 
 def gated(near, far, back, back_t, w, act, gate_grad, up_grad, grads, near_t):
@@ -237,11 +245,6 @@
         out[...] = (near[rows, :].astype(f32) + other[rows, :].astype(f32)).astype(out.dtype)
 
 
-def halve_two(ids, near_a, other_a, near_b, other_b, own, p1, p2, p3):
-    for n, (near, other) in enumerate(((near_a, other_a), (near_b, other_b))):
-        halve(ids, near, other, own.at[n], p1.at[n], p2.at[n], p3.at[n])
-
-
 def summed(own, parts):
     total = own[...]
     for part in parts:
@@ -259,9 +262,13 @@
     low[...] = v.astype(bf16)
 
 
-def finish(ids, own, a1, a2, a3, hidden, tok, grad, gain, done):
+def add_parts(ids, own, a1, a2, a3, total):
+    total[...] = summed(own, (a1, a2, a3))
+
+
+def finish(ids, out_sum, own, a1, a2, a3, hidden, tok, grad, gain, done):
     length, y, c = ids[0], ids[3], ids[4]
-    o, g = [summed(own.at[n], [a.at[n] for a in (a1, a2, a3)]) for n in range(2)]
+    o, g = out_sum[...], summed(own, (a1, a2, a3))
     t = lax.broadcasted_iota(jnp.int32, (PART, 1), 0) + HALF * c + PART * y
     done[0] = jnp.where(t < length, o + hidden[...], 0.0).astype(bf16)
     x = tok[...].astype(f32)
@@ -598,9 +605,12 @@
     )[None]
 
     cosine, sine = tables()
-    back, back_t, back_part, tok_part = whole(
+    back, back_t, back_part, tok_part, tok_half = whole(
         prepare,
-        [((T, D), bf16), ((D, T), bf16), ((PART, D), bf16), ((PART, D), bf16)],
+        [
+            ((T, D), bf16), ((D, T), bf16),
+            ((PART, D), bf16), ((PART, D), bf16), ((HALF, D), bf16),
+        ],
         [ids, cotangent[0], tok],
     )
     normed, heads, att_sent, lse, joint_w = whole(
@@ -616,21 +626,33 @@
     att_far = swap_core(att_near)
     mixer_near = gather(shift_y, query_w[:, ROWS:])
     mixer_far = [swap_core(v) for v in mixer_near]
-    hidden_part, normed_near, rows_w = whole(
+    mixer, rows_w = whole(
+        assemble, [((D, D), bf16), ((JC, D), bf16)], [ids] + mixer_near + mixer_far
+    )
+
+    def fixed(shape):
+        return pl.BlockSpec(shape, lambda i: (0,) * len(shape))
+
+    hidden_part, normed_near = pl.pallas_call(
         mix,
-        [((PART, D), f32), ((HALF, D), bf16), ((JC, D), bf16)],
-        [ids, att_near] + mixer_near + mixer_far + [tok, gain_second],
-        scratch=[
-            pltpu.VMEM((HALF, D), f32), pltpu.VMEM((HALF, D), bf16), pltpu.VMEM((D, D), bf16),
+        grid=(4,),
+        out_shape=[jax.ShapeDtypeStruct((PART, D), f32), jax.ShapeDtypeStruct((HALF, D), bf16)],
+        in_specs=[
+            SM,
+            fixed((MP, HALF, JC)),
+            pl.BlockSpec((D, 384), lambda i: (0, i)),
+            pl.BlockSpec((HALF, 384), lambda i: (0, i)),
+            fixed((1, D)),
         ],
-    )
+        out_specs=[fixed((PART, D)), fixed((HALF, D))],
+        scratch_shapes=[pltpu.VMEM((HALF, D), f32), pltpu.VMEM((HALF, D), bf16)],
+        compiler_params=pltpu.CompilerParams(vmem_limit_bytes=60 * MiB),
+        cost_estimate=SMALL,
+    )(ids, att_near, mixer, tok_half, gain_second)
     normed_far = swap_core(normed_near)
 
     def columns(n):
         return pl.BlockSpec((n, 256), lambda i: (0, i))
-
-    def fixed(shape):
-        return pl.BlockSpec(shape, lambda i: (0,) * len(shape))
 
     block = pl.BlockSpec((DP, 3, ROWS, 256), lambda i: (0, 0, 0, i))
     act, gate_grad, up_grad, ff_grads = pl.pallas_call(
@@ -657,15 +679,17 @@
         cost_estimate=SMALL,
     )(gate_grad, up_grad, ff)
 
-    def half_sum(body, pairs, after=()):
-        shape = (PART, D) if len(pairs) == 1 else (len(pairs), PART, D)
-        given = [v for near, far in pairs for v in (near, swap_core(far))]
+    def half_sum(near, far, after=()):
         own, *parts = whole(
-            body, [(shape, f32)] + [(shape, bf16)] * 3, [ids] + given, after=after, limit=16
+            halve,
+            [((PART, D), f32)] + [((PART, D), bf16)] * 3,
+            [ids, near, swap_core(far)],
+            after=after,
+            limit=8,
         )
         return [own] + [shift_y(v, k) for v, k in zip(parts, (1, -1, 2))]
 
-    normed_second_parts = half_sum(halve, [(near, far)])
+    normed_second_parts = half_sum(near, far)
     out_near, out_far = pl.pallas_call(
         spread_out,
         grid=(2,),
@@ -685,6 +709,7 @@
         after=[out_far],
         limit=8,
     )
+    out_parts = half_sum(out_near, out_far)
     low_near = jnp.stack(gather(shift_y, low))
     low_far = swap_core(low_near)
     heads_grad, hidden_low, own_kind, other_kind, input_near, input_far, chunks = whole(
@@ -703,12 +728,17 @@
             pltpu.VMEM((1, DP * MP * 40), f32),
             pltpu.VMEM((DP, MP * 40), f32),
         ],
+        after=[out_parts[0]],
+    )
+    (out_sum,) = whole(
+        add_parts, [((PART, D), f32)], [ids] + out_parts, limit=8, after=[heads_grad]
     )
     both, left, right = whole(
         group_parts,
         [((T, JC), bf16), ((T, HEAD), bf16), ((T, HEAD), bf16)],
         [ids, own_kind, swap_core(other_kind)],
         limit=8,
+        after=[out_sum],
     )
     left, right, both = to_last_chip(left, 0), to_last_chip(right, 2), to_last_chip(both, 1)
     moved = exchange(chunks, "mp")
@@ -716,6 +746,7 @@
         weigh_mixer,
         [((DP, ROWS, MC), bf16)],
         [ids, att_near, att_far, hidden_low],
+        after=[out_sum],
     )
     (joint_parts,) = whole(
         weigh_joint,
@@ -730,13 +761,11 @@
 
     squares = exchange(squares, ("dp", "mp"))
 
-    parts = half_sum(
-        halve_two, [(out_near, out_far), (input_near, input_far)], after=[joint_parts]
-    )
+    parts = half_sum(input_near, input_far, after=[joint_parts])
     (done,) = whole(
         finish,
         [((2, PART, D), bf16)],
-        [ids] + parts + [hidden_part, tok_part, hidden_grad, gain_first],
+        [ids, out_sum] + parts + [hidden_part, tok_part, hidden_grad, gain_first],
         limit=8,
     )
     done_parts = gather(shift_y, done)

time: 294 us -> 287 us (0.976)
  waiting for transfers between devices: 79.5 us -> 63.1 us
  Pallas kernels: 91.4 us -> 96.8 us
  starting transfers between devices: 90.1 us -> 94.7 us
    ppermute x18 -> x21, waiting for transfers between devices: 30.3 us -> 19.4 us  [shift_y(): return lax.ppermute(v, 'mp', [(i, (i + 2 * k) % MP) for i in range(MP)])]
    pallas_call x0 -> x1, Pallas kernels: none -> 6.23 us  [body(): pl.pallas_call(mix, grid=(4,), out_shape=[jax.ShapeDtypeStruct((PART, D),...]
    all_to_all x6, waiting for transfers between devices: 37.3 us -> 32.7 us  [exchange(): return lax.all_to_all(v, axis, split_axis=0, concat_axis=0, tiled=True)]
    ppermute x13, starting transfers between devices: 9.27 us -> 12.9 us  [swap_core(): return lax.ppermute(v, 'mp', [(i, i ^ 1) for i in range(MP)])]
    ppermute x18 -> x21, starting transfers between devices: 22.4 us -> 25.5 us  [shift_y(): return lax.ppermute(v, 'mp', [(i, (i + 2 * k) % MP) for i in range(MP)])]
    pallas_call x13 -> x15, Pallas kernels: 48.2 us -> 47.3 us  [whole(): pl.pallas_call(bare, out_shape=[jax.ShapeDtypeStruct(s, d) for s, d in ou...]
    unnamed x70 -> x82, local copies, waits for them, and re-layouts: 8.31 us -> 8.15 us
  transfers between devices with their start and end apart: 42 -> 45, of which waited for: 20 -> 20; matrix products, arithmetic and copies ran while one was open for 2% -> 2% of each run, Pallas kernels for 24% -> 26%
where the time goes in v5:
time: 287 us; the launch traced here: 286 us
  Pallas kernels  96.8 us (34%)
  starting transfers between devices  94.7 us (33%)
  waiting for transfers between devices  63.1 us (22%)
  between operations  15.4 us (5%)
  local copies, waits for them, and re-layouts  12.8 us (4%)
  other arithmetic  3.28 us (1%)
    all_to_all x6, starting transfers between devices, exchange(): return lax.all_to_all(v, axis, split_axis=0, concat_axis=0, tiled=True)  51.1 us
    pallas_call x15, Pallas kernels, whole(): pl.pallas_call(bare, out_shape=[jax.ShapeDtypeStruct(s, d) for s, d in ou...  47.3 us
    all_to_all x6, waiting for transfers between devices, exchange(): return lax.all_to_all(v, axis, split_axis=0, concat_axis=0, tiled=True)  32.7 us
    ppermute x21, starting transfers between devices, shift_y(): return lax.ppermute(v, 'mp', [(i, (i + 2 * k) % MP) for i in range(MP)])  25.5 us
    ppermute x21, waiting for transfers between devices, shift_y(): return lax.ppermute(v, 'mp', [(i, (i + 2 * k) % MP) for i in range(MP)])  19.4 us
    pallas_call x1, Pallas kernels, body(): pl.pallas_call(gated, grid=(pl.cdiv(FP, 256),), out_shape=[jax.ShapeDtype...  18.4 us
    ppermute x13, starting transfers between devices, swap_core(): return lax.ppermute(v, 'mp', [(i, i ^ 1) for i in range(MP)])  12.9 us
    ppermute x13, waiting for transfers between devices, swap_core(): return lax.ppermute(v, 'mp', [(i, i ^ 1) for i in range(MP)])  11 us
  transfers between devices with their start and end apart: 45, of which 20 were waited for; matrix products, arithmetic and copies ran while one was open for 2% of the time, Pallas kernels for 26%

profile of v5, /device:TPU:1, one launch (start us, length us, event | category | flops | bytes accessed | tf_op | source)
XLA Modules:
  0.0 286.1 jit_solution(5724965169102943822)
XLA Ops:
  13.5 7.7 %all-to-all-start = ((bf16[16,176,256]{2,1,0:T(8,128)(2,1)}), bf16[16,176,256]{2,1,0:T(8,128)(2,1)S(1)}, u32[]{:S(2)}, u32[]{:S(2)}) async-start(bf16[16,176,256]{2,1,0:T(8,128)(2,1)} %broadcast_in_dim.27), calls=%async_computation | async-start | bytes 2883584 | tf_op jit(solution)/shard_map/all_to_all | solution.py:63
  28.8 19.3 %all-to-all-done.refs_6_ = bf16[16,176,256]{2,1,0:T(8,128)(2,1)S(1)} async-done(((bf16[16,176,256]{2,1,0:T(8,128)(2,1)}), bf16[16,176,256]{2,1,0:T(8,128)(2,1)S(1)}, u32[]{:S(2)}, u32[]{:S(2)}) %all-to-all-start) | async-done | bytes 1441824 | tf_op jit(solution)/shard_map/all_to_all | solution.py:63
  49.2 6.6 %all-to-all-start.1 = ((bf16[16,112,256]{2,1,0:T(8,128)(2,1)}), bf16[16,112,256]{2,1,0:T(8,128)(2,1)S(1)}, u32[]{:S(2)}, u32[]{:S(2)}) async-start(bf16[16,112,256]{2,1,0:T(8,128)(2,1)} %broadcast_in_dim.28), calls=%async_computation.1 | async-start | bytes 1835008 | tf_op jit(solution)/shard_map/all_to_all | solution.py:63
  57.1 4.6 %shard_map.331 = (bf16[512,1536]{1,0:T(8,128)(2,1)}, bf16[1536,512]{1,0:T(8,128)(2,1)}, bf16[64,1536]{1,0:T(8,128)(2,1)}, bf16[64,1536]{1,0:T(8,128)(2,1)}, bf16[256,1536]{1,0:T(8,128)(2,1)}) custom-call(s32[5]{0:T(128)} %stack.61.refs_0_.ids, bf16[512,1536]{1,0:T(8,128)(2,1)} %bitcast.59, bf16[512,1536]{1,0:T(8,128)(2,1)} %bitcast.53), custom_call_target="tpu_custom_call" | custom-call | flops 1 | bytes 1 | tf_op jit(solution)/shard_map/pallas_call | solution.py:91
  69.5 8.8 %shard_map.332 = (bf16[512,1536]{1,0:T(8,128)(2,1)}, bf16[512,512]{1,0:T(8,128)(2,1)}, bf16[8,256,256]{2,1,0:T(8,128)(2,1)}, f32[512,256]{1,0:T(8,128)}, bf16[1536,512]{1,0:T(8,128)(2,1)}) custom-call(s32[5]{0:T(128)} %stack.61.refs_0_.ids, bf16[512,1536]{1,0:T(8,128)(2,1)} %bitcast.54, f32[1,1536]{1,0:T(1,128)} %broadcast_in_dim.29.refs_2_.refs_9_, ...), custom_call_target="tpu_custom_call" | custom-call | flops 1 | bytes 1 | tf_op jit(solution)/shard_map/pallas_call | solution.py:91
  78.3 16.2 %all-to-all-start.2 = ((bf16[8,256,256]{2,1,0:T(8,128)(2,1)}), bf16[8,256,256]{2,1,0:T(8,128)(2,1)}, u32[]{:S(2)}, u32[]{:S(2)}) async-start(bf16[8,256,256]{2,1,0:T(8,128)(2,1)} %get-tuple-element.91), calls=%async_computation.2 | async-start | bytes 2097152 | tf_op jit(solution)/shard_map/all_to_all | solution.py:63
  99.9 5.6 %shard_map.333 = (bf16[1536,1536]{1,0:T(8,128)(2,1)}, bf16[256,1536]{1,0:T(8,128)(2,1)}) custom-call(s32[5]{0:T(128)} %stack.61.refs_0_.ids, bf16[16,80,256]{2,1,0:T(8,128)(2,1)} %copy-done.26, bf16[16,80,256]{2,1,0:T(8,128)(2,1)} %collective-permute-done.4.refs_2_, bf16[16,80,256]{2,1,0:T(8,128)(2,1)} %collective-permute-done.5.refs_3_, ...), custom_call_target="tpu_custom_call" | custom-call | flops 1 | bytes 1 | tf_op jit(solution)/shard_map/pallas_call | solution.py:91
  105.5 4.2 %all-to-all-done.2.att.refs_1_ = bf16[8,256,256]{2,1,0:T(8,128)(2,1)} async-done(((bf16[8,256,256]{2,1,0:T(8,128)(2,1)}), bf16[8,256,256]{2,1,0:T(8,128)(2,1)}, u32[]{:S(2)}, u32[]{:S(2)}) %all-to-all-start.2) | async-done | bytes 1048608 | tf_op jit(solution)/shard_map/all_to_all | solution.py:63
  109.7 6.2 %shard_map.334 = (f32[64,1536]{1,0:T(8,128)}, bf16[256,1536]{1,0:T(8,128)(2,1)}) custom-call(s32[5]{0:T(128)} %stack.61.refs_0_.ids, bf16[8,256,256]{2,1,0:T(8,128)(2,1)} %all-to-all-done.2.att.refs_1_, bf16[1536,1536]{1,0:T(8,128)(2,1)} %get-tuple-element.92.mixer, bf16[256,1536]{1,0:T(8,128)(2,1)} %get-tuple-element.93.tok, ...), custom_call_target="tpu_custom_call" | custom-call | flops 1 | bytes 1 | tf_op jit(solution)/shard_map/pallas_call | solution.py:636
  119.8 18.4 %shard_map.335 = (bf16[512,1152]{1,0:T(8,128)(2,1)}, bf16[512,1152]{1,0:T(8,128)(2,1)}, bf16[512,1152]{1,0:T(8,128)(2,1)}, bf16[16,3,96,1152]{3,2,1,0:T(8,128)(2,1)}) custom-call(bf16[256,1536]{1,0:T(8,128)(2,1)} %get-tuple-element.94.near, bf16[256,1536]{1,0:T(8,128)(2,1)} %copy-done.30, bf16[512,1536]{1,0:T(8,128)(2,1)} %get-tuple-element.90.refs_8_.back, ...), custom_call_target="tpu_custom_call" | custom-call | flops 1 | bytes 1 | tf_op jit(solution)/shard_map/pallas_call | solution.py:658
  138.3 8.0 %shard_map.338 = (bf16[256,1536]{1,0:T(8,128)(2,1)}, bf16[256,1536]{1,0:T(8,128)(2,1)}) custom-call(bf16[512,1152]{1,0:T(8,128)(2,1)} %get-tuple-element.103.gate_grad, bf16[512,1152]{1,0:T(8,128)(2,1)} %get-tuple-element.104.up_grad, bf16[16,3,96,1152]{3,2,1,0:T(8,128)(2,1)} %bitcast.51), custom_call_target="tpu_custom_call" | custom-call | flops 1 | bytes 1 | tf_op jit(solution)/shard_map/pallas_call | solution.py:671
  153.4 5.2 %shard_map.336 = (bf16[256,1536]{1,0:T(8,128)(2,1)}, bf16[256,1536]{1,0:T(8,128)(2,1)}) custom-call(bf16[512,1152]{1,0:T(8,128)(2,1)} %get-tuple-element.96.act, bf16[16,3,96,1152]{3,2,1,0:T(8,128)(2,1)} %bitcast.52), custom_call_target="tpu_custom_call" | custom-call | flops 1 | bytes 1 | tf_op jit(solution)/shard_map/pallas_call | solution.py:693
  169.8 4.2 %collective-permute-done.22 = bf16[64,1536]{1,0:T(8,128)(2,1)S(1)} collective-permute-done((bf16[64,1536]{1,0:T(8,128)(2,1)S(1)}, bf16[64,1536]{1,0:T(8,128)(2,1)S(1)}, u32[]{:S(2)}, u32[]{:S(2)}) %collective-permute-start.22) | collective-permute-done | bytes 196640 | tf_op jit(solution)/shard_map/ppermute | solution.py:47
  182.9 12.3 %shard_map.341 = (bf16[512,512]{1,0:T(8,128)(2,1)}, bf16[512,384]{1,0:T(8,128)(2,1)}, bf16[512,128]{1,0:T(8,128)(2,1)}, bf16[512,128]{1,0:T(8,128)(2,1)}, bf16[2...) custom-call(s32[5]{0:T(128)} %stack.61.refs_0_.ids, bf16[4,64,1536]{2,1,0:T(8,128)(2,1)} %copy-done.25, ...), custom_call_target="tpu_custom_call" | custom-call | flops 1 | bytes 1 | tf_op jit(solution)/shard_map/pallas_call | solution.py:91
  199.2 3.8 %collective-permute-start.26 = (bf16[512,128]{1,0:T(8,128)(2,1)S(1)}, bf16[512,128]{1,0:T(8,128)(2,1)S(1)}, u32[]{:S(2)}, u32[]{:S(2)}) collective-permute-start(bf16[512,128]{1,0:T(8,128)(2,1)S(1)} %get-tuple-element.125), channel_id=1, source_target_pairs={{0,6},{1,7},{8,14},{9,15},{16,22},{17,23},{24,30},{25,31},{32,38},... | collective-permute-start | bytes 393224 | tf_op jit(solution)/shard_map/ppermute | solution.py:55
  203.7 3.7 %all-to-all-start.3 = ((bf16[8,32,128]{2,1,0:T(8,128)(2,1)}), bf16[8,32,128]{2,1,0:T(8,128)(2,1)S(1)}, u32[]{:S(2)}, u32[]{:S(2)}) async-start(bf16[8,32,128]{2,1,0:T(8,128)(2,1)} %get-tuple-element.128), calls=%async_computation.3 | async-start | bytes 131072 | tf_op jit(solution)/shard_map/all_to_all | solution.py:63
  208.3 3.2 %shard_map.344.refs_7_ = bf16[16,96,192]{2,1,0:T(8,128)(2,1)} custom-call(s32[5]{0:T(128)} %stack.61.refs_0_.ids, bf16[8,256,256]{2,1,0:T(8,128)(2,1)} %all-to-all-done.2.att.refs_1_, bf16[8,256,256]{2,1,0:T(8,128)(2,1)} %copy-done.28, bf16[512,384]{1,0:T(8,128)(2,1)} %get-tuple-element.129.refs_3_, f32[64,1536]{1,0:T(8,128)} %copy-done.1), custom_call_target="tpu_custom_call" | custom-call | flops 1 | bytes 1 | tf_op jit(solution)/shard_map/pallas_call | solution.py:91
  213.0 3.8 %shard_map.345.refs_3_ = bf16[16,104,448]{2,1,0:T(8,128)(2,1)} custom-call(s32[5]{0:T(128)} %stack.61.refs_0_.ids, bf16[512,1536]{1,0:T(8,128)(2,1)} %get-tuple-element.122.refs_1_, bf16[512,512]{1,0:T(8,128)(2,1)} %get-tuple-element.119.refs_5_.refs_2_, bf16[512,128]{1,0:T(8,128)(2,1)} %copy-done.38, bf16[512,128]{1,0:T(8,128)(2,1)} %copy-done.39, ...), custom_call_target="tpu_custom_call" | custom-call | flops 1 | bytes 1 | tf_op jit(solution)/shard_map/pallas_call | solution.py:91
  216.8 6.7 %all-to-all-start.4 = ((bf16[16,104,448]{2,1,0:T(8,128)(2,1)}), bf16[16,104,448]{2,1,0:T(8,128)(2,1)}, u32[]{:S(2)}, u32[]{:S(2)}) async-start(bf16[16,104,448]{2,1,0:T(8,128)(2,1)} %shard_map.345.refs_3_), calls=%async_computation.4 | async-start | bytes 3407872 | tf_op jit(solution)/shard_map/all_to_all | solution.py:63
  231.2 3.8 %collective-permute-done.30.refs_3_ = bf16[64,1536]{1,0:T(8,128)(2,1)S(1)} collective-permute-done((bf16[64,1536]{1,0:T(8,128)(2,1)S(1)}, bf16[64,1536]{1,0:T(8,128)(2,1)S(1)}, u32[]{:S(2)}, u32[]{:S(2)}) %collective-permute-start.30) | collective-permute-done | bytes 196640 | tf_op jit(solution)/shard_map/ppermute | solution.py:47
  235.1 5.1 %collective-permute-done.32.refs_5_ = bf16[64,1536]{1,0:T(8,128)(2,1)S(1)} collective-permute-done((bf16[64,1536]{1,0:T(8,128)(2,1)S(1)}, bf16[64,1536]{1,0:T(8,128)(2,1)S(1)}, u32[]{:S(2)}, u32[]{:S(2)}) %collective-permute-start.32) | collective-permute-done | bytes 196640 | tf_op jit(solution)/shard_map/ppermute | solution.py:47
  248.2 10.3 %all-to-all-start.5 = ((f32[128,1,128]{2,1,0:T(1,128)}), f32[128,1,128]{2,1,0:T(1,128)S(1)}, u32[]{:S(2)}, u32[]{:S(2)}) async-start(f32[128,1,128]{2,1,0:T(1,128)} %get-tuple-element.137), calls=%async_computation.5 | async-start | bytes 131072 | tf_op jit(solution)/shard_map/all_to_all | solution.py:63
  261.0 6.9 %all-to-all-done.5.refs_5_.squares = f32[128,1,128]{2,1,0:T(1,128)S(1)} async-done(((f32[128,1,128]{2,1,0:T(1,128)}), f32[128,1,128]{2,1,0:T(1,128)S(1)}, u32[]{:S(2)}, u32[]{:S(2)}) %all-to-all-start.5) | async-done | bytes 65568 | tf_op jit(solution)/shard_map/all_to_all | solution.py:63
  270.1 6.7 %shard_map.352 = (f32[1,128]{1,0:T(1,128)}, f32[96,256]{1,0:T(8,128)}, f32[96,256]{1,0:T(8,128)}, f32[96,256]{1,0:T(8,128)}, f32[96,192]{1,0:T(8,128)}, /*index=...) custom-call(f32[128,1,128]{2,1,0:T(1,128)} %copy-done.10, ...), custom_call_target="tpu_custom_call" | custom-call | flops 1 | bytes 1 | tf_op jit(solution)/shard_map/pallas_call | solution.py:813
  (220 shorter events, 89.3 us)
Async XLA Ops:
  7.2 111.7 %all-gather.3.cloned.1.call-start = ((), (), s32[]{:S(2)}) async-start(), calls=%async_computation.7 | async-start | bytes 11280384 | tf_op jit(solution)/shard_map/all_gather | solution.py:571
  13.5 34.6 %all-to-all-start = ((bf16[16,176,256]{2,1,0:T(8,128)(2,1)}), bf16[16,176,256]{2,1,0:T(8,128)(2,1)S(1)}, u32[]{:S(2)}, u32[]{:S(2)}) async-start(bf16[16,176,256]{2,1,0:T(8,128)(2,1)} %broadcast_in_dim.27), calls=%async_computation | async-start | bytes 2883584 | tf_op jit(solution)/shard_map/all_to_all | solution.py:63
  49.2 18.5 %all-to-all-start.1 = ((bf16[16,112,256]{2,1,0:T(8,128)(2,1)}), bf16[16,112,256]{2,1,0:T(8,128)(2,1)S(1)}, u32[]{:S(2)}, u32[]{:S(2)}) async-start(bf16[16,112,256]{2,1,0:T(8,128)(2,1)} %broadcast_in_dim.28), calls=%async_computation.1 | async-start | bytes 1835008 | tf_op jit(solution)/shard_map/all_to_all | solution.py:63
  61.7 32.9 %collective-permute-start.6 = (bf16[16,80,256]{2,1,0:T(8,128)(2,1)S(1)}, bf16[16,80,256]{2,1,0:T(8,128)(2,1)S(1)}, u32[]{:S(2)}, u32[]{:S(2)}) collective-permute-start(bf16[16,80,256]{2,1,0:T(8,128)(2,1)S(1)} %slice.135.refs_1_), channel_id=1, source_target_pairs={{0,4},{1,5},{2,6},{3,7},{4,0},{5,1},{6,2},{7,3},{8,12},{9,13},{10,... | collective-permute-start | bytes 1966088 | tf_op jit(solution)/shard_map/ppermute | solution.py:47
  64.8 30.3 %collective-permute-start.4 = (bf16[16,80,256]{2,1,0:T(8,128)(2,1)S(1)}, bf16[16,80,256]{2,1,0:T(8,128)(2,1)}, u32[]{:S(2)}, u32[]{:S(2)}) collective-permute-start(bf16[16,80,256]{2,1,0:T(8,128)(2,1)S(1)} %slice.135.refs_1_), channel_id=1, source_target_pairs={{0,2},{1,3},{2,4},{3,5},{4,6},{5,7},{6,0},{7,1},{8,10},{9,11},{10,... | collective-permute-start | bytes 1966088 | tf_op jit(solution)/shard_map/ppermute | solution.py:47
  65.2 30.0 %collective-permute-start.5 = (bf16[16,80,256]{2,1,0:T(8,128)(2,1)S(1)}, bf16[16,80,256]{2,1,0:T(8,128)(2,1)}, u32[]{:S(2)}, u32[]{:S(2)}) collective-permute-start(bf16[16,80,256]{2,1,0:T(8,128)(2,1)S(1)} %slice.135.refs_1_), channel_id=1, source_target_pairs={{0,6},{1,7},{2,0},{3,1},{4,2},{5,3},{6,4},{7,5},{8,14},{9,15},{10,... | collective-permute-start | bytes 1966088 | tf_op jit(solution)/shard_map/ppermute | solution.py:47
  78.3 31.4 %all-to-all-start.2 = ((bf16[8,256,256]{2,1,0:T(8,128)(2,1)}), bf16[8,256,256]{2,1,0:T(8,128)(2,1)}, u32[]{:S(2)}, u32[]{:S(2)}) async-start(bf16[8,256,256]{2,1,0:T(8,128)(2,1)} %get-tuple-element.91), calls=%async_computation.2 | async-start | bytes 2097152 | tf_op jit(solution)/shard_map/all_to_all | solution.py:63
  94.5 150.9 %reduce-scatter.4.cloned.1.call-start = ((), (), s32[]{:S(2)}) async-start(), calls=%async_computation.8 | async-start | bytes 11280384
  153.4 8.3 %collective-permute-start.19 = (bf16[64,1536]{1,0:T(8,128)(2,1)S(1)}, bf16[64,1536]{1,0:T(8,128)(2,1)S(1)}, u32[]{:S(2)}, u32[]{:S(2)}) collective-permute-start(bf16[64,1536]{1,0:T(8,128)(2,1)S(1)} %get-tuple-element.110), channel_id=1, source_target_pairs={{0,4},{1,5},{2,6},{3,7},{4,0},{5,1},{6,2},{7,3},{8,12},{9,13},{10,... | collective-permute-start | bytes 589832 | tf_op jit(solution)/shard_map/ppermute | solution.py:47
  166.5 10.9 %collective-permute-start.12 = (bf16[256,1536]{1,0:T(8,128)(2,1)}, bf16[256,1536]{1,0:T(8,128)(2,1)S(1)}, u32[]{:S(2)}, u32[]{:S(2)}) collective-permute-start(bf16[256,1536]{1,0:T(8,128)(2,1)} %get-tuple-element.98.refs_8_), channel_id=1, source_target_pairs={{0,1},{1,0},{2,3},{3,2},{4,5},{5,4},{6,7},{7,6},{8,9},{9,8},{10,11... | collective-permute-start | bytes 2359304 | tf_op jit(solution)/shard_map/ppermute | solution.py:59
  177.3 30.1 %collective-permute-start.29 = (bf16[8,256,256]{2,1,0:T(8,128)(2,1)}, bf16[8,256,256]{2,1,0:T(8,128)(2,1)S(1)}, u32[]{:S(2)}, u32[]{:S(2)}) collective-permute-start(bf16[8,256,256]{2,1,0:T(8,128)(2,1)} %all-to-all-done.2.att.refs_1_), channel_id=1, source_target_pairs={{0,1},{1,0},{2,3},{3,2},{4,5},{5,4},{6,7},{7,6},{8,9},{9,8},{10,11... | collective-permute-start | bytes 3145736 | tf_op jit(solution)/shard_map/ppermute | solution.py:59
  178.9 17.0 %collective-permute-start.13 = (bf16[64,1536]{1,0:T(8,128)(2,1)S(1)}, bf16[64,1536]{1,0:T(8,128)(2,1)S(1)}, u32[]{:S(2)}, u32[]{:S(2)}) collective-permute-start(bf16[64,1536]{1,0:T(8,128)(2,1)S(1)} %get-tuple-element.100), channel_id=1, source_target_pairs={{0,2},{1,3},{2,4},{3,5},{4,6},{5,7},{6,0},{7,1},{8,10},{9,11},{10,... | collective-permute-start | bytes 589832 | tf_op jit(solution)/shard_map/ppermute | solution.py:47
  179.1 16.7 %collective-permute-start.14 = (bf16[64,1536]{1,0:T(8,128)(2,1)S(1)}, bf16[64,1536]{1,0:T(8,128)(2,1)S(1)}, u32[]{:S(2)}, u32[]{:S(2)}) collective-permute-start(bf16[64,1536]{1,0:T(8,128)(2,1)S(1)} %get-tuple-element.101), channel_id=1, source_target_pairs={{0,6},{1,7},{2,0},{3,1},{4,2},{5,3},{6,4},{7,5},{8,14},{9,15},{10,... | collective-permute-start | bytes 589832 | tf_op jit(solution)/shard_map/ppermute | solution.py:47
  181.5 14.3 %collective-permute-start.15 = (bf16[64,1536]{1,0:T(8,128)(2,1)S(1)}, bf16[64,1536]{1,0:T(8,128)(2,1)S(1)}, u32[]{:S(2)}, u32[]{:S(2)}) collective-permute-start(bf16[64,1536]{1,0:T(8,128)(2,1)S(1)} %get-tuple-element.102), channel_id=1, source_target_pairs={{0,4},{1,5},{2,6},{3,7},{4,0},{5,1},{6,2},{7,3},{8,12},{9,13},{10,... | collective-permute-start | bytes 589832 | tf_op jit(solution)/shard_map/ppermute | solution.py:47
  198.5 13.7 %collective-permute-start.28 = (bf16[512,256]{1,0:T(8,128)(2,1)S(1)}, bf16[512,256]{1,0:T(8,128)(2,1)S(1)}, u32[]{:S(2)}, u32[]{:S(2)}) collective-permute-start(bf16[512,256]{1,0:T(8,128)(2,1)S(1)} %get-tuple-element.127), channel_id=1, source_target_pairs={{2,6},{3,7},{10,14},{11,15},{18,22},{19,23},{26,30},{27,31},{34,38... | collective-permute-start | bytes 786440 | tf_op jit(solution)/shard_map/ppermute | solution.py:55
  199.2 13.0 %collective-permute-start.26 = (bf16[512,128]{1,0:T(8,128)(2,1)S(1)}, bf16[512,128]{1,0:T(8,128)(2,1)S(1)}, u32[]{:S(2)}, u32[]{:S(2)}) collective-permute-start(bf16[512,128]{1,0:T(8,128)(2,1)S(1)} %get-tuple-element.125), channel_id=1, source_target_pairs={{0,6},{1,7},{8,14},{9,15},{16,22},{17,23},{24,30},{25,31},{32,38},... | collective-permute-start | bytes 393224 | tf_op jit(solution)/shard_map/ppermute | solution.py:55
  203.0 9.2 %collective-permute-start.27 = (bf16[512,128]{1,0:T(8,128)(2,1)S(1)}, bf16[512,128]{1,0:T(8,128)(2,1)S(1)}, u32[]{:S(2)}, u32[]{:S(2)}) collective-permute-start(bf16[512,128]{1,0:T(8,128)(2,1)S(1)} %get-tuple-element.126), channel_id=1, source_target_pairs={{4,6},{5,7},{12,14},{13,15},{20,22},{21,23},{28,30},{29,31},{36,38... | collective-permute-start | bytes 393224 | tf_op jit(solution)/shard_map/ppermute | solution.py:55
  203.7 8.5 %all-to-all-start.3 = ((bf16[8,32,128]{2,1,0:T(8,128)(2,1)}), bf16[8,32,128]{2,1,0:T(8,128)(2,1)S(1)}, u32[]{:S(2)}, u32[]{:S(2)}) async-start(bf16[8,32,128]{2,1,0:T(8,128)(2,1)} %get-tuple-element.128), calls=%async_computation.3 | async-start | bytes 131072 | tf_op jit(solution)/shard_map/all_to_all | solution.py:63
  216.8 28.5 %all-to-all-start.4 = ((bf16[16,104,448]{2,1,0:T(8,128)(2,1)}), bf16[16,104,448]{2,1,0:T(8,128)(2,1)}, u32[]{:S(2)}, u32[]{:S(2)}) async-start(bf16[16,104,448]{2,1,0:T(8,128)(2,1)} %shard_map.345.refs_3_), calls=%async_computation.4 | async-start | bytes 3407872 | tf_op jit(solution)/shard_map/all_to_all | solution.py:63
  230.3 9.9 %collective-permute-start.32 = (bf16[64,1536]{1,0:T(8,128)(2,1)S(1)}, bf16[64,1536]{1,0:T(8,128)(2,1)S(1)}, u32[]{:S(2)}, u32[]{:S(2)}) collective-permute-start(bf16[64,1536]{1,0:T(8,128)(2,1)S(1)} %get-tuple-element.133), channel_id=1, source_target_pairs={{0,4},{1,5},{2,6},{3,7},{4,0},{5,1},{6,2},{7,3},{8,12},{9,13},{10,... | collective-permute-start | bytes 589832 | tf_op jit(solution)/shard_map/ppermute | solution.py:47
  241.2 17.4 %collective-permute-start.33 = (bf16[2,64,1536]{2,1,0:T(8,128)(2,1)S(1)}, bf16[2,64,1536]{2,1,0:T(8,128)(2,1)S(1)}, u32[]{:S(2)}, u32[]{:S(2)}) collective-permute-start(bf16[2,64,1536]{2,1,0:T(8,128)(2,1)S(1)} %shard_map.347.p0.refs_1_), channel_id=1, source_target_pairs={{0,2},{1,3},{2,4},{3,5},{4,6},{5,7},{6,0},{7,1},{8,10},{9,11},{10,... | collective-permute-start | bytes 1179656 | tf_op jit(solution)/shard_map/ppermute | solution.py:47
  241.8 16.8 %collective-permute-start.34 = (bf16[2,64,1536]{2,1,0:T(8,128)(2,1)S(1)}, bf16[2,64,1536]{2,1,0:T(8,128)(2,1)S(1)}, u32[]{:S(2)}, u32[]{:S(2)}) collective-permute-start(bf16[2,64,1536]{2,1,0:T(8,128)(2,1)S(1)} %shard_map.347.p0.refs_1_), channel_id=1, source_target_pairs={{0,6},{1,7},{2,0},{3,1},{4,2},{5,3},{6,4},{7,5},{8,14},{9,15},{10,... | collective-permute-start | bytes 1179656 | tf_op jit(solution)/shard_map/ppermute | solution.py:47
  243.9 14.7 %collective-permute-start.35 = (bf16[2,64,1536]{2,1,0:T(8,128)(2,1)S(1)}, bf16[2,64,1536]{2,1,0:T(8,128)(2,1)S(1)}, u32[]{:S(2)}, u32[]{:S(2)}) collective-permute-start(bf16[2,64,1536]{2,1,0:T(8,128)(2,1)S(1)} %shard_map.347.p0.refs_1_), channel_id=1, source_target_pairs={{0,4},{1,5},{2,6},{3,7},{4,0},{5,1},{6,2},{7,3},{8,12},{9,13},{10,... | collective-permute-start | bytes 1179656 | tf_op jit(solution)/shard_map/ppermute | solution.py:47
  248.2 19.7 %all-to-all-start.5 = ((f32[128,1,128]{2,1,0:T(1,128)}), f32[128,1,128]{2,1,0:T(1,128)S(1)}, u32[]{:S(2)}, u32[]{:S(2)}) async-start(f32[128,1,128]{2,1,0:T(1,128)} %get-tuple-element.137), calls=%async_computation.5 | async-start | bytes 131072 | tf_op jit(solution)/shard_map/all_to_all | solution.py:63
  (62 other events, 392.1 us)
Sparse Core Ops, SparseCore 0:
  10.2 103.7 all-gather.2
  138.4 88.3 reduce-scatter.3

commit v6 on v5

--- a/solution.py
+++ b/solution.py
@@ -397,22 +397,20 @@
     for r in range(4):
         cols = slice(384 * r, 384 * (r + 1))
         part = tn(normed[:, cols], g).astype(bf16)
-        parts[4 * r : 4 * (r + 1), :ROWS, :JC] = part.reshape(4, ROWS, JC)
-    parts[:, :ROWS, JC:] = mixer_parts[...]
+        parts[4 * r : 4 * (r + 1), :ROWS, :] = part.reshape(4, ROWS, JC)
+    parts[:, ROWS : ROWS + 80, :] = mixer_parts[...]
     vec = moved[0].astype(f32)
     for j in range(1, MP):
         vec += moved[j].astype(f32)
     vec = vec[:DP] + vec[DP:]
     high = vec.astype(bf16).astype(f32)
-    rest = jnp.zeros((8, MC), bf16)
     for d in range(DP):
-        parts[d, ROWS:, :HEAD] = jnp.broadcast_to(high[d : d + 1], (8, HEAD)).astype(bf16)
+        parts[d, ROWS + 80 :, :HEAD] = jnp.broadcast_to(high[d : d + 1], (8, HEAD)).astype(bf16)
         low = (vec - high)[d : d + 1]
-        parts[d, ROWS:, HEAD:JC] = jnp.broadcast_to(low, (8, HEAD)).astype(bf16)
-        parts[d, ROWS:, JC:] = rest
-
-
-def weigh_mixer(ids, near, far, low, parts):
+        parts[d, ROWS + 80 :, HEAD:] = jnp.broadcast_to(low, (8, HEAD)).astype(bf16)
+
+
+def weigh_mixer(ids, near, far, low, packed, parts):
     c = ids[4]
 
     def own_columns(half):
@@ -421,7 +419,7 @@
 
     mine, other = own_columns(c), own_columns(1 - c)
     for j in range(KEY_AT):
-        part = (tn(near[j], mine) + tn(far[j], other)).astype(bf16)
+        part = tn(near[j], mine) + tn(far[j], other)
         start = JC * j
         while start < JC * (j + 1):
             stop = min((start // ROWS + 1) * ROWS, JC * (j + 1))
@@ -430,22 +428,40 @@
                 start - JC * j : stop - JC * j
             ]
             start = stop
-
-
-def settle_grads(ids, moved, ff, joint, mixer, vector, squares):
+    for d in range(DP):
+        left, right = parts[d, :, :HEAD], parts[d, :, HEAD:]
+        packed[d, :48, :HEAD] = left[:48].astype(bf16)
+        packed[d, :48, HEAD:] = left[48:].astype(bf16)
+        packed[d, 48:, :HEAD] = jnp.concatenate([right[:32], right[32:64]], 1).astype(bf16)
+        packed[d, 48:, HEAD:] = jnp.concatenate(
+            [right[64:], jnp.zeros((32, JC - MC), f32)], 1
+        ).astype(bf16)
+
+
+def square_sums(ids, ff, sums):
+    total = jnp.zeros((1, FP), f32)
+    for m in range(3):
+        v = ff[m].astype(f32)
+        total += jnp.sum(v * v, 0, keepdims=True)
+    sums[...] = jnp.full(sums.shape, jnp.sum(total), f32)
+
+
+def settle_grads(ids, moved, sums, joint, mixer, vector, squares):
     total = moved[0].astype(f32)
     for d in range(1, DP):
         total += moved[d].astype(f32)
-    joint[...] = total[:ROWS, :JC]
-    mixer[...] = total[:ROWS, JC:]
-    vec = total[ROWS : ROWS + 1, :HEAD] + total[ROWS : ROWS + 1, HEAD:JC]
+    joint[...] = total[:ROWS]
+    left, right = total[ROWS : ROWS + 48], total[ROWS + 48 : ROWS + 80]
+    mixer[:48, :HEAD] = left[:, :HEAD]
+    mixer[48:, :HEAD] = left[:, HEAD:]
+    mixer[:32, HEAD:] = right[:, : MC - HEAD]
+    mixer[32:64, HEAD:] = right[:, MC - HEAD : HEAD]
+    mixer[64:, HEAD:] = right[:, HEAD:MC]
+    vec = total[ROWS + 80 : ROWS + 81, :HEAD] + total[ROWS + 80 : ROWS + 81, HEAD:]
     vector[...] = vec
-    total = total[:ROWS]
+    total = total[: ROWS + 80]
     total = jnp.sum(total * total) + jnp.sum(vec * vec)
-    for m in range(3):
-        v = ff[m].astype(f32)
-        total += jnp.sum(v * v)
-    squares[...] = jnp.full(squares.shape, total, f32)
+    squares[...] = jnp.broadcast_to((sums[...] + total)[None], squares.shape)
 
 
 def update(
@@ -744,19 +760,21 @@
     moved = exchange(chunks, "mp")
     (mixer_parts,) = whole(
         weigh_mixer,
-        [((DP, ROWS, MC), bf16)],
+        [((DP, 80, JC), bf16)],
         [ids, att_near, att_far, hidden_low],
+        scratch=[pltpu.VMEM((DP, ROWS, MC), f32)],
         after=[out_sum],
     )
     (joint_parts,) = whole(
         weigh_joint,
-        [((DP, ROWS + 8, JC + MC), bf16)],
+        [((DP, ROWS + 88, JC), bf16)],
         [ids, normed, heads_grad, left, right, both, moved, mixer_parts],
     )
+    (ff_sums,) = whole(square_sums, [((1, HEAD), f32)], [ids, ff_shard])
     joint_shard, mixer_shard, vector_shard, squares = whole(
         settle_grads,
         [((ROWS, JC), f32), ((ROWS, MC), f32), ((1, HEAD), f32), ((DP * MP, 1, HEAD), f32)],
-        [ids, exchange(joint_parts, "dp"), ff_shard],
+        [ids, exchange(joint_parts, "dp"), ff_sums],
     )
 
     squares = exchange(squares, ("dp", "mp"))
@@ -767,6 +785,7 @@
         [((2, PART, D), bf16)],
         [ids, out_sum] + parts + [hidden_part, tok_part, hidden_grad, gain_first],
         limit=8,
+        after=[ff_sums],
     )
     done_parts = gather(shift_y, done)
     anywhere = pl.BlockSpec(memory_space=pl.ANY)

time: 287 us -> 290 us (1.010)
    unnamed x82 -> x86, local copies, waits for them, and re-layouts: 8.15 us -> 10.8 us
    pallas_call x15 -> x16, Pallas kernels: 47.3 us -> 49.3 us  [whole(): pl.pallas_call(bare, out_shape=[jax.ShapeDtypeStruct(s, d) for s, d in ou...]
  transfers between devices with their start and end apart: 45 -> 45, of which waited for: 20 -> 20; matrix products, arithmetic and copies ran while one was open for 2% -> 2% of each run, Pallas kernels for 26% -> 27%
where the time goes in v6:
time: 290 us; the launch traced here: 289 us
  Pallas kernels  98.6 us (34%)
  starting transfers between devices  95.6 us (33%)
  waiting for transfers between devices  60.8 us (21%)
  local copies, waits for them, and re-layouts  15.4 us (5%)
  between operations  15.4 us (5%)
  other arithmetic  3.28 us (1%)
    all_to_all x6, starting transfers between devices, exchange(): return lax.all_to_all(v, axis, split_axis=0, concat_axis=0, tiled=True)  51.9 us
    pallas_call x16, Pallas kernels, whole(): pl.pallas_call(bare, out_shape=[jax.ShapeDtypeStruct(s, d) for s, d in ou...  49.3 us
    all_to_all x6, waiting for transfers between devices, exchange(): return lax.all_to_all(v, axis, split_axis=0, concat_axis=0, tiled=True)  32 us
    ppermute x21, starting transfers between devices, shift_y(): return lax.ppermute(v, 'mp', [(i, (i + 2 * k) % MP) for i in range(MP)])  25.7 us
    pallas_call x1, Pallas kernels, body(): pl.pallas_call(gated, grid=(pl.cdiv(FP, 256),), out_shape=[jax.ShapeDtype...  18.3 us
    ppermute x21, waiting for transfers between devices, shift_y(): return lax.ppermute(v, 'mp', [(i, (i + 2 * k) % MP) for i in range(MP)])  17.8 us
    ppermute x13, starting transfers between devices, swap_core(): return lax.ppermute(v, 'mp', [(i, i ^ 1) for i in range(MP)])  12.9 us
    ppermute x13, waiting for transfers between devices, swap_core(): return lax.ppermute(v, 'mp', [(i, i ^ 1) for i in range(MP)])  11 us
  transfers between devices with their start and end apart: 45, of which 20 were waited for; matrix products, arithmetic and copies ran while one was open for 2% of the time, Pallas kernels for 27%

profile of v6, /device:TPU:1, one launch (start us, length us, event | category | flops | bytes accessed | tf_op | source)
XLA Modules:
  0.0 289.1 jit_solution(9620171884830587351)
XLA Ops:
  13.5 7.7 %all-to-all-start = ((bf16[16,176,256]{2,1,0:T(8,128)(2,1)}), bf16[16,176,256]{2,1,0:T(8,128)(2,1)S(1)}, u32[]{:S(2)}, u32[]{:S(2)}) async-start(bf16[16,176,256]{2,1,0:T(8,128)(2,1)} %broadcast_in_dim.27), calls=%async_computation | async-start | bytes 2883584 | tf_op jit(solution)/shard_map/all_to_all | solution.py:63
  28.8 19.3 %all-to-all-done.refs_6_ = bf16[16,176,256]{2,1,0:T(8,128)(2,1)S(1)} async-done(((bf16[16,176,256]{2,1,0:T(8,128)(2,1)}), bf16[16,176,256]{2,1,0:T(8,128)(2,1)S(1)}, u32[]{:S(2)}, u32[]{:S(2)}) %all-to-all-start) | async-done | bytes 1441824 | tf_op jit(solution)/shard_map/all_to_all | solution.py:63
  49.2 6.6 %all-to-all-start.1 = ((bf16[16,112,256]{2,1,0:T(8,128)(2,1)}), bf16[16,112,256]{2,1,0:T(8,128)(2,1)S(1)}, u32[]{:S(2)}, u32[]{:S(2)}) async-start(bf16[16,112,256]{2,1,0:T(8,128)(2,1)} %broadcast_in_dim.28), calls=%async_computation.1 | async-start | bytes 1835008 | tf_op jit(solution)/shard_map/all_to_all | solution.py:63
  57.1 4.6 %shard_map.331 = (bf16[512,1536]{1,0:T(8,128)(2,1)}, bf16[1536,512]{1,0:T(8,128)(2,1)}, bf16[64,1536]{1,0:T(8,128)(2,1)}, bf16[64,1536]{1,0:T(8,128)(2,1)}, bf16[256,1536]{1,0:T(8,128)(2,1)}) custom-call(s32[5]{0:T(128)} %stack.61.refs_0_.ids, bf16[512,1536]{1,0:T(8,128)(2,1)} %bitcast.59, bf16[512,1536]{1,0:T(8,128)(2,1)} %bitcast.53), custom_call_target="tpu_custom_call" | custom-call | flops 1 | bytes 1 | tf_op jit(solution)/shard_map/pallas_call | solution.py:91
  69.5 8.8 %shard_map.332 = (bf16[512,1536]{1,0:T(8,128)(2,1)}, bf16[512,512]{1,0:T(8,128)(2,1)}, bf16[8,256,256]{2,1,0:T(8,128)(2,1)}, f32[512,256]{1,0:T(8,128)}, bf16[1536,512]{1,0:T(8,128)(2,1)}) custom-call(s32[5]{0:T(128)} %stack.61.refs_0_.ids, bf16[512,1536]{1,0:T(8,128)(2,1)} %bitcast.54, f32[1,1536]{1,0:T(1,128)} %broadcast_in_dim.29.refs_2_.refs_9_, ...), custom_call_target="tpu_custom_call" | custom-call | flops 1 | bytes 1 | tf_op jit(solution)/shard_map/pallas_call | solution.py:91
  78.3 16.2 %all-to-all-start.2 = ((bf16[8,256,256]{2,1,0:T(8,128)(2,1)}), bf16[8,256,256]{2,1,0:T(8,128)(2,1)S(1)}, u32[]{:S(2)}, u32[]{:S(2)}) async-start(bf16[8,256,256]{2,1,0:T(8,128)(2,1)} %get-tuple-element.91), calls=%async_computation.2 | async-start | bytes 2097152 | tf_op jit(solution)/shard_map/all_to_all | solution.py:63
  99.8 5.6 %shard_map.333 = (bf16[1536,1536]{1,0:T(8,128)(2,1)}, bf16[256,1536]{1,0:T(8,128)(2,1)}) custom-call(s32[5]{0:T(128)} %stack.61.refs_0_.ids, bf16[16,80,256]{2,1,0:T(8,128)(2,1)} %copy-done.30, bf16[16,80,256]{2,1,0:T(8,128)(2,1)} %collective-permute-done.4.refs_2_, bf16[16,80,256]{2,1,0:T(8,128)(2,1)} %collective-permute-done.5.refs_3_, ...), custom_call_target="tpu_custom_call" | custom-call | flops 1 | bytes 1 | tf_op jit(solution)/shard_map/pallas_call | solution.py:91
  105.5 4.1 %all-to-all-done.2.att.refs_1_ = bf16[8,256,256]{2,1,0:T(8,128)(2,1)S(1)} async-done(((bf16[8,256,256]{2,1,0:T(8,128)(2,1)}), bf16[8,256,256]{2,1,0:T(8,128)(2,1)S(1)}, u32[]{:S(2)}, u32[]{:S(2)}) %all-to-all-start.2) | async-done | bytes 1048608 | tf_op jit(solution)/shard_map/all_to_all | solution.py:63
  110.6 6.2 %shard_map.334 = (f32[64,1536]{1,0:T(8,128)}, bf16[256,1536]{1,0:T(8,128)(2,1)}) custom-call(s32[5]{0:T(128)} %stack.61.refs_0_.ids, bf16[8,256,256]{2,1,0:T(8,128)(2,1)} %copy-done.25, bf16[1536,1536]{1,0:T(8,128)(2,1)} %get-tuple-element.92.mixer, bf16[256,1536]{1,0:T(8,128)(2,1)} %get-tuple-element.93.tok, f32[1,1536]{1,0:T(1,128)} %broadcast_in_dim.31.gain.refs_7_), custom_call_target="tpu_custom_call" | custom-call | flops 1 | bytes 1 | tf_op jit(solution)/shard_map/pallas_call | solution.py:652
  120.7 18.3 %shard_map.335 = (bf16[512,1152]{1,0:T(8,128)(2,1)}, bf16[512,1152]{1,0:T(8,128)(2,1)}, bf16[512,1152]{1,0:T(8,128)(2,1)}, bf16[16,3,96,1152]{3,2,1,0:T(8,128)(2,1)}) custom-call(bf16[256,1536]{1,0:T(8,128)(2,1)} %get-tuple-element.94.near, bf16[256,1536]{1,0:T(8,128)(2,1)} %copy-done.33, bf16[512,1536]{1,0:T(8,128)(2,1)} %get-tuple-element.90.refs_8_.back, ...), custom_call_target="tpu_custom_call" | custom-call | flops 1 | bytes 1 | tf_op jit(solution)/shard_map/pallas_call | solution.py:674
  139.0 8.0 %shard_map.338 = (bf16[256,1536]{1,0:T(8,128)(2,1)}, bf16[256,1536]{1,0:T(8,128)(2,1)}) custom-call(bf16[512,1152]{1,0:T(8,128)(2,1)} %get-tuple-element.103.gate_grad, bf16[512,1152]{1,0:T(8,128)(2,1)} %get-tuple-element.104.up_grad, bf16[16,3,96,1152]{3,2,1,0:T(8,128)(2,1)} %bitcast.51), custom_call_target="tpu_custom_call" | custom-call | flops 1 | bytes 1 | tf_op jit(solution)/shard_map/pallas_call | solution.py:687
  154.2 5.2 %shard_map.336 = (bf16[256,1536]{1,0:T(8,128)(2,1)}, bf16[256,1536]{1,0:T(8,128)(2,1)}) custom-call(bf16[512,1152]{1,0:T(8,128)(2,1)} %get-tuple-element.96.act, bf16[16,3,96,1152]{3,2,1,0:T(8,128)(2,1)} %bitcast.52), custom_call_target="tpu_custom_call" | custom-call | flops 1 | bytes 1 | tf_op jit(solution)/shard_map/pallas_call | solution.py:709
  169.9 4.1 %collective-permute-done.22 = bf16[64,1536]{1,0:T(8,128)(2,1)S(1)} collective-permute-done((bf16[64,1536]{1,0:T(8,128)(2,1)S(1)}, bf16[64,1536]{1,0:T(8,128)(2,1)S(1)}, u32[]{:S(2)}, u32[]{:S(2)}) %collective-permute-start.22) | collective-permute-done | bytes 196640 | tf_op jit(solution)/shard_map/ppermute | solution.py:47
  174.2 3.2 %collective-permute-start.23 = (bf16[4,64,1536]{2,1,0:T(8,128)(2,1)S(1)}, bf16[4,64,1536]{2,1,0:T(8,128)(2,1)S(1)}, u32[]{:S(2)}, u32[]{:S(2)}) collective-permute-start(bf16[4,64,1536]{2,1,0:T(8,128)(2,1)S(1)} %pad_maximum_fusion.refs_1_), channel_id=1, source_target_pairs={{0,1},{1,0},{2,3},{3,2},{4,5},{5,4},{6,7},{7,6},{8,9},{9,8},{10,11... | collective-permute-start | bytes 2359304 | tf_op jit(solution)/shard_map/ppermute | solution.py:59
  183.0 12.3 %shard_map.341 = (bf16[512,512]{1,0:T(8,128)(2,1)}, bf16[512,384]{1,0:T(8,128)(2,1)}, bf16[512,128]{1,0:T(8,128)(2,1)}, bf16[512,128]{1,0:T(8,128)(2,1)}, bf16[2...) custom-call(s32[5]{0:T(128)} %stack.61.refs_0_.ids, bf16[4,64,1536]{2,1,0:T(8,128)(2,1)} %copy-done.29, ...), custom_call_target="tpu_custom_call" | custom-call | flops 1 | bytes 1 | tf_op jit(solution)/shard_map/pallas_call | solution.py:91
  199.4 3.8 %collective-permute-start.26 = (bf16[512,128]{1,0:T(8,128)(2,1)S(1)}, bf16[512,128]{1,0:T(8,128)(2,1)S(1)}, u32[]{:S(2)}, u32[]{:S(2)}) collective-permute-start(bf16[512,128]{1,0:T(8,128)(2,1)S(1)} %get-tuple-element.125), channel_id=1, source_target_pairs={{0,6},{1,7},{8,14},{9,15},{16,22},{17,23},{24,30},{25,31},{32,38},... | collective-permute-start | bytes 393224 | tf_op jit(solution)/shard_map/ppermute | solution.py:55
  203.8 3.7 %all-to-all-start.3 = ((bf16[8,32,128]{2,1,0:T(8,128)(2,1)}), bf16[8,32,128]{2,1,0:T(8,128)(2,1)S(1)}, u32[]{:S(2)}, u32[]{:S(2)}) async-start(bf16[8,32,128]{2,1,0:T(8,128)(2,1)} %get-tuple-element.128), calls=%async_computation.3 | async-start | bytes 131072 | tf_op jit(solution)/shard_map/all_to_all | solution.py:63
  207.5 3.3 %shard_map.344.refs_7_ = bf16[16,80,256]{2,1,0:T(8,128)(2,1)} custom-call(s32[5]{0:T(128)} %stack.61.refs_0_.ids, bf16[8,256,256]{2,1,0:T(8,128)(2,1)} %copy-done.25, bf16[8,256,256]{2,1,0:T(8,128)(2,1)} %collective-permute-done.29.refs_2_, bf16[512,384]{1,0:T(8,128)(2,1)} %get-tuple-element.129.refs_3_, f32[64,1536]{1,0:T(8,128)} %copy-done.1), custom_call_target="tpu_custom_call" | custom-call | flops 1 | bytes 1 | tf_op jit(solution)/shard_map/pallas_call | solution.py:91
  213.2 3.6 %shard_map.345.refs_3_ = bf16[16,184,256]{2,1,0:T(8,128)(2,1)} custom-call(s32[5]{0:T(128)} %stack.61.refs_0_.ids, bf16[512,1536]{1,0:T(8,128)(2,1)} %get-tuple-element.122.refs_1_, bf16[512,512]{1,0:T(8,128)(2,1)} %get-tuple-element.119.refs_5_.refs_2_, bf16[512,128]{1,0:T(8,128)(2,1)} %copy-done.40, bf16[512,128]{1,0:T(8,128)(2,1)} %copy-done.41, ...), custom_call_target="tpu_custom_call" | custom-call | flops 1 | bytes 1 | tf_op jit(solution)/shard_map/pallas_call | solution.py:91
  216.8 6.5 %all-to-all-start.4 = ((bf16[16,184,256]{2,1,0:T(8,128)(2,1)}), bf16[16,184,256]{2,1,0:T(8,128)(2,1)}, u32[]{:S(2)}, u32[]{:S(2)}) async-start(bf16[16,184,256]{2,1,0:T(8,128)(2,1)} %shard_map.345.refs_3_), calls=%async_computation.4 | async-start | bytes 3014656 | tf_op jit(solution)/shard_map/all_to_all | solution.py:63
  236.4 5.1 %collective-permute-done.32.refs_5_ = bf16[64,1536]{1,0:T(8,128)(2,1)S(1)} collective-permute-done((bf16[64,1536]{1,0:T(8,128)(2,1)}, bf16[64,1536]{1,0:T(8,128)(2,1)S(1)}, u32[]{:S(2)}, u32[]{:S(2)}) %collective-permute-start.32) | collective-permute-done | bytes 196640 | tf_op jit(solution)/shard_map/ppermute | solution.py:47
  250.2 11.2 %all-to-all-start.5 = ((f32[128,1,128]{2,1,0:T(1,128)}), f32[128,1,128]{2,1,0:T(1,128)S(1)}, u32[]{:S(2)}, u32[]{:S(2)}) async-start(f32[128,1,128]{2,1,0:T(1,128)} %get-tuple-element.137), calls=%async_computation.5 | async-start | bytes 131072 | tf_op jit(solution)/shard_map/all_to_all | solution.py:63
  264.0 6.9 %all-to-all-done.5.refs_5_.squares = f32[128,1,128]{2,1,0:T(1,128)S(1)} async-done(((f32[128,1,128]{2,1,0:T(1,128)}), f32[128,1,128]{2,1,0:T(1,128)S(1)}, u32[]{:S(2)}, u32[]{:S(2)}) %all-to-all-start.5) | async-done | bytes 65568 | tf_op jit(solution)/shard_map/all_to_all | solution.py:63
  273.0 6.7 %shard_map.353 = (f32[1,128]{1,0:T(1,128)}, f32[96,256]{1,0:T(8,128)}, f32[96,256]{1,0:T(8,128)}, f32[96,256]{1,0:T(8,128)}, f32[96,192]{1,0:T(8,128)}, /*index=...) custom-call(f32[128,1,128]{2,1,0:T(1,128)} %copy-done.10, ...), custom_call_target="tpu_custom_call" | custom-call | flops 1 | bytes 1 | tf_op jit(solution)/shard_map/pallas_call | solution.py:832
  (225 shorter events, 92.5 us)
Async XLA Ops:
  7.2 112.6 %all-gather.3.cloned.1.call-start = ((), (), s32[]{:S(2)}) async-start(), calls=%async_computation.7 | async-start | bytes 11280384 | tf_op jit(solution)/shard_map/all_gather | solution.py:587
  13.5 34.6 %all-to-all-start = ((bf16[16,176,256]{2,1,0:T(8,128)(2,1)}), bf16[16,176,256]{2,1,0:T(8,128)(2,1)S(1)}, u32[]{:S(2)}, u32[]{:S(2)}) async-start(bf16[16,176,256]{2,1,0:T(8,128)(2,1)} %broadcast_in_dim.27), calls=%async_computation | async-start | bytes 2883584 | tf_op jit(solution)/shard_map/all_to_all | solution.py:63
  49.2 18.5 %all-to-all-start.1 = ((bf16[16,112,256]{2,1,0:T(8,128)(2,1)}), bf16[16,112,256]{2,1,0:T(8,128)(2,1)S(1)}, u32[]{:S(2)}, u32[]{:S(2)}) async-start(bf16[16,112,256]{2,1,0:T(8,128)(2,1)} %broadcast_in_dim.28), calls=%async_computation.1 | async-start | bytes 1835008 | tf_op jit(solution)/shard_map/all_to_all | solution.py:63
  61.7 32.9 %collective-permute-start.6 = (bf16[16,80,256]{2,1,0:T(8,128)(2,1)S(1)}, bf16[16,80,256]{2,1,0:T(8,128)(2,1)}, u32[]{:S(2)}, u32[]{:S(2)}) collective-permute-start(bf16[16,80,256]{2,1,0:T(8,128)(2,1)S(1)} %slice.135.refs_1_), channel_id=1, source_target_pairs={{0,4},{1,5},{2,6},{3,7},{4,0},{5,1},{6,2},{7,3},{8,12},{9,13},{10,... | collective-permute-start | bytes 1966088 | tf_op jit(solution)/shard_map/ppermute | solution.py:47
  64.8 30.3 %collective-permute-start.4 = (bf16[16,80,256]{2,1,0:T(8,128)(2,1)S(1)}, bf16[16,80,256]{2,1,0:T(8,128)(2,1)}, u32[]{:S(2)}, u32[]{:S(2)}) collective-permute-start(bf16[16,80,256]{2,1,0:T(8,128)(2,1)S(1)} %slice.135.refs_1_), channel_id=1, source_target_pairs={{0,2},{1,3},{2,4},{3,5},{4,6},{5,7},{6,0},{7,1},{8,10},{9,11},{10,... | collective-permute-start | bytes 1966088 | tf_op jit(solution)/shard_map/ppermute | solution.py:47
  65.2 30.0 %collective-permute-start.5 = (bf16[16,80,256]{2,1,0:T(8,128)(2,1)S(1)}, bf16[16,80,256]{2,1,0:T(8,128)(2,1)}, u32[]{:S(2)}, u32[]{:S(2)}) collective-permute-start(bf16[16,80,256]{2,1,0:T(8,128)(2,1)S(1)} %slice.135.refs_1_), channel_id=1, source_target_pairs={{0,6},{1,7},{2,0},{3,1},{4,2},{5,3},{6,4},{7,5},{8,14},{9,15},{10,... | collective-permute-start | bytes 1966088 | tf_op jit(solution)/shard_map/ppermute | solution.py:47
  78.3 31.3 %all-to-all-start.2 = ((bf16[8,256,256]{2,1,0:T(8,128)(2,1)}), bf16[8,256,256]{2,1,0:T(8,128)(2,1)S(1)}, u32[]{:S(2)}, u32[]{:S(2)}) async-start(bf16[8,256,256]{2,1,0:T(8,128)(2,1)} %get-tuple-element.91), calls=%async_computation.2 | async-start | bytes 2097152 | tf_op jit(solution)/shard_map/all_to_all | solution.py:63
  94.5 137.9 %reduce-scatter.4.cloned.1.call-start = ((), (), s32[]{:S(2)}) async-start(), calls=%async_computation.8 | async-start | bytes 11280384
  154.2 8.3 %collective-permute-start.19 = (bf16[64,1536]{1,0:T(8,128)(2,1)S(1)}, bf16[64,1536]{1,0:T(8,128)(2,1)S(1)}, u32[]{:S(2)}, u32[]{:S(2)}) collective-permute-start(bf16[64,1536]{1,0:T(8,128)(2,1)S(1)} %get-tuple-element.110), channel_id=1, source_target_pairs={{0,4},{1,5},{2,6},{3,7},{4,0},{5,1},{6,2},{7,3},{8,12},{9,13},{10,... | collective-permute-start | bytes 589832 | tf_op jit(solution)/shard_map/ppermute | solution.py:47
  166.7 10.8 %collective-permute-start.12 = (bf16[256,1536]{1,0:T(8,128)(2,1)}, bf16[256,1536]{1,0:T(8,128)(2,1)S(1)}, u32[]{:S(2)}, u32[]{:S(2)}) collective-permute-start(bf16[256,1536]{1,0:T(8,128)(2,1)} %get-tuple-element.98.refs_8_), channel_id=1, source_target_pairs={{0,1},{1,0},{2,3},{3,2},{4,5},{5,4},{6,7},{7,6},{8,9},{9,8},{10,11... | collective-permute-start | bytes 2359304 | tf_op jit(solution)/shard_map/ppermute | solution.py:59
  177.4 30.1 %collective-permute-start.29 = (bf16[8,256,256]{2,1,0:T(8,128)(2,1)S(1)}, bf16[8,256,256]{2,1,0:T(8,128)(2,1)}, u32[]{:S(2)}, u32[]{:S(2)}) collective-permute-start(bf16[8,256,256]{2,1,0:T(8,128)(2,1)S(1)} %copy-done.26), channel_id=1, source_target_pairs={{0,1},{1,0},{2,3},{3,2},{4,5},{5,4},{6,7},{7,6},{8,9},{9,8},{10,11... | collective-permute-start | bytes 3145736 | tf_op jit(solution)/shard_map/ppermute | solution.py:59
  179.0 17.0 %collective-permute-start.13 = (bf16[64,1536]{1,0:T(8,128)(2,1)S(1)}, bf16[64,1536]{1,0:T(8,128)(2,1)S(1)}, u32[]{:S(2)}, u32[]{:S(2)}) collective-permute-start(bf16[64,1536]{1,0:T(8,128)(2,1)S(1)} %get-tuple-element.100), channel_id=1, source_target_pairs={{0,2},{1,3},{2,4},{3,5},{4,6},{5,7},{6,0},{7,1},{8,10},{9,11},{10,... | collective-permute-start | bytes 589832 | tf_op jit(solution)/shard_map/ppermute | solution.py:47
  179.3 16.7 %collective-permute-start.14 = (bf16[64,1536]{1,0:T(8,128)(2,1)S(1)}, bf16[64,1536]{1,0:T(8,128)(2,1)S(1)}, u32[]{:S(2)}, u32[]{:S(2)}) collective-permute-start(bf16[64,1536]{1,0:T(8,128)(2,1)S(1)} %get-tuple-element.101), channel_id=1, source_target_pairs={{0,6},{1,7},{2,0},{3,1},{4,2},{5,3},{6,4},{7,5},{8,14},{9,15},{10,... | collective-permute-start | bytes 589832 | tf_op jit(solution)/shard_map/ppermute | solution.py:47
  181.7 14.3 %collective-permute-start.15 = (bf16[64,1536]{1,0:T(8,128)(2,1)S(1)}, bf16[64,1536]{1,0:T(8,128)(2,1)S(1)}, u32[]{:S(2)}, u32[]{:S(2)}) collective-permute-start(bf16[64,1536]{1,0:T(8,128)(2,1)S(1)} %get-tuple-element.102), channel_id=1, source_target_pairs={{0,4},{1,5},{2,6},{3,7},{4,0},{5,1},{6,2},{7,3},{8,12},{9,13},{10,... | collective-permute-start | bytes 589832 | tf_op jit(solution)/shard_map/ppermute | solution.py:47
  198.7 13.7 %collective-permute-start.28 = (bf16[512,256]{1,0:T(8,128)(2,1)S(1)}, bf16[512,256]{1,0:T(8,128)(2,1)S(1)}, u32[]{:S(2)}, u32[]{:S(2)}) collective-permute-start(bf16[512,256]{1,0:T(8,128)(2,1)S(1)} %get-tuple-element.127), channel_id=1, source_target_pairs={{2,6},{3,7},{10,14},{11,15},{18,22},{19,23},{26,30},{27,31},{34,38... | collective-permute-start | bytes 786440 | tf_op jit(solution)/shard_map/ppermute | solution.py:55
  199.4 13.0 %collective-permute-start.26 = (bf16[512,128]{1,0:T(8,128)(2,1)S(1)}, bf16[512,128]{1,0:T(8,128)(2,1)S(1)}, u32[]{:S(2)}, u32[]{:S(2)}) collective-permute-start(bf16[512,128]{1,0:T(8,128)(2,1)S(1)} %get-tuple-element.125), channel_id=1, source_target_pairs={{0,6},{1,7},{8,14},{9,15},{16,22},{17,23},{24,30},{25,31},{32,38},... | collective-permute-start | bytes 393224 | tf_op jit(solution)/shard_map/ppermute | solution.py:55
  203.1 9.2 %collective-permute-start.27 = (bf16[512,128]{1,0:T(8,128)(2,1)S(1)}, bf16[512,128]{1,0:T(8,128)(2,1)S(1)}, u32[]{:S(2)}, u32[]{:S(2)}) collective-permute-start(bf16[512,128]{1,0:T(8,128)(2,1)S(1)} %get-tuple-element.126), channel_id=1, source_target_pairs={{4,6},{5,7},{12,14},{13,15},{20,22},{21,23},{28,30},{29,31},{36,38... | collective-permute-start | bytes 393224 | tf_op jit(solution)/shard_map/ppermute | solution.py:55
  203.8 8.5 %all-to-all-start.3 = ((bf16[8,32,128]{2,1,0:T(8,128)(2,1)}), bf16[8,32,128]{2,1,0:T(8,128)(2,1)S(1)}, u32[]{:S(2)}, u32[]{:S(2)}) async-start(bf16[8,32,128]{2,1,0:T(8,128)(2,1)} %get-tuple-element.128), calls=%async_computation.3 | async-start | bytes 131072 | tf_op jit(solution)/shard_map/all_to_all | solution.py:63
  216.8 31.0 %all-to-all-start.4 = ((bf16[16,184,256]{2,1,0:T(8,128)(2,1)}), bf16[16,184,256]{2,1,0:T(8,128)(2,1)}, u32[]{:S(2)}, u32[]{:S(2)}) async-start(bf16[16,184,256]{2,1,0:T(8,128)(2,1)} %shard_map.345.refs_3_), calls=%async_computation.4 | async-start | bytes 3014656 | tf_op jit(solution)/shard_map/all_to_all | solution.py:63
  231.4 10.1 %collective-permute-start.32 = (bf16[64,1536]{1,0:T(8,128)(2,1)}, bf16[64,1536]{1,0:T(8,128)(2,1)S(1)}, u32[]{:S(2)}, u32[]{:S(2)}) collective-permute-start(bf16[64,1536]{1,0:T(8,128)(2,1)} %get-tuple-element.133), channel_id=1, source_target_pairs={{0,4},{1,5},{2,6},{3,7},{4,0},{5,1},{6,2},{7,3},{8,12},{9,13},{10,... | collective-permute-start | bytes 589832 | tf_op jit(solution)/shard_map/ppermute | solution.py:47
  245.1 16.4 %collective-permute-start.33 = (bf16[2,64,1536]{2,1,0:T(8,128)(2,1)S(1)}, bf16[2,64,1536]{2,1,0:T(8,128)(2,1)S(1)}, u32[]{:S(2)}, u32[]{:S(2)}) collective-permute-start(bf16[2,64,1536]{2,1,0:T(8,128)(2,1)S(1)} %shard_map.348.p0.refs_1_), channel_id=1, source_target_pairs={{0,2},{1,3},{2,4},{3,5},{4,6},{5,7},{6,0},{7,1},{8,10},{9,11},{10,... | collective-permute-start | bytes 1179656 | tf_op jit(solution)/shard_map/ppermute | solution.py:47
  245.7 15.8 %collective-permute-start.34 = (bf16[2,64,1536]{2,1,0:T(8,128)(2,1)S(1)}, bf16[2,64,1536]{2,1,0:T(8,128)(2,1)S(1)}, u32[]{:S(2)}, u32[]{:S(2)}) collective-permute-start(bf16[2,64,1536]{2,1,0:T(8,128)(2,1)S(1)} %shard_map.348.p0.refs_1_), channel_id=1, source_target_pairs={{0,6},{1,7},{2,0},{3,1},{4,2},{5,3},{6,4},{7,5},{8,14},{9,15},{10,... | collective-permute-start | bytes 1179656 | tf_op jit(solution)/shard_map/ppermute | solution.py:47
  247.8 13.8 %collective-permute-start.35 = (bf16[2,64,1536]{2,1,0:T(8,128)(2,1)S(1)}, bf16[2,64,1536]{2,1,0:T(8,128)(2,1)S(1)}, u32[]{:S(2)}, u32[]{:S(2)}) collective-permute-start(bf16[2,64,1536]{2,1,0:T(8,128)(2,1)S(1)} %shard_map.348.p0.refs_1_), channel_id=1, source_target_pairs={{0,4},{1,5},{2,6},{3,7},{4,0},{5,1},{6,2},{7,3},{8,12},{9,13},{10,... | collective-permute-start | bytes 1179656 | tf_op jit(solution)/shard_map/ppermute | solution.py:47
  250.2 20.6 %all-to-all-start.5 = ((f32[128,1,128]{2,1,0:T(1,128)}), f32[128,1,128]{2,1,0:T(1,128)S(1)}, u32[]{:S(2)}, u32[]{:S(2)}) async-start(f32[128,1,128]{2,1,0:T(1,128)} %get-tuple-element.137), calls=%async_computation.5 | async-start | bytes 131072 | tf_op jit(solution)/shard_map/all_to_all | solution.py:63
  (64 other events, 394.2 us)
Sparse Core Ops, SparseCore 0:
  10.2 103.7 all-gather.2
  139.1 88.4 reduce-scatter.3

commit v7 on v6

--- a/solution.py
+++ b/solution.py
@@ -82,7 +82,7 @@
     return lax.dot_general(a, b, (((0,), (0,)), ((), ())), preferred_element_type=f32)
 
 
-def whole(body, outs, args, scratch=(), limit=60, after=()):
+def whole(body, outs, args, scratch=(), limit=60, after=(), loose=()):
     n = len(args)
 
     def bare(*refs):
@@ -91,7 +91,9 @@
     return pl.pallas_call(
         bare,
         out_shape=[jax.ShapeDtypeStruct(s, d) for s, d in outs],
-        in_specs=[SM] + [VM] * (n - 1) + [pl.BlockSpec(memory_space=pl.ANY)] * len(after),
+        in_specs=[SM]
+        + [pl.BlockSpec(memory_space=pl.ANY) if k in loose else VM for k in range(1, n)]
+        + [pl.BlockSpec(memory_space=pl.ANY)] * len(after),
         out_specs=[VM] * len(outs),
         scratch_shapes=list(scratch),
         compiler_params=pltpu.CompilerParams(vmem_limit_bytes=limit * MiB),
@@ -260,10 +262,6 @@
     v = back[...].astype(f32) + norm_back(h, scale, gain[...], g)
     grad[...] = v
     low[...] = v.astype(bf16)
-
-
-def add_parts(ids, own, a1, a2, a3, total):
-    total[...] = summed(own, (a1, a2, a3))
 
 
 def finish(ids, out_sum, own, a1, a2, a3, hidden, tok, grad, gain, done):
@@ -369,16 +367,25 @@
 def back_to_input(
     ids, near_low, far_low, rows_w, heads, lse, cosine, sine, w, tok, second_part,
     grads, window, own_kind, other_kind, near, far, chunks,
-    low, att_grad, key_grad, value_grad, gain_part, vec, blocks,
+    low, att_grad, key_grad, value_grad, gain_part, vec, blocks, w_held, tok_held, sems,
 ):
+    copies = [
+        pltpu.make_async_copy(w, w_held, sems.at[0]),
+        pltpu.make_async_copy(tok, tok_held, sems.at[1]),
+    ]
+    for copy in copies:
+        copy.start()
     attend_back(
         ids, near_low, far_low, rows_w, heads, lse, cosine, sine,
         grads, window, own_kind, other_kind, low, att_grad, key_grad, value_grad,
     )
-    joint_back(ids, grads, w, tok, second_part, near, far, chunks, gain_part, vec, blocks)
-
-
-def group_parts(ids, own, other, both, left, right):
+    for copy in copies:
+        copy.wait()
+    joint_back(ids, grads, w_held, tok_held, second_part, near, far, chunks, gain_part, vec, blocks)
+
+
+def group_parts(ids, own, other, o0, o1, o2, o3, both, left, right, out_sum):
+    out_sum[...] = summed(o0, (o1, o2, o3))
     own_group = lax.div(jnp.minimum(ids[2], KEY_AT - 1), 3)
     partner = ids[2] + 1 - 2 * ids[4]
     other_group = lax.div(jnp.minimum(partner, KEY_AT - 1), 3)
@@ -438,15 +445,7 @@
         ).astype(bf16)
 
 
-def square_sums(ids, ff, sums):
-    total = jnp.zeros((1, FP), f32)
-    for m in range(3):
-        v = ff[m].astype(f32)
-        total += jnp.sum(v * v, 0, keepdims=True)
-    sums[...] = jnp.full(sums.shape, jnp.sum(total), f32)
-
-
-def settle_grads(ids, moved, sums, joint, mixer, vector, squares):
+def settle_grads(ids, moved, ff, joint, mixer, vector, squares):
     total = moved[0].astype(f32)
     for d in range(1, DP):
         total += moved[d].astype(f32)
@@ -461,7 +460,10 @@
     vector[...] = vec
     total = total[: ROWS + 80]
     total = jnp.sum(total * total) + jnp.sum(vec * vec)
-    squares[...] = jnp.broadcast_to((sums[...] + total)[None], squares.shape)
+    for m in range(3):
+        v = ff[m].astype(f32)
+        total += jnp.sum(v * v)
+    squares[...] = jnp.full(squares.shape, total, f32)
 
 
 def update(
@@ -743,18 +745,18 @@
             pltpu.VMEM((1, D), f32),
             pltpu.VMEM((1, DP * MP * 40), f32),
             pltpu.VMEM((DP, MP * 40), f32),
+            pltpu.VMEM((D, 2 * JC), bf16),
+            pltpu.VMEM((T, D), bf16),
+            pltpu.SemaphoreType.DMA((2,)),
         ],
         after=[out_parts[0]],
-    )
-    (out_sum,) = whole(
-        add_parts, [((PART, D), f32)], [ids] + out_parts, limit=8, after=[heads_grad]
-    )
-    both, left, right = whole(
+        loose=(8, 9),
+    )
+    both, left, right, out_sum = whole(
         group_parts,
-        [((T, JC), bf16), ((T, HEAD), bf16), ((T, HEAD), bf16)],
-        [ids, own_kind, swap_core(other_kind)],
+        [((T, JC), bf16), ((T, HEAD), bf16), ((T, HEAD), bf16), ((PART, D), f32)],
+        [ids, own_kind, swap_core(other_kind)] + out_parts,
         limit=8,
-        after=[out_sum],
     )
     left, right, both = to_last_chip(left, 0), to_last_chip(right, 2), to_last_chip(both, 1)
     moved = exchange(chunks, "mp")
@@ -770,11 +772,10 @@
         [((DP, ROWS + 88, JC), bf16)],
         [ids, normed, heads_grad, left, right, both, moved, mixer_parts],
     )
-    (ff_sums,) = whole(square_sums, [((1, HEAD), f32)], [ids, ff_shard])
     joint_shard, mixer_shard, vector_shard, squares = whole(
         settle_grads,
         [((ROWS, JC), f32), ((ROWS, MC), f32), ((1, HEAD), f32), ((DP * MP, 1, HEAD), f32)],
-        [ids, exchange(joint_parts, "dp"), ff_sums],
+        [ids, exchange(joint_parts, "dp"), ff_shard],
     )
 
     squares = exchange(squares, ("dp", "mp"))
@@ -785,7 +786,6 @@
         [((2, PART, D), bf16)],
         [ids, out_sum] + parts + [hidden_part, tok_part, hidden_grad, gain_first],
         limit=8,
-        after=[ff_sums],
     )
     done_parts = gather(shift_y, done)
     anywhere = pl.BlockSpec(memory_space=pl.ANY)

time: 290 us -> 286 us (0.986)
  Pallas kernels: 98.6 us -> 94.9 us
  waiting for transfers between devices: 60.8 us -> 63.7 us
  local copies, waits for them, and re-layouts: 15.4 us -> 12.5 us
    pallas_call x16 -> x14, Pallas kernels: 49.3 us -> 45.5 us  [whole(): pl.pallas_call(bare, out_shape=[jax.ShapeDtypeStruct(s, d) for s, d in ou...]
    unnamed x86 -> x76, local copies, waits for them, and re-layouts: 10.8 us -> 7.82 us
  transfers between devices with their start and end apart: 45 -> 45, of which waited for: 20 -> 20; matrix products, arithmetic and copies ran while one was open for 2% -> 2% of each run, Pallas kernels for 27% -> 26%
where the time goes in v7:
time: 286 us; the launch traced here: 285 us
  starting transfers between devices  95.7 us (33%)
  Pallas kernels  94.9 us (33%)
  waiting for transfers between devices  63.7 us (22%)
  between operations  15.4 us (5%)
  local copies, waits for them, and re-layouts  12.5 us (4%)
  other arithmetic  3.27 us (1%)
    all_to_all x6, starting transfers between devices, exchange(): return lax.all_to_all(v, axis, split_axis=0, concat_axis=0, tiled=True)  52.2 us
    pallas_call x14, Pallas kernels, whole(): pl.pallas_call(bare, out_shape=[jax.ShapeDtypeStruct(s, d) for s, d in ou...  45.5 us
    all_to_all x6, waiting for transfers between devices, exchange(): return lax.all_to_all(v, axis, split_axis=0, concat_axis=0, tiled=True)  32.1 us
    ppermute x21, starting transfers between devices, shift_y(): return lax.ppermute(v, 'mp', [(i, (i + 2 * k) % MP) for i in range(MP)])  25.4 us
    ppermute x21, waiting for transfers between devices, shift_y(): return lax.ppermute(v, 'mp', [(i, (i + 2 * k) % MP) for i in range(MP)])  19.5 us
    pallas_call x1, Pallas kernels, body(): pl.pallas_call(gated, grid=(pl.cdiv(FP, 256),), out_shape=[jax.ShapeDtype...  18.4 us
    ppermute x13, starting transfers between devices, swap_core(): return lax.ppermute(v, 'mp', [(i, i ^ 1) for i in range(MP)])  13 us
    ppermute x13, waiting for transfers between devices, swap_core(): return lax.ppermute(v, 'mp', [(i, i ^ 1) for i in range(MP)])  12.1 us
  transfers between devices with their start and end apart: 45, of which 20 were waited for; matrix products, arithmetic and copies ran while one was open for 2% of the time, Pallas kernels for 26%

profile of v7, /device:TPU:1, one launch (start us, length us, event | category | flops | bytes accessed | tf_op | source)
XLA Modules:
  0.0 285.5 jit_solution(13356861941953363442)
XLA Ops:
  13.5 7.7 %all-to-all-start = ((bf16[16,176,256]{2,1,0:T(8,128)(2,1)}), bf16[16,176,256]{2,1,0:T(8,128)(2,1)S(1)}, u32[]{:S(2)}, u32[]{:S(2)}) async-start(bf16[16,176,256]{2,1,0:T(8,128)(2,1)} %broadcast_in_dim.27), calls=%async_computation | async-start | bytes 2883584 | tf_op jit(solution)/shard_map/all_to_all | solution.py:63
  28.8 19.3 %all-to-all-done.refs_6_ = bf16[16,176,256]{2,1,0:T(8,128)(2,1)S(1)} async-done(((bf16[16,176,256]{2,1,0:T(8,128)(2,1)}), bf16[16,176,256]{2,1,0:T(8,128)(2,1)S(1)}, u32[]{:S(2)}, u32[]{:S(2)}) %all-to-all-start) | async-done | bytes 1441824 | tf_op jit(solution)/shard_map/all_to_all | solution.py:63
  49.2 6.6 %all-to-all-start.1 = ((bf16[16,112,256]{2,1,0:T(8,128)(2,1)}), bf16[16,112,256]{2,1,0:T(8,128)(2,1)S(1)}, u32[]{:S(2)}, u32[]{:S(2)}) async-start(bf16[16,112,256]{2,1,0:T(8,128)(2,1)} %broadcast_in_dim.28), calls=%async_computation.1 | async-start | bytes 1835008 | tf_op jit(solution)/shard_map/all_to_all | solution.py:63
  57.1 4.6 %shard_map.331 = (bf16[512,1536]{1,0:T(8,128)(2,1)}, bf16[1536,512]{1,0:T(8,128)(2,1)}, bf16[64,1536]{1,0:T(8,128)(2,1)}, bf16[64,1536]{1,0:T(8,128)(2,1)}, bf16[256,1536]{1,0:T(8,128)(2,1)}) custom-call(s32[5]{0:T(128)} %stack.61.refs_0_.ids, bf16[512,1536]{1,0:T(8,128)(2,1)} %bitcast.59, bf16[512,1536]{1,0:T(8,128)(2,1)} %bitcast.53), custom_call_target="tpu_custom_call" | custom-call | flops 1 | bytes 1 | tf_op jit(solution)/shard_map/pallas_call | solution.py:91
  69.5 8.9 %shard_map.332 = (bf16[512,1536]{1,0:T(8,128)(2,1)}, bf16[512,512]{1,0:T(8,128)(2,1)}, bf16[8,256,256]{2,1,0:T(8,128)(2,1)}, f32[512,256]{1,0:T(8,128)}, bf16[1536,512]{1,0:T(8,128)(2,1)}) custom-call(s32[5]{0:T(128)} %stack.61.refs_0_.ids, bf16[512,1536]{1,0:T(8,128)(2,1)} %bitcast.54, f32[1,1536]{1,0:T(1,128)} %broadcast_in_dim.29.refs_2_.refs_9_, ...), custom_call_target="tpu_custom_call" | custom-call | flops 1 | bytes 1 | tf_op jit(solution)/shard_map/pallas_call | solution.py:91
  78.4 16.1 %all-to-all-start.2 = ((bf16[8,256,256]{2,1,0:T(8,128)(2,1)}), bf16[8,256,256]{2,1,0:T(8,128)(2,1)S(1)}, u32[]{:S(2)}, u32[]{:S(2)}) async-start(bf16[8,256,256]{2,1,0:T(8,128)(2,1)} %get-tuple-element.92), calls=%async_computation.2 | async-start | bytes 2097152 | tf_op jit(solution)/shard_map/all_to_all | solution.py:63
  99.9 5.6 %shard_map.333 = (bf16[1536,1536]{1,0:T(8,128)(2,1)}, bf16[256,1536]{1,0:T(8,128)(2,1)}) custom-call(s32[5]{0:T(128)} %stack.61.refs_0_.ids, bf16[16,80,256]{2,1,0:T(8,128)(2,1)} %copy-done.25, bf16[16,80,256]{2,1,0:T(8,128)(2,1)} %collective-permute-done.4.refs_2_, bf16[16,80,256]{2,1,0:T(8,128)(2,1)} %collective-permute-done.5.refs_3_, ...), custom_call_target="tpu_custom_call" | custom-call | flops 1 | bytes 1 | tf_op jit(solution)/shard_map/pallas_call | solution.py:91
  105.5 4.1 %all-to-all-done.2.att.refs_1_ = bf16[8,256,256]{2,1,0:T(8,128)(2,1)S(1)} async-done(((bf16[8,256,256]{2,1,0:T(8,128)(2,1)}), bf16[8,256,256]{2,1,0:T(8,128)(2,1)S(1)}, u32[]{:S(2)}, u32[]{:S(2)}) %all-to-all-start.2) | async-done | bytes 1048608 | tf_op jit(solution)/shard_map/all_to_all | solution.py:63
  110.7 6.2 %shard_map.334 = (f32[64,1536]{1,0:T(8,128)}, bf16[256,1536]{1,0:T(8,128)(2,1)}) custom-call(s32[5]{0:T(128)} %stack.61.refs_0_.ids, bf16[8,256,256]{2,1,0:T(8,128)(2,1)} %copy-done.20, bf16[1536,1536]{1,0:T(8,128)(2,1)} %get-tuple-element.93.mixer, bf16[256,1536]{1,0:T(8,128)(2,1)} %get-tuple-element.94.tok, f32[1,1536]{1,0:T(1,128)} %broadcast_in_dim.31.gain.refs_7_), custom_call_target="tpu_custom_call" | custom-call | flops 1 | bytes 1 | tf_op jit(solution)/shard_map/pallas_call | solution.py:654
  120.8 18.4 %shard_map.335 = (bf16[512,1152]{1,0:T(8,128)(2,1)}, bf16[512,1152]{1,0:T(8,128)(2,1)}, bf16[512,1152]{1,0:T(8,128)(2,1)}, bf16[16,3,96,1152]{3,2,1,0:T(8,128)(2,1)}) custom-call(bf16[256,1536]{1,0:T(8,128)(2,1)} %get-tuple-element.95.near, bf16[256,1536]{1,0:T(8,128)(2,1)} %copy-done.28, bf16[512,1536]{1,0:T(8,128)(2,1)} %get-tuple-element.91.refs_8_.back, ...), custom_call_target="tpu_custom_call" | custom-call | flops 1 | bytes 1 | tf_op jit(solution)/shard_map/pallas_call | solution.py:676
  139.2 8.0 %shard_map.336 = (bf16[256,1536]{1,0:T(8,128)(2,1)}, bf16[256,1536]{1,0:T(8,128)(2,1)}) custom-call(bf16[512,1152]{1,0:T(8,128)(2,1)} %get-tuple-element.97.gate_grad, bf16[512,1152]{1,0:T(8,128)(2,1)} %get-tuple-element.98.up_grad, bf16[16,3,96,1152]{3,2,1,0:T(8,128)(2,1)} %bitcast.51), custom_call_target="tpu_custom_call" | custom-call | flops 1 | bytes 1 | tf_op jit(solution)/shard_map/pallas_call | solution.py:689
  154.3 5.2 %shard_map.338 = (bf16[256,1536]{1,0:T(8,128)(2,1)}, bf16[256,1536]{1,0:T(8,128)(2,1)}) custom-call(bf16[512,1152]{1,0:T(8,128)(2,1)} %get-tuple-element.107.act, bf16[16,3,96,1152]{3,2,1,0:T(8,128)(2,1)} %bitcast.52), custom_call_target="tpu_custom_call" | custom-call | flops 1 | bytes 1 | tf_op jit(solution)/shard_map/pallas_call | solution.py:711
  170.0 4.2 %collective-permute-done.18 = bf16[64,1536]{1,0:T(8,128)(2,1)S(1)} collective-permute-done((bf16[64,1536]{1,0:T(8,128)(2,1)S(1)}, bf16[64,1536]{1,0:T(8,128)(2,1)S(1)}, u32[]{:S(2)}, u32[]{:S(2)}) %collective-permute-start.18) | collective-permute-done | bytes 196640 | tf_op jit(solution)/shard_map/ppermute | solution.py:47
  183.1 11.2 %shard_map.341 = (bf16[512,512]{1,0:T(8,128)(2,1)}, bf16[512,384]{1,0:T(8,128)(2,1)}, bf16[512,128]{1,0:T(8,128)(2,1)}, bf16[512,128]{1,0:T(8,128)(2,1)}, bf16[2...) custom-call(s32[5]{0:T(128)} %stack.61.refs_0_.ids, bf16[4,64,1536]{2,1,0:T(8,128)(2,1)} %copy-done.24, ...), custom_call_target="tpu_custom_call" | custom-call | flops 1 | bytes 1 | tf_op jit(solution)/shard_map/pallas_call | solution.py:91
  199.4 3.8 %collective-permute-start.26 = (bf16[512,128]{1,0:T(8,128)(2,1)S(1)}, bf16[512,128]{1,0:T(8,128)(2,1)S(1)}, u32[]{:S(2)}, u32[]{:S(2)}) collective-permute-start(bf16[512,128]{1,0:T(8,128)(2,1)S(1)} %get-tuple-element.127), channel_id=1, source_target_pairs={{0,6},{1,7},{8,14},{9,15},{16,22},{17,23},{24,30},{25,31},{32,38},... | collective-permute-start | bytes 393224 | tf_op jit(solution)/shard_map/ppermute | solution.py:55
  203.9 4.0 %all-to-all-start.3 = ((bf16[8,32,128]{2,1,0:T(8,128)(2,1)}), bf16[8,32,128]{2,1,0:T(8,128)(2,1)S(1)}, u32[]{:S(2)}, u32[]{:S(2)}) async-start(bf16[8,32,128]{2,1,0:T(8,128)(2,1)} %get-tuple-element.130), calls=%async_computation.3 | async-start | bytes 131072 | tf_op jit(solution)/shard_map/all_to_all | solution.py:63
  207.9 3.3 %shard_map.343.refs_7_ = bf16[16,80,256]{2,1,0:T(8,128)(2,1)} custom-call(s32[5]{0:T(128)} %stack.61.refs_0_.ids, bf16[8,256,256]{2,1,0:T(8,128)(2,1)} %copy-done.20, bf16[8,256,256]{2,1,0:T(8,128)(2,1)} %collective-permute-done.29.refs_2_, bf16[512,384]{1,0:T(8,128)(2,1)} %get-tuple-element.131.refs_3_, f32[64,1536]{1,0:T(8,128)} %copy-done.4), custom_call_target="tpu_custom_call" | custom-call | flops 1 | bytes 1 | tf_op jit(solution)/shard_map/pallas_call | solution.py:91
  213.6 3.6 %shard_map.344.refs_3_ = bf16[16,184,256]{2,1,0:T(8,128)(2,1)} custom-call(s32[5]{0:T(128)} %stack.61.refs_0_.ids, bf16[512,1536]{1,0:T(8,128)(2,1)} %get-tuple-element.125.refs_1_, bf16[512,512]{1,0:T(8,128)(2,1)} %get-tuple-element.126.refs_2_, bf16[512,128]{1,0:T(8,128)(2,1)} %copy-done.35, bf16[512,128]{1,0:T(8,128)(2,1)} %copy-done.36, ...), custom_call_target="tpu_custom_call" | custom-call | flops 1 | bytes 1 | tf_op jit(solution)/shard_map/pallas_call | solution.py:91
  217.2 6.5 %all-to-all-start.4 = ((bf16[16,184,256]{2,1,0:T(8,128)(2,1)}), bf16[16,184,256]{2,1,0:T(8,128)(2,1)}, u32[]{:S(2)}, u32[]{:S(2)}) async-start(bf16[16,184,256]{2,1,0:T(8,128)(2,1)} %shard_map.344.refs_3_), calls=%async_computation.4 | async-start | bytes 3014656 | tf_op jit(solution)/shard_map/all_to_all | solution.py:63
  231.2 4.1 %collective-permute-done.30.refs_3_ = bf16[64,1536]{1,0:T(8,128)(2,1)S(1)} collective-permute-done((bf16[64,1536]{1,0:T(8,128)(2,1)S(1)}, bf16[64,1536]{1,0:T(8,128)(2,1)S(1)}, u32[]{:S(2)}, u32[]{:S(2)}) %collective-permute-start.30) | collective-permute-done | bytes 196640 | tf_op jit(solution)/shard_map/ppermute | solution.py:47
  235.3 4.8 %collective-permute-done.32.refs_5_ = bf16[64,1536]{1,0:T(8,128)(2,1)S(1)} collective-permute-done((bf16[64,1536]{1,0:T(8,128)(2,1)S(1)}, bf16[64,1536]{1,0:T(8,128)(2,1)S(1)}, u32[]{:S(2)}, u32[]{:S(2)}) %collective-permute-start.32) | collective-permute-done | bytes 196640 | tf_op jit(solution)/shard_map/ppermute | solution.py:47
  246.6 11.3 %all-to-all-start.5 = ((f32[128,1,128]{2,1,0:T(1,128)}), f32[128,1,128]{2,1,0:T(1,128)S(1)}, u32[]{:S(2)}, u32[]{:S(2)}) async-start(f32[128,1,128]{2,1,0:T(1,128)} %get-tuple-element.139), calls=%async_computation.5 | async-start | bytes 131072 | tf_op jit(solution)/shard_map/all_to_all | solution.py:63
  260.4 6.9 %all-to-all-done.5.refs_5_.squares = f32[128,1,128]{2,1,0:T(1,128)S(1)} async-done(((f32[128,1,128]{2,1,0:T(1,128)}), f32[128,1,128]{2,1,0:T(1,128)S(1)}, u32[]{:S(2)}, u32[]{:S(2)}) %all-to-all-start.5) | async-done | bytes 65568 | tf_op jit(solution)/shard_map/all_to_all | solution.py:63
  269.5 6.7 %shard_map.351 = (f32[1,128]{1,0:T(1,128)}, f32[96,256]{1,0:T(8,128)}, f32[96,256]{1,0:T(8,128)}, f32[96,256]{1,0:T(8,128)}, f32[96,192]{1,0:T(8,128)}, /*index=...) custom-call(f32[128,1,128]{2,1,0:T(1,128)} %copy-done.9, ...), custom_call_target="tpu_custom_call" | custom-call | flops 1 | bytes 1 | tf_op jit(solution)/shard_map/pallas_call | solution.py:832
  (213 shorter events, 88.8 us)
Async XLA Ops:
  7.2 112.7 %all-gather.3.cloned.1.call-start = ((), (), s32[]{:S(2)}) async-start(), calls=%async_computation.7 | async-start | bytes 11280384 | tf_op jit(solution)/shard_map/all_gather | solution.py:589
  13.5 34.6 %all-to-all-start = ((bf16[16,176,256]{2,1,0:T(8,128)(2,1)}), bf16[16,176,256]{2,1,0:T(8,128)(2,1)S(1)}, u32[]{:S(2)}, u32[]{:S(2)}) async-start(bf16[16,176,256]{2,1,0:T(8,128)(2,1)} %broadcast_in_dim.27), calls=%async_computation | async-start | bytes 2883584 | tf_op jit(solution)/shard_map/all_to_all | solution.py:63
  49.2 18.5 %all-to-all-start.1 = ((bf16[16,112,256]{2,1,0:T(8,128)(2,1)}), bf16[16,112,256]{2,1,0:T(8,128)(2,1)S(1)}, u32[]{:S(2)}, u32[]{:S(2)}) async-start(bf16[16,112,256]{2,1,0:T(8,128)(2,1)} %broadcast_in_dim.28), calls=%async_computation.1 | async-start | bytes 1835008 | tf_op jit(solution)/shard_map/all_to_all | solution.py:63
  61.7 32.9 %collective-permute-start.6 = (bf16[16,80,256]{2,1,0:T(8,128)(2,1)S(1)}, bf16[16,80,256]{2,1,0:T(8,128)(2,1)}, u32[]{:S(2)}, u32[]{:S(2)}) collective-permute-start(bf16[16,80,256]{2,1,0:T(8,128)(2,1)S(1)} %slice.135.refs_1_), channel_id=1, source_target_pairs={{0,4},{1,5},{2,6},{3,7},{4,0},{5,1},{6,2},{7,3},{8,12},{9,13},{10,... | collective-permute-start | bytes 1966088 | tf_op jit(solution)/shard_map/ppermute | solution.py:47
  64.8 30.3 %collective-permute-start.4 = (bf16[16,80,256]{2,1,0:T(8,128)(2,1)S(1)}, bf16[16,80,256]{2,1,0:T(8,128)(2,1)}, u32[]{:S(2)}, u32[]{:S(2)}) collective-permute-start(bf16[16,80,256]{2,1,0:T(8,128)(2,1)S(1)} %slice.135.refs_1_), channel_id=1, source_target_pairs={{0,2},{1,3},{2,4},{3,5},{4,6},{5,7},{6,0},{7,1},{8,10},{9,11},{10,... | collective-permute-start | bytes 1966088 | tf_op jit(solution)/shard_map/ppermute | solution.py:47
  65.2 30.0 %collective-permute-start.5 = (bf16[16,80,256]{2,1,0:T(8,128)(2,1)S(1)}, bf16[16,80,256]{2,1,0:T(8,128)(2,1)}, u32[]{:S(2)}, u32[]{:S(2)}) collective-permute-start(bf16[16,80,256]{2,1,0:T(8,128)(2,1)S(1)} %slice.135.refs_1_), channel_id=1, source_target_pairs={{0,6},{1,7},{2,0},{3,1},{4,2},{5,3},{6,4},{7,5},{8,14},{9,15},{10,... | collective-permute-start | bytes 1966088 | tf_op jit(solution)/shard_map/ppermute | solution.py:47
  78.4 31.2 %all-to-all-start.2 = ((bf16[8,256,256]{2,1,0:T(8,128)(2,1)}), bf16[8,256,256]{2,1,0:T(8,128)(2,1)S(1)}, u32[]{:S(2)}, u32[]{:S(2)}) async-start(bf16[8,256,256]{2,1,0:T(8,128)(2,1)} %get-tuple-element.92), calls=%async_computation.2 | async-start | bytes 2097152 | tf_op jit(solution)/shard_map/all_to_all | solution.py:63
  94.5 149.3 %reduce-scatter.4.cloned.1.call-start = ((), (), s32[]{:S(2)}) async-start(), calls=%async_computation.8 | async-start | bytes 11280384
  154.3 8.3 %collective-permute-start.15 = (bf16[64,1536]{1,0:T(8,128)(2,1)S(1)}, bf16[64,1536]{1,0:T(8,128)(2,1)S(1)}, u32[]{:S(2)}, u32[]{:S(2)}) collective-permute-start(bf16[64,1536]{1,0:T(8,128)(2,1)S(1)} %get-tuple-element.104), channel_id=1, source_target_pairs={{0,4},{1,5},{2,6},{3,7},{4,0},{5,1},{6,2},{7,3},{8,12},{9,13},{10,... | collective-permute-start | bytes 589832 | tf_op jit(solution)/shard_map/ppermute | solution.py:47
  166.8 10.8 %collective-permute-start.20 = (bf16[256,1536]{1,0:T(8,128)(2,1)}, bf16[256,1536]{1,0:T(8,128)(2,1)S(1)}, u32[]{:S(2)}, u32[]{:S(2)}) collective-permute-start(bf16[256,1536]{1,0:T(8,128)(2,1)} %get-tuple-element.108.refs_8_), channel_id=1, source_target_pairs={{0,1},{1,0},{2,3},{3,2},{4,5},{5,4},{6,7},{7,6},{8,9},{9,8},{10,11... | collective-permute-start | bytes 2359304 | tf_op jit(solution)/shard_map/ppermute | solution.py:59
  177.5 30.4 %collective-permute-start.29 = (bf16[8,256,256]{2,1,0:T(8,128)(2,1)S(1)}, bf16[8,256,256]{2,1,0:T(8,128)(2,1)}, u32[]{:S(2)}, u32[]{:S(2)}) collective-permute-start(bf16[8,256,256]{2,1,0:T(8,128)(2,1)S(1)} %copy-done.21), channel_id=1, source_target_pairs={{0,1},{1,0},{2,3},{3,2},{4,5},{5,4},{6,7},{7,6},{8,9},{9,8},{10,11... | collective-permute-start | bytes 3145736 | tf_op jit(solution)/shard_map/ppermute | solution.py:59
  179.1 16.0 %collective-permute-start.22 = (bf16[64,1536]{1,0:T(8,128)(2,1)S(1)}, bf16[64,1536]{1,0:T(8,128)(2,1)S(1)}, u32[]{:S(2)}, u32[]{:S(2)}) collective-permute-start(bf16[64,1536]{1,0:T(8,128)(2,1)S(1)} %get-tuple-element.119), channel_id=1, source_target_pairs={{0,2},{1,3},{2,4},{3,5},{4,6},{5,7},{6,0},{7,1},{8,10},{9,11},{10,... | collective-permute-start | bytes 589832 | tf_op jit(solution)/shard_map/ppermute | solution.py:47
  179.4 15.8 %collective-permute-start.23 = (bf16[64,1536]{1,0:T(8,128)(2,1)S(1)}, bf16[64,1536]{1,0:T(8,128)(2,1)S(1)}, u32[]{:S(2)}, u32[]{:S(2)}) collective-permute-start(bf16[64,1536]{1,0:T(8,128)(2,1)S(1)} %get-tuple-element.120), channel_id=1, source_target_pairs={{0,6},{1,7},{2,0},{3,1},{4,2},{5,3},{6,4},{7,5},{8,14},{9,15},{10,... | collective-permute-start | bytes 589832 | tf_op jit(solution)/shard_map/ppermute | solution.py:47
  181.8 13.4 %collective-permute-start.24 = (bf16[64,1536]{1,0:T(8,128)(2,1)S(1)}, bf16[64,1536]{1,0:T(8,128)(2,1)S(1)}, u32[]{:S(2)}, u32[]{:S(2)}) collective-permute-start(bf16[64,1536]{1,0:T(8,128)(2,1)S(1)} %get-tuple-element.121), channel_id=1, source_target_pairs={{0,4},{1,5},{2,6},{3,7},{4,0},{5,1},{6,2},{7,3},{8,12},{9,13},{10,... | collective-permute-start | bytes 589832 | tf_op jit(solution)/shard_map/ppermute | solution.py:47
  198.7 14.1 %collective-permute-start.28 = (bf16[512,256]{1,0:T(8,128)(2,1)S(1)}, bf16[512,256]{1,0:T(8,128)(2,1)S(1)}, u32[]{:S(2)}, u32[]{:S(2)}) collective-permute-start(bf16[512,256]{1,0:T(8,128)(2,1)S(1)} %get-tuple-element.129), channel_id=1, source_target_pairs={{2,6},{3,7},{10,14},{11,15},{18,22},{19,23},{26,30},{27,31},{34,38... | collective-permute-start | bytes 786440 | tf_op jit(solution)/shard_map/ppermute | solution.py:55
  199.4 13.4 %collective-permute-start.26 = (bf16[512,128]{1,0:T(8,128)(2,1)S(1)}, bf16[512,128]{1,0:T(8,128)(2,1)S(1)}, u32[]{:S(2)}, u32[]{:S(2)}) collective-permute-start(bf16[512,128]{1,0:T(8,128)(2,1)S(1)} %get-tuple-element.127), channel_id=1, source_target_pairs={{0,6},{1,7},{8,14},{9,15},{16,22},{17,23},{24,30},{25,31},{32,38},... | collective-permute-start | bytes 393224 | tf_op jit(solution)/shard_map/ppermute | solution.py:55
  203.2 9.5 %collective-permute-start.27 = (bf16[512,128]{1,0:T(8,128)(2,1)S(1)}, bf16[512,128]{1,0:T(8,128)(2,1)S(1)}, u32[]{:S(2)}, u32[]{:S(2)}) collective-permute-start(bf16[512,128]{1,0:T(8,128)(2,1)S(1)} %get-tuple-element.128), channel_id=1, source_target_pairs={{4,6},{5,7},{12,14},{13,15},{20,22},{21,23},{28,30},{29,31},{36,38... | collective-permute-start | bytes 393224 | tf_op jit(solution)/shard_map/ppermute | solution.py:55
  203.9 8.9 %all-to-all-start.3 = ((bf16[8,32,128]{2,1,0:T(8,128)(2,1)}), bf16[8,32,128]{2,1,0:T(8,128)(2,1)S(1)}, u32[]{:S(2)}, u32[]{:S(2)}) async-start(bf16[8,32,128]{2,1,0:T(8,128)(2,1)} %get-tuple-element.130), calls=%async_computation.3 | async-start | bytes 131072 | tf_op jit(solution)/shard_map/all_to_all | solution.py:63
  217.2 26.6 %all-to-all-start.4 = ((bf16[16,184,256]{2,1,0:T(8,128)(2,1)}), bf16[16,184,256]{2,1,0:T(8,128)(2,1)}, u32[]{:S(2)}, u32[]{:S(2)}) async-start(bf16[16,184,256]{2,1,0:T(8,128)(2,1)} %shard_map.344.refs_3_), calls=%async_computation.4 | async-start | bytes 3014656 | tf_op jit(solution)/shard_map/all_to_all | solution.py:63
  230.6 9.6 %collective-permute-start.32 = (bf16[64,1536]{1,0:T(8,128)(2,1)S(1)}, bf16[64,1536]{1,0:T(8,128)(2,1)S(1)}, u32[]{:S(2)}, u32[]{:S(2)}) collective-permute-start(bf16[64,1536]{1,0:T(8,128)(2,1)S(1)} %get-tuple-element.135), channel_id=1, source_target_pairs={{0,4},{1,5},{2,6},{3,7},{4,0},{5,1},{6,2},{7,3},{8,12},{9,13},{10,... | collective-permute-start | bytes 589832 | tf_op jit(solution)/shard_map/ppermute | solution.py:47
  241.1 16.8 %collective-permute-start.33 = (bf16[2,64,1536]{2,1,0:T(8,128)(2,1)S(1)}, bf16[2,64,1536]{2,1,0:T(8,128)(2,1)S(1)}, u32[]{:S(2)}, u32[]{:S(2)}) collective-permute-start(bf16[2,64,1536]{2,1,0:T(8,128)(2,1)S(1)} %shard_map.346.p0.refs_1_), channel_id=1, source_target_pairs={{0,2},{1,3},{2,4},{3,5},{4,6},{5,7},{6,0},{7,1},{8,10},{9,11},{10,... | collective-permute-start | bytes 1179656 | tf_op jit(solution)/shard_map/ppermute | solution.py:47
  241.6 16.3 %collective-permute-start.34 = (bf16[2,64,1536]{2,1,0:T(8,128)(2,1)S(1)}, bf16[2,64,1536]{2,1,0:T(8,128)(2,1)S(1)}, u32[]{:S(2)}, u32[]{:S(2)}) collective-permute-start(bf16[2,64,1536]{2,1,0:T(8,128)(2,1)S(1)} %shard_map.346.p0.refs_1_), channel_id=1, source_target_pairs={{0,6},{1,7},{2,0},{3,1},{4,2},{5,3},{6,4},{7,5},{8,14},{9,15},{10,... | collective-permute-start | bytes 1179656 | tf_op jit(solution)/shard_map/ppermute | solution.py:47
  243.8 14.1 %collective-permute-start.35 = (bf16[2,64,1536]{2,1,0:T(8,128)(2,1)S(1)}, bf16[2,64,1536]{2,1,0:T(8,128)(2,1)S(1)}, u32[]{:S(2)}, u32[]{:S(2)}) collective-permute-start(bf16[2,64,1536]{2,1,0:T(8,128)(2,1)S(1)} %shard_map.346.p0.refs_1_), channel_id=1, source_target_pairs={{0,4},{1,5},{2,6},{3,7},{4,0},{5,1},{6,2},{7,3},{8,12},{9,13},{10,... | collective-permute-start | bytes 1179656 | tf_op jit(solution)/shard_map/ppermute | solution.py:47
  246.6 20.7 %all-to-all-start.5 = ((f32[128,1,128]{2,1,0:T(1,128)}), f32[128,1,128]{2,1,0:T(1,128)S(1)}, u32[]{:S(2)}, u32[]{:S(2)}) async-start(f32[128,1,128]{2,1,0:T(1,128)} %get-tuple-element.139), calls=%async_computation.5 | async-start | bytes 131072 | tf_op jit(solution)/shard_map/all_to_all | solution.py:63
  (59 other events, 384.2 us)
Sparse Core Ops, SparseCore 0:
  10.2 103.7 all-gather.2
  139.3 88.2 reduce-scatter.3

commit v8 on v7

--- a/solution.py
+++ b/solution.py
@@ -29,6 +29,7 @@
 FP = 1152
 DP = 16
 MP = 8
+VEC = 5120
 ROWS = D // DP
 JC = 256
 MC = 192
@@ -126,20 +127,38 @@
 
 
 def attend(
-    ids, tok, gain, bias, cosine, sine, query_w, pair_w,
-    normed, heads, out, lse, w,
+    ids, tok, cosine, sine, query_w, pair_w,
+    normed, heads, out, lse, w, vec,
 ):
+    for d in range(DP):
+        rows = pair_w[d, ROWS:, :].astype(f32)
+        pieces = []
+        for y in range(4):
+            v = rows[3 * y : 3 * y + 1] + rows[3 * y + 1 : 3 * y + 2] + rows[3 * y + 2 : 3 * y + 3]
+            pieces += [v[:, :40], v[:, HEAD : HEAD + 40]]
+        vec[:, 320 * d : 320 * (d + 1)] = jnp.concatenate(pieces, 1)
+    key_start = 2 * D + JC * KEY_AT + HEAD * lax.div(jnp.minimum(ids[2], KEY_AT - 1), 3)
+    bias = jnp.concatenate(
+        [
+            vec[:, at(2 * D + JC * ids[2], JC, JC)],
+            vec[:, at(key_start, HEAD, HEAD)],
+            vec[:, at(key_start + JC, HEAD, HEAD)],
+        ],
+        1,
+    )
     w[:, :JC] = query_w[:, :ROWS, :].reshape(D, JC)
     w[:, JC:] = pair_w[:, :ROWS, :].reshape(D, JC)
+
+    gain = vec[:, :D]
 
     @pl.loop(0, T // 128)
     def _(i):
         rows = at(i * 128, 128, 128)
         x = tok[rows, :].astype(f32)
         s = lax.rsqrt(jnp.mean(x * x, -1, keepdims=True) + EPS_NORM)
-        n = (x * s * gain[...]).astype(bf16)
+        n = (x * s * gain).astype(bf16)
         normed[rows, :] = n
-        j = nn(n, w[...]) + bias[...]
+        j = nn(n, w[...]) + bias
         for h in range(4):
             cols = slice(HEAD * h, HEAD * (h + 1))
             u = j[:, cols]
@@ -179,7 +198,7 @@
     rows_w[...] = mixer[at(JC * jnp.minimum(ids[2], KEY_AT - 1), JC, JC), :]
 
 
-def mix(ids, att, mixer, tok, gain, hidden_part, normed, hidden, side):
+def mix(ids, att, mixer, tok, vec, hidden_part, normed, hidden, side):
     i = pl.program_id(0)
 
     @pl.when(i == 0)
@@ -196,7 +215,7 @@
         for r in range(0, HALF, 64):
             v = hidden[r : r + 64, :]
             s = lax.rsqrt(jnp.mean(v * v, -1, keepdims=True) + EPS_NORM)
-            normed[r : r + 64, :] = (v * s * gain[...]).astype(bf16)
+            normed[r : r + 64, :] = (v * s * vec[:, D : 2 * D]).astype(bf16)
 
 
 def gated(near, far, back, back_t, w, act, gate_grad, up_grad, grads, near_t):
@@ -611,17 +630,6 @@
     vec = lax.dynamic_slice_in_dim(jnp.concatenate([vec, vec]), (4 - y) % 4, 4, 0)
     sent = jnp.concatenate([pair, vec.reshape(12, JC), query_w[0, :4]], 0)
     pair_w = exchange(jnp.broadcast_to(sent, (DP,) + sent.shape), "dp")
-    vec = pair_w[:, ROWS : ROWS + 12].astype(f32).reshape(DP, 4, 3, 2, HEAD)[..., :40]
-    vec = vec[:, :, 0] + vec[:, :, 1] + vec[:, :, 2]
-    vec = vec.reshape(-1)
-
-    gain_first, gain_second = vec[None, :D], vec[None, D : 2 * D]
-    key_start = JC * KEY_AT + HEAD * (jnp.minimum(mp, KEY_AT - 1) // 3)
-    starts = ((JC * mp, JC), (key_start, HEAD), (key_start + JC, HEAD))
-    bias = jnp.concatenate(
-        [lax.dynamic_slice_in_dim(vec, 2 * D + start, size, 0) for start, size in starts]
-    )[None]
-
     cosine, sine = tables()
     back, back_t, back_part, tok_part, tok_half = whole(
         prepare,
@@ -631,15 +639,16 @@
         ],
         [ids, cotangent[0], tok],
     )
-    normed, heads, att_sent, lse, joint_w = whole(
+    normed, heads, att_sent, lse, joint_w, vec = whole(
         attend,
         [
             ((T, D), bf16), ((T, 2 * JC), bf16), ((MP, HALF, JC), bf16),
-            ((T, JC), f32), ((D, 2 * JC), bf16),
+            ((T, JC), f32), ((D, 2 * JC), bf16), ((1, VEC), f32),
         ],
-        [ids, tok, gain_first, bias, cosine, sine, query_w, pair_w],
+        [ids, tok, cosine, sine, query_w, pair_w],
         after=[back],
     )
+    gain_first, gain_second = vec[:, :D], vec[:, D : 2 * D]
     att_near = exchange(att_sent, "mp")
     att_far = swap_core(att_near)
     mixer_near = gather(shift_y, query_w[:, ROWS:])
@@ -660,13 +669,13 @@
             fixed((MP, HALF, JC)),
             pl.BlockSpec((D, 384), lambda i: (0, i)),
             pl.BlockSpec((HALF, 384), lambda i: (0, i)),
-            fixed((1, D)),
+            fixed((1, VEC)),
         ],
         out_specs=[fixed((PART, D)), fixed((HALF, D))],
         scratch_shapes=[pltpu.VMEM((HALF, D), f32), pltpu.VMEM((HALF, D), bf16)],
         compiler_params=pltpu.CompilerParams(vmem_limit_bytes=60 * MiB),
         cost_estimate=SMALL,
-    )(ids, att_near, mixer, tok_half, gain_second)
+    )(ids, att_near, mixer, tok_half, vec)
     normed_far = swap_core(normed_near)
 
     def columns(n):

time: 286 us -> 286 us (level)
    unnamed x76 -> x74, local copies, waits for them, and re-layouts: 7.82 us -> 8.77 us
  transfers between devices with their start and end apart: 45 -> 45, of which waited for: 20 -> 20; matrix products, arithmetic and copies ran while one was open for 2% -> 1% of each run, Pallas kernels for 26% -> 26%
where the time goes in v8:
time: 286 us; the launch traced here: 285 us
  starting transfers between devices  95.7 us (33%)
  Pallas kernels  94.7 us (33%)
  waiting for transfers between devices  64.7 us (23%)
  between operations  15.3 us (5%)
  local copies, waits for them, and re-layouts  11.8 us (4%)
    all_to_all x6, starting transfers between devices, exchange(): return lax.all_to_all(v, axis, split_axis=0, concat_axis=0, tiled=True)  52.3 us
    pallas_call x14, Pallas kernels, whole(): pl.pallas_call(bare, out_shape=[jax.ShapeDtypeStruct(s, d) for s, d in ou...  45.4 us
    all_to_all x6, waiting for transfers between devices, exchange(): return lax.all_to_all(v, axis, split_axis=0, concat_axis=0, tiled=True)  32.4 us
    ppermute x21, starting transfers between devices, shift_y(): return lax.ppermute(v, 'mp', [(i, (i + 2 * k) % MP) for i in range(MP)])  25.4 us
    ppermute x21, waiting for transfers between devices, shift_y(): return lax.ppermute(v, 'mp', [(i, (i + 2 * k) % MP) for i in range(MP)])  19.4 us
    pallas_call x1, Pallas kernels, body(): pl.pallas_call(gated, grid=(pl.cdiv(FP, 256),), out_shape=[jax.ShapeDtype...  18.3 us
    ppermute x13, starting transfers between devices, swap_core(): return lax.ppermute(v, 'mp', [(i, i ^ 1) for i in range(MP)])  12.9 us
    ppermute x13, waiting for transfers between devices, swap_core(): return lax.ppermute(v, 'mp', [(i, i ^ 1) for i in range(MP)])  12.7 us
  transfers between devices with their start and end apart: 45, of which 20 were waited for; matrix products, arithmetic and copies ran while one was open for 1% of the time, Pallas kernels for 26%

profile of v8, /device:TPU:1, one launch (start us, length us, event | category | flops | bytes accessed | tf_op | source)
XLA Modules:
  0.0 284.9 jit_solution(16684710126623381396)
XLA Ops:
  13.5 7.7 %all-to-all-start = ((bf16[16,176,256]{2,1,0:T(8,128)(2,1)}), bf16[16,176,256]{2,1,0:T(8,128)(2,1)S(1)}, u32[]{:S(2)}, u32[]{:S(2)}) async-start(bf16[16,176,256]{2,1,0:T(8,128)(2,1)} %broadcast_in_dim.18), calls=%async_computation | async-start | bytes 2883584 | tf_op jit(solution)/shard_map/all_to_all | solution.py:64
  28.8 19.3 %all-to-all-done.refs_4_ = bf16[16,176,256]{2,1,0:T(8,128)(2,1)S(1)} async-done(((bf16[16,176,256]{2,1,0:T(8,128)(2,1)}), bf16[16,176,256]{2,1,0:T(8,128)(2,1)S(1)}, u32[]{:S(2)}, u32[]{:S(2)}) %all-to-all-start) | async-done | bytes 1441824 | tf_op jit(solution)/shard_map/all_to_all | solution.py:64
  49.2 6.6 %all-to-all-start.1 = ((bf16[16,112,256]{2,1,0:T(8,128)(2,1)}), bf16[16,112,256]{2,1,0:T(8,128)(2,1)S(1)}, u32[]{:S(2)}, u32[]{:S(2)}) async-start(bf16[16,112,256]{2,1,0:T(8,128)(2,1)} %broadcast_in_dim.19), calls=%async_computation.1 | async-start | bytes 1835008 | tf_op jit(solution)/shard_map/all_to_all | solution.py:64
  62.9 4.3 %shard_map.331 = (bf16[512,1536]{1,0:T(8,128)(2,1)}, bf16[1536,512]{1,0:T(8,128)(2,1)}, bf16[64,1536]{1,0:T(8,128)(2,1)}, bf16[64,1536]{1,0:T(8,128)(2,1)}, bf16[256,1536]{1,0:T(8,128)(2,1)}) custom-call(s32[5]{0:T(128)} %stack.61.refs_0_.ids, bf16[512,1536]{1,0:T(8,128)(2,1)} %bitcast.56, bf16[512,1536]{1,0:T(8,128)(2,1)} %bitcast.50), custom_call_target="tpu_custom_call" | custom-call | flops 1 | bytes 1 | tf_op jit(solution)/shard_map/pallas_call | solution.py:92
  68.7 8.9 %shard_map.332 = (bf16[512,1536]{1,0:T(8,128)(2,1)}, bf16[512,512]{1,0:T(8,128)(2,1)}, bf16[8,256,256]{2,1,0:T(8,128)(2,1)}, f32[512,256]{1,0:T(8,128)}, bf16[1536,512]{1,0:T(8,128)(2,1)}, /*index=5*/f32[1,5120]{1,0:T(1,128)}) custom-call(s32[5]{0:T(128)} %stack.61.refs_0_.ids, bf16[512,1536]{1,0:T(8,128)(2,1)} %bitcast.51, ...), custom_call_target="tpu_custom_call" | custom-call | flops 1 | bytes 1 | tf_op jit(solution)/shard_map/pallas_call | solution.py:92
  77.6 16.1 %all-to-all-start.2 = ((bf16[8,256,256]{2,1,0:T(8,128)(2,1)}), bf16[8,256,256]{2,1,0:T(8,128)(2,1)S(1)}, u32[]{:S(2)}, u32[]{:S(2)}) async-start(bf16[8,256,256]{2,1,0:T(8,128)(2,1)} %get-tuple-element.93), calls=%async_computation.2 | async-start | bytes 2097152 | tf_op jit(solution)/shard_map/all_to_all | solution.py:64
  99.1 5.6 %shard_map.333 = (bf16[1536,1536]{1,0:T(8,128)(2,1)}, bf16[256,1536]{1,0:T(8,128)(2,1)}) custom-call(s32[5]{0:T(128)} %stack.61.refs_0_.ids, bf16[16,80,256]{2,1,0:T(8,128)(2,1)} %copy-done.23, bf16[16,80,256]{2,1,0:T(8,128)(2,1)} %collective-permute-done.4.refs_2_, bf16[16,80,256]{2,1,0:T(8,128)(2,1)} %collective-permute-done.5.refs_3_, ...), custom_call_target="tpu_custom_call" | custom-call | flops 1 | bytes 1 | tf_op jit(solution)/shard_map/pallas_call | solution.py:92
  104.7 4.2 %all-to-all-done.2.att.refs_1_ = bf16[8,256,256]{2,1,0:T(8,128)(2,1)S(1)} async-done(((bf16[8,256,256]{2,1,0:T(8,128)(2,1)}), bf16[8,256,256]{2,1,0:T(8,128)(2,1)S(1)}, u32[]{:S(2)}, u32[]{:S(2)}) %all-to-all-start.2) | async-done | bytes 1048608 | tf_op jit(solution)/shard_map/all_to_all | solution.py:64
  109.9 6.2 %shard_map.334 = (f32[64,1536]{1,0:T(8,128)}, bf16[256,1536]{1,0:T(8,128)(2,1)}) custom-call(s32[5]{0:T(128)} %stack.61.refs_0_.ids, bf16[8,256,256]{2,1,0:T(8,128)(2,1)} %copy-done.18, bf16[1536,1536]{1,0:T(8,128)(2,1)} %get-tuple-element.94.mixer, bf16[256,1536]{1,0:T(8,128)(2,1)} %get-tuple-element.95.tok, f32[1,5120]{1,0:T(1,128)} %get-tuple-element.96.vec), custom_call_target="tpu_custom_call" | custom-call | flops 1 | bytes 1 | tf_op jit(solution)/shard_map/pallas_call | solution.py:663
  120.0 18.3 %shard_map.335 = (bf16[512,1152]{1,0:T(8,128)(2,1)}, bf16[512,1152]{1,0:T(8,128)(2,1)}, bf16[512,1152]{1,0:T(8,128)(2,1)}, bf16[16,3,96,1152]{3,2,1,0:T(8,128)(2,1)}) custom-call(bf16[256,1536]{1,0:T(8,128)(2,1)} %get-tuple-element.97.near, bf16[256,1536]{1,0:T(8,128)(2,1)} %copy-done.26, bf16[512,1536]{1,0:T(8,128)(2,1)} %get-tuple-element.92.refs_6_.back, ...), custom_call_target="tpu_custom_call" | custom-call | flops 1 | bytes 1 | tf_op jit(solution)/shard_map/pallas_call | solution.py:685
  138.4 8.0 %shard_map.336 = (bf16[256,1536]{1,0:T(8,128)(2,1)}, bf16[256,1536]{1,0:T(8,128)(2,1)}) custom-call(bf16[512,1152]{1,0:T(8,128)(2,1)} %get-tuple-element.99.gate_grad, bf16[512,1152]{1,0:T(8,128)(2,1)} %get-tuple-element.100.up_grad, bf16[16,3,96,1152]{3,2,1,0:T(8,128)(2,1)} %bitcast.48), custom_call_target="tpu_custom_call" | custom-call | flops 1 | bytes 1 | tf_op jit(solution)/shard_map/pallas_call | solution.py:698
  153.5 5.2 %shard_map.338 = (bf16[256,1536]{1,0:T(8,128)(2,1)}, bf16[256,1536]{1,0:T(8,128)(2,1)}) custom-call(bf16[512,1152]{1,0:T(8,128)(2,1)} %get-tuple-element.109.act, bf16[16,3,96,1152]{3,2,1,0:T(8,128)(2,1)} %bitcast.49), custom_call_target="tpu_custom_call" | custom-call | flops 1 | bytes 1 | tf_op jit(solution)/shard_map/pallas_call | solution.py:720
  169.3 4.2 %collective-permute-done.18 = bf16[64,1536]{1,0:T(8,128)(2,1)S(1)} collective-permute-done((bf16[64,1536]{1,0:T(8,128)(2,1)S(1)}, bf16[64,1536]{1,0:T(8,128)(2,1)S(1)}, u32[]{:S(2)}, u32[]{:S(2)}) %collective-permute-start.18) | collective-permute-done | bytes 196640 | tf_op jit(solution)/shard_map/ppermute | solution.py:48
  182.4 11.3 %shard_map.341 = (bf16[512,512]{1,0:T(8,128)(2,1)}, bf16[512,384]{1,0:T(8,128)(2,1)}, bf16[512,128]{1,0:T(8,128)(2,1)}, bf16[512,128]{1,0:T(8,128)(2,1)}, bf16[2...) custom-call(s32[5]{0:T(128)} %stack.61.refs_0_.ids, bf16[4,64,1536]{2,1,0:T(8,128)(2,1)} %copy-done.22, ...), custom_call_target="tpu_custom_call" | custom-call | flops 1 | bytes 1 | tf_op jit(solution)/shard_map/pallas_call | solution.py:92
  198.7 3.8 %collective-permute-start.26 = (bf16[512,128]{1,0:T(8,128)(2,1)S(1)}, bf16[512,128]{1,0:T(8,128)(2,1)S(1)}, u32[]{:S(2)}, u32[]{:S(2)}) collective-permute-start(bf16[512,128]{1,0:T(8,128)(2,1)S(1)} %get-tuple-element.129), channel_id=1, source_target_pairs={{0,6},{1,7},{8,14},{9,15},{16,22},{17,23},{24,30},{25,31},{32,38},... | collective-permute-start | bytes 393224 | tf_op jit(solution)/shard_map/ppermute | solution.py:56
  203.2 4.0 %all-to-all-start.3 = ((bf16[8,32,128]{2,1,0:T(8,128)(2,1)}), bf16[8,32,128]{2,1,0:T(8,128)(2,1)S(1)}, u32[]{:S(2)}, u32[]{:S(2)}) async-start(bf16[8,32,128]{2,1,0:T(8,128)(2,1)} %get-tuple-element.132), calls=%async_computation.3 | async-start | bytes 131072 | tf_op jit(solution)/shard_map/all_to_all | solution.py:64
  207.2 3.3 %shard_map.343.refs_7_ = bf16[16,80,256]{2,1,0:T(8,128)(2,1)} custom-call(s32[5]{0:T(128)} %stack.61.refs_0_.ids, bf16[8,256,256]{2,1,0:T(8,128)(2,1)} %copy-done.18, bf16[8,256,256]{2,1,0:T(8,128)(2,1)} %collective-permute-done.29.refs_2_, bf16[512,384]{1,0:T(8,128)(2,1)} %get-tuple-element.133.refs_3_, f32[64,1536]{1,0:T(8,128)} %copy-done.4), custom_call_target="tpu_custom_call" | custom-call | flops 1 | bytes 1 | tf_op jit(solution)/shard_map/pallas_call | solution.py:92
  212.8 3.6 %shard_map.344.refs_3_ = bf16[16,184,256]{2,1,0:T(8,128)(2,1)} custom-call(s32[5]{0:T(128)} %stack.61.refs_0_.ids, bf16[512,1536]{1,0:T(8,128)(2,1)} %get-tuple-element.127.refs_1_, bf16[512,512]{1,0:T(8,128)(2,1)} %get-tuple-element.128.refs_2_, bf16[512,128]{1,0:T(8,128)(2,1)} %copy-done.33, bf16[512,128]{1,0:T(8,128)(2,1)} %copy-done.34, ...), custom_call_target="tpu_custom_call" | custom-call | flops 1 | bytes 1 | tf_op jit(solution)/shard_map/pallas_call | solution.py:92
  216.5 6.6 %all-to-all-start.4 = ((bf16[16,184,256]{2,1,0:T(8,128)(2,1)}), bf16[16,184,256]{2,1,0:T(8,128)(2,1)}, u32[]{:S(2)}, u32[]{:S(2)}) async-start(bf16[16,184,256]{2,1,0:T(8,128)(2,1)} %shard_map.344.refs_3_), calls=%async_computation.4 | async-start | bytes 3014656 | tf_op jit(solution)/shard_map/all_to_all | solution.py:64
  230.5 4.1 %collective-permute-done.30.refs_3_ = bf16[64,1536]{1,0:T(8,128)(2,1)S(1)} collective-permute-done((bf16[64,1536]{1,0:T(8,128)(2,1)S(1)}, bf16[64,1536]{1,0:T(8,128)(2,1)S(1)}, u32[]{:S(2)}, u32[]{:S(2)}) %collective-permute-start.30) | collective-permute-done | bytes 196640 | tf_op jit(solution)/shard_map/ppermute | solution.py:48
  234.7 4.8 %collective-permute-done.32.refs_5_ = bf16[64,1536]{1,0:T(8,128)(2,1)S(1)} collective-permute-done((bf16[64,1536]{1,0:T(8,128)(2,1)S(1)}, bf16[64,1536]{1,0:T(8,128)(2,1)S(1)}, u32[]{:S(2)}, u32[]{:S(2)}) %collective-permute-start.32) | collective-permute-done | bytes 196640 | tf_op jit(solution)/shard_map/ppermute | solution.py:48
  246.0 11.3 %all-to-all-start.5 = ((f32[128,1,128]{2,1,0:T(1,128)}), f32[128,1,128]{2,1,0:T(1,128)S(1)}, u32[]{:S(2)}, u32[]{:S(2)}) async-start(f32[128,1,128]{2,1,0:T(1,128)} %get-tuple-element.141), calls=%async_computation.5 | async-start | bytes 131072 | tf_op jit(solution)/shard_map/all_to_all | solution.py:64
  259.8 6.9 %all-to-all-done.5.refs_5_.squares = f32[128,1,128]{2,1,0:T(1,128)S(1)} async-done(((f32[128,1,128]{2,1,0:T(1,128)}), f32[128,1,128]{2,1,0:T(1,128)S(1)}, u32[]{:S(2)}, u32[]{:S(2)}) %all-to-all-start.5) | async-done | bytes 65568 | tf_op jit(solution)/shard_map/all_to_all | solution.py:64
  268.8 6.7 %shard_map.351 = (f32[1,128]{1,0:T(1,128)}, f32[96,256]{1,0:T(8,128)}, f32[96,256]{1,0:T(8,128)}, f32[96,256]{1,0:T(8,128)}, f32[96,192]{1,0:T(8,128)}, /*index=...) custom-call(f32[128,1,128]{2,1,0:T(1,128)} %copy-done.9, ...), custom_call_target="tpu_custom_call" | custom-call | flops 1 | bytes 1 | tf_op jit(solution)/shard_map/pallas_call | solution.py:841
  (200 shorter events, 88.3 us)
Async XLA Ops:
  7.2 111.9 %all-gather.3.cloned.1.call-start = ((), (), s32[]{:S(2)}) async-start(), calls=%async_computation.7 | async-start | bytes 11280384 | tf_op jit(solution)/shard_map/all_gather | solution.py:608
  13.5 34.6 %all-to-all-start = ((bf16[16,176,256]{2,1,0:T(8,128)(2,1)}), bf16[16,176,256]{2,1,0:T(8,128)(2,1)S(1)}, u32[]{:S(2)}, u32[]{:S(2)}) async-start(bf16[16,176,256]{2,1,0:T(8,128)(2,1)} %broadcast_in_dim.18), calls=%async_computation | async-start | bytes 2883584 | tf_op jit(solution)/shard_map/all_to_all | solution.py:64
  49.2 18.5 %all-to-all-start.1 = ((bf16[16,112,256]{2,1,0:T(8,128)(2,1)}), bf16[16,112,256]{2,1,0:T(8,128)(2,1)S(1)}, u32[]{:S(2)}, u32[]{:S(2)}) async-start(bf16[16,112,256]{2,1,0:T(8,128)(2,1)} %broadcast_in_dim.19), calls=%async_computation.1 | async-start | bytes 1835008 | tf_op jit(solution)/shard_map/all_to_all | solution.py:64
  55.9 38.0 %collective-permute-start.6 = (bf16[16,80,256]{2,1,0:T(8,128)(2,1)S(1)}, bf16[16,80,256]{2,1,0:T(8,128)(2,1)}, u32[]{:S(2)}, u32[]{:S(2)}) collective-permute-start(bf16[16,80,256]{2,1,0:T(8,128)(2,1)S(1)} %slice.110.refs_1_), channel_id=1, source_target_pairs={{0,4},{1,5},{2,6},{3,7},{4,0},{5,1},{6,2},{7,3},{8,12},{9,13},{10,... | collective-permute-start | bytes 1966088 | tf_op jit(solution)/shard_map/ppermute | solution.py:48
  59.0 35.4 %collective-permute-start.4 = (bf16[16,80,256]{2,1,0:T(8,128)(2,1)S(1)}, bf16[16,80,256]{2,1,0:T(8,128)(2,1)}, u32[]{:S(2)}, u32[]{:S(2)}) collective-permute-start(bf16[16,80,256]{2,1,0:T(8,128)(2,1)S(1)} %slice.110.refs_1_), channel_id=1, source_target_pairs={{0,2},{1,3},{2,4},{3,5},{4,6},{5,7},{6,0},{7,1},{8,10},{9,11},{10,... | collective-permute-start | bytes 1966088 | tf_op jit(solution)/shard_map/ppermute | solution.py:48
  59.4 35.0 %collective-permute-start.5 = (bf16[16,80,256]{2,1,0:T(8,128)(2,1)S(1)}, bf16[16,80,256]{2,1,0:T(8,128)(2,1)}, u32[]{:S(2)}, u32[]{:S(2)}) collective-permute-start(bf16[16,80,256]{2,1,0:T(8,128)(2,1)S(1)} %slice.110.refs_1_), channel_id=1, source_target_pairs={{0,6},{1,7},{2,0},{3,1},{4,2},{5,3},{6,4},{7,5},{8,14},{9,15},{10,... | collective-permute-start | bytes 1966088 | tf_op jit(solution)/shard_map/ppermute | solution.py:48
  77.6 31.2 %all-to-all-start.2 = ((bf16[8,256,256]{2,1,0:T(8,128)(2,1)}), bf16[8,256,256]{2,1,0:T(8,128)(2,1)S(1)}, u32[]{:S(2)}, u32[]{:S(2)}) async-start(bf16[8,256,256]{2,1,0:T(8,128)(2,1)} %get-tuple-element.93), calls=%async_computation.2 | async-start | bytes 2097152 | tf_op jit(solution)/shard_map/all_to_all | solution.py:64
  93.8 149.4 %reduce-scatter.4.cloned.1.call-start = ((), (), s32[]{:S(2)}) async-start(), calls=%async_computation.8 | async-start | bytes 11280384
  153.5 8.4 %collective-permute-start.15 = (bf16[64,1536]{1,0:T(8,128)(2,1)S(1)}, bf16[64,1536]{1,0:T(8,128)(2,1)S(1)}, u32[]{:S(2)}, u32[]{:S(2)}) collective-permute-start(bf16[64,1536]{1,0:T(8,128)(2,1)S(1)} %get-tuple-element.106), channel_id=1, source_target_pairs={{0,4},{1,5},{2,6},{3,7},{4,0},{5,1},{6,2},{7,3},{8,12},{9,13},{10,... | collective-permute-start | bytes 589832 | tf_op jit(solution)/shard_map/ppermute | solution.py:48
  166.0 10.8 %collective-permute-start.20 = (bf16[256,1536]{1,0:T(8,128)(2,1)}, bf16[256,1536]{1,0:T(8,128)(2,1)S(1)}, u32[]{:S(2)}, u32[]{:S(2)}) collective-permute-start(bf16[256,1536]{1,0:T(8,128)(2,1)} %get-tuple-element.110.refs_8_), channel_id=1, source_target_pairs={{0,1},{1,0},{2,3},{3,2},{4,5},{5,4},{6,7},{7,6},{8,9},{9,8},{10,11... | collective-permute-start | bytes 2359304 | tf_op jit(solution)/shard_map/ppermute | solution.py:60
  176.7 30.4 %collective-permute-start.29 = (bf16[8,256,256]{2,1,0:T(8,128)(2,1)S(1)}, bf16[8,256,256]{2,1,0:T(8,128)(2,1)}, u32[]{:S(2)}, u32[]{:S(2)}) collective-permute-start(bf16[8,256,256]{2,1,0:T(8,128)(2,1)S(1)} %copy-done.19), channel_id=1, source_target_pairs={{0,1},{1,0},{2,3},{3,2},{4,5},{5,4},{6,7},{7,6},{8,9},{9,8},{10,11... | collective-permute-start | bytes 3145736 | tf_op jit(solution)/shard_map/ppermute | solution.py:60
  178.3 16.1 %collective-permute-start.22 = (bf16[64,1536]{1,0:T(8,128)(2,1)S(1)}, bf16[64,1536]{1,0:T(8,128)(2,1)S(1)}, u32[]{:S(2)}, u32[]{:S(2)}) collective-permute-start(bf16[64,1536]{1,0:T(8,128)(2,1)S(1)} %get-tuple-element.121), channel_id=1, source_target_pairs={{0,2},{1,3},{2,4},{3,5},{4,6},{5,7},{6,0},{7,1},{8,10},{9,11},{10,... | collective-permute-start | bytes 589832 | tf_op jit(solution)/shard_map/ppermute | solution.py:48
  178.6 15.8 %collective-permute-start.23 = (bf16[64,1536]{1,0:T(8,128)(2,1)S(1)}, bf16[64,1536]{1,0:T(8,128)(2,1)S(1)}, u32[]{:S(2)}, u32[]{:S(2)}) collective-permute-start(bf16[64,1536]{1,0:T(8,128)(2,1)S(1)} %get-tuple-element.122), channel_id=1, source_target_pairs={{0,6},{1,7},{2,0},{3,1},{4,2},{5,3},{6,4},{7,5},{8,14},{9,15},{10,... | collective-permute-start | bytes 589832 | tf_op jit(solution)/shard_map/ppermute | solution.py:48
  181.0 13.4 %collective-permute-start.24 = (bf16[64,1536]{1,0:T(8,128)(2,1)S(1)}, bf16[64,1536]{1,0:T(8,128)(2,1)S(1)}, u32[]{:S(2)}, u32[]{:S(2)}) collective-permute-start(bf16[64,1536]{1,0:T(8,128)(2,1)S(1)} %get-tuple-element.123), channel_id=1, source_target_pairs={{0,4},{1,5},{2,6},{3,7},{4,0},{5,1},{6,2},{7,3},{8,12},{9,13},{10,... | collective-permute-start | bytes 589832 | tf_op jit(solution)/shard_map/ppermute | solution.py:48
  198.0 14.0 %collective-permute-start.28 = (bf16[512,256]{1,0:T(8,128)(2,1)S(1)}, bf16[512,256]{1,0:T(8,128)(2,1)S(1)}, u32[]{:S(2)}, u32[]{:S(2)}) collective-permute-start(bf16[512,256]{1,0:T(8,128)(2,1)S(1)} %get-tuple-element.131), channel_id=1, source_target_pairs={{2,6},{3,7},{10,14},{11,15},{18,22},{19,23},{26,30},{27,31},{34,38... | collective-permute-start | bytes 786440 | tf_op jit(solution)/shard_map/ppermute | solution.py:56
  198.7 13.3 %collective-permute-start.26 = (bf16[512,128]{1,0:T(8,128)(2,1)S(1)}, bf16[512,128]{1,0:T(8,128)(2,1)S(1)}, u32[]{:S(2)}, u32[]{:S(2)}) collective-permute-start(bf16[512,128]{1,0:T(8,128)(2,1)S(1)} %get-tuple-element.129), channel_id=1, source_target_pairs={{0,6},{1,7},{8,14},{9,15},{16,22},{17,23},{24,30},{25,31},{32,38},... | collective-permute-start | bytes 393224 | tf_op jit(solution)/shard_map/ppermute | solution.py:56
  202.5 9.6 %collective-permute-start.27 = (bf16[512,128]{1,0:T(8,128)(2,1)S(1)}, bf16[512,128]{1,0:T(8,128)(2,1)S(1)}, u32[]{:S(2)}, u32[]{:S(2)}) collective-permute-start(bf16[512,128]{1,0:T(8,128)(2,1)S(1)} %get-tuple-element.130), channel_id=1, source_target_pairs={{4,6},{5,7},{12,14},{13,15},{20,22},{21,23},{28,30},{29,31},{36,38... | collective-permute-start | bytes 393224 | tf_op jit(solution)/shard_map/ppermute | solution.py:56
  203.2 8.9 %all-to-all-start.3 = ((bf16[8,32,128]{2,1,0:T(8,128)(2,1)}), bf16[8,32,128]{2,1,0:T(8,128)(2,1)S(1)}, u32[]{:S(2)}, u32[]{:S(2)}) async-start(bf16[8,32,128]{2,1,0:T(8,128)(2,1)} %get-tuple-element.132), calls=%async_computation.3 | async-start | bytes 131072 | tf_op jit(solution)/shard_map/all_to_all | solution.py:64
  216.5 26.7 %all-to-all-start.4 = ((bf16[16,184,256]{2,1,0:T(8,128)(2,1)}), bf16[16,184,256]{2,1,0:T(8,128)(2,1)}, u32[]{:S(2)}, u32[]{:S(2)}) async-start(bf16[16,184,256]{2,1,0:T(8,128)(2,1)} %shard_map.344.refs_3_), calls=%async_computation.4 | async-start | bytes 3014656 | tf_op jit(solution)/shard_map/all_to_all | solution.py:64
  229.9 9.6 %collective-permute-start.32 = (bf16[64,1536]{1,0:T(8,128)(2,1)S(1)}, bf16[64,1536]{1,0:T(8,128)(2,1)S(1)}, u32[]{:S(2)}, u32[]{:S(2)}) collective-permute-start(bf16[64,1536]{1,0:T(8,128)(2,1)S(1)} %get-tuple-element.137), channel_id=1, source_target_pairs={{0,4},{1,5},{2,6},{3,7},{4,0},{5,1},{6,2},{7,3},{8,12},{9,13},{10,... | collective-permute-start | bytes 589832 | tf_op jit(solution)/shard_map/ppermute | solution.py:48
  240.5 16.8 %collective-permute-start.33 = (bf16[2,64,1536]{2,1,0:T(8,128)(2,1)S(1)}, bf16[2,64,1536]{2,1,0:T(8,128)(2,1)S(1)}, u32[]{:S(2)}, u32[]{:S(2)}) collective-permute-start(bf16[2,64,1536]{2,1,0:T(8,128)(2,1)S(1)} %shard_map.346.p0.refs_1_), channel_id=1, source_target_pairs={{0,2},{1,3},{2,4},{3,5},{4,6},{5,7},{6,0},{7,1},{8,10},{9,11},{10,... | collective-permute-start | bytes 1179656 | tf_op jit(solution)/shard_map/ppermute | solution.py:48
  241.0 16.3 %collective-permute-start.34 = (bf16[2,64,1536]{2,1,0:T(8,128)(2,1)S(1)}, bf16[2,64,1536]{2,1,0:T(8,128)(2,1)S(1)}, u32[]{:S(2)}, u32[]{:S(2)}) collective-permute-start(bf16[2,64,1536]{2,1,0:T(8,128)(2,1)S(1)} %shard_map.346.p0.refs_1_), channel_id=1, source_target_pairs={{0,6},{1,7},{2,0},{3,1},{4,2},{5,3},{6,4},{7,5},{8,14},{9,15},{10,... | collective-permute-start | bytes 1179656 | tf_op jit(solution)/shard_map/ppermute | solution.py:48
  243.2 14.1 %collective-permute-start.35 = (bf16[2,64,1536]{2,1,0:T(8,128)(2,1)S(1)}, bf16[2,64,1536]{2,1,0:T(8,128)(2,1)S(1)}, u32[]{:S(2)}, u32[]{:S(2)}) collective-permute-start(bf16[2,64,1536]{2,1,0:T(8,128)(2,1)S(1)} %shard_map.346.p0.refs_1_), channel_id=1, source_target_pairs={{0,4},{1,5},{2,6},{3,7},{4,0},{5,1},{6,2},{7,3},{8,12},{9,13},{10,... | collective-permute-start | bytes 1179656 | tf_op jit(solution)/shard_map/ppermute | solution.py:48
  246.0 20.7 %all-to-all-start.5 = ((f32[128,1,128]{2,1,0:T(1,128)}), f32[128,1,128]{2,1,0:T(1,128)S(1)}, u32[]{:S(2)}, u32[]{:S(2)}) async-start(f32[128,1,128]{2,1,0:T(1,128)} %get-tuple-element.141), calls=%async_computation.5 | async-start | bytes 131072 | tf_op jit(solution)/shard_map/all_to_all | solution.py:64
  (58 other events, 373.4 us)
Sparse Core Ops, SparseCore 0:
  10.2 103.7 all-gather.2
  138.5 88.4 reduce-scatter.3

commit v9 on v8

--- a/solution.py
+++ b/solution.py
@@ -283,14 +283,17 @@
     low[...] = v.astype(bf16)
 
 
-def finish(ids, out_sum, own, a1, a2, a3, hidden, tok, grad, gain, done):
+def finish_out(ids, total, hidden, done):
     length, y, c = ids[0], ids[3], ids[4]
-    o, g = out_sum[...], summed(own, (a1, a2, a3))
     t = lax.broadcasted_iota(jnp.int32, (PART, 1), 0) + HALF * c + PART * y
-    done[0] = jnp.where(t < length, o + hidden[...], 0.0).astype(bf16)
+    done[...] = jnp.where(t < length, total[...] + hidden[...], 0.0).astype(bf16)
+
+
+def finish_in(ids, own, a1, a2, a3, tok, grad, gain, done):
     x = tok[...].astype(f32)
     scale = lax.rsqrt(jnp.mean(x * x, -1, keepdims=True) + EPS_NORM)
-    done[1] = (grad[...] + norm_back(x, scale, gain[...], g)).astype(bf16)
+    g = summed(own, (a1, a2, a3))
+    done[...] = (grad[...] + norm_back(x, scale, gain[...], g)).astype(bf16)
 
 
 def attend_back(
@@ -532,7 +535,7 @@
     for k, e in enumerate(RELATIVE):
         place = at(PART * lax.rem(ids[3] + e + 4, 4), PART, PART)
         for n in range(2):
-            rows[n, place, :] = pieces[k][n].astype(f32)
+            rows[n, place, :] = pieces[n][k][...].astype(f32)
     copies = [
         pltpu.make_async_copy(rows.at[n], out.at[0, at(HALF * half, HALF, HALF)], sems.at[n])
         for n, out in enumerate(outs)
@@ -543,19 +546,22 @@
         copy.wait()
 
 
-def settle_near(ids, p0, p1, p2, p3, output, input_grad, token, rows, sems):
+def settle_near(
+    ids, a0, a1, a2, a3, b0, b1, b2, b3, output, input_grad, token, rows, sems
+):
     token[...] = jnp.zeros_like(token)
-    write_half(ids, ids[4], (p0, p1, p2, p3), (output, input_grad), rows, sems)
+    pieces = (a0, a1, a2, a3), (b0, b1, b2, b3)
+    write_half(ids, ids[4], pieces, (output, input_grad), rows, sems)
 
 
 def settle_far(ids, far, _a, _b, output, input_grad, rows, sems):
-    pieces = [far.at[k] for k in range(4)]
+    pieces = [[far.at[4 * n + k] for k in range(4)] for n in range(2)]
     write_half(ids, 1 - ids[4], pieces, (output, input_grad), rows, sems)
 
 
-def pile(ids, p0, p1, p2, p3, out):
-    for k, p in enumerate((p0, p1, p2, p3)):
-        out[k] = p[...]
+def pile(ids, *refs):
+    for k, p in enumerate(refs[:-1]):
+        refs[-1][k] = p[...]
 
 
 def norm_back(v, scale, gain, grad):
@@ -791,26 +797,31 @@
 
     parts = half_sum(input_near, input_far, after=[joint_parts])
     (done,) = whole(
-        finish,
-        [((2, PART, D), bf16)],
-        [ids, out_sum] + parts + [hidden_part, tok_part, hidden_grad, gain_first],
+        finish_out, [((PART, D), bf16)], [ids, out_sum, hidden_part], limit=8, after=[joint_parts]
+    )
+    done_parts = gather(shift_y, done)
+    (done,) = whole(
+        finish_in,
+        [((PART, D), bf16)],
+        [ids] + parts + [tok_part, hidden_grad, gain_first],
         limit=8,
-    )
-    done_parts = gather(shift_y, done)
+        after=done_parts[1:],
+    )
+    done_parts += gather(shift_y, done)
     anywhere = pl.BlockSpec(memory_space=pl.ANY)
     results = [jax.ShapeDtypeStruct((1, T, D), f32)] * 2
     held = [pltpu.VMEM((2, HALF, D), f32), pltpu.SemaphoreType.DMA((2,))]
     *halves, token = pl.pallas_call(
         settle_near,
         out_shape=results + [jax.ShapeDtypeStruct((8, HEAD), f32)],
-        in_specs=[SM] + [VM] * 4,
+        in_specs=[SM] + [VM] * 8,
         out_specs=[anywhere] * 2 + [VM],
         scratch_shapes=held,
         compiler_params=pltpu.CompilerParams(vmem_limit_bytes=16 * MiB),
         cost_estimate=SMALL,
     )(ids, *done_parts)
     (done_near,) = whole(
-        pile, [((4, 2, PART, D), bf16)], [ids] + done_parts, after=[squares, token], limit=8
+        pile, [((8, PART, D), bf16)], [ids] + done_parts, after=[squares, token], limit=8
     )
     output, input_grad = pl.pallas_call(
         settle_far,

time: 286 us -> 291 us (1.017)
    ppermute x21 -> x24, waiting for transfers between devices: 19.4 us -> 24.5 us  [shift_y(): return lax.ppermute(v, 'mp', [(i, (i + 2 * k) % MP) for i in range(MP)])]
    ppermute x21 -> x24, starting transfers between devices: 25.4 us -> 28.5 us  [shift_y(): return lax.ppermute(v, 'mp', [(i, (i + 2 * k) % MP) for i in range(MP)])]
    pallas_call x14 -> x15, Pallas kernels: 45.4 us -> 46.9 us  [whole(): pl.pallas_call(bare, out_shape=[jax.ShapeDtypeStruct(s, d) for s, d in ou...]
    unnamed x74 -> x76, local copies, waits for them, and re-layouts: 8.77 us -> 8.14 us
  transfers between devices with their start and end apart: 45 -> 48, of which waited for: 20 -> 20; matrix products, arithmetic and copies ran while one was open for 1% -> 1% of each run, Pallas kernels for 26% -> 25%
where the time goes in v9:
time: 291 us
  starting transfers between devices  98.4 us (34%)
  Pallas kernels  96.3 us (33%)
  waiting for transfers between devices  66.7 us (23%)
  between operations  15.3 us (5%)
  local copies, waits for them, and re-layouts  11.1 us (4%)
    all_to_all x6, starting transfers between devices, exchange(): return lax.all_to_all(v, axis, split_axis=0, concat_axis=0, tiled=True)  51.7 us
    pallas_call x15, Pallas kernels, whole(): pl.pallas_call(bare, out_shape=[jax.ShapeDtypeStruct(s, d) for s, d in ou...  46.9 us
    all_to_all x6, waiting for transfers between devices, exchange(): return lax.all_to_all(v, axis, split_axis=0, concat_axis=0, tiled=True)  31.6 us
    ppermute x24, starting transfers between devices, shift_y(): return lax.ppermute(v, 'mp', [(i, (i + 2 * k) % MP) for i in range(MP)])  28.5 us
    ppermute x24, waiting for transfers between devices, shift_y(): return lax.ppermute(v, 'mp', [(i, (i + 2 * k) % MP) for i in range(MP)])  24.5 us
    pallas_call x1, Pallas kernels, body(): pl.pallas_call(gated, grid=(pl.cdiv(FP, 256),), out_shape=[jax.ShapeDtype...  18.4 us
    ppermute x13, starting transfers between devices, swap_core(): return lax.ppermute(v, 'mp', [(i, i ^ 1) for i in range(MP)])  13 us
    ppermute x13, waiting for transfers between devices, swap_core(): return lax.ppermute(v, 'mp', [(i, i ^ 1) for i in range(MP)])  10.5 us
  transfers between devices with their start and end apart: 48, of which 20 were waited for; matrix products, arithmetic and copies ran while one was open for 1% of the time, Pallas kernels for 25%

profile of v9, /device:TPU:1, one launch (start us, length us, event | category | flops | bytes accessed | tf_op | source)
XLA Modules:
  0.0 290.5 jit_solution(16235538646629067122)
XLA Ops:
  13.6 7.7 %all-to-all-start = ((bf16[16,176,256]{2,1,0:T(8,128)(2,1)}), bf16[16,176,256]{2,1,0:T(8,128)(2,1)S(1)}, u32[]{:S(2)}, u32[]{:S(2)}) async-start(bf16[16,176,256]{2,1,0:T(8,128)(2,1)} %broadcast_in_dim.18), calls=%async_computation | async-start | bytes 2883584 | tf_op jit(solution)/shard_map/all_to_all | solution.py:64
  28.9 19.3 %all-to-all-done.refs_4_ = bf16[16,176,256]{2,1,0:T(8,128)(2,1)S(1)} async-done(((bf16[16,176,256]{2,1,0:T(8,128)(2,1)}), bf16[16,176,256]{2,1,0:T(8,128)(2,1)S(1)}, u32[]{:S(2)}, u32[]{:S(2)}) %all-to-all-start) | async-done | bytes 1441824 | tf_op jit(solution)/shard_map/all_to_all | solution.py:64
  49.2 6.6 %all-to-all-start.1 = ((bf16[16,112,256]{2,1,0:T(8,128)(2,1)}), bf16[16,112,256]{2,1,0:T(8,128)(2,1)S(1)}, u32[]{:S(2)}, u32[]{:S(2)}) async-start(bf16[16,112,256]{2,1,0:T(8,128)(2,1)} %broadcast_in_dim.19), calls=%async_computation.1 | async-start | bytes 1835008 | tf_op jit(solution)/shard_map/all_to_all | solution.py:64
  62.9 4.3 %shard_map.331 = (bf16[512,1536]{1,0:T(8,128)(2,1)}, bf16[1536,512]{1,0:T(8,128)(2,1)}, bf16[64,1536]{1,0:T(8,128)(2,1)}, bf16[64,1536]{1,0:T(8,128)(2,1)}, bf16[256,1536]{1,0:T(8,128)(2,1)}) custom-call(s32[5]{0:T(128)} %stack.61.refs_0_.ids, bf16[512,1536]{1,0:T(8,128)(2,1)} %bitcast.56, bf16[512,1536]{1,0:T(8,128)(2,1)} %bitcast.50), custom_call_target="tpu_custom_call" | custom-call | flops 1 | bytes 1 | tf_op jit(solution)/shard_map/pallas_call | solution.py:92
  68.7 8.9 %shard_map.332 = (bf16[512,1536]{1,0:T(8,128)(2,1)}, bf16[512,512]{1,0:T(8,128)(2,1)}, bf16[8,256,256]{2,1,0:T(8,128)(2,1)}, f32[512,256]{1,0:T(8,128)}, bf16[1536,512]{1,0:T(8,128)(2,1)}, /*index=5*/f32[1,5120]{1,0:T(1,128)}) custom-call(s32[5]{0:T(128)} %stack.61.refs_0_.ids, bf16[512,1536]{1,0:T(8,128)(2,1)} %bitcast.51, ...), custom_call_target="tpu_custom_call" | custom-call | flops 1 | bytes 1 | tf_op jit(solution)/shard_map/pallas_call | solution.py:92
  77.7 16.1 %all-to-all-start.2 = ((bf16[8,256,256]{2,1,0:T(8,128)(2,1)}), bf16[8,256,256]{2,1,0:T(8,128)(2,1)}, u32[]{:S(2)}, u32[]{:S(2)}) async-start(bf16[8,256,256]{2,1,0:T(8,128)(2,1)} %get-tuple-element.93), calls=%async_computation.2 | async-start | bytes 2097152 | tf_op jit(solution)/shard_map/all_to_all | solution.py:64
  100.0 5.6 %shard_map.333 = (bf16[1536,1536]{1,0:T(8,128)(2,1)}, bf16[256,1536]{1,0:T(8,128)(2,1)}) custom-call(s32[5]{0:T(128)} %stack.61.refs_0_.ids, bf16[16,80,256]{2,1,0:T(8,128)(2,1)} %copy-done.21, bf16[16,80,256]{2,1,0:T(8,128)(2,1)} %copy-done.25, bf16[16,80,256]{2,1,0:T(8,128)(2,1)} %copy-done.26, bf16[16,80,256]{2,1,0:T(8,128)(2,1)} %collective-permute-done.6.refs_4_, ...), custom_call_target="tpu_custom_call" | custom-call | flops 1 | bytes 1 | tf_op jit(solution)/shard_map/pallas_call | solution.py:92
  105.6 3.3 %all-to-all-done.2.att.refs_1_ = bf16[8,256,256]{2,1,0:T(8,128)(2,1)} async-done(((bf16[8,256,256]{2,1,0:T(8,128)(2,1)}), bf16[8,256,256]{2,1,0:T(8,128)(2,1)}, u32[]{:S(2)}, u32[]{:S(2)}) %all-to-all-start.2) | async-done | bytes 1048608 | tf_op jit(solution)/shard_map/all_to_all | solution.py:64
  109.0 6.2 %shard_map.334 = (f32[64,1536]{1,0:T(8,128)}, bf16[256,1536]{1,0:T(8,128)(2,1)}) custom-call(s32[5]{0:T(128)} %stack.61.refs_0_.ids, bf16[8,256,256]{2,1,0:T(8,128)(2,1)} %all-to-all-done.2.att.refs_1_, bf16[1536,1536]{1,0:T(8,128)(2,1)} %get-tuple-element.94.mixer, bf16[256,1536]{1,0:T(8,128)(2,1)} %get-tuple-element.95.tok, f32[1,5120]{1,0:T(1,128)} %get-tuple-element.96.vec), custom_call_target="tpu_custom_call" | custom-call | flops 1 | bytes 1 | tf_op jit(solution)/shard_map/pallas_call | solution.py:669
  119.1 18.4 %shard_map.335 = (bf16[512,1152]{1,0:T(8,128)(2,1)}, bf16[512,1152]{1,0:T(8,128)(2,1)}, bf16[512,1152]{1,0:T(8,128)(2,1)}, bf16[16,3,96,1152]{3,2,1,0:T(8,128)(2,1)}) custom-call(bf16[256,1536]{1,0:T(8,128)(2,1)} %get-tuple-element.97.near, bf16[256,1536]{1,0:T(8,128)(2,1)} %copy-done.24, bf16[512,1536]{1,0:T(8,128)(2,1)} %get-tuple-element.92.refs_6_.back, ...), custom_call_target="tpu_custom_call" | custom-call | flops 1 | bytes 1 | tf_op jit(solution)/shard_map/pallas_call | solution.py:691
  137.5 8.0 %shard_map.336 = (bf16[256,1536]{1,0:T(8,128)(2,1)}, bf16[256,1536]{1,0:T(8,128)(2,1)}) custom-call(bf16[512,1152]{1,0:T(8,128)(2,1)} %get-tuple-element.99.gate_grad, bf16[512,1152]{1,0:T(8,128)(2,1)} %get-tuple-element.100.up_grad, bf16[16,3,96,1152]{3,2,1,0:T(8,128)(2,1)} %bitcast.48), custom_call_target="tpu_custom_call" | custom-call | flops 1 | bytes 1 | tf_op jit(solution)/shard_map/pallas_call | solution.py:704
  152.7 5.2 %shard_map.338 = (bf16[256,1536]{1,0:T(8,128)(2,1)}, bf16[256,1536]{1,0:T(8,128)(2,1)}) custom-call(bf16[512,1152]{1,0:T(8,128)(2,1)} %get-tuple-element.109.act, bf16[16,3,96,1152]{3,2,1,0:T(8,128)(2,1)} %bitcast.49), custom_call_target="tpu_custom_call" | custom-call | flops 1 | bytes 1 | tf_op jit(solution)/shard_map/pallas_call | solution.py:726
  168.4 4.2 %collective-permute-done.18 = bf16[64,1536]{1,0:T(8,128)(2,1)S(1)} collective-permute-done((bf16[64,1536]{1,0:T(8,128)(2,1)S(1)}, bf16[64,1536]{1,0:T(8,128)(2,1)S(1)}, u32[]{:S(2)}, u32[]{:S(2)}) %collective-permute-start.18) | collective-permute-done | bytes 196640 | tf_op jit(solution)/shard_map/ppermute | solution.py:48
  181.5 11.2 %shard_map.341 = (bf16[512,512]{1,0:T(8,128)(2,1)}, bf16[512,384]{1,0:T(8,128)(2,1)}, bf16[512,128]{1,0:T(8,128)(2,1)}, bf16[512,128]{1,0:T(8,128)(2,1)}, bf16[2...) custom-call(s32[5]{0:T(128)} %stack.61.refs_0_.ids, bf16[4,64,1536]{2,1,0:T(8,128)(2,1)} %copy-done.20, ...), custom_call_target="tpu_custom_call" | custom-call | flops 1 | bytes 1 | tf_op jit(solution)/shard_map/pallas_call | solution.py:92
  197.8 3.8 %collective-permute-start.25 = (bf16[512,128]{1,0:T(8,128)(2,1)S(1)}, bf16[512,128]{1,0:T(8,128)(2,1)S(1)}, u32[]{:S(2)}, u32[]{:S(2)}) collective-permute-start(bf16[512,128]{1,0:T(8,128)(2,1)S(1)} %get-tuple-element.127), channel_id=1, source_target_pairs={{0,6},{1,7},{8,14},{9,15},{16,22},{17,23},{24,30},{25,31},{32,38},... | collective-permute-start | bytes 393224 | tf_op jit(solution)/shard_map/ppermute | solution.py:56
  202.3 4.0 %all-to-all-start.3 = ((bf16[8,32,128]{2,1,0:T(8,128)(2,1)}), bf16[8,32,128]{2,1,0:T(8,128)(2,1)S(1)}, u32[]{:S(2)}, u32[]{:S(2)}) async-start(bf16[8,32,128]{2,1,0:T(8,128)(2,1)} %get-tuple-element.130), calls=%async_computation.3 | async-start | bytes 131072 | tf_op jit(solution)/shard_map/all_to_all | solution.py:64
  206.3 3.3 %shard_map.343.refs_7_ = bf16[16,80,256]{2,1,0:T(8,128)(2,1)} custom-call(s32[5]{0:T(128)} %stack.61.refs_0_.ids, bf16[8,256,256]{2,1,0:T(8,128)(2,1)} %all-to-all-done.2.att.refs_1_, bf16[8,256,256]{2,1,0:T(8,128)(2,1)} %collective-permute-done.28.refs_2_, bf16[512,384]{1,0:T(8,128)(2,1)} %get-tuple-element.131.refs_3_, f32[64,1536]{1,0:T(8,128)} %copy-done.4), custom_call_target="tpu_custom_call" | custom-call | flops 1 | bytes 1 | tf_op jit(solution)/shard_map/pallas_call | solution.py:92
  211.9 3.7 %shard_map.344.refs_3_ = bf16[16,184,256]{2,1,0:T(8,128)(2,1)} custom-call(s32[5]{0:T(128)} %stack.61.refs_0_.ids, bf16[512,1536]{1,0:T(8,128)(2,1)} %get-tuple-element.125.refs_1_, bf16[512,512]{1,0:T(8,128)(2,1)} %get-tuple-element.126.refs_2_, bf16[512,128]{1,0:T(8,128)(2,1)} %copy-done.34, bf16[512,128]{1,0:T(8,128)(2,1)} %copy-done.35, ...), custom_call_target="tpu_custom_call" | custom-call | flops 1 | bytes 1 | tf_op jit(solution)/shard_map/pallas_call | solution.py:92
  215.6 6.6 %all-to-all-start.4 = ((bf16[16,184,256]{2,1,0:T(8,128)(2,1)}), bf16[16,184,256]{2,1,0:T(8,128)(2,1)}, u32[]{:S(2)}, u32[]{:S(2)}) async-start(bf16[16,184,256]{2,1,0:T(8,128)(2,1)} %shard_map.344.refs_3_), calls=%async_computation.4 | async-start | bytes 3014656 | tf_op jit(solution)/shard_map/all_to_all | solution.py:64
  236.7 3.3 %collective-permute-done.33.refs_2_ = bf16[64,1536]{1,0:T(8,128)(2,1)S(1)} collective-permute-done((bf16[64,1536]{1,0:T(8,128)(2,1)S(1)}, bf16[64,1536]{1,0:T(8,128)(2,1)S(1)}, u32[]{:S(2)}, u32[]{:S(2)}) %collective-permute-start.33) | collective-permute-done | bytes 196640 | tf_op jit(solution)/shard_map/ppermute | solution.py:48
  240.0 5.0 %collective-permute-done.35.refs_4_ = bf16[64,1536]{1,0:T(8,128)(2,1)S(1)} collective-permute-done((bf16[64,1536]{1,0:T(8,128)(2,1)S(1)}, bf16[64,1536]{1,0:T(8,128)(2,1)S(1)}, u32[]{:S(2)}, u32[]{:S(2)}) %collective-permute-start.35) | collective-permute-done | bytes 196640 | tf_op jit(solution)/shard_map/ppermute | solution.py:48
  251.7 10.7 %all-to-all-start.5 = ((f32[128,1,128]{2,1,0:T(1,128)}), f32[128,1,128]{2,1,0:T(1,128)S(1)}, u32[]{:S(2)}, u32[]{:S(2)}) async-start(f32[128,1,128]{2,1,0:T(1,128)} %get-tuple-element.141), calls=%async_computation.5 | async-start | bytes 131072 | tf_op jit(solution)/shard_map/all_to_all | solution.py:64
  264.9 6.9 %all-to-all-done.5.refs_9_.squares = f32[128,1,128]{2,1,0:T(1,128)S(1)} async-done(((f32[128,1,128]{2,1,0:T(1,128)}), f32[128,1,128]{2,1,0:T(1,128)S(1)}, u32[]{:S(2)}, u32[]{:S(2)}) %all-to-all-start.5) | async-done | bytes 65568 | tf_op jit(solution)/shard_map/all_to_all | solution.py:64
  274.5 6.7 %shard_map.352 = (f32[1,128]{1,0:T(1,128)}, f32[96,256]{1,0:T(8,128)}, f32[96,256]{1,0:T(8,128)}, f32[96,256]{1,0:T(8,128)}, f32[96,192]{1,0:T(8,128)}, /*index=...) custom-call(f32[128,1,128]{2,1,0:T(1,128)} %copy-done.9, ...), custom_call_target="tpu_custom_call" | custom-call | flops 1 | bytes 1 | tf_op jit(solution)/shard_map/pallas_call | solution.py:852
  (209 shorter events, 96.1 us)
Async XLA Ops:
  7.2 111.0 %all-gather.3.cloned.1.call-start = ((), (), s32[]{:S(2)}) async-start(), calls=%async_computation.7 | async-start | bytes 11280384 | tf_op jit(solution)/shard_map/all_gather | solution.py:614
  13.6 34.6 %all-to-all-start = ((bf16[16,176,256]{2,1,0:T(8,128)(2,1)}), bf16[16,176,256]{2,1,0:T(8,128)(2,1)S(1)}, u32[]{:S(2)}, u32[]{:S(2)}) async-start(bf16[16,176,256]{2,1,0:T(8,128)(2,1)} %broadcast_in_dim.18), calls=%async_computation | async-start | bytes 2883584 | tf_op jit(solution)/shard_map/all_to_all | solution.py:64
  49.2 18.6 %all-to-all-start.1 = ((bf16[16,112,256]{2,1,0:T(8,128)(2,1)}), bf16[16,112,256]{2,1,0:T(8,128)(2,1)S(1)}, u32[]{:S(2)}, u32[]{:S(2)}) async-start(bf16[16,112,256]{2,1,0:T(8,128)(2,1)} %broadcast_in_dim.19), calls=%async_computation.1 | async-start | bytes 1835008 | tf_op jit(solution)/shard_map/all_to_all | solution.py:64
  55.9 38.0 %collective-permute-start.6 = (bf16[16,80,256]{2,1,0:T(8,128)(2,1)S(1)}, bf16[16,80,256]{2,1,0:T(8,128)(2,1)}, u32[]{:S(2)}, u32[]{:S(2)}) collective-permute-start(bf16[16,80,256]{2,1,0:T(8,128)(2,1)S(1)} %slice.110.refs_1_), channel_id=1, source_target_pairs={{0,4},{1,5},{2,6},{3,7},{4,0},{5,1},{6,2},{7,3},{8,12},{9,13},{10,... | collective-permute-start | bytes 1966088 | tf_op jit(solution)/shard_map/ppermute | solution.py:48
  59.0 35.4 %collective-permute-start.4 = (bf16[16,80,256]{2,1,0:T(8,128)(2,1)S(1)}, bf16[16,80,256]{2,1,0:T(8,128)(2,1)S(1)}, u32[]{:S(2)}, u32[]{:S(2)}) collective-permute-start(bf16[16,80,256]{2,1,0:T(8,128)(2,1)S(1)} %slice.110.refs_1_), channel_id=1, source_target_pairs={{0,2},{1,3},{2,4},{3,5},{4,6},{5,7},{6,0},{7,1},{8,10},{9,11},{10,... | collective-permute-start | bytes 1966088 | tf_op jit(solution)/shard_map/ppermute | solution.py:48
  59.5 35.0 %collective-permute-start.5 = (bf16[16,80,256]{2,1,0:T(8,128)(2,1)S(1)}, bf16[16,80,256]{2,1,0:T(8,128)(2,1)S(1)}, u32[]{:S(2)}, u32[]{:S(2)}) collective-permute-start(bf16[16,80,256]{2,1,0:T(8,128)(2,1)S(1)} %slice.110.refs_1_), channel_id=1, source_target_pairs={{0,6},{1,7},{2,0},{3,1},{4,2},{5,3},{6,4},{7,5},{8,14},{9,15},{10,... | collective-permute-start | bytes 1966088 | tf_op jit(solution)/shard_map/ppermute | solution.py:48
  77.7 31.3 %all-to-all-start.2 = ((bf16[8,256,256]{2,1,0:T(8,128)(2,1)}), bf16[8,256,256]{2,1,0:T(8,128)(2,1)}, u32[]{:S(2)}, u32[]{:S(2)}) async-start(bf16[8,256,256]{2,1,0:T(8,128)(2,1)} %get-tuple-element.93), calls=%async_computation.2 | async-start | bytes 2097152 | tf_op jit(solution)/shard_map/all_to_all | solution.py:64
  93.8 155.2 %reduce-scatter.4.cloned.1.call-start = ((), (), s32[]{:S(2)}) async-start(), calls=%async_computation.8 | async-start | bytes 11280384
  165.1 10.8 %collective-permute-start.20 = (bf16[256,1536]{1,0:T(8,128)(2,1)}, bf16[256,1536]{1,0:T(8,128)(2,1)S(1)}, u32[]{:S(2)}, u32[]{:S(2)}) collective-permute-start(bf16[256,1536]{1,0:T(8,128)(2,1)} %get-tuple-element.110.refs_8_), channel_id=1, source_target_pairs={{0,1},{1,0},{2,3},{3,2},{4,5},{5,4},{6,7},{7,6},{8,9},{9,8},{10,11... | collective-permute-start | bytes 2359304 | tf_op jit(solution)/shard_map/ppermute | solution.py:60
  175.8 30.4 %collective-permute-start.28 = (bf16[8,256,256]{2,1,0:T(8,128)(2,1)}, bf16[8,256,256]{2,1,0:T(8,128)(2,1)}, u32[]{:S(2)}, u32[]{:S(2)}) collective-permute-start(bf16[8,256,256]{2,1,0:T(8,128)(2,1)} %all-to-all-done.2.att.refs_1_), channel_id=1, source_target_pairs={{0,1},{1,0},{2,3},{3,2},{4,5},{5,4},{6,7},{7,6},{8,9},{9,8},{10,11... | collective-permute-start | bytes 3145736 | tf_op jit(solution)/shard_map/ppermute | solution.py:60
  177.4 16.0 %collective-permute-start.22 = (bf16[64,1536]{1,0:T(8,128)(2,1)S(1)}, bf16[64,1536]{1,0:T(8,128)(2,1)S(1)}, u32[]{:S(2)}, u32[]{:S(2)}) collective-permute-start(bf16[64,1536]{1,0:T(8,128)(2,1)S(1)} %get-tuple-element.121), channel_id=1, source_target_pairs={{0,2},{1,3},{2,4},{3,5},{4,6},{5,7},{6,0},{7,1},{8,10},{9,11},{10,... | collective-permute-start | bytes 589832 | tf_op jit(solution)/shard_map/ppermute | solution.py:48
  177.7 15.8 %collective-permute-start.23 = (bf16[64,1536]{1,0:T(8,128)(2,1)S(1)}, bf16[64,1536]{1,0:T(8,128)(2,1)S(1)}, u32[]{:S(2)}, u32[]{:S(2)}) collective-permute-start(bf16[64,1536]{1,0:T(8,128)(2,1)S(1)} %get-tuple-element.122), channel_id=1, source_target_pairs={{0,6},{1,7},{2,0},{3,1},{4,2},{5,3},{6,4},{7,5},{8,14},{9,15},{10,... | collective-permute-start | bytes 589832 | tf_op jit(solution)/shard_map/ppermute | solution.py:48
  180.1 13.4 %collective-permute-start.24 = (bf16[64,1536]{1,0:T(8,128)(2,1)S(1)}, bf16[64,1536]{1,0:T(8,128)(2,1)S(1)}, u32[]{:S(2)}, u32[]{:S(2)}) collective-permute-start(bf16[64,1536]{1,0:T(8,128)(2,1)S(1)} %get-tuple-element.123), channel_id=1, source_target_pairs={{0,4},{1,5},{2,6},{3,7},{4,0},{5,1},{6,2},{7,3},{8,12},{9,13},{10,... | collective-permute-start | bytes 589832 | tf_op jit(solution)/shard_map/ppermute | solution.py:48
  197.1 14.1 %collective-permute-start.27 = (bf16[512,256]{1,0:T(8,128)(2,1)S(1)}, bf16[512,256]{1,0:T(8,128)(2,1)S(1)}, u32[]{:S(2)}, u32[]{:S(2)}) collective-permute-start(bf16[512,256]{1,0:T(8,128)(2,1)S(1)} %get-tuple-element.129), channel_id=1, source_target_pairs={{2,6},{3,7},{10,14},{11,15},{18,22},{19,23},{26,30},{27,31},{34,38... | collective-permute-start | bytes 786440 | tf_op jit(solution)/shard_map/ppermute | solution.py:56
  197.8 13.4 %collective-permute-start.25 = (bf16[512,128]{1,0:T(8,128)(2,1)S(1)}, bf16[512,128]{1,0:T(8,128)(2,1)S(1)}, u32[]{:S(2)}, u32[]{:S(2)}) collective-permute-start(bf16[512,128]{1,0:T(8,128)(2,1)S(1)} %get-tuple-element.127), channel_id=1, source_target_pairs={{0,6},{1,7},{8,14},{9,15},{16,22},{17,23},{24,30},{25,31},{32,38},... | collective-permute-start | bytes 393224 | tf_op jit(solution)/shard_map/ppermute | solution.py:56
  215.6 33.4 %all-to-all-start.4 = ((bf16[16,184,256]{2,1,0:T(8,128)(2,1)}), bf16[16,184,256]{2,1,0:T(8,128)(2,1)}, u32[]{:S(2)}, u32[]{:S(2)}) async-start(bf16[16,184,256]{2,1,0:T(8,128)(2,1)} %shard_map.344.refs_3_), calls=%async_computation.4 | async-start | bytes 3014656 | tf_op jit(solution)/shard_map/all_to_all | solution.py:64
  226.7 10.0 %collective-permute-start.31 = (bf16[64,1536]{1,0:T(8,128)(2,1)S(1)}, bf16[64,1536]{1,0:T(8,128)(2,1)S(1)}, u32[]{:S(2)}, u32[]{:S(2)}) collective-permute-start(bf16[64,1536]{1,0:T(8,128)(2,1)S(1)} %shard_map.345.a0.refs_1_), channel_id=1, source_target_pairs={{0,4},{1,5},{2,6},{3,7},{4,0},{5,1},{6,2},{7,3},{8,12},{9,13},{10,... | collective-permute-start | bytes 589832 | tf_op jit(solution)/shard_map/ppermute | solution.py:48
  228.0 12.0 %collective-permute-start.33 = (bf16[64,1536]{1,0:T(8,128)(2,1)S(1)}, bf16[64,1536]{1,0:T(8,128)(2,1)S(1)}, u32[]{:S(2)}, u32[]{:S(2)}) collective-permute-start(bf16[64,1536]{1,0:T(8,128)(2,1)S(1)} %get-tuple-element.135), channel_id=1, source_target_pairs={{0,2},{1,3},{2,4},{3,5},{4,6},{5,7},{6,0},{7,1},{8,10},{9,11},{10,... | collective-permute-start | bytes 589832 | tf_op jit(solution)/shard_map/ppermute | solution.py:48
  228.9 11.1 %collective-permute-start.34 = (bf16[64,1536]{1,0:T(8,128)(2,1)S(1)}, bf16[64,1536]{1,0:T(8,128)(2,1)S(1)}, u32[]{:S(2)}, u32[]{:S(2)}) collective-permute-start(bf16[64,1536]{1,0:T(8,128)(2,1)S(1)} %get-tuple-element.136), channel_id=1, source_target_pairs={{0,6},{1,7},{2,0},{3,1},{4,2},{5,3},{6,4},{7,5},{8,14},{9,15},{10,... | collective-permute-start | bytes 589832 | tf_op jit(solution)/shard_map/ppermute | solution.py:48
  231.8 13.2 %collective-permute-start.35 = (bf16[64,1536]{1,0:T(8,128)(2,1)S(1)}, bf16[64,1536]{1,0:T(8,128)(2,1)S(1)}, u32[]{:S(2)}, u32[]{:S(2)}) collective-permute-start(bf16[64,1536]{1,0:T(8,128)(2,1)S(1)} %get-tuple-element.137), channel_id=1, source_target_pairs={{0,4},{1,5},{2,6},{3,7},{4,0},{5,1},{6,2},{7,3},{8,12},{9,13},{10,... | collective-permute-start | bytes 589832 | tf_op jit(solution)/shard_map/ppermute | solution.py:48
  245.9 16.5 %collective-permute-start.36 = (bf16[64,1536]{1,0:T(8,128)(2,1)S(1)}, bf16[64,1536]{1,0:T(8,128)(2,1)S(1)}, u32[]{:S(2)}, u32[]{:S(2)}) collective-permute-start(bf16[64,1536]{1,0:T(8,128)(2,1)S(1)} %shard_map.347.b0.refs_5_), channel_id=1, source_target_pairs={{0,2},{1,3},{2,4},{3,5},{4,6},{5,7},{6,0},{7,1},{8,10},{9,11},{10,... | collective-permute-start | bytes 589832 | tf_op jit(solution)/shard_map/ppermute | solution.py:48
  246.5 15.9 %collective-permute-start.37 = (bf16[64,1536]{1,0:T(8,128)(2,1)S(1)}, bf16[64,1536]{1,0:T(8,128)(2,1)S(1)}, u32[]{:S(2)}, u32[]{:S(2)}) collective-permute-start(bf16[64,1536]{1,0:T(8,128)(2,1)S(1)} %shard_map.347.b0.refs_5_), channel_id=1, source_target_pairs={{0,6},{1,7},{2,0},{3,1},{4,2},{5,3},{6,4},{7,5},{8,14},{9,15},{10,... | collective-permute-start | bytes 589832 | tf_op jit(solution)/shard_map/ppermute | solution.py:48
  248.6 13.8 %collective-permute-start.38 = (bf16[64,1536]{1,0:T(8,128)(2,1)S(1)}, bf16[64,1536]{1,0:T(8,128)(2,1)S(1)}, u32[]{:S(2)}, u32[]{:S(2)}) collective-permute-start(bf16[64,1536]{1,0:T(8,128)(2,1)S(1)} %shard_map.347.b0.refs_5_), channel_id=1, source_target_pairs={{0,4},{1,5},{2,6},{3,7},{4,0},{5,1},{6,2},{7,3},{8,12},{9,13},{10,... | collective-permute-start | bytes 589832 | tf_op jit(solution)/shard_map/ppermute | solution.py:48
  251.7 20.1 %all-to-all-start.5 = ((f32[128,1,128]{2,1,0:T(1,128)}), f32[128,1,128]{2,1,0:T(1,128)S(1)}, u32[]{:S(2)}, u32[]{:S(2)}) async-start(f32[128,1,128]{2,1,0:T(1,128)} %get-tuple-element.141), calls=%async_computation.5 | async-start | bytes 131072 | tf_op jit(solution)/shard_map/all_to_all | solution.py:64
  (62 other events, 392.0 us)
Sparse Core Ops, SparseCore 0:
  10.2 103.7 all-gather.2
  137.6 88.4 reduce-scatter.3

commit v10 on v8

--- a/solution.py
+++ b/solution.py
@@ -64,11 +64,11 @@
     return lax.all_to_all(v, axis, split_axis=0, concat_axis=0, tiled=True)
 
 
-RELATIVE = (0, -1, 1, 2)
+RELATIVE = (0, 2, -1, 1)
 
 
 def gather(shift, v):
-    return [v, shift(v, 1), shift(v, -1), shift(v, 2)]
+    return [v, shift(v, 2), shift(v, 1), shift(v, -1)]
 
 
 def nn(a, b):
@@ -714,7 +714,7 @@
             after=after,
             limit=8,
         )
-        return [own] + [shift_y(v, k) for v, k in zip(parts, (1, -1, 2))]
+        return [own, shift_y(parts[2], 2), shift_y(parts[0], 1), shift_y(parts[1], -1)]
 
     normed_second_parts = half_sum(near, far)
     out_near, out_far = pl.pallas_call(

time: 286 us -> 285 us (level)
  starting transfers between devices: 95.7 us -> 89 us
  waiting for transfers between devices: 64.7 us -> 71.1 us
    ppermute x21, waiting for transfers between devices: 19.4 us -> 30.6 us  [shift_y(): return lax.ppermute(v, 'mp', [(i, (i + 2 * k) % MP) for i in range(MP)])]
    all_to_all x6, waiting for transfers between devices: 32.4 us -> 27.7 us  [exchange(): return lax.all_to_all(v, axis, split_axis=0, concat_axis=0, tiled=True)]
    ppermute x13, starting transfers between devices: 12.9 us -> 9.36 us  [swap_core(): return lax.ppermute(v, 'mp', [(i, i ^ 1) for i in range(MP)])]
  transfers between devices with their start and end apart: 45 -> 45, of which waited for: 20 -> 21; matrix products, arithmetic and copies ran while one was open for 1% -> 1% of each run, Pallas kernels for 26% -> 26%
where the time goes in v10:
time: 285 us; the launch traced here: 284 us
  Pallas kernels  94.7 us (33%)
  starting transfers between devices  89 us (31%)
  waiting for transfers between devices  71.1 us (25%)
  between operations  15.3 us (5%)
  local copies, waits for them, and re-layouts  11.8 us (4%)
    all_to_all x6, starting transfers between devices, exchange(): return lax.all_to_all(v, axis, split_axis=0, concat_axis=0, tiled=True)  49.6 us
    pallas_call x14, Pallas kernels, whole(): pl.pallas_call(bare, out_shape=[jax.ShapeDtypeStruct(s, d) for s, d in ou...  45.3 us
    ppermute x21, waiting for transfers between devices, shift_y(): return lax.ppermute(v, 'mp', [(i, (i + 2 * k) % MP) for i in range(MP)])  30.6 us
    all_to_all x6, waiting for transfers between devices, exchange(): return lax.all_to_all(v, axis, split_axis=0, concat_axis=0, tiled=True)  27.7 us
    ppermute x21, starting transfers between devices, shift_y(): return lax.ppermute(v, 'mp', [(i, (i + 2 * k) % MP) for i in range(MP)])  25.6 us
    pallas_call x1, Pallas kernels, body(): pl.pallas_call(gated, grid=(pl.cdiv(FP, 256),), out_shape=[jax.ShapeDtype...  18.3 us
    ppermute x13, waiting for transfers between devices, swap_core(): return lax.ppermute(v, 'mp', [(i, i ^ 1) for i in range(MP)])  12.7 us
    ppermute x13, starting transfers between devices, swap_core(): return lax.ppermute(v, 'mp', [(i, i ^ 1) for i in range(MP)])  9.36 us
  transfers between devices with their start and end apart: 45, of which 21 were waited for; matrix products, arithmetic and copies ran while one was open for 1% of the time, Pallas kernels for 26%

profile of v10, /device:TPU:1, one launch (start us, length us, event | category | flops | bytes accessed | tf_op | source)
XLA Modules:
  0.0 284.4 jit_solution(15927723997262572855)
XLA Ops:
  13.5 7.7 %all-to-all-start = ((bf16[16,176,256]{2,1,0:T(8,128)(2,1)}), bf16[16,176,256]{2,1,0:T(8,128)(2,1)S(1)}, u32[]{:S(2)}, u32[]{:S(2)}) async-start(bf16[16,176,256]{2,1,0:T(8,128)(2,1)} %broadcast_in_dim.18), calls=%async_computation | async-start | bytes 2883584 | tf_op jit(solution)/shard_map/all_to_all | solution.py:64
  28.8 19.3 %all-to-all-done.refs_4_ = bf16[16,176,256]{2,1,0:T(8,128)(2,1)S(1)} async-done(((bf16[16,176,256]{2,1,0:T(8,128)(2,1)}), bf16[16,176,256]{2,1,0:T(8,128)(2,1)S(1)}, u32[]{:S(2)}, u32[]{:S(2)}) %all-to-all-start) | async-done | bytes 1441824 | tf_op jit(solution)/shard_map/all_to_all | solution.py:64
  49.2 6.6 %all-to-all-start.1 = ((bf16[16,112,256]{2,1,0:T(8,128)(2,1)}), bf16[16,112,256]{2,1,0:T(8,128)(2,1)S(1)}, u32[]{:S(2)}, u32[]{:S(2)}) async-start(bf16[16,112,256]{2,1,0:T(8,128)(2,1)} %broadcast_in_dim.19), calls=%async_computation.1 | async-start | bytes 1835008 | tf_op jit(solution)/shard_map/all_to_all | solution.py:64
  61.1 4.3 %shard_map.331 = (bf16[512,1536]{1,0:T(8,128)(2,1)}, bf16[1536,512]{1,0:T(8,128)(2,1)}, bf16[64,1536]{1,0:T(8,128)(2,1)}, bf16[64,1536]{1,0:T(8,128)(2,1)}, bf16[256,1536]{1,0:T(8,128)(2,1)}) custom-call(s32[5]{0:T(128)} %stack.61.refs_0_.ids, bf16[512,1536]{1,0:T(8,128)(2,1)} %bitcast.56, bf16[512,1536]{1,0:T(8,128)(2,1)} %bitcast.50), custom_call_target="tpu_custom_call" | custom-call | flops 1 | bytes 1 | tf_op jit(solution)/shard_map/pallas_call | solution.py:92
  68.7 8.9 %shard_map.332 = (bf16[512,1536]{1,0:T(8,128)(2,1)}, bf16[512,512]{1,0:T(8,128)(2,1)}, bf16[8,256,256]{2,1,0:T(8,128)(2,1)}, f32[512,256]{1,0:T(8,128)}, bf16[1536,512]{1,0:T(8,128)(2,1)}, /*index=5*/f32[1,5120]{1,0:T(1,128)}) custom-call(s32[5]{0:T(128)} %stack.61.refs_0_.ids, bf16[512,1536]{1,0:T(8,128)(2,1)} %bitcast.51, ...), custom_call_target="tpu_custom_call" | custom-call | flops 1 | bytes 1 | tf_op jit(solution)/shard_map/pallas_call | solution.py:92
  77.6 16.1 %all-to-all-start.2 = ((bf16[8,256,256]{2,1,0:T(8,128)(2,1)}), bf16[8,256,256]{2,1,0:T(8,128)(2,1)S(1)}, u32[]{:S(2)}, u32[]{:S(2)}) async-start(bf16[8,256,256]{2,1,0:T(8,128)(2,1)} %get-tuple-element.93), calls=%async_computation.2 | async-start | bytes 2097152 | tf_op jit(solution)/shard_map/all_to_all | solution.py:64
  99.1 5.6 %shard_map.333 = (bf16[1536,1536]{1,0:T(8,128)(2,1)}, bf16[256,1536]{1,0:T(8,128)(2,1)}) custom-call(s32[5]{0:T(128)} %stack.61.refs_0_.ids, bf16[16,80,256]{2,1,0:T(8,128)(2,1)} %copy-done.23, bf16[16,80,256]{2,1,0:T(8,128)(2,1)} %collective-permute-done.4.refs_2_, bf16[16,80,256]{2,1,0:T(8,128)(2,1)} %collective-permute-done.5.refs_3_, ...), custom_call_target="tpu_custom_call" | custom-call | flops 1 | bytes 1 | tf_op jit(solution)/shard_map/pallas_call | solution.py:92
  104.7 4.2 %all-to-all-done.2.att.refs_1_ = bf16[8,256,256]{2,1,0:T(8,128)(2,1)S(1)} async-done(((bf16[8,256,256]{2,1,0:T(8,128)(2,1)}), bf16[8,256,256]{2,1,0:T(8,128)(2,1)S(1)}, u32[]{:S(2)}, u32[]{:S(2)}) %all-to-all-start.2) | async-done | bytes 1048608 | tf_op jit(solution)/shard_map/all_to_all | solution.py:64
  109.9 6.2 %shard_map.334 = (f32[64,1536]{1,0:T(8,128)}, bf16[256,1536]{1,0:T(8,128)(2,1)}) custom-call(s32[5]{0:T(128)} %stack.61.refs_0_.ids, bf16[8,256,256]{2,1,0:T(8,128)(2,1)} %copy-done.18, bf16[1536,1536]{1,0:T(8,128)(2,1)} %get-tuple-element.94.mixer, bf16[256,1536]{1,0:T(8,128)(2,1)} %get-tuple-element.95.tok, f32[1,5120]{1,0:T(1,128)} %get-tuple-element.96.vec), custom_call_target="tpu_custom_call" | custom-call | flops 1 | bytes 1 | tf_op jit(solution)/shard_map/pallas_call | solution.py:663
  120.0 18.3 %shard_map.335 = (bf16[512,1152]{1,0:T(8,128)(2,1)}, bf16[512,1152]{1,0:T(8,128)(2,1)}, bf16[512,1152]{1,0:T(8,128)(2,1)}, bf16[16,3,96,1152]{3,2,1,0:T(8,128)(2,1)}) custom-call(bf16[256,1536]{1,0:T(8,128)(2,1)} %get-tuple-element.97.near, bf16[256,1536]{1,0:T(8,128)(2,1)} %copy-done.26, bf16[512,1536]{1,0:T(8,128)(2,1)} %get-tuple-element.92.refs_6_.back, ...), custom_call_target="tpu_custom_call" | custom-call | flops 1 | bytes 1 | tf_op jit(solution)/shard_map/pallas_call | solution.py:685
  138.4 8.0 %shard_map.336 = (bf16[256,1536]{1,0:T(8,128)(2,1)}, bf16[256,1536]{1,0:T(8,128)(2,1)}) custom-call(bf16[512,1152]{1,0:T(8,128)(2,1)} %get-tuple-element.99.gate_grad, bf16[512,1152]{1,0:T(8,128)(2,1)} %get-tuple-element.100.up_grad, bf16[16,3,96,1152]{3,2,1,0:T(8,128)(2,1)} %bitcast.48), custom_call_target="tpu_custom_call" | custom-call | flops 1 | bytes 1 | tf_op jit(solution)/shard_map/pallas_call | solution.py:698
  153.8 5.2 %shard_map.338 = (bf16[256,1536]{1,0:T(8,128)(2,1)}, bf16[256,1536]{1,0:T(8,128)(2,1)}) custom-call(bf16[512,1152]{1,0:T(8,128)(2,1)} %get-tuple-element.109.act, bf16[16,3,96,1152]{3,2,1,0:T(8,128)(2,1)} %bitcast.49), custom_call_target="tpu_custom_call" | custom-call | flops 1 | bytes 1 | tf_op jit(solution)/shard_map/pallas_call | solution.py:720
  159.0 4.3 %collective-permute-done.14.refs_3_ = bf16[64,1536]{1,0:T(8,128)(2,1)S(1)} collective-permute-done((bf16[64,1536]{1,0:T(8,128)(2,1)S(1)}, bf16[64,1536]{1,0:T(8,128)(2,1)S(1)}, u32[]{:S(2)}, u32[]{:S(2)}) %collective-permute-start.14) | collective-permute-done | bytes 196640 | tf_op jit(solution)/shard_map/ppermute | solution.py:48
  172.0 5.1 %collective-permute-done.17 = bf16[64,1536]{1,0:T(8,128)(2,1)S(1)} collective-permute-done((bf16[64,1536]{1,0:T(8,128)(2,1)S(1)}, bf16[64,1536]{1,0:T(8,128)(2,1)S(1)}, u32[]{:S(2)}, u32[]{:S(2)}) %collective-permute-start.17) | collective-permute-done | bytes 196640 | tf_op jit(solution)/shard_map/ppermute | solution.py:48
  183.9 11.3 %shard_map.341 = (bf16[512,512]{1,0:T(8,128)(2,1)}, bf16[512,384]{1,0:T(8,128)(2,1)}, bf16[512,128]{1,0:T(8,128)(2,1)}, bf16[512,128]{1,0:T(8,128)(2,1)}, bf16[2...) custom-call(s32[5]{0:T(128)} %stack.61.refs_0_.ids, bf16[4,64,1536]{2,1,0:T(8,128)(2,1)} %copy-done.22, ...), custom_call_target="tpu_custom_call" | custom-call | flops 1 | bytes 1 | tf_op jit(solution)/shard_map/pallas_call | solution.py:92
  204.2 4.0 %all-to-all-start.3 = ((bf16[8,32,128]{2,1,0:T(8,128)(2,1)}), bf16[8,32,128]{2,1,0:T(8,128)(2,1)S(1)}, u32[]{:S(2)}, u32[]{:S(2)}) async-start(bf16[8,32,128]{2,1,0:T(8,128)(2,1)} %get-tuple-element.132), calls=%async_computation.3 | async-start | bytes 131072 | tf_op jit(solution)/shard_map/all_to_all | solution.py:64
  208.3 3.3 %shard_map.343.refs_7_ = bf16[16,80,256]{2,1,0:T(8,128)(2,1)} custom-call(s32[5]{0:T(128)} %stack.61.refs_0_.ids, bf16[8,256,256]{2,1,0:T(8,128)(2,1)} %copy-done.18, bf16[8,256,256]{2,1,0:T(8,128)(2,1)} %collective-permute-done.29.refs_2_, bf16[512,384]{1,0:T(8,128)(2,1)} %get-tuple-element.133.refs_3_, f32[64,1536]{1,0:T(8,128)} %copy-done.4), custom_call_target="tpu_custom_call" | custom-call | flops 1 | bytes 1 | tf_op jit(solution)/shard_map/pallas_call | solution.py:92
  213.9 3.6 %shard_map.344.refs_3_ = bf16[16,184,256]{2,1,0:T(8,128)(2,1)} custom-call(s32[5]{0:T(128)} %stack.61.refs_0_.ids, bf16[512,1536]{1,0:T(8,128)(2,1)} %get-tuple-element.127.refs_1_, bf16[512,512]{1,0:T(8,128)(2,1)} %get-tuple-element.128.refs_2_, bf16[512,128]{1,0:T(8,128)(2,1)} %copy-done.33, bf16[512,128]{1,0:T(8,128)(2,1)} %copy-done.34, ...), custom_call_target="tpu_custom_call" | custom-call | flops 1 | bytes 1 | tf_op jit(solution)/shard_map/pallas_call | solution.py:92
  217.6 6.6 %all-to-all-start.4 = ((bf16[16,184,256]{2,1,0:T(8,128)(2,1)}), bf16[16,184,256]{2,1,0:T(8,128)(2,1)}, u32[]{:S(2)}, u32[]{:S(2)}) async-start(bf16[16,184,256]{2,1,0:T(8,128)(2,1)} %shard_map.344.refs_3_), calls=%async_computation.4 | async-start | bytes 3014656 | tf_op jit(solution)/shard_map/all_to_all | solution.py:64
  231.9 4.2 %collective-permute-done.30.refs_3_ = bf16[64,1536]{1,0:T(8,128)(2,1)S(1)} collective-permute-done((bf16[64,1536]{1,0:T(8,128)(2,1)S(1)}, bf16[64,1536]{1,0:T(8,128)(2,1)S(1)}, u32[]{:S(2)}, u32[]{:S(2)}) %collective-permute-start.30) | collective-permute-done | bytes 196640 | tf_op jit(solution)/shard_map/ppermute | solution.py:48
  236.1 4.8 %collective-permute-done.31.refs_4_ = bf16[64,1536]{1,0:T(8,128)(2,1)S(1)} collective-permute-done((bf16[64,1536]{1,0:T(8,128)(2,1)S(1)}, bf16[64,1536]{1,0:T(8,128)(2,1)S(1)}, u32[]{:S(2)}, u32[]{:S(2)}) %collective-permute-start.31) | collective-permute-done | bytes 196640 | tf_op jit(solution)/shard_map/ppermute | solution.py:48
  248.3 8.6 %all-to-all-start.5 = ((f32[128,1,128]{2,1,0:T(1,128)}), f32[128,1,128]{2,1,0:T(1,128)S(1)}, u32[]{:S(2)}, u32[]{:S(2)}) async-start(f32[128,1,128]{2,1,0:T(1,128)} %get-tuple-element.141), calls=%async_computation.5 | async-start | bytes 131072 | tf_op jit(solution)/shard_map/all_to_all | solution.py:64
  256.9 6.5 %collective-permute-done.34.p2.refs_3_ = bf16[2,64,1536]{2,1,0:T(8,128)(2,1)S(1)} collective-permute-done((bf16[2,64,1536]{2,1,0:T(8,128)(2,1)S(1)}, bf16[2,64,1536]{2,1,0:T(8,128)(2,1)S(1)}, u32[]{:S(2)}, u32[]{:S(2)}) %collective-permute-start.34) | collective-permute-done | bytes 393248 | tf_op jit(solution)/shard_map/ppermute | solution.py:48
  268.4 6.7 %shard_map.351 = (f32[1,128]{1,0:T(1,128)}, f32[96,256]{1,0:T(8,128)}, f32[96,256]{1,0:T(8,128)}, f32[96,256]{1,0:T(8,128)}, f32[96,192]{1,0:T(8,128)}, /*index=...) custom-call(f32[128,1,128]{2,1,0:T(1,128)} %copy-done.9, ...), custom_call_target="tpu_custom_call" | custom-call | flops 1 | bytes 1 | tf_op jit(solution)/shard_map/pallas_call | solution.py:841
  (200 shorter events, 89.5 us)
Async XLA Ops:
  7.2 111.9 %all-gather.3.cloned.1.call-start = ((), (), s32[]{:S(2)}) async-start(), calls=%async_computation.7 | async-start | bytes 11280384 | tf_op jit(solution)/shard_map/all_gather | solution.py:608
  13.5 34.6 %all-to-all-start = ((bf16[16,176,256]{2,1,0:T(8,128)(2,1)}), bf16[16,176,256]{2,1,0:T(8,128)(2,1)S(1)}, u32[]{:S(2)}, u32[]{:S(2)}) async-start(bf16[16,176,256]{2,1,0:T(8,128)(2,1)} %broadcast_in_dim.18), calls=%async_computation | async-start | bytes 2883584 | tf_op jit(solution)/shard_map/all_to_all | solution.py:64
  49.2 18.5 %all-to-all-start.1 = ((bf16[16,112,256]{2,1,0:T(8,128)(2,1)}), bf16[16,112,256]{2,1,0:T(8,128)(2,1)S(1)}, u32[]{:S(2)}, u32[]{:S(2)}) async-start(bf16[16,112,256]{2,1,0:T(8,128)(2,1)} %broadcast_in_dim.19), calls=%async_computation.1 | async-start | bytes 1835008 | tf_op jit(solution)/shard_map/all_to_all | solution.py:64
  55.9 38.0 %collective-permute-start.6 = (bf16[16,80,256]{2,1,0:T(8,128)(2,1)S(1)}, bf16[16,80,256]{2,1,0:T(8,128)(2,1)}, u32[]{:S(2)}, u32[]{:S(2)}) collective-permute-start(bf16[16,80,256]{2,1,0:T(8,128)(2,1)S(1)} %slice.110.refs_1_), channel_id=1, source_target_pairs={{0,6},{1,7},{2,0},{3,1},{4,2},{5,3},{6,4},{7,5},{8,14},{9,15},{10,... | collective-permute-start | bytes 1966088 | tf_op jit(solution)/shard_map/ppermute | solution.py:48
  58.8 35.5 %collective-permute-start.4 = (bf16[16,80,256]{2,1,0:T(8,128)(2,1)S(1)}, bf16[16,80,256]{2,1,0:T(8,128)(2,1)}, u32[]{:S(2)}, u32[]{:S(2)}) collective-permute-start(bf16[16,80,256]{2,1,0:T(8,128)(2,1)S(1)} %slice.110.refs_1_), channel_id=1, source_target_pairs={{0,4},{1,5},{2,6},{3,7},{4,0},{5,1},{6,2},{7,3},{8,12},{9,13},{10,... | collective-permute-start | bytes 1966088 | tf_op jit(solution)/shard_map/ppermute | solution.py:48
  59.1 35.4 %collective-permute-start.5 = (bf16[16,80,256]{2,1,0:T(8,128)(2,1)S(1)}, bf16[16,80,256]{2,1,0:T(8,128)(2,1)}, u32[]{:S(2)}, u32[]{:S(2)}) collective-permute-start(bf16[16,80,256]{2,1,0:T(8,128)(2,1)S(1)} %slice.110.refs_1_), channel_id=1, source_target_pairs={{0,2},{1,3},{2,4},{3,5},{4,6},{5,7},{6,0},{7,1},{8,10},{9,11},{10,... | collective-permute-start | bytes 1966088 | tf_op jit(solution)/shard_map/ppermute | solution.py:48
  77.6 31.2 %all-to-all-start.2 = ((bf16[8,256,256]{2,1,0:T(8,128)(2,1)}), bf16[8,256,256]{2,1,0:T(8,128)(2,1)S(1)}, u32[]{:S(2)}, u32[]{:S(2)}) async-start(bf16[8,256,256]{2,1,0:T(8,128)(2,1)} %get-tuple-element.93), calls=%async_computation.2 | async-start | bytes 2097152 | tf_op jit(solution)/shard_map/all_to_all | solution.py:64
  93.8 151.7 %reduce-scatter.4.cloned.1.call-start = ((), (), s32[]{:S(2)}) async-start(), calls=%async_computation.8 | async-start | bytes 11280384
  151.1 12.2 %collective-permute-start.14 = (bf16[64,1536]{1,0:T(8,128)(2,1)S(1)}, bf16[64,1536]{1,0:T(8,128)(2,1)S(1)}, u32[]{:S(2)}, u32[]{:S(2)}) collective-permute-start(bf16[64,1536]{1,0:T(8,128)(2,1)S(1)} %get-tuple-element.105), channel_id=1, source_target_pairs={{0,2},{1,3},{2,4},{3,5},{4,6},{5,7},{6,0},{7,1},{8,10},{9,11},{10,... | collective-permute-start | bytes 589832 | tf_op jit(solution)/shard_map/ppermute | solution.py:48
  152.3 11.1 %collective-permute-start.15 = (bf16[64,1536]{1,0:T(8,128)(2,1)S(1)}, bf16[64,1536]{1,0:T(8,128)(2,1)S(1)}, u32[]{:S(2)}, u32[]{:S(2)}) collective-permute-start(bf16[64,1536]{1,0:T(8,128)(2,1)S(1)} %get-tuple-element.106), channel_id=1, source_target_pairs={{0,6},{1,7},{2,0},{3,1},{4,2},{5,3},{6,4},{7,5},{8,14},{9,15},{10,... | collective-permute-start | bytes 589832 | tf_op jit(solution)/shard_map/ppermute | solution.py:48
  164.9 12.2 %collective-permute-start.17 = (bf16[64,1536]{1,0:T(8,128)(2,1)S(1)}, bf16[64,1536]{1,0:T(8,128)(2,1)S(1)}, u32[]{:S(2)}, u32[]{:S(2)}) collective-permute-start(bf16[64,1536]{1,0:T(8,128)(2,1)S(1)} %get-tuple-element.111), channel_id=1, source_target_pairs={{0,2},{1,3},{2,4},{3,5},{4,6},{5,7},{6,0},{7,1},{8,10},{9,11},{10,... | collective-permute-start | bytes 589832 | tf_op jit(solution)/shard_map/ppermute | solution.py:48
  166.1 11.1 %collective-permute-start.18 = (bf16[64,1536]{1,0:T(8,128)(2,1)S(1)}, bf16[64,1536]{1,0:T(8,128)(2,1)S(1)}, u32[]{:S(2)}, u32[]{:S(2)}) collective-permute-start(bf16[64,1536]{1,0:T(8,128)(2,1)S(1)} %get-tuple-element.111), channel_id=1, source_target_pairs={{0,6},{1,7},{2,0},{3,1},{4,2},{5,3},{6,4},{7,5},{8,14},{9,15},{10,... | collective-permute-start | bytes 589832 | tf_op jit(solution)/shard_map/ppermute | solution.py:48
  177.7 30.5 %collective-permute-start.29 = (bf16[8,256,256]{2,1,0:T(8,128)(2,1)S(1)}, bf16[8,256,256]{2,1,0:T(8,128)(2,1)}, u32[]{:S(2)}, u32[]{:S(2)}) collective-permute-start(bf16[8,256,256]{2,1,0:T(8,128)(2,1)S(1)} %copy-done.19), channel_id=1, source_target_pairs={{0,1},{1,0},{2,3},{3,2},{4,5},{5,4},{6,7},{7,6},{8,9},{9,8},{10,11... | collective-permute-start | bytes 3145736 | tf_op jit(solution)/shard_map/ppermute | solution.py:60
  179.3 16.9 %collective-permute-start.22 = (bf16[64,1536]{1,0:T(8,128)(2,1)S(1)}, bf16[64,1536]{1,0:T(8,128)(2,1)S(1)}, u32[]{:S(2)}, u32[]{:S(2)}) collective-permute-start(bf16[64,1536]{1,0:T(8,128)(2,1)S(1)} %get-tuple-element.121), channel_id=1, source_target_pairs={{0,4},{1,5},{2,6},{3,7},{4,0},{5,1},{6,2},{7,3},{8,12},{9,13},{10,... | collective-permute-start | bytes 589832 | tf_op jit(solution)/shard_map/ppermute | solution.py:48
  180.4 15.9 %collective-permute-start.23 = (bf16[64,1536]{1,0:T(8,128)(2,1)S(1)}, bf16[64,1536]{1,0:T(8,128)(2,1)S(1)}, u32[]{:S(2)}, u32[]{:S(2)}) collective-permute-start(bf16[64,1536]{1,0:T(8,128)(2,1)S(1)} %get-tuple-element.122), channel_id=1, source_target_pairs={{0,2},{1,3},{2,4},{3,5},{4,6},{5,7},{6,0},{7,1},{8,10},{9,11},{10,... | collective-permute-start | bytes 589832 | tf_op jit(solution)/shard_map/ppermute | solution.py:48
  180.9 15.4 %collective-permute-start.24 = (bf16[64,1536]{1,0:T(8,128)(2,1)S(1)}, bf16[64,1536]{1,0:T(8,128)(2,1)S(1)}, u32[]{:S(2)}, u32[]{:S(2)}) collective-permute-start(bf16[64,1536]{1,0:T(8,128)(2,1)S(1)} %get-tuple-element.123), channel_id=1, source_target_pairs={{0,6},{1,7},{2,0},{3,1},{4,2},{5,3},{6,4},{7,5},{8,14},{9,15},{10,... | collective-permute-start | bytes 589832 | tf_op jit(solution)/shard_map/ppermute | solution.py:48
  199.9 13.3 %collective-permute-start.28 = (bf16[512,256]{1,0:T(8,128)(2,1)S(1)}, bf16[512,256]{1,0:T(8,128)(2,1)S(1)}, u32[]{:S(2)}, u32[]{:S(2)}) collective-permute-start(bf16[512,256]{1,0:T(8,128)(2,1)S(1)} %get-tuple-element.131), channel_id=1, source_target_pairs={{2,6},{3,7},{10,14},{11,15},{18,22},{19,23},{26,30},{27,31},{34,38... | collective-permute-start | bytes 786440 | tf_op jit(solution)/shard_map/ppermute | solution.py:56
  200.5 12.6 %collective-permute-start.26 = (bf16[512,128]{1,0:T(8,128)(2,1)S(1)}, bf16[512,128]{1,0:T(8,128)(2,1)S(1)}, u32[]{:S(2)}, u32[]{:S(2)}) collective-permute-start(bf16[512,128]{1,0:T(8,128)(2,1)S(1)} %get-tuple-element.129), channel_id=1, source_target_pairs={{0,6},{1,7},{8,14},{9,15},{16,22},{17,23},{24,30},{25,31},{32,38},... | collective-permute-start | bytes 393224 | tf_op jit(solution)/shard_map/ppermute | solution.py:56
  217.6 27.9 %all-to-all-start.4 = ((bf16[16,184,256]{2,1,0:T(8,128)(2,1)}), bf16[16,184,256]{2,1,0:T(8,128)(2,1)}, u32[]{:S(2)}, u32[]{:S(2)}) async-start(bf16[16,184,256]{2,1,0:T(8,128)(2,1)} %shard_map.344.refs_3_), calls=%async_computation.4 | async-start | bytes 3014656 | tf_op jit(solution)/shard_map/all_to_all | solution.py:64
  229.2 11.7 %collective-permute-start.31 = (bf16[64,1536]{1,0:T(8,128)(2,1)S(1)}, bf16[64,1536]{1,0:T(8,128)(2,1)S(1)}, u32[]{:S(2)}, u32[]{:S(2)}) collective-permute-start(bf16[64,1536]{1,0:T(8,128)(2,1)S(1)} %get-tuple-element.136), channel_id=1, source_target_pairs={{0,2},{1,3},{2,4},{3,5},{4,6},{5,7},{6,0},{7,1},{8,10},{9,11},{10,... | collective-permute-start | bytes 589832 | tf_op jit(solution)/shard_map/ppermute | solution.py:48
  241.9 15.0 %collective-permute-start.33 = (bf16[2,64,1536]{2,1,0:T(8,128)(2,1)S(1)}, bf16[2,64,1536]{2,1,0:T(8,128)(2,1)S(1)}, u32[]{:S(2)}, u32[]{:S(2)}) collective-permute-start(bf16[2,64,1536]{2,1,0:T(8,128)(2,1)S(1)} %shard_map.346.p0.refs_1_), channel_id=1, source_target_pairs={{0,4},{1,5},{2,6},{3,7},{4,0},{5,1},{6,2},{7,3},{8,12},{9,13},{10,... | collective-permute-start | bytes 1179656 | tf_op jit(solution)/shard_map/ppermute | solution.py:48
  242.8 20.6 %collective-permute-start.34 = (bf16[2,64,1536]{2,1,0:T(8,128)(2,1)S(1)}, bf16[2,64,1536]{2,1,0:T(8,128)(2,1)S(1)}, u32[]{:S(2)}, u32[]{:S(2)}) collective-permute-start(bf16[2,64,1536]{2,1,0:T(8,128)(2,1)S(1)} %shard_map.346.p0.refs_1_), channel_id=1, source_target_pairs={{0,2},{1,3},{2,4},{3,5},{4,6},{5,7},{6,0},{7,1},{8,10},{9,11},{10,... | collective-permute-start | bytes 1179656 | tf_op jit(solution)/shard_map/ppermute | solution.py:48
  244.6 18.8 %collective-permute-start.35 = (bf16[2,64,1536]{2,1,0:T(8,128)(2,1)S(1)}, bf16[2,64,1536]{2,1,0:T(8,128)(2,1)S(1)}, u32[]{:S(2)}, u32[]{:S(2)}) collective-permute-start(bf16[2,64,1536]{2,1,0:T(8,128)(2,1)S(1)} %shard_map.346.p0.refs_1_), channel_id=1, source_target_pairs={{0,6},{1,7},{2,0},{3,1},{4,2},{5,3},{6,4},{7,5},{8,14},{9,15},{10,... | collective-permute-start | bytes 1179656 | tf_op jit(solution)/shard_map/ppermute | solution.py:48
  248.3 18.0 %all-to-all-start.5 = ((f32[128,1,128]{2,1,0:T(1,128)}), f32[128,1,128]{2,1,0:T(1,128)S(1)}, u32[]{:S(2)}, u32[]{:S(2)}) async-start(f32[128,1,128]{2,1,0:T(1,128)} %get-tuple-element.141), calls=%async_computation.5 | async-start | bytes 131072 | tf_op jit(solution)/shard_map/all_to_all | solution.py:64
  (58 other events, 389.6 us)
Sparse Core Ops, SparseCore 0:
  10.2 103.7 all-gather.2
  138.5 88.5 reduce-scatter.3
